TPU v7x, 32 devices: a whole 2x2x4 slice. The times are simulated.
32 devices in a mesh: dp: 4 (over z), seq: 8 (over y, x, core).
Axes of the slice: x: 2, y: 2, z: 4, core: 2. Of those that a mesh axis runs over, the one named last changes fastest.
Arguments:
- inputs: bfloat16 [4096, 1536], P(('dp', 'seq')), may hold values from -6 to 6
- output_grad: bfloat16 [4096, 1536], P(('dp', 'seq')), may hold values from -6 to 6
- document_starts: int32 [4, 4], P('dp'), may hold values from 0 to 1023, as said below
- joined_weight: float32 [1536, 2048], P(('dp', 'seq')), may hold values from -0.15625 to 0.15625
- out_weight: float32 [1536, 1536], P(('dp', 'seq')), may hold values from -1.25 to 1.25
- units_weight: float32 [8960, 3, 1536], P(('dp', 'seq')), may hold values from -0.15625 to 0.15625
- small_params: float32 [256, 20], P(('dp', 'seq')), may hold values from -1 to 2
- joined_first: float32 [1536, 2048], P(('dp', 'seq')), may hold values from -160 to 160
- joined_second: float32 [1536, 2048], P(('dp', 'seq')), may hold values from 1724.6316 to 13797.053
- out_first: float32 [1536, 1536], P(('dp', 'seq')), may hold values from -7 to 7
- out_second: float32 [1536, 1536], P(('dp', 'seq')), may hold values from 2.994152 to 23.953217
- units_first: float32 [8960, 3, 1536], P(('dp', 'seq')), may hold values from -20 to 20
- units_second: float32 [8960, 3, 1536], P(('dp', 'seq')), may hold values from 26.947369 to 215.57895
- small_first: float32 [256, 20], P(('dp', 'seq')), may hold values from -80 to 80
- small_second: float32 [256, 20], P(('dp', 'seq')), may hold values from 431.1579 to 3449.2632
Outputs:
- block_output: bfloat16 [4096, 1536], P(('dp', 'seq'))
- input_grad: float32 [4096, 1536], P(('dp', 'seq'))
- joined_next: float32 [1536, 2048], P(('dp', 'seq'))
- joined_first_next: float32 [1536, 2048], P(('dp', 'seq'))
- joined_second_next: float32 [1536, 2048], P(('dp', 'seq'))
- joined_low: bfloat16 [1536, 2048], P(('dp', 'seq'))
- out_next: float32 [1536, 1536], P(('dp', 'seq'))
- out_first_next: float32 [1536, 1536], P(('dp', 'seq'))
- out_second_next: float32 [1536, 1536], P(('dp', 'seq'))
- out_low: bfloat16 [1536, 1536], P(('dp', 'seq'))
- units_next: float32 [8960, 3, 1536], P(('dp', 'seq'))
- units_first_next: float32 [8960, 3, 1536], P(('dp', 'seq'))
- units_second_next: float32 [8960, 3, 1536], P(('dp', 'seq'))
- units_low: bfloat16 [8960, 3, 1536], P(('dp', 'seq'))
- small_next: float32 [256, 20], P(('dp', 'seq'))
- small_first_next: float32 [256, 20], P(('dp', 'seq'))
- small_second_next: float32 [256, 20], P(('dp', 'seq'))
- small_low: bfloat16 [256, 20], P(('dp', 'seq'))
Inputs may be any that keep to these rules, and one draw needn't show every extreme that they name: `document_starts`: within a row the starts rise strictly and the first is 0; in each row one document begins among the group's first 128 tokens and ends among its last 128.
All inputs are finite; a program needn't handle non-finite values.
Results may differ from a plain program's by a relative error of at most 0.02.
Values may be sent and summed in bfloat16 or wider, within the bound.
No kernel may reach another device: no remote copies, remote signals or barrier semaphores. Data moves between devices by JAX's collectives and lax.ppermute only.
A program may use at most 448 MiB of HBM per device.

v0:
```python
import math

import jax
import jax.numpy as jnp
from jax import lax
from jax.sharding import PartitionSpec as P

D = 1536
HEADS = 12
KV_HEADS = 2
HEAD_DIM = 128
FF = 8960
BLOCK = 256
STEP = 5
QW = 1536
KW = 256
QKV = 2048


NORM_EPS = 1e-06
ROPE_BASE = 1000000.0
BETA_ONE = 0.9
BETA_TWO = 0.95
ADAM_EPS = 1e-08
DECAY = 0.1


def norm_scale(rows):
    return lax.rsqrt(jnp.mean(rows * rows, axis=1, keepdims=True) + NORM_EPS)


def unpack_small(small):
    gain_cols = D // KW
    group = HEADS // KV_HEADS
    gain_one = small[:, :gain_cols].reshape(D)
    gain_two = small[:, gain_cols : 2 * gain_cols].reshape(D)
    query_bias = small[:, 2 * gain_cols : 2 * gain_cols + group].reshape(KV_HEADS, HEAD_DIM, group)
    query_bias = jnp.transpose(query_bias, (0, 2, 1)).reshape(QW)
    key_bias = small[:, 2 * gain_cols + group]
    value_bias = small[:, 2 * gain_cols + group + 1]
    return (gain_one, gain_two, jnp.concatenate([query_bias, key_bias, value_bias]))


def pack_small(gain_one, gain_two, bias):
    gain_cols = D // KW
    group = HEADS // KV_HEADS
    query_part = jnp.transpose(bias[:QW].reshape(KV_HEADS, group, HEAD_DIM), (0, 2, 1)).reshape(
        KW, group
    )
    return jnp.concatenate(
        [
            gain_one.reshape(KW, gain_cols),
            gain_two.reshape(KW, gain_cols),
            query_part,
            bias[QW : QW + KW][:, None],
            bias[QW + KW :][:, None],
        ],
        axis=1,
    )


def layout(starts_row, first, count):
    places = first + jnp.arange(count, dtype=jnp.int32)
    before = starts_row[None, :] <= places[:, None]
    documents = jnp.sum(before.astype(jnp.int32), axis=1) - 1
    begin = jnp.max(jnp.where(before, starts_row[None, :], 0), axis=1)
    offset = places - begin
    return (documents, offset // BLOCK, offset)


def turning(offset):
    half = HEAD_DIM // 2
    frequency = ROPE_BASE ** (-(2.0 * jnp.arange(half, dtype=jnp.float32)) / HEAD_DIM)
    angle = offset.astype(jnp.float32)[:, None] * frequency[None, :]
    angle = jnp.concatenate([angle, angle], axis=1)
    return (jnp.cos(angle)[:, None, :], jnp.sin(angle)[:, None, :])


def rotate(values, cosine, sine):
    half = values.shape[-1] // 2
    turned = jnp.concatenate([-values[..., half:], values[..., :half]], axis=-1)
    return values * cosine + turned * sine


def rotate_back(grads, cosine, sine):
    half = grads.shape[-1] // 2
    moved = grads * sine
    turned = jnp.concatenate([moved[..., half:], -moved[..., :half]], axis=-1)
    return grads * cosine + turned


def optimizer_step(weight, grad, first, second, rate, decay):
    first = BETA_ONE * first + (1.0 - BETA_ONE) * grad
    second = BETA_TWO * second + (1.0 - BETA_TWO) * grad * grad
    fixed_first = first / (1.0 - BETA_ONE**STEP)
    fixed_second = second / (1.0 - BETA_TWO**STEP)
    weight = weight - rate * (fixed_first / (jnp.sqrt(fixed_second) + ADAM_EPS) + decay * weight)
    return (weight, first, second, weight.astype(jnp.bfloat16))


def unit_forward(normed_rows, units):
    gate = jnp.einsum("td,ud->tu", normed_rows, units[:, 0, :], preferred_element_type=jnp.float32)
    up = jnp.einsum("td,ud->tu", normed_rows, units[:, 1, :], preferred_element_type=jnp.float32)
    return (gate, up)


def unit_backward(normed_rows, back_rows, units):
    gate, up = unit_forward(normed_rows, units)
    sigma = jax.nn.sigmoid(gate)
    active = gate * sigma
    hidden = (active * up).astype(jnp.bfloat16)
    pulled = jnp.einsum("td,ud->tu", back_rows, units[:, 2, :], preferred_element_type=jnp.float32)
    gate_grad = (pulled * up * sigma * (1.0 + gate * (1.0 - sigma))).astype(jnp.bfloat16)
    up_grad = (pulled * active).astype(jnp.bfloat16)
    return (hidden, gate_grad, up_grad)


def body(
    inputs,
    output_grad,
    document_starts,
    joined_weight,
    out_weight,
    units_weight,
    small_params,
    joined_first,
    joined_second,
    out_first,
    out_second,
    units_first,
    units_second,
    small_first,
    small_second,
):
    count = inputs.shape[0]
    seq_count = lax.axis_size("seq")
    dp_count = lax.axis_size("dp")
    seq_index = lax.axis_index("seq")
    group_len = count * seq_count
    first = seq_index * count
    starts_row = document_starts[0]
    group = HEADS // KV_HEADS
    scale = HEAD_DIM ** (-0.5)
    units_half = units_weight.astype(jnp.bfloat16)
    full_joined, full_out, full_small = (
        lax.all_gather(joined_weight.astype(jnp.bfloat16), ("dp", "seq"), axis=0, tiled=True),
        lax.all_gather(out_weight.astype(jnp.bfloat16), ("dp", "seq"), axis=0, tiled=True),
        lax.all_gather(small_params.astype(jnp.bfloat16), ("dp", "seq"), axis=0, tiled=True),
    )
    gain_one, gain_two, bias = unpack_small(full_small.astype(jnp.float32))
    rows = inputs.astype(jnp.float32)
    scale_one = norm_scale(rows)
    normed_one = (rows * scale_one * gain_one).astype(jnp.bfloat16)
    mixed = jnp.dot(normed_one, full_joined, preferred_element_type=jnp.float32) + bias
    documents, blocks, offset = layout(starts_row, first, count)
    cosine, sine = turning(offset)
    query = rotate(mixed[:, :QW].reshape(count, HEADS, HEAD_DIM), cosine, sine).astype(jnp.bfloat16)
    query = query.reshape(count, KV_HEADS, group, HEAD_DIM)
    keys_own = rotate(
        mixed[:, QW : QW + KW].reshape(count, KV_HEADS, HEAD_DIM), cosine, sine
    ).astype(jnp.bfloat16)
    values_own = mixed[:, QW + KW :].reshape(count, KV_HEADS, HEAD_DIM).astype(jnp.bfloat16)
    keys_all, values_all = (
        lax.all_gather(keys_own, "seq", axis=0, tiled=True),
        lax.all_gather(values_own, "seq", axis=0, tiled=True),
    )
    all_documents, all_blocks, unused_offset = layout(starts_row, 0, group_len)
    span = min(512, group_len)
    turns = group_len // span

    def key_block(index):
        start = index * span
        keys = lax.dynamic_slice_in_dim(keys_all, start, span, 0)
        values = lax.dynamic_slice_in_dim(values_all, start, span, 0)
        key_documents = lax.dynamic_slice_in_dim(all_documents, start, span, 0)
        key_blocks = lax.dynamic_slice_in_dim(all_blocks, start, span, 0)
        seen = (documents[:, None] == key_documents[None, :]) & (
            key_blocks[None, :] <= blocks[:, None]
        )
        return (keys, values, seen)

    def block_scores(keys):
        return jnp.einsum("qcgd,kcd->cgqk", query, keys, preferred_element_type=jnp.float32) * scale

    def stat_step(index, carry):
        keys, values, seen = key_block(index)

        def stat_compute(inner):
            highest, total = inner
            scores = jnp.where(seen, block_scores(keys), -1e30)
            new_high = jnp.maximum(highest, jnp.max(scores, axis=-1))
            grown = jnp.sum(jnp.where(seen, jnp.exp(scores - new_high[..., None]), 0.0), axis=-1)
            return (new_high, total * jnp.exp(highest - new_high) + grown)

        return lax.cond(jnp.any(seen), stat_compute, lambda inner: inner, carry)

    start_high = jnp.full((KV_HEADS, group, count), -1e30, jnp.float32)
    start_total = jnp.zeros((KV_HEADS, group, count), jnp.float32)
    highest, total = lax.fori_loop(0, turns, stat_step, (start_high, start_total))
    log_total = highest + jnp.log(total)

    def out_step(index, carry):
        keys, values, seen = key_block(index)

        def out_compute(inner):
            weights = jnp.where(
                seen, jnp.exp(block_scores(keys) - log_total[..., None]), 0.0
            ).astype(jnp.bfloat16)
            return inner + jnp.einsum(
                "cgqk,kcd->qcgd", weights, values, preferred_element_type=jnp.float32
            )

        return lax.cond(jnp.any(seen), out_compute, lambda inner: inner, carry)

    attended = lax.fori_loop(
        0, turns, out_step, jnp.zeros((count, KV_HEADS, group, HEAD_DIM), jnp.float32)
    )
    attended_low = attended.reshape(count, QW).astype(jnp.bfloat16)
    middle = rows + jnp.dot(attended_low, full_out, preferred_element_type=jnp.float32)
    scale_two = norm_scale(middle)
    normed_two = (middle * scale_two * gain_two).astype(jnp.bfloat16)
    piece = lax.all_gather(units_half, ("dp", "seq"), axis=0, tiled=True)
    gate, up = unit_forward(normed_two, piece)
    hidden = (jax.nn.silu(gate) * up).astype(jnp.bfloat16)
    branch_two = jnp.einsum("tu,ud->td", hidden, piece[:, 2, :], preferred_element_type=jnp.float32)
    piece = lax.all_gather(units_half, ("dp", "seq"), axis=0, tiled=True)
    hidden, gate_grad, up_grad = unit_backward(normed_two, output_grad, piece)
    normed_grad = jnp.einsum(
        "tu,ud->td", gate_grad, piece[:, 0, :], preferred_element_type=jnp.float32
    )
    normed_grad = normed_grad + jnp.einsum(
        "tu,ud->td", up_grad, piece[:, 1, :], preferred_element_type=jnp.float32
    )
    hidden_all = hidden
    gate_all = gate_grad
    up_all = up_grad
    normed_grad, hidden_all, gate_all, up_all = (normed_grad, hidden_all, gate_all, up_all)
    block_output = (middle + branch_two).astype(jnp.bfloat16)
    unit_width = FF // (dp_count * seq_count)
    split_shape = (count, dp_count, seq_count, unit_width)
    hidden_columns, gate_columns, up_columns = (
        lax.all_to_all(
            hidden_all.reshape(split_shape), "seq", split_axis=2, concat_axis=0, tiled=True
        ),
        lax.all_to_all(
            gate_all.reshape(split_shape), "seq", split_axis=2, concat_axis=0, tiled=True
        ),
        lax.all_to_all(up_all.reshape(split_shape), "seq", split_axis=2, concat_axis=0, tiled=True),
    )
    column_shape = (group_len, dp_count, unit_width)
    hidden_columns = hidden_columns.reshape(column_shape)
    gate_columns = gate_columns.reshape(column_shape)
    up_columns = up_columns.reshape(column_shape)
    weighted_two = gain_two * normed_grad
    middle_grad = (
        output_grad.astype(jnp.float32)
        + scale_two * weighted_two
        - middle * scale_two**3 * jnp.mean(weighted_two * middle, axis=1, keepdims=True)
    )
    gain_two_grad = jnp.sum(normed_grad * middle * scale_two, axis=0)
    branch_grad = middle_grad.astype(jnp.bfloat16)
    attended_grad = jnp.einsum(
        "td,ed->te", branch_grad, full_out, preferred_element_type=jnp.float32
    )
    attended_grad = attended_grad.astype(jnp.bfloat16).reshape(count, KV_HEADS, group, HEAD_DIM)
    delta = jnp.einsum("qcgd,qcgd->cgq", attended_grad.astype(jnp.float32), attended)

    def back_step(index, carry):
        keys, values, seen = key_block(index)
        start = index * span

        def back_compute(inner):
            query_grad, key_grads, value_grads = inner
            weights = jnp.where(seen, jnp.exp(block_scores(keys) - log_total[..., None]), 0.0)
            pulled = jnp.einsum(
                "qcgd,kcd->cgqk", attended_grad, values, preferred_element_type=jnp.float32
            )
            score_grad = (weights * (pulled - delta[..., None])).astype(jnp.bfloat16)
            query_grad = query_grad + jnp.einsum(
                "cgqk,kcd->qcgd", score_grad, keys, preferred_element_type=jnp.float32
            )
            key_part = jnp.einsum(
                "cgqk,qcgd->kcd", score_grad, query, preferred_element_type=jnp.float32
            )
            value_part = jnp.einsum(
                "cgqk,qcgd->kcd",
                weights.astype(jnp.bfloat16),
                attended_grad,
                preferred_element_type=jnp.float32,
            )
            key_grads = lax.dynamic_update_slice_in_dim(key_grads, key_part, start, 0)
            value_grads = lax.dynamic_update_slice_in_dim(value_grads, value_part, start, 0)
            return (query_grad, key_grads, value_grads)

        return lax.cond(jnp.any(seen), back_compute, lambda inner: inner, carry)

    key_zero = jnp.zeros((group_len, KV_HEADS, HEAD_DIM), jnp.float32)
    query_grad, key_grads, value_grads = lax.fori_loop(
        0,
        turns,
        back_step,
        (jnp.zeros((count, KV_HEADS, group, HEAD_DIM), jnp.float32), key_zero, key_zero),
    )
    key_sum, value_sum = (
        lax.psum_scatter(
            key_grads.astype(jnp.bfloat16), "seq", scatter_dimension=0, tiled=True
        ).astype(jnp.float32),
        lax.psum_scatter(
            value_grads.astype(jnp.bfloat16), "seq", scatter_dimension=0, tiled=True
        ).astype(jnp.float32),
    )
    query_pre = rotate_back(
        (query_grad * scale).reshape(count, HEADS, HEAD_DIM), cosine, sine
    ).reshape(count, QW)
    key_pre = rotate_back(key_sum * scale, cosine, sine).reshape(count, KW)
    mixed_grad = jnp.concatenate([query_pre, key_pre, value_sum.reshape(count, KW)], axis=1).astype(
        jnp.bfloat16
    )
    bias_grad = jnp.sum(mixed_grad.astype(jnp.float32), axis=0)
    normed_one_grad = jnp.einsum(
        "te,de->td", mixed_grad, full_joined, preferred_element_type=jnp.float32
    )
    weighted_one = gain_one * normed_one_grad
    input_grad = (
        middle_grad
        + scale_one * weighted_one
        - rows * scale_one**3 * jnp.mean(weighted_one * rows, axis=1, keepdims=True)
    )
    gain_one_grad = jnp.sum(normed_one_grad * rows * scale_one, axis=0)
    small_grad_term = pack_small(gain_one_grad, gain_two_grad, bias_grad)
    feature_width = D // (dp_count * seq_count)
    query_width = QW // (dp_count * seq_count)

    def own_columns(piece, width):
        shaped = piece.reshape(piece.shape[0], dp_count, seq_count, width)
        return lax.dynamic_index_in_dim(shaped, seq_index, 2, keepdims=False)

    normed_piece = lax.all_gather(normed_one, "seq", axis=0, tiled=True)
    attended_piece = lax.all_gather(attended_low, "seq", axis=0, tiled=True)
    mixed_piece = lax.all_gather(mixed_grad, "seq", axis=0, tiled=True)
    branch_piece = lax.all_gather(branch_grad, "seq", axis=0, tiled=True)
    second_piece = lax.all_gather(normed_two, "seq", axis=0, tiled=True)
    back_piece = lax.all_gather(output_grad, "seq", axis=0, tiled=True)
    units_term = jnp.stack(
        [
            jnp.einsum(
                "rnc,rd->ncd", gate_columns, second_piece, preferred_element_type=jnp.float32
            ),
            jnp.einsum("rnc,rd->ncd", up_columns, second_piece, preferred_element_type=jnp.float32),
            jnp.einsum(
                "rnc,rd->ncd", hidden_columns, back_piece, preferred_element_type=jnp.float32
            ),
        ],
        axis=2,
    )
    joined_term = jnp.einsum(
        "rnc,re->nce",
        own_columns(normed_piece, feature_width),
        mixed_piece,
        preferred_element_type=jnp.float32,
    )
    outer_term = jnp.einsum(
        "rnc,rd->ncd",
        own_columns(attended_piece, query_width),
        branch_piece,
        preferred_element_type=jnp.float32,
    )
    units_sum, joined_sum, outer_sum = (
        lax.psum_scatter(
            units_term.astype(jnp.bfloat16), "dp", scatter_dimension=0, tiled=True
        ).astype(jnp.float32),
        lax.psum_scatter(
            joined_term.astype(jnp.bfloat16), "dp", scatter_dimension=0, tiled=True
        ).astype(jnp.float32),
        lax.psum_scatter(
            outer_term.astype(jnp.bfloat16), "dp", scatter_dimension=0, tiled=True
        ).astype(jnp.float32),
    )
    units_grad = units_sum.reshape(unit_width, 3, D)
    joined_grad = joined_sum.reshape(feature_width, QKV)
    out_grad_part = outer_sum.reshape(query_width, D)
    small_grad = lax.psum_scatter(small_grad_term, ("dp", "seq"), scatter_dimension=0, tiled=True)
    joined = optimizer_step(
        joined_weight, joined_grad, joined_first, joined_second, 2.0 / math.sqrt(D), DECAY
    )
    outer = optimizer_step(
        out_weight, out_grad_part, out_first, out_second, 2.0 / math.sqrt(QW // 64), DECAY
    )
    units_new = optimizer_step(
        units_weight, units_grad, units_first, units_second, 2.0 / math.sqrt(D), DECAY
    )
    small = optimizer_step(small_params, small_grad, small_first, small_second, 0.5, 0.0)
    return (
        block_output,
        input_grad,
        joined[0],
        joined[1],
        joined[2],
        joined[3],
        outer[0],
        outer[1],
        outer[2],
        outer[3],
        units_new[0],
        units_new[1],
        units_new[2],
        units_new[3],
        small[0],
        small[1],
        small[2],
        small[3],
    )


def solution(mesh):
    in_specs = (
        P(("dp", "seq"), None),
        P(("dp", "seq"), None),
        P("dp", None),
        P(("dp", "seq"), None),
        P(("dp", "seq"), None),
        P(("dp", "seq"), None, None),
        P(("dp", "seq"), None),
        P(("dp", "seq"), None),
        P(("dp", "seq"), None),
        P(("dp", "seq"), None),
        P(("dp", "seq"), None),
        P(("dp", "seq"), None, None),
        P(("dp", "seq"), None, None),
        P(("dp", "seq"), None),
        P(("dp", "seq"), None),
    )
    out_specs = (
        P(("dp", "seq"), None),
        P(("dp", "seq"), None),
        P(("dp", "seq"), None),
        P(("dp", "seq"), None),
        P(("dp", "seq"), None),
        P(("dp", "seq"), None),
        P(("dp", "seq"), None),
        P(("dp", "seq"), None),
        P(("dp", "seq"), None),
        P(("dp", "seq"), None),
        P(("dp", "seq"), None, None),
        P(("dp", "seq"), None, None),
        P(("dp", "seq"), None, None),
        P(("dp", "seq"), None, None),
        P(("dp", "seq"), None),
        P(("dp", "seq"), None),
        P(("dp", "seq"), None),
        P(("dp", "seq"), None),
    )
    return jax.shard_map(body, mesh=mesh, in_specs=in_specs, out_specs=out_specs, check_vma=False)
```

profile of v0, /device:TPU:7, one launch (start us, length us, event | category | flops | bytes accessed | tf_op | source)
XLA Modules:
  0.0 1427.8 jit_solution(15476511734683370740)
XLA Ops:
  10.7 4.3 convert_element_type.164
  15.1 34.4 %all_gather.37 = bf16[256,20]{1,0:T(8,128)(2,1)S(1)} all-gather(bf16[8,20]{1,0:T(8,128)(2,1)S(1)} %convert_element_type.152), channel_id=1, replica_groups=mesh['dp'=4,'seq'=8] {'dp','seq'}, dimensions={0}, use_global_device_ids=true | all-gather | bytes 10560 | tf_op jit(solution)/shard_map/all_gather | solution.py:148
  54.4 27.4 %all-gather.10.cloned.1.call-done = bf16[1536,2048]{1,0:T(8,128)(2,1)} async-done(((bf16[48,2048]{1,0:T(8,128)(2,1)}), bf16[1536,2048]{1,0:T(8,128)(2,1)}) %all-gather.10.cloned.1.call-update) | async-done | bytes 6291472 | tf_op jit(solution)/shard_map/all_gather | solution.py:146
  81.8 3.8 convolution_add_fusion.1
  86.9 10.8 all_gather.39
  97.8 9.0 all_gather.40
  106.7 6.2 while.48
  113.6 7.7 while.49
  115.3 2.2 conditional.7
  115.3 2.2 fusion.10
  119.1 2.2 conditional.7
  119.1 2.2 fusion.10
  122.3 25.2 %all-gather.12.cloned.1.call-done = bf16[1536,1536]{1,0:T(8,128)(2,1)} async-done(((bf16[48,1536]{1,0:T(8,128)(2,1)}), bf16[1536,1536]{1,0:T(8,128)(2,1)}) %all-gather.12.cloned.1.call-update) | async-done | bytes 4718608 | tf_op jit(solution)/shard_map/all_gather | solution.py:147
  147.5 3.4 multiply_reduce_fusion.3
  151.0 429.2 %all-gather.14.cloned.1.call-done = bf16[8960,3,1536]{2,0,1:T(8,128)(2,1)} async-done(((bf16[280,3,1536]{2,0,1:T(8,128)(2,1)}), bf16[8960,3,1536]{2,0,1:T(8,128)(2,1)}) %all-gather.14.cloned.1.call-update) | async-done | bytes 82575376 | tf_op jit(solution)/shard_map/all_gather | solution.py:222
  580.2 15.3 %fusion.50 = f32[128,8960]{1,0:T(8,128)} fusion(bf16[128,1536]{1,0:T(8,128)(2,1)S(1)} %multiply_convert_fusion.3, bf16[8960,3,1536]{2,0,1:T(8,128)(2,1)} %all-gather.14.cloned.1.call-done), kind=kOutput, calls=%fused_computation.56 | convolution fusion | flops 3523215360 | bytes 32505856 | tf_op jit(solution)/shard_map/td,ud->tu/dot_general | solution.py:102
  595.6 15.4 %fusion.52 = f32[128,8960]{1,0:T(8,128)} fusion(bf16[128,1536]{1,0:T(8,128)(2,1)} %copy-done.12, bf16[8960,3,1536]{2,0,1:T(8,128)(2,1)} %all-gather.14.cloned.1.call-done), kind=kOutput, calls=%fused_computation.58 | convolution fusion | flops 3523215360 | bytes 32505856 | tf_op jit(solution)/shard_map/td,ud->tu/dot_general | solution.py:103
  610.9 18.5 %multiply_convert_fusion = (bf16[128,8960]{1,0:T(8,128)(2,1)}, bf16[128,8960]{1,0:T(8,128)(2,1)}, bf16[128,8960]{1,0:T(8,128)(2,1)}) fusion(f32[128,8960]{1,0:T(8,128)} %fusion.50, f32[128,8960]{1,0:T(8,128)} %fusion.52, bf16[128,1536]{1,0:T(8,128)(2,1)S(1)} %copy-done.10, bf16[8960,3,1536]{2,0,1:T(8,128)(2,1)} %all-gather.14.cloned.1.call-done), kind=kOutput, calls=%fused_computation.68 | convolution fusion | flops 3540418560 | bytes 43974656 | tf_op jit(solution)/shard_map/td,ud->tu/dot_general | solution.py:112
  629.5 11.8 fusion.49
  641.3 11.6 multiply_reduce_fusion.1
  654.9 4.0 convolution_convert_fusion.3
  662.8 20.3 %while.50 = (s32[]{:T(128)}, f32[128,2,6,128]{3,0,2,1:T(8,128)S(1)}, bf16[1024,2,128]{2,0,1:T(8,128)(2,1)}, bf16[1024,2,128]{2,0,1:T(8,128)(2,1)}, s32[128]{0:T(...) while((s32[]{:T(128)}, ...), condition=%wide.region_23.24_spmd, body=%wide.region_19.23_spmd.sunk | while | flops 1014956032 | bytes 35647016 | solution.py:298
  664.4 8.5 conditional.8
  665.6 1.8 fusion.22
  669.7 3.3 fusion.34
  674.6 8.5 conditional.8
  679.8 3.3 fusion.34
  689.7 25.0 %reduce-scatter.8.cloned.1.call-done = bf16[128,2,128]{2,0,1:T(8,128)(2,1)} async-done(((bf16[1024,2,128]{2,0,1:T(8,128)(2,1)}), bf16[128,2,128]{2,0,1:T(8,128)(2,1)}) %reduce-scatter.8.cloned.1.call-update) | async-done | bytes 65552 | tf_op jit(solution)/shard_map/reduce_scatter | solution.py:308
  715.5 37.1 %reduce-scatter.6.cloned.1.call-done = bf16[128,2,128]{2,0,1:T(8,128)(2,1)} async-done(((bf16[1024,2,128]{2,0,1:T(8,128)(2,1)}), bf16[128,2,128]{2,0,1:T(8,128)(2,1)}) %reduce-scatter.6.cloned.1.call-update) | async-done | bytes 65552 | tf_op jit(solution)/shard_map/reduce_scatter | solution.py:305
  756.2 3.8 copy.157
  761.6 5.8 all-to-all-start.2
  767.4 4.2 copy.154
  771.5 3.2 copy.155
  774.7 27.3 %all-to-all-done.2 = bf16[128,4,8,280]{0,3,1,2:T(8,128)(2,1)S(1)} async-done(((bf16[128,4,8,280]{0,3,1,2:T(8,128)(2,1)}), bf16[128,4,8,280]{0,3,1,2:T(8,128)(2,1)S(1)}, u32[]{:S(2)}, u32[]{:S(2)}) %all-to-all-start.2) | async-done | bytes 2293792 | tf_op jit(solution)/shard_map/all_to_all | solution.py:242
  802.1 7.8 all-to-all-start.1
  809.8 4.2 copy.151
  814.0 3.3 copy.152
  817.3 23.7 %all-to-all-done.1 = bf16[128,4,8,280]{0,3,1,2:T(8,128)(2,1)} async-done(((bf16[128,4,8,280]{0,3,1,2:T(8,128)(2,1)}), bf16[128,4,8,280]{0,3,1,2:T(8,128)(2,1)}, u32[]{:S(2)}, u32[]{:S(2)}) %all-to-all-start.1) | async-done | bytes 2293792 | tf_op jit(solution)/shard_map/all_to_all | solution.py:248
  840.9 7.7 all-to-all-start
  848.6 4.6 copy.150
  853.2 3.9 copy.156
  857.2 4.8 reshape.276
  862.0 33.3 %all-gather.22.cloned.1.call-done = bf16[1024,1536]{1,0:T(8,128)(2,1)} async-done(((bf16[128,1536]{1,0:T(8,128)(2,1)}), bf16[1024,1536]{1,0:T(8,128)(2,1)}) %all-gather.22.cloned.1.call-update) | async-done | bytes 3145744 | tf_op jit(solution)/shard_map/all_gather | solution.py:341
  895.3 3.6 fusion.68
  899.0 31.1 %all-gather.24.cloned.1.call-done = bf16[1024,1536]{1,0:T(8,128)(2,1)} async-done(((bf16[128,1536]{1,0:T(8,128)(2,1)}), bf16[1024,1536]{1,0:T(8,128)(2,1)}) %all-gather.24.cloned.1.call-update) | async-done | bytes 3145744 | tf_op jit(solution)/shard_map/all_gather | solution.py:342
  930.1 8.1 fusion.61
  938.2 2.3 copy.159
  940.5 5.0 reshape.278
  945.5 2.5 copy.153
  948.0 2.4 reshape.274
  950.4 8.1 fusion.60
  958.5 10.1 all-gather.18.cloned.1.call-done
  968.6 4.2 fusion.71
  972.9 30.0 %all-gather.26.cloned.1.call-done = bf16[1024,1536]{1,0:T(8,128)(2,1)} async-done(((bf16[128,1536]{1,0:T(8,128)(2,1)}), bf16[1024,1536]{1,0:T(8,128)(2,1)}) %all-gather.26.cloned.1.call-update) | async-done | bytes 3145744 | tf_op jit(solution)/shard_map/all_gather | solution.py:343
  1002.9 5.8 fusion.62
  1008.7 8.2 pad_maximum_fusion
  1018.4 12.5 fusion.76
  1031.0 2.4 fusion.84
  1034.3 42.2 %all-reduce.1 = f32[256,20]{1,0:T(8,128)S(1)} all-reduce(f32[256,20]{1,0:T(8,128)S(1)} %concatenate.50), channel_id=7, replica_groups=mesh['dp'=4,'seq'=8] {'dp','seq'}, use_global_device_ids=true, to_apply=%region_33.34.clone | all-reduce | flops 5120 | bytes 40960
  1077.2 2.3 fusion.81
  1079.5 2.0 fusion.118
  1081.5 2.4 fusion.121
  1083.9 323.5 %all-reduce.4.cloned.1.call-done = bf16[4,280,3,1536]{3,1,0,2:T(8,128)(2,1)} async-done(((bf16[4,280,3,1536]{3,1,0,2:T(8,128)(2,1)}), bf16[4,280,3,1536]{3,1,0,2:T(8,128)(2,1)}) %all-reduce.4.cloned.1.call-update) | async-done | bytes 10321936
  1407.4 13.6 fusion.115
  (244 shorter events, 52.6 us)
Async XLA Ops:
  7.2 74.6 %all-gather.10.cloned.1.call-start = ((), (), s32[]{:S(2)}) async-start(), calls=%async_computation.7 | async-start | bytes 6488064 | tf_op jit(solution)/shard_map/all_gather | solution.py:146
  9.0 138.5 %all-gather.12.cloned.1.call-start = ((), (), s32[]{:S(2)}) async-start(), calls=%async_computation.8 | async-start | bytes 4866048 | tf_op jit(solution)/shard_map/all_gather | solution.py:147
  10.7 4.4 copy-start.30
  10.7 569.6 %all-gather.14.cloned.1.call-start = ((), (), s32[]{:S(2)}) async-start(), calls=%async_computation.9 | async-start | bytes 85155840 | tf_op jit(solution)/shard_map/all_gather | solution.py:222
  15.0 34.9 %copy-start.38 = (s32[1,4]{1,0:T(1,128)S(1)}, s32[1,4]{1,0:T(1,128)}, u32[]{:S(2)}) copy-start(s32[1,4]{1,0:T(1,128)} %param.29) | copy-start | bytes 52
  15.0 38.5 %copy-start.1 = (bf16[128,1536]{1,0:T(8,128)(2,1)S(1)}, bf16[128,1536]{1,0:T(8,128)(2,1)}, u32[]{:S(2)}) copy-start(bf16[128,1536]{1,0:T(8,128)(2,1)} %param.27) | copy-start | bytes 1179652
  15.0 699.7 %reduce-scatter.8.cloned.1.call-start = ((), (), s32[]{:S(2)}) async-start(), calls=%async_computation.11 | async-start | bytes 589824 | tf_op jit(solution)/shard_map/reduce_scatter | solution.py:308
  49.7 35.8 %copy-start.27 = (f32[1536]{0:T(1024)}, f32[1536]{0:T(1024)S(1)}, u32[]{:S(2)}) copy-start(f32[1536]{0:T(1024)S(1)} %mul.456) | copy-start | bytes 18436
  50.9 35.1 %copy-start.15 = (f32[128,128]{0,1:T(8,128)}, f32[128,128]{0,1:T(8,128)S(1)}, u32[]{:S(2)}) copy-start(f32[128,128]{0,1:T(8,128)S(1)} %get-tuple-element.1038) | copy-start | bytes 196612
  54.2 31.4 %copy-start.34 = (f32[128]{0:T(128)}, f32[128]{0:T(128)S(1)}, u32[]{:S(2)}) copy-start(f32[128]{0:T(128)S(1)} %get-tuple-element.1043) | copy-start | bytes 1540
  54.4 31.2 %copy-start.5 = (bf16[128,1536]{1,0:T(8,128)(2,1)}, bf16[128,1536]{1,0:T(8,128)(2,1)S(1)}, u32[]{:S(2)}) copy-start(bf16[128,1536]{1,0:T(8,128)(2,1)S(1)} %fusion.79) | copy-start | bytes 1179652
  85.9 0.8 copy-start.23
  85.9 0.9 copy-start.24
  121.3 26.1 %copy-start.17 = (bf16[1024,2,128]{2,0,1:T(8,128)(2,1)}, bf16[1024,2,128]{2,0,1:T(8,128)(2,1)S(1)}, u32[]{:S(2)}) copy-start(bf16[1024,2,128]{2,0,1:T(8,128)(2,1)S(1)} %get-tuple-element.1483) | copy-start | bytes 1572868
  147.5 3.4 copy-start.29
  150.8 502.1 %copy-start.3 = (f32[128,1536]{1,0:T(8,128)}, f32[128,1536]{1,0:T(8,128)S(1)}, u32[]{:S(2)}) copy-start(f32[128,1536]{1,0:T(8,128)S(1)} %get-tuple-element.1049) | copy-start | bytes 2359300
  151.0 429.2 %copy-start.12 = (bf16[128,1536]{1,0:T(8,128)(2,1)}, bf16[128,1536]{1,0:T(8,128)(2,1)S(1)}, u32[]{:S(2)}) copy-start(bf16[128,1536]{1,0:T(8,128)(2,1)S(1)} %multiply_convert_fusion.3) | copy-start | bytes 1179652
  595.6 15.4 %copy-start.10 = (bf16[128,1536]{1,0:T(8,128)(2,1)S(1)}, bf16[128,1536]{1,0:T(8,128)(2,1)}, u32[]{:S(2)}) copy-start(bf16[128,1536]{1,0:T(8,128)(2,1)} %param.28) | copy-start | bytes 1179652
  629.5 11.8 copy-start.8
  641.3 11.6 copy-start.11
  654.1 0.8 copy-start.7
  662.8 23.8 %copy-start.26 = (f32[128,128]{0,1:T(8,128)S(1)}, f32[128,128]{0,1:T(8,128)}, u32[]{:S(2)}) copy-start(f32[128,128]{0,1:T(8,128)} %get-tuple-element.1037) | copy-start | bytes 196612
  662.8 24.6 %copy-start.25 = (f32[128,128]{0,1:T(8,128)S(1)}, f32[128,128]{0,1:T(8,128)}, u32[]{:S(2)}) copy-start(f32[128,128]{0,1:T(8,128)} %get-tuple-element.1036) | copy-start | bytes 196612
  664.4 1.0 copy-start.18
  664.5 1.1 copy-start.19
  664.5 1.1 copy-start.32
  665.1 3.3 copy-start
  674.6 1.0 copy-start.18
  674.6 1.1 copy-start.19
  674.6 1.1 copy-start.32
  675.2 3.3 copy-start
  683.1 69.5 %reduce-scatter.6.cloned.1.call-start = ((), (), s32[]{:S(2)}) async-start(), calls=%async_computation.10 | async-start | bytes 589824 | tf_op jit(solution)/shard_map/reduce_scatter | solution.py:305
  683.7 164.9 %all-gather.16.cloned.1.call-start = ((), (), s32[]{:S(2)}) async-start(), calls=%async_computation.12 | async-start | bytes 3538944 | tf_op jit(solution)/shard_map/all_gather | solution.py:338
  684.3 177.7 %all-gather.20.cloned.1.call-start = ((), (), s32[]{:S(2)}) async-start(), calls=%async_computation.15 | async-start | bytes 3538944 | tf_op jit(solution)/shard_map/all_gather | solution.py:339
  685.1 210.3 %all-gather.22.cloned.1.call-start = ((), (), s32[]{:S(2)}) async-start(), calls=%async_computation.16 | async-start | bytes 3538944 | tf_op jit(solution)/shard_map/all_gather | solution.py:341
  685.8 3.0 copy-start.16
  685.8 244.3 %all-gather.24.cloned.1.call-start = ((), (), s32[]{:S(2)}) async-start(), calls=%async_computation.18 | async-start | bytes 3538944 | tf_op jit(solution)/shard_map/all_gather | solution.py:342
  686.6 282.1 %all-gather.18.cloned.1.call-start = ((), (), s32[]{:S(2)}) async-start(), calls=%async_computation.13 | async-start | bytes 4718592 | tf_op jit(solution)/shard_map/all_gather | solution.py:340
  755.5 247.4 %all-gather.26.cloned.1.call-start = ((), (), s32[]{:S(2)}) async-start(), calls=%async_computation.19 | async-start | bytes 3538944 | tf_op jit(solution)/shard_map/all_gather | solution.py:343
  761.6 40.5 %all-to-all-start.2 = ((bf16[128,4,8,280]{0,3,1,2:T(8,128)(2,1)}), bf16[128,4,8,280]{0,3,1,2:T(8,128)(2,1)S(1)}, u32[]{:S(2)}, u32[]{:S(2)}) async-start(bf16[128,4,8,280]{0,3,1,2:T(8,128)(2,1)} %copy.158), calls=%async_computation.6 | async-start | bytes 4587520 | tf_op jit(solution)/shard_map/all_to_all | solution.py:242
  802.1 38.9 %all-to-all-start.1 = ((bf16[128,4,8,280]{0,3,1,2:T(8,128)(2,1)}), bf16[128,4,8,280]{0,3,1,2:T(8,128)(2,1)}, u32[]{:S(2)}, u32[]{:S(2)}) async-start(bf16[128,4,8,280]{0,3,1,2:T(8,128)(2,1)} %copy.155), calls=%async_computation.5 | async-start | bytes 4587520 | tf_op jit(solution)/shard_map/all_to_all | solution.py:248
  840.9 104.6 %all-to-all-start = ((bf16[128,4,8,280]{0,3,1,2:T(8,128)(2,1)}), bf16[128,4,8,280]{0,3,1,2:T(8,128)(2,1)}, u32[]{:S(2)}, u32[]{:S(2)}) async-start(bf16[128,4,8,280]{0,3,1,2:T(8,128)(2,1)} %copy.152), calls=%async_computation.4 | async-start | bytes 4587520 | tf_op jit(solution)/shard_map/all_to_all | solution.py:245
  848.6 230.9 %reduce-scatter.12.cloned.1.call-start = ((), (), s32[]{:S(2)}) async-start(), calls=%async_computation.17 | async-start | bytes 737280 | tf_op jit(solution)/shard_map/reduce_scatter | solution.py:375
  899.0 182.6 %reduce-scatter.10.cloned.1.call-start = ((), (), s32[]{:S(2)}) async-start(), calls=%async_computation.14 | async-start | bytes 983040 | tf_op jit(solution)/shard_map/reduce_scatter | solution.py:372
  958.5 44.4 %copy-start.9 = (bf16[1024,4,280]{0,2,1:T(8,128)(2,1)S(1)}, bf16[1024,4,280]{0,2,1:T(8,128)(2,1)}, u32[]{:S(2)}) copy-start(bf16[1024,4,280]{0,2,1:T(8,128)(2,1)} %reshape.278) | copy-start | bytes 6881284
  972.8 434.6 %all-reduce.4.cloned.1.call-start = ((), (), s32[]{:S(2)}) async-start(), calls=%async_computation.20 | async-start | bytes 20643840
  1016.9 0.7 copy-start.40
  1016.9 1.3 copy-start.33
  1016.9 1.4 copy-start.4
  1016.9 14.0 slice-start
  1018.4 12.6 slice-start.1
  1018.4 12.6 copy-start.2
  1018.4 12.5 copy-start.6
  1018.4 12.5 copy-start.28
  1018.4 12.5 copy-start.35
  1031.0 45.5 %copy-start.31 = (f32[8,20]{1,0:T(8,128)S(1)}, f32[8,20]{1,0:T(8,128)}, u32[]{:S(2)}) copy-start(f32[8,20]{1,0:T(8,128)} %param.33) | copy-start | bytes 1924
  1031.0 45.5 %copy-start.36 = (f32[8,20]{1,0:T(8,128)S(1)}, f32[8,20]{1,0:T(8,128)}, u32[]{:S(2)}) copy-start(f32[8,20]{1,0:T(8,128)} %param.40) | copy-start | bytes 1924
  1031.0 45.5 %copy-start.37 = (f32[8,20]{1,0:T(8,128)S(1)}, f32[8,20]{1,0:T(8,128)}, u32[]{:S(2)}) copy-start(f32[8,20]{1,0:T(8,128)} %param.41) | copy-start | bytes 1924
  1031.0 46.2 %copy-start.39 = (f32[128]{0:T(128)S(1)}, f32[128]{0:T(128)}, u32[]{:S(2)}) copy-start(f32[128]{0:T(128)} %get-tuple-element.1042) | copy-start | bytes 1540
  1033.4 46.1 %copy-start.14 = (f32[48,1536]{1,0:T(8,128)S(1)}, f32[48,1536]{1,0:T(8,128)}, u32[]{:S(2)}) copy-start(f32[48,1536]{1,0:T(8,128)} %param.31) | copy-start | bytes 884740
  1033.4 46.1 %copy-start.21 = (f32[48,1536]{1,0:T(8,128)S(1)}, f32[48,1536]{1,0:T(8,128)}, u32[]{:S(2)}) copy-start(f32[48,1536]{1,0:T(8,128)} %param.36) | copy-start | bytes 884740
  1033.6 48.0 %copy-start.13 = (f32[48,2048]{1,0:T(8,128)S(1)}, f32[48,2048]{1,0:T(8,128)}, u32[]{:S(2)}) copy-start(f32[48,2048]{1,0:T(8,128)} %param.30) | copy-start | bytes 1179652
  1033.6 47.9 %copy-start.20 = (f32[48,2048]{1,0:T(8,128)S(1)}, f32[48,2048]{1,0:T(8,128)}, u32[]{:S(2)}) copy-start(f32[48,2048]{1,0:T(8,128)} %param.34) | copy-start | bytes 1179652
  1034.2 45.3 %copy-start.22 = (f32[48,1536]{1,0:T(8,128)S(1)}, f32[48,1536]{1,0:T(8,128)}, u32[]{:S(2)}) copy-start(f32[48,1536]{1,0:T(8,128)} %param.37) | copy-start | bytes 884740
Sparse Core Ops, SparseCore 0:
  11.5 70.2 all-gather.9
  85.2 62.1 all-gather.11
  151.0 429.1 all-gather.13
  683.3 31.3 reduce-scatter.7
  718.5 34.1 reduce-scatter.5
  755.0 50.1 all-gather.15
  807.6 43.3 all-gather.19
  852.9 42.3 all-gather.21
  897.8 32.3 all-gather.23
  931.9 36.7 all-gather.17
  970.5 32.3 all-gather.25
  1005.1 20.4 reduce-scatter.11
  1028.4 22.4 reduce-scatter.9
  1053.2 354.1 all-reduce.3
where the time goes:
time: 1440 us; the launch traced here: 1430 us
  waiting for transfers between devices  1030 us (72%)
  matrix products  150 us (10%)
  blocking collectives  96.4 us (7%)
  local copies, waits for them, and re-layouts  61.8 us (4%)
  other arithmetic  51.7 us (4%)
  starting transfers between devices  21.8 us (2%)
  between operations  15 us (1%)
    all_gather x1, waiting for transfers between devices, body(): piece = lax.all_gather(units_half, ('dp', 'seq'), axis=0, tiled=True)  429 us
    unnamed x15, waiting for transfers between devices  327 us
    unnamed x1, blocking collectives  42.2 us
    reduce_scatter x1, waiting for transfers between devices, body(): lax.psum_scatter(key_grads.astype(jnp.bfloat16), 'seq', scatter_dimension...  37.1 us
    all_gather x1, blocking collectives, body(): lax.all_gather(small_params.astype(jnp.bfloat16), ('dp', 'seq'), axis=0,...  34.4 us
    all_gather x1, waiting for transfers between devices, body(): branch_piece = lax.all_gather(branch_grad, 'seq', axis=0, tiled=True)  33.3 us
    all_gather x1, waiting for transfers between devices, body(): second_piece = lax.all_gather(normed_two, 'seq', axis=0, tiled=True)  31.1 us
    all_gather x1, waiting for transfers between devices, body(): back_piece = lax.all_gather(output_grad, 'seq', axis=0, tiled=True)  30 us
  transfers between devices with their start and end apart: 17, of which 12 were waited for; matrix products, arithmetic and copies ran while one was open for 10% of the time, Pallas kernels for 0%

commit v1 on v0

v1 whole, which is shorter than its diff:
```python
import math

import jax
import jax.numpy as jnp
from jax import lax
from jax.sharding import Mesh
from jax.sharding import PartitionSpec as P

D = 1536
HEADS = 12
KV_HEADS = 2
HEAD_DIM = 128
FF = 8960
BLOCK = 256
STEP = 5
QW = 1536
KW = 256
QKV = 2048


NORM_EPS = 1e-06
ROPE_BASE = 1000000.0
BETA_ONE = 0.9
BETA_TWO = 0.95
ADAM_EPS = 1e-08
DECAY = 0.1


DP = ("zh", "zl")
SEQ = ("y", "x", "c")
ALL = DP + SEQ


def shift(value, axis, step):
    count = lax.axis_size(axis)
    return lax.ppermute(value, axis, [(i, (i + step) % count) for i in range(count)])


def rotations(value, axis):
    return [value] + [shift(value, axis, step) for step in range(1, lax.axis_size(axis))]


def gather_rows(value):
    result = []
    for number, block in enumerate(rotations(value, "zh")):
        if number % 2 == 0:
            grid = [rotations(item, "y") for item in rotations(block, "x")]
            grid = [[grid[i][j] for i in range(len(grid))] for j in range(len(grid[0]))]
        else:
            grid = [rotations(item, "x") for item in rotations(block, "y")]
        result.append([item for line in grid for item in line])
    return result


def low(value):
    return value.astype(jnp.bfloat16)


def wide(value):
    return value.astype(jnp.float32)


def add_back(blocks, axis):
    total = wide(blocks[0])
    for step in range(1, len(blocks)):
        total = total + wide(shift(low(blocks[step]), axis, -step))
    return total


def scatter_rows(parts):
    across, along = lax.axis_size("x"), lax.axis_size("y")
    lines = []
    for number, blocks in enumerate(parts):
        grid = [blocks[j * across : (j + 1) * across] for j in range(along)]
        if number % 2 == 0:
            sums = [add_back([grid[j][i] for j in range(along)], "y") for i in range(across)]
            lines.append(add_back(sums, "x"))
        else:
            sums = [add_back(grid[j], "x") for j in range(along)]
            lines.append(add_back(sums, "y"))
    return add_back(lines, "zh")


def norm_scale(rows):
    return lax.rsqrt(jnp.mean(rows * rows, axis=1, keepdims=True) + NORM_EPS)


def unpack_small(small):
    gain_cols = D // KW
    group = HEADS // KV_HEADS
    gain_one = small[:, :gain_cols].reshape(D)
    gain_two = small[:, gain_cols : 2 * gain_cols].reshape(D)
    query_bias = small[:, 2 * gain_cols : 2 * gain_cols + group].reshape(KV_HEADS, HEAD_DIM, group)
    query_bias = jnp.transpose(query_bias, (0, 2, 1)).reshape(QW)
    key_bias = small[:, 2 * gain_cols + group]
    value_bias = small[:, 2 * gain_cols + group + 1]
    return (gain_one, gain_two, jnp.concatenate([query_bias, key_bias, value_bias]))


def pack_small(gain_one, gain_two, bias):
    gain_cols = D // KW
    group = HEADS // KV_HEADS
    query_part = jnp.transpose(bias[:QW].reshape(KV_HEADS, group, HEAD_DIM), (0, 2, 1)).reshape(
        KW, group
    )
    return jnp.concatenate(
        [
            gain_one.reshape(KW, gain_cols),
            gain_two.reshape(KW, gain_cols),
            query_part,
            bias[QW : QW + KW][:, None],
            bias[QW + KW :][:, None],
        ],
        axis=1,
    )


def layout(starts_row, first, count):
    places = first + jnp.arange(count, dtype=jnp.int32)
    before = starts_row[None, :] <= places[:, None]
    documents = jnp.sum(before.astype(jnp.int32), axis=1) - 1
    begin = jnp.max(jnp.where(before, starts_row[None, :], 0), axis=1)
    offset = places - begin
    return (documents, offset // BLOCK, offset)


def turning(offset):
    half = HEAD_DIM // 2
    frequency = ROPE_BASE ** (-(2.0 * jnp.arange(half, dtype=jnp.float32)) / HEAD_DIM)
    angle = offset.astype(jnp.float32)[:, None] * frequency[None, :]
    angle = jnp.concatenate([angle, angle], axis=1)
    return (jnp.cos(angle)[:, None, :], jnp.sin(angle)[:, None, :])


def rotate(values, cosine, sine):
    half = values.shape[-1] // 2
    turned = jnp.concatenate([-values[..., half:], values[..., :half]], axis=-1)
    return values * cosine + turned * sine


def rotate_back(grads, cosine, sine):
    half = grads.shape[-1] // 2
    moved = grads * sine
    turned = jnp.concatenate([moved[..., half:], -moved[..., :half]], axis=-1)
    return grads * cosine + turned


def optimizer_step(weight, grad, first, second, rate, decay):
    first = BETA_ONE * first + (1.0 - BETA_ONE) * grad
    second = BETA_TWO * second + (1.0 - BETA_TWO) * grad * grad
    fixed_first = first / (1.0 - BETA_ONE**STEP)
    fixed_second = second / (1.0 - BETA_TWO**STEP)
    weight = weight - rate * (fixed_first / (jnp.sqrt(fixed_second) + ADAM_EPS) + decay * weight)
    return (weight, first, second, weight.astype(jnp.bfloat16))


def body(
    inputs,
    output_grad,
    document_starts,
    joined_weight,
    out_weight,
    units_weight,
    small_params,
    joined_first,
    joined_second,
    out_first,
    out_second,
    units_first,
    units_second,
    small_first,
    small_second,
):
    count = inputs.shape[0]
    seq_count = lax.axis_size(SEQ)
    dp_count = lax.axis_size(DP)
    devices = seq_count * dp_count
    seq_index = lax.axis_index(SEQ)
    group_len = count * seq_count
    first = seq_index * count
    starts_row = document_starts[0]
    group = HEADS // KV_HEADS
    scale = HEAD_DIM ** (-0.5)
    feature_width = joined_weight.shape[0]
    query_width = out_weight.shape[0]
    unit_width = units_weight.shape[0]

    small_rows, small_cols = small_params.shape
    small_block = jnp.pad(
        low(small_params), ((0, feature_width - small_rows), (0, 128 - small_cols))
    )
    packed = jnp.concatenate([low(joined_weight), low(out_weight), small_block], axis=1)
    packed = lax.all_gather(packed, ALL, axis=0, tiled=True)
    full_joined = packed[:, :QKV]
    full_out = packed[:, QKV : QKV + D]
    full_small = packed[:, QKV + D :].reshape(devices, feature_width, 128)
    full_small = full_small[:, :small_rows, :small_cols].reshape(devices * small_rows, small_cols)

    units_half = low(jnp.transpose(units_weight, (1, 0, 2)))
    mine = [units_half[2], units_half[0], units_half[1]]
    kinds = []
    for item in mine:
        slots = []
        for block in rotations(item, "zl"):
            slots += rotations(block, "c")
        kinds.append(jnp.concatenate(slots, axis=0))
    down_rows, gate_rows, up_rows = kinds

    back_blocks = gather_rows(output_grad)
    back_parts = [jnp.concatenate(blocks, axis=0) for blocks in back_blocks]

    gain_one, gain_two, bias = unpack_small(wide(full_small))
    rows = wide(inputs)
    scale_one = norm_scale(rows)
    normed_one = low(rows * scale_one * gain_one)
    mixed = jnp.dot(normed_one, full_joined, preferred_element_type=jnp.float32) + bias
    documents, blocks, offset = layout(starts_row, first, count)
    cosine, sine = turning(offset)
    query = low(rotate(mixed[:, :QW].reshape(count, HEADS, HEAD_DIM), cosine, sine))
    query = query.reshape(count, KV_HEADS, group, HEAD_DIM)
    keys_own = low(rotate(mixed[:, QW : QW + KW].reshape(count, KV_HEADS, HEAD_DIM), cosine, sine))
    values_own = low(mixed[:, QW + KW :])
    pair = jnp.concatenate([keys_own.reshape(count, KW), values_own], axis=1)
    pair_all = lax.all_gather(pair, SEQ, axis=0, tiled=True)
    keys = pair_all[:, :KW].reshape(group_len, KV_HEADS, HEAD_DIM)
    values = pair_all[:, KW:].reshape(group_len, KV_HEADS, HEAD_DIM)
    all_documents, all_blocks, unused_offset = layout(starts_row, 0, group_len)
    seen = (documents[:, None] == all_documents[None, :]) & (all_blocks[None, :] <= blocks[:, None])

    scores = jnp.einsum("qcgd,kcd->cgqk", query, keys, preferred_element_type=jnp.float32) * scale
    scores = jnp.where(seen, scores, -1e30)
    highest = jnp.max(scores, axis=-1, keepdims=True)
    total = jnp.sum(jnp.where(seen, jnp.exp(scores - highest), 0.0), axis=-1, keepdims=True)
    log_total = highest + jnp.log(total)
    weights = jnp.where(seen, jnp.exp(scores - log_total), 0.0)
    attended = jnp.einsum(
        "cgqk,kcd->qcgd", low(weights), values, preferred_element_type=jnp.float32
    )
    attended_low = low(attended.reshape(count, QW))
    middle = rows + jnp.dot(attended_low, full_out, preferred_element_type=jnp.float32)
    scale_two = norm_scale(middle)
    normed_two = low(middle * scale_two * gain_two)

    sent = jnp.concatenate(
        [
            normed_one.reshape(count, dp_count, seq_count, feature_width),
            attended_low.reshape(count, dp_count, seq_count, query_width),
        ],
        axis=3,
    )
    sent = jnp.transpose(sent, (2, 0, 1, 3)).reshape(
        seq_count * count, dp_count * (feature_width + query_width)
    )
    owned = lax.all_to_all(sent, SEQ, split_axis=0, concat_axis=0, tiled=True)
    owned = owned.reshape(group_len, dp_count, feature_width + query_width)
    normed_owned = owned[:, :, :feature_width].reshape(group_len, dp_count * feature_width)
    attended_owned = owned[:, :, feature_width:].reshape(group_len, dp_count * query_width)

    dot_rows = lambda left, right: jnp.einsum(
        "td,ud->tu", left, right, preferred_element_type=jnp.float32
    )
    dot_units = lambda left, right: jnp.einsum(
        "tu,ud->td", left, right, preferred_element_type=jnp.float32
    )
    normed_parts, hidden_parts, gate_parts, up_parts = [], [], [], []
    for part_blocks, back in zip(gather_rows(normed_two), back_parts):
        normed = jnp.concatenate(part_blocks, axis=0)
        pulled = dot_rows(back, down_rows)
        gate = dot_rows(normed, gate_rows)
        up = dot_rows(normed, up_rows)
        sigma = jax.nn.sigmoid(gate)
        active = gate * sigma
        normed_parts.append(normed)
        hidden_parts.append(low(active * up))
        gate_parts.append(low(pulled * up * sigma * (1.0 + gate * (1.0 - sigma))))
        up_parts.append(low(pulled * active))
    cut = lambda value: [value[i : i + count] for i in range(0, value.shape[0], count)]
    grad_terms = [
        cut(dot_units(gate, gate_rows) + dot_units(up, up_rows))
        for gate, up in zip(gate_parts, up_parts)
    ]
    normed_grad = scatter_rows(grad_terms)
    branch_terms = [cut(dot_units(hidden, down_rows)) for hidden in hidden_parts]
    branch_two = scatter_rows(branch_terms)
    block_output = low(middle + branch_two)

    total_over = lambda lefts, rights: sum(
        jnp.einsum("tu,td->ud", left, right, preferred_element_type=jnp.float32)
        for left, right in zip(lefts, rights)
    )
    units_term = jnp.stack(
        [
            total_over(gate_parts, normed_parts),
            total_over(up_parts, normed_parts),
            total_over(hidden_parts, back_parts),
        ]
    )
    low_count, core_count = lax.axis_size("zl"), lax.axis_size("c")
    units_term = units_term.reshape(3, low_count, core_count, unit_width, D)
    units_term = add_back([units_term[:, :, i] for i in range(core_count)], "c")
    units_grad = add_back([units_term[:, i] for i in range(low_count)], "zl")
    units_grad = jnp.transpose(units_grad, (1, 0, 2))

    weighted_two = gain_two * normed_grad
    middle_grad = (
        wide(output_grad)
        + scale_two * weighted_two
        - middle * scale_two**3 * jnp.mean(weighted_two * middle, axis=1, keepdims=True)
    )
    gain_two_grad = jnp.sum(normed_grad * middle * scale_two, axis=0)
    branch_grad = low(middle_grad)
    branch_all = lax.all_gather(branch_grad, SEQ, axis=0, tiled=True)
    attended_grad = low(
        jnp.einsum("td,ed->te", branch_grad, full_out, preferred_element_type=jnp.float32)
    ).reshape(count, KV_HEADS, group, HEAD_DIM)
    delta = jnp.einsum("qcgd,qcgd->cgq", wide(attended_grad), attended)
    pulled = jnp.einsum("qcgd,kcd->cgqk", attended_grad, values, preferred_element_type=jnp.float32)
    score_grad = low(weights * (pulled - delta[..., None]))
    query_grad = jnp.einsum(
        "cgqk,kcd->qcgd", score_grad, keys, preferred_element_type=jnp.float32
    )
    key_part = jnp.einsum("cgqk,qcgd->kcd", score_grad, query, preferred_element_type=jnp.float32)
    value_part = jnp.einsum(
        "cgqk,qcgd->kcd", low(weights), attended_grad, preferred_element_type=jnp.float32
    )
    pair_part = jnp.concatenate(
        [key_part.reshape(group_len, KW), value_part.reshape(group_len, KW)], axis=1
    )
    pair_sum = wide(lax.psum_scatter(low(pair_part), SEQ, scatter_dimension=0, tiled=True))
    query_pre = rotate_back(
        (query_grad * scale).reshape(count, HEADS, HEAD_DIM), cosine, sine
    ).reshape(count, QW)
    key_pre = rotate_back(
        (pair_sum[:, :KW] * scale).reshape(count, KV_HEADS, HEAD_DIM), cosine, sine
    ).reshape(count, KW)
    mixed_grad = low(jnp.concatenate([query_pre, key_pre, pair_sum[:, KW:]], axis=1))
    mixed_all = lax.all_gather(mixed_grad, SEQ, axis=0, tiled=True)
    bias_grad = jnp.sum(wide(mixed_grad), axis=0)
    normed_one_grad = jnp.einsum(
        "te,de->td", mixed_grad, full_joined, preferred_element_type=jnp.float32
    )
    weighted_one = gain_one * normed_one_grad
    input_grad = (
        middle_grad
        + scale_one * weighted_one
        - rows * scale_one**3 * jnp.mean(weighted_one * rows, axis=1, keepdims=True)
    )
    gain_one_grad = jnp.sum(normed_one_grad * rows * scale_one, axis=0)
    small_term = pack_small(gain_one_grad, gain_two_grad, bias_grad)
    small_grad = lax.psum_scatter(small_term, ALL, scatter_dimension=0, tiled=True)

    joined_term = jnp.einsum(
        "rc,re->ce", normed_owned, mixed_all, preferred_element_type=jnp.float32
    )
    outer_term = jnp.einsum(
        "rc,re->ce", attended_owned, branch_all, preferred_element_type=jnp.float32
    )
    joined_grad = wide(lax.psum_scatter(low(joined_term), DP, scatter_dimension=0, tiled=True))
    outer_grad = wide(lax.psum_scatter(low(outer_term), DP, scatter_dimension=0, tiled=True))
    joined = optimizer_step(
        joined_weight, joined_grad, joined_first, joined_second, 2.0 / math.sqrt(D), DECAY
    )
    outer = optimizer_step(
        out_weight, outer_grad, out_first, out_second, 2.0 / math.sqrt(QW // 64), DECAY
    )
    units_new = optimizer_step(
        units_weight, units_grad, units_first, units_second, 2.0 / math.sqrt(D), DECAY
    )
    small = optimizer_step(small_params, small_grad, small_first, small_second, 0.5, 0.0)
    return (block_output, input_grad) + joined + outer + units_new + small


def solution(mesh):
    groups, members = mesh.devices.shape
    fine = Mesh(mesh.devices.reshape(groups // 2, 2, members // 4, 2, 2), ALL)
    flat, cube = P(ALL, None), P(ALL, None, None)
    in_specs = (flat, flat, P(DP, None), flat, flat, cube, flat) + (flat,) * 4 + (cube,) * 2 + (flat,) * 2
    out_specs = (flat,) * 10 + (cube,) * 4 + (flat,) * 4
    return jax.shard_map(body, mesh=fine, in_specs=in_specs, out_specs=out_specs, check_vma=False)
```

time: 1440 us -> 586 us (0.41)
  waiting for transfers between devices: 1030 us -> 223 us
  matrix products: 150 us -> 124 us
  local copies, waits for them, and re-layouts: 61.8 us -> 39 us
  blocking collectives: 96.4 us -> 77 us
  starting transfers between devices: 21.8 us -> 37.5 us
    all_gather x9 -> x4, waiting for transfers between devices: 586 us -> 67.7 us  [the longest x1 67.7 us: body(): packed = lax.all_gather(packed, ALL, axis=0, tiled=True)]
    unnamed x15 -> x7, waiting for transfers between devices: 327 us -> 0.11 us
    ppermute x0 -> x39, waiting for transfers between devices: none -> 137 us  [shift(): lax.ppermute(value, axis, [(i, (i + step) % count) for i in range(count)])]
    reduce_scatter x4 -> x3, waiting for transfers between devices: 62.1 us -> 5.52 us  [the longest x1 5.5 us: body(): lax.psum_scatter(low(joined_term), DP, scatter_dimension=0, tiled=True)]
    all_gather x3 -> x0, blocking collectives: 54.2 us -> none  [the longest x1 34.4 us: body(): lax.all_gather(small_params.astype(jnp.bfloat16), ('dp', 'seq'), axis=0,...]
    all_to_all x3 -> x1, waiting for transfers between devices: 51 us -> 12.1 us  [body(): owned = lax.all_to_all(sent, SEQ, split_axis=0, concat_axis=0, tiled=True)]
    unnamed x1, blocking collectives: 42.2 us -> 77 us
    ppermute x0 -> x39, starting transfers between devices: none -> 32.7 us  [shift(): lax.ppermute(value, axis, [(i, (i + step) % count) for i in range(count)])]
  transfers between devices with their start and end apart: 17 -> 47, of which waited for: 12 -> 16; matrix products, arithmetic and copies ran while one was open for 10% -> 33% of each run, Pallas kernels for 0% -> 0%
where the time goes in v1:
time: 586 us; the launch traced here: 577 us
  waiting for transfers between devices  223 us (38%)
  matrix products  124 us (21%)
  blocking collectives  77 us (13%)
  other arithmetic  61 us (10%)
  local copies, waits for them, and re-layouts  39 us (7%)
  starting transfers between devices  37.5 us (6%)
  between operations  16.2 us (3%)
    ppermute x39, waiting for transfers between devices, shift(): lax.ppermute(value, axis, [(i, (i + step) % count) for i in range(count)])  137 us
    unnamed x1, blocking collectives  77 us
    all_gather x1, waiting for transfers between devices, body(): packed = lax.all_gather(packed, ALL, axis=0, tiled=True)  67.7 us
    ppermute x39, starting transfers between devices, shift(): lax.ppermute(value, axis, [(i, (i + step) % count) for i in range(count)])  32.7 us
    dot_general x6, matrix products, body(): jnp.einsum('tu,td->ud', left, right, preferred_element_type=jnp.float32)  30.5 us
    dot_general x6, matrix products, body(): jnp.einsum('td,ud->tu', left, right, preferred_element_type=jnp.float32)  26.2 us
    dot_general x6, matrix products, body(): jnp.einsum('tu,ud->td', left, right, preferred_element_type=jnp.float32)  24.4 us
    convert_element_type x4, other arithmetic, optimizer_step(): return (weight, first, second, weight.astype(jnp.bfloat16))  20.9 us
  transfers between devices with their start and end apart: 47, of which 16 were waited for; matrix products, arithmetic and copies ran while one was open for 33% of the time, Pallas kernels for 0%

profile of v1, /device:TPU:7, one launch (start us, length us, event | category | flops | bytes accessed | tf_op | source)
XLA Modules:
  0.0 577.4 jit_solution(12115810088142407195)
XLA Ops:
  10.8 2.8 convert_bitcast_fusion
  13.6 1.5 slice_bitcast_fusion.1
  17.4 2.3 collective-permute-start.29
  22.8 28.0 %collective-permute-done.29 = bf16[128,1536]{1,0:T(8,128)(2,1)} collective-permute-done((bf16[128,1536]{1,0:T(8,128)(2,1)S(1)}, bf16[128,1536]{1,0:T(8,128)(2,1)}, u32[]{:S(2)}, u32[]{:S(2)}) %collective-permute-start.29) | collective-permute-done | bytes 393248 | tf_op jit(solution)/shard_map/ppermute | solution.py:36
  50.9 1.8 constant_dynamic-update-slice_fusion.11
  52.7 67.7 %all-gather.5.cloned.1.call-done = bf16[1536,3712]{1,0:T(8,128)(2,1)} async-done(((bf16[48,3712]{1,0:T(8,128)(2,1)}), bf16[1536,3712]{1,0:T(8,128)(2,1)}) %all-gather.5.cloned.1.call-update) | async-done | bytes 11403280 | tf_op jit(solution)/shard_map/all_gather | solution.py:193
  122.2 3.9 fusion.21
  128.7 1.8 constant_dynamic-update-slice_fusion.6
  131.4 1.8 constant_dynamic-update-slice_fusion.5
  133.5 6.3 %collective-permute-done.31 = bf16[128,1536]{1,0:T(8,128)(2,1)S(1)} collective-permute-done((bf16[128,1536]{1,0:T(8,128)(2,1)}, bf16[128,1536]{1,0:T(8,128)(2,1)S(1)}, u32[]{:S(2)}, u32[]{:S(2)}) %collective-permute-start.31) | collective-permute-done | bytes 393248 | tf_op jit(solution)/shard_map/ppermute | solution.py:36
  141.0 1.8 constant_dynamic-update-slice_fusion.10
  143.5 6.2 %collective-permute-done.25 = bf16[128,1536]{1,0:T(8,128)(2,1)S(1)} collective-permute-done((bf16[128,1536]{1,0:T(8,128)(2,1)}, bf16[128,1536]{1,0:T(8,128)(2,1)S(1)}, u32[]{:S(2)}, u32[]{:S(2)}) %collective-permute-start.25) | collective-permute-done | bytes 393248 | tf_op jit(solution)/shard_map/ppermute | solution.py:36
  149.7 2.3 collective-permute-start.6
  159.7 2.7 copy-done
  164.1 4.5 bitcast_convert_fusion
  168.6 3.4 multiply_reduce_fusion.2
  174.9 4.4 fusion.84
  180.0 12.3 %collective-permute-done.15 = bf16[128,1536]{1,0:T(8,128)(2,1)S(1)} collective-permute-done((bf16[128,1536]{1,0:T(8,128)(2,1)S(1)}, bf16[128,1536]{1,0:T(8,128)(2,1)S(1)}, u32[]{:S(2)}, u32[]{:S(2)}) %collective-permute-start.15) | collective-permute-done | bytes 393248 | tf_op jit(solution)/shard_map/ppermute | solution.py:36
  193.8 3.9 fusion.85
  198.8 3.4 collective-permute-done.1
  203.3 7.3 %collective-permute-done.2 = bf16[128,1536]{1,0:T(8,128)(2,1)S(1)} collective-permute-done((bf16[128,1536]{1,0:T(8,128)(2,1)S(1)}, bf16[128,1536]{1,0:T(8,128)(2,1)S(1)}, u32[]{:S(2)}, u32[]{:S(2)}) %collective-permute-start.2) | collective-permute-done | bytes 393248 | tf_op jit(solution)/shard_map/ppermute | solution.py:36
  210.6 3.8 fusion.81
  214.4 4.3 multiply_convert_fusion.3
  218.7 4.6 fusion.89
  223.3 3.5 fusion.114
  228.4 3.9 fusion.116
  234.7 4.7 fusion.79
  240.9 4.8 fusion.90
  245.8 5.0 multiply_convert_fusion.1
  250.8 4.8 fusion.88
  255.5 3.6 fusion.113
  260.0 4.1 fusion.115
  266.8 24.8 %collective-permute-done.20 = bf16[128,1536]{1,0:T(8,128)(2,1)S(1)} collective-permute-done((bf16[128,1536]{1,0:T(8,128)(2,1)S(1)}, bf16[128,1536]{1,0:T(8,128)(2,1)S(1)}, u32[]{:S(2)}, u32[]{:S(2)}) %collective-permute-start.20) | collective-permute-done | bytes 393248 | tf_op jit(solution)/shard_map/ppermute | solution.py:36
  292.1 2.0 collective-permute-start.19
  294.1 4.1 collective-permute-done.35
  301.0 8.2 %collective-permute-done.21 = bf16[128,1536]{1,0:T(8,128)(2,1)S(1)} collective-permute-done((bf16[128,1536]{1,0:T(8,128)(2,1)S(1)}, bf16[128,1536]{1,0:T(8,128)(2,1)S(1)}, u32[]{:S(2)}, u32[]{:S(2)}) %collective-permute-start.21) | collective-permute-done | bytes 393248 | tf_op jit(solution)/shard_map/ppermute | solution.py:36
  309.4 2.4 collective-permute-start.22
  311.8 25.7 %collective-permute-done.36 = bf16[128,1536]{1,0:T(8,128)(2,1)S(1)} collective-permute-done((bf16[128,1536]{1,0:T(8,128)(2,1)S(1)}, bf16[128,1536]{1,0:T(8,128)(2,1)S(1)}, u32[]{:S(2)}, u32[]{:S(2)}) %collective-permute-start.36) | collective-permute-done | bytes 393248 | tf_op jit(solution)/shard_map/ppermute | solution.py:36
  338.0 8.0 %collective-permute-done.22 = bf16[128,1536]{1,0:T(8,128)(2,1)S(1)} collective-permute-done((bf16[128,1536]{1,0:T(8,128)(2,1)S(1)}, bf16[128,1536]{1,0:T(8,128)(2,1)S(1)}, u32[]{:S(2)}, u32[]{:S(2)}) %collective-permute-start.22) | collective-permute-done | bytes 393248 | tf_op jit(solution)/shard_map/ppermute | solution.py:36
  347.4 4.1 fusion.24
  351.8 4.6 fusion.30
  357.6 5.2 fusion.2
  362.8 1.9 fusion.29
  364.8 2.1 copy.172
  366.9 2.3 pad_maximum_fusion.5
  369.5 6.6 %fusion.80 = f32[1120,1536]{1,0:T(8,128)} fusion(bf16[512,1120]{0,1:T(8,128)(2,1)} %copy-done.60, bf16[128,1536]{1,0:T(8,128)(2,1)} %copy-done.57, bf16[128,1536]{1,0:T(8,128)(2,1)} %copy-done.56, bf16[128,1536]{1,0:T(8,128)(2,1)} %copy-done.55, bf16[128,1536]{1,0:T(8,128)(2,1)S(1)} %copy-done.37), kind=kOutput, calls=%fused_computation.208 | convolution fusion | flops 1767899136 | bytes 9601024 | tf_op jit(solution)/shard_map/tu,td->ud/dot_general | solution.py:288
  376.0 2.0 fusion.117
  378.0 6.2 %convolution_add_fusion = f32[1120,1536]{1,0:T(8,128)} fusion(f32[1120,1536]{1,0:T(8,128)S(1)} %fusion.117, bf16[512,1120]{0,1:T(8,128)(2,1)S(1)} %copy-done.12, bf16[512,1536]{1,0:T(8,128)(2,1)} %constant_dynamic-update-slice_fusion.8), kind=kOutput, calls=%fused_computation.4 | convolution fusion | flops 1763328000 | bytes 16482304 | tf_op jit(solution)/shard_map/tu,td->ud/dot_general | solution.py:288
  384.3 5.9 %convolution_add_fusion.1 = f32[1120,1536]{1,0:T(8,128)S(1)} fusion(f32[1120,1536]{1,0:T(8,128)} %fusion.79, bf16[512,1120]{0,1:T(8,128)(2,1)} %copy-done.10, bf16[512,1536]{1,0:T(8,128)(2,1)} %copy-done.1), kind=kOutput, calls=%fused_computation.5 | convolution fusion | flops 1763328000 | bytes 16482304 | tf_op jit(solution)/shard_map/tu,td->ud/dot_general | solution.py:288
  390.2 5.1 convolution_add_fusion.2
  395.4 7.6 %pad_maximum_fusion = f32[3,2,2,280,1536]{4,3,2,1,0:T(8,128)} fusion(f32[1,2,2,280,1536]{4,3,2,1,0:T(8,128)S(1)} %bitcast.190, f32[1,2,2,280,1536]{4,3,2,1,0:T(8,128)S(1)} %bitcast.191, f32[1,2,2,280,1536]{4,3,2,1,0:T(8,128)S(1)} %bitcast.192), kind=kLoop, calls=%fused_computation | loop fusion | flops 10321920 | bytes 41287680 | tf_op jit(solution)/shard_map/stack | solution.py:291
  403.0 7.0 %fusion.9 = bf16[3,2,280,1536]{3,2,0,1:T(8,128)(2,1)} fusion(f32[3,2,2,280,1536]{4,3,2,1,0:T(8,128)} %pad_maximum_fusion), kind=kLoop, calls=%fused_computation.20 | loop fusion | bytes 10321920 | tf_op jit(solution)/shard_map/convert_element_type | solution.py:56
  417.7 4.1 all-to-all-start
  422.0 12.1 %all-to-all-done = bf16[8,128,384]{1,2,0:T(8,128)(2,1)S(1)} async-done(((bf16[8,128,384]{1,2,0:T(8,128)(2,1)}), bf16[8,128,384]{1,2,0:T(8,128)(2,1)S(1)}, u32[]{:S(2)}, u32[]{:S(2)}) %all-to-all-start) | async-done | bytes 786464 | tf_op jit(solution)/shard_map/all_to_all | solution.py:254
  434.9 11.3 %fusion = f32[3,2,280,1536]{3,2,0,1:T(8,128)} fusion(bf16[3,2,280,1536]{3,2,0,1:T(8,128)(2,1)} %collective-permute-done.37, f32[3,2,2,280,1536]{4,3,2,1,0:T(8,128)} %pad_maximum_fusion), kind=kLoop, calls=%fused_computation.3 | loop fusion | flops 5160960 | bytes 25804800 | tf_op jit(solution)/shard_map/add | solution.py:66
  446.2 4.3 fusion.17
  450.8 5.4 fusion.38
  456.3 3.6 convolution_convert_fusion
  460.8 77.0 %all-reduce.1 = f32[256,20]{1,0:T(8,128)S(1)} all-reduce(f32[256,20]{1,0:T(8,128)S(1)} %concatenate.99), channel_id=5, replica_groups=mesh['zh'=2,'zl'=2,'y'=2,'x'=2,'c'=2] {'zh','zl','y','x','c'}, use_global_device_ids=true, to_apply=%region_16.17.clone | all-reduce | flops 5120 | bytes 40960
  539.6 4.6 convolution_convert_fusion.1
  544.3 16.0 %fusion.93 = (bf16[280,3,1536]{2,0,1:T(8,128)(2,1)}, f32[280,3,1536]{2,0,1:T(8,128)}, f32[280,3,1536]{2,0,1:T(8,128)}, f32[280,3,1536]{2,0,1:T(8,128)}) fusion(f32[280,3,1536]{2,0,1:T(8,128)} %param.20, bf16[3,280,1536]{2,1,0:T(8,128)(2,1)} %collective-permute-done.38, f32[3,2,280,1536]{3,2,0,1:T(8,128)} %fusion, f32[280,3,1536]{2,0,1:T(8,128)} %param.26, ...), kind=kLoop, calls=%fused_computation.220 | loop fusion | flops 23224320 | bytes 41287680 | tf_op jit(solution)/shard_map/convert_element_type | solution.py:154
  560.4 2.0 fusion.95
  562.4 5.5 reduce-scatter.6.cloned.1.call-done
  567.9 2.2 fusion.98
  (313 shorter events, 60.4 us)
Async XLA Ops:
  7.2 113.1 %all-gather.5.cloned.1.call-start = ((), (), s32[]{:S(2)}) async-start(), calls=%async_computation.4 | async-start | bytes 11759616 | tf_op jit(solution)/shard_map/all_gather | solution.py:193
  10.7 145.8 %all-gather.7.cloned.1.call-start = ((), (), s32[]{:S(2)}) async-start(), calls=%async_computation.5 | async-start | bytes 1179648 | tf_op jit(solution)/shard_map/all_gather | solution.py:224
  15.1 137.7 %collective-permute-start.10 = (bf16[280,1536]{1,0:T(8,128)(2,1)}, bf16[280,1536]{1,0:T(8,128)(2,1)}, u32[]{:S(2)}, u32[]{:S(2)}) collective-permute-start(bf16[280,1536]{1,0:T(8,128)(2,1)} %get-tuple-element.55), channel_id=1, source_target_pairs={{0,8},{8,0},{1,9},{9,1},{2,10},{10,2},{3,11},{11,3},{4,12},{12,4},... | collective-permute-start | bytes 2580488 | tf_op jit(solution)/shard_map/ppermute | solution.py:36
  16.4 155.8 %collective-permute-start.9 = (bf16[280,1536]{1,0:T(8,128)(2,1)}, bf16[280,1536]{1,0:T(8,128)(2,1)}, u32[]{:S(2)}, u32[]{:S(2)}) collective-permute-start(bf16[280,1536]{1,0:T(8,128)(2,1)} %get-tuple-element.55), channel_id=1, source_target_pairs={{0,1},{1,0},{2,3},{3,2},{4,5},{5,4},{6,7},{7,6},{8,9},{9,8},{10,11... | collective-permute-start | bytes 2580488 | tf_op jit(solution)/shard_map/ppermute | solution.py:36
  17.4 33.4 %collective-permute-start.29 = (bf16[128,1536]{1,0:T(8,128)(2,1)S(1)}, bf16[128,1536]{1,0:T(8,128)(2,1)}, u32[]{:S(2)}, u32[]{:S(2)}) collective-permute-start(bf16[128,1536]{1,0:T(8,128)(2,1)S(1)} %copy-done.15), channel_id=1, source_target_pairs={{0,16},{16,0},{1,17},{17,1},{2,18},{18,2},{3,19},{19,3},{4,20},{20... | collective-permute-start | bytes 1179656 | tf_op jit(solution)/shard_map/ppermute | solution.py:36
  19.7 107.9 %collective-permute-start.23 = (bf16[128,1536]{1,0:T(8,128)(2,1)S(1)}, bf16[128,1536]{1,0:T(8,128)(2,1)}, u32[]{:S(2)}, u32[]{:S(2)}) collective-permute-start(bf16[128,1536]{1,0:T(8,128)(2,1)S(1)} %copy-done.15), channel_id=1, source_target_pairs={{0,2},{2,0},{1,3},{3,1},{4,6},{6,4},{5,7},{7,5},{8,10},{10,8},{9,1... | collective-permute-start | bytes 1179656 | tf_op jit(solution)/shard_map/ppermute | solution.py:36
  19.9 110.6 %collective-permute-start.24 = (bf16[128,1536]{1,0:T(8,128)(2,1)S(1)}, bf16[128,1536]{1,0:T(8,128)(2,1)}, u32[]{:S(2)}, u32[]{:S(2)}) collective-permute-start(bf16[128,1536]{1,0:T(8,128)(2,1)S(1)} %copy-done.15), channel_id=1, source_target_pairs={{0,4},{4,0},{1,5},{5,1},{2,6},{6,2},{3,7},{7,3},{8,12},{12,8},{9,1... | collective-permute-start | bytes 1179656 | tf_op jit(solution)/shard_map/ppermute | solution.py:36
  20.6 101.4 %copy-start.25 = (f32[128,128]{0,1:T(8,128)}, f32[128,128]{0,1:T(8,128)S(1)}, u32[]{:S(2)}) copy-start(f32[128,128]{0,1:T(8,128)S(1)} %get-tuple-element.82) | copy-start | bytes 196612
  20.6 101.4 %copy-start.27 = (f32[128,128]{0,1:T(8,128)}, f32[128,128]{0,1:T(8,128)S(1)}, u32[]{:S(2)}) copy-start(f32[128,128]{0,1:T(8,128)S(1)} %get-tuple-element.83) | copy-start | bytes 196612
  20.7 105.7 %copy-start.31 = (f32[128,128]{1,0:T(8,128)}, f32[128,128]{1,0:T(8,128)S(1)}, u32[]{:S(2)}) copy-start(f32[128,128]{1,0:T(8,128)S(1)} %copy.117) | copy-start | bytes 196612
  21.5 330.4 %copy-start.13 = (pred[128,1024]{0,1:T(8,128)(4,1)}, pred[128,1024]{0,1:T(8,128)(4,1)S(1)}, u32[]{:S(2)}) copy-start(pred[128,1024]{0,1:T(8,128)(4,1)S(1)} %compare_and_fusion) | copy-start | bytes 393220
  22.0 100.2 %copy-start.52 = (f32[128]{0:T(128)}, f32[128]{0:T(128)S(1)}, u32[]{:S(2)}) copy-start(f32[128]{0:T(128)S(1)} %get-tuple-element.87) | copy-start | bytes 1540
  50.8 82.4 %collective-permute-start.30 = (bf16[128,1536]{1,0:T(8,128)(2,1)}, bf16[128,1536]{1,0:T(8,128)(2,1)}, u32[]{:S(2)}, u32[]{:S(2)}) collective-permute-start(bf16[128,1536]{1,0:T(8,128)(2,1)} %collective-permute-done.29), channel_id=1, source_target_pairs={{0,2},{2,0},{1,3},{3,1},{4,6},{6,4},{5,7},{7,5},{8,10},{10,8},{9,1... | collective-permute-start | bytes 1179656 | tf_op jit(solution)/shard_map/ppermute | solution.py:36
  126.7 28.2 %copy-start.22 = (f32[128,2,128]{2,1,0:T(2,128)}, f32[128,2,128]{2,1,0:T(2,128)S(1)}, u32[]{:S(2)}) copy-start(f32[128,2,128]{2,1,0:T(2,128)S(1)} %mul.453) | copy-start | bytes 393220
  127.5 284.5 %reduce-scatter.4.cloned.1.call-start = ((), (), s32[]{:S(2)}) async-start(), calls=%async_computation.6 | async-start | bytes 1179648 | tf_op jit(solution)/shard_map/reduce_scatter | solution.py:329
  127.5 12.2 %collective-permute-start.31 = (bf16[128,1536]{1,0:T(8,128)(2,1)}, bf16[128,1536]{1,0:T(8,128)(2,1)S(1)}, u32[]{:S(2)}, u32[]{:S(2)}) collective-permute-start(bf16[128,1536]{1,0:T(8,128)(2,1)} %collective-permute-done.29), channel_id=1, source_target_pairs={{0,4},{4,0},{1,5},{5,1},{2,6},{6,2},{3,7},{7,3},{8,12},{12,8},{9,1... | collective-permute-start | bytes 1179656 | tf_op jit(solution)/shard_map/ppermute | solution.py:36
  130.5 22.8 %collective-permute-start.7 = (bf16[280,1536]{1,0:T(8,128)(2,1)}, bf16[280,1536]{1,0:T(8,128)(2,1)}, u32[]{:S(2)}, u32[]{:S(2)}) collective-permute-start(bf16[280,1536]{1,0:T(8,128)(2,1)} %get-tuple-element.56), channel_id=1, source_target_pairs={{0,8},{8,0},{1,9},{9,1},{2,10},{10,2},{3,11},{11,3},{4,12},{12,4},... | collective-permute-start | bytes 2580488 | tf_op jit(solution)/shard_map/ppermute | solution.py:36
  133.1 16.6 %collective-permute-start.25 = (bf16[128,1536]{1,0:T(8,128)(2,1)}, bf16[128,1536]{1,0:T(8,128)(2,1)S(1)}, u32[]{:S(2)}, u32[]{:S(2)}) collective-permute-start(bf16[128,1536]{1,0:T(8,128)(2,1)} %collective-permute-done.23), channel_id=1, source_target_pairs={{0,4},{4,0},{1,5},{5,1},{2,6},{6,2},{3,7},{7,3},{8,12},{12,8},{9,1... | collective-permute-start | bytes 1179656 | tf_op jit(solution)/shard_map/ppermute | solution.py:36
  139.8 13.8 %collective-permute-start.32 = (bf16[128,1536]{1,0:T(8,128)(2,1)S(1)}, bf16[128,1536]{1,0:T(8,128)(2,1)S(1)}, u32[]{:S(2)}, u32[]{:S(2)}) collective-permute-start(bf16[128,1536]{1,0:T(8,128)(2,1)S(1)} %collective-permute-done.31), channel_id=1, source_target_pairs={{0,2},{2,0},{1,3},{3,1},{4,6},{6,4},{5,7},{7,5},{8,10},{10,8},{9,1... | collective-permute-start | bytes 1179656 | tf_op jit(solution)/shard_map/ppermute | solution.py:36
  149.7 29.6 %collective-permute-start.6 = (bf16[280,1536]{1,0:T(8,128)(2,1)}, bf16[280,1536]{1,0:T(8,128)(2,1)}, u32[]{:S(2)}, u32[]{:S(2)}) collective-permute-start(bf16[280,1536]{1,0:T(8,128)(2,1)} %get-tuple-element.56), channel_id=1, source_target_pairs={{0,1},{1,0},{2,3},{3,2},{4,5},{5,4},{6,7},{7,6},{8,9},{9,8},{10,11... | collective-permute-start | bytes 2580488 | tf_op jit(solution)/shard_map/ppermute | solution.py:36
  152.8 27.2 %collective-permute-start.4 = (bf16[280,1536]{1,0:T(8,128)(2,1)}, bf16[280,1536]{1,0:T(8,128)(2,1)}, u32[]{:S(2)}, u32[]{:S(2)}) collective-permute-start(bf16[280,1536]{1,0:T(8,128)(2,1)} %get-tuple-element.57), channel_id=1, source_target_pairs={{0,8},{8,0},{1,9},{9,1},{2,10},{10,2},{3,11},{11,3},{4,12},{12,4},... | collective-permute-start | bytes 2580488 | tf_op jit(solution)/shard_map/ppermute | solution.py:36
  153.3 20.4 %collective-permute-start.11 = (bf16[280,1536]{1,0:T(8,128)(2,1)}, bf16[280,1536]{1,0:T(8,128)(2,1)}, u32[]{:S(2)}, u32[]{:S(2)}) collective-permute-start(bf16[280,1536]{1,0:T(8,128)(2,1)} %collective-permute-done.10), channel_id=1, source_target_pairs={{0,1},{1,0},{2,3},{3,2},{4,5},{5,4},{6,7},{7,6},{8,9},{9,8},{10,11... | collective-permute-start | bytes 2580488 | tf_op jit(solution)/shard_map/ppermute | solution.py:36
  153.6 44.2 %collective-permute-start.8 = (bf16[280,1536]{1,0:T(8,128)(2,1)}, bf16[280,1536]{1,0:T(8,128)(2,1)}, u32[]{:S(2)}, u32[]{:S(2)}) collective-permute-start(bf16[280,1536]{1,0:T(8,128)(2,1)} %collective-permute-done.7), channel_id=1, source_target_pairs={{0,1},{1,0},{2,3},{3,2},{4,5},{5,4},{6,7},{7,6},{8,9},{9,8},{10,11... | collective-permute-start | bytes 2580488 | tf_op jit(solution)/shard_map/ppermute | solution.py:36
  172.2 62.5 %copy-start.36 = (bf16[128,1536]{1,0:T(8,128)(2,1)}, bf16[128,1536]{1,0:T(8,128)(2,1)S(1)}, u32[]{:S(2)}) copy-start(bf16[128,1536]{1,0:T(8,128)(2,1)S(1)} %multiply_convert_fusion.6) | copy-start | bytes 1179652
  172.2 20.1 %collective-permute-start.15 = (bf16[128,1536]{1,0:T(8,128)(2,1)S(1)}, bf16[128,1536]{1,0:T(8,128)(2,1)S(1)}, u32[]{:S(2)}, u32[]{:S(2)}) collective-permute-start(bf16[128,1536]{1,0:T(8,128)(2,1)S(1)} %multiply_convert_fusion.6), channel_id=1, source_target_pairs={{0,16},{16,0},{1,17},{17,1},{2,18},{18,2},{3,19},{19,3},{4,20},{20... | collective-permute-start | bytes 1179656 | tf_op jit(solution)/shard_map/ppermute | solution.py:36
  173.7 19.8 %collective-permute-start = (bf16[128,1536]{1,0:T(8,128)(2,1)S(1)}, bf16[128,1536]{1,0:T(8,128)(2,1)S(1)}, u32[]{:S(2)}, u32[]{:S(2)}) collective-permute-start(bf16[128,1536]{1,0:T(8,128)(2,1)S(1)} %multiply_convert_fusion.6), channel_id=1, source_target_pairs={{0,2},{2,0},{1,3},{3,1},{4,6},{6,4},{5,7},{7,5},{8,10},{10,8},{9,1... | collective-permute-start | bytes 1179656 | tf_op jit(solution)/shard_map/ppermute | solution.py:36
  179.3 31.3 %copy-start.30 = (bf16[280,1536]{1,0:T(8,128)(2,1)S(1)}, bf16[280,1536]{1,0:T(8,128)(2,1)}, u32[]{:S(2)}) copy-start(bf16[280,1536]{1,0:T(8,128)(2,1)} %get-tuple-element.56) | copy-start | bytes 2580484
  179.3 35.1 %collective-permute-start.3 = (bf16[280,1536]{1,0:T(8,128)(2,1)S(1)}, bf16[280,1536]{1,0:T(8,128)(2,1)S(1)}, u32[]{:S(2)}, u32[]{:S(2)}) collective-permute-start(bf16[280,1536]{1,0:T(8,128)(2,1)S(1)} %copy-done.29), channel_id=1, source_target_pairs={{0,1},{1,0},{2,3},{3,2},{4,5},{5,4},{6,7},{7,6},{8,9},{9,8},{10,11... | collective-permute-start | bytes 2580488 | tf_op jit(solution)/shard_map/ppermute | solution.py:36
  179.9 34.5 %collective-permute-start.5 = (bf16[280,1536]{1,0:T(8,128)(2,1)}, bf16[280,1536]{1,0:T(8,128)(2,1)S(1)}, u32[]{:S(2)}, u32[]{:S(2)}) collective-permute-start(bf16[280,1536]{1,0:T(8,128)(2,1)} %collective-permute-done.4), channel_id=1, source_target_pairs={{0,1},{1,0},{2,3},{3,2},{4,5},{5,4},{6,7},{7,6},{8,9},{9,8},{10,11... | collective-permute-start | bytes 2580488 | tf_op jit(solution)/shard_map/ppermute | solution.py:36
  192.3 9.9 %collective-permute-start.1 = (bf16[128,1536]{1,0:T(8,128)(2,1)S(1)}, bf16[128,1536]{1,0:T(8,128)(2,1)S(1)}, u32[]{:S(2)}, u32[]{:S(2)}) collective-permute-start(bf16[128,1536]{1,0:T(8,128)(2,1)S(1)} %multiply_convert_fusion.6), channel_id=1, source_target_pairs={{0,4},{4,0},{1,5},{5,1},{2,6},{6,2},{3,7},{7,3},{8,12},{12,8},{9,1... | collective-permute-start | bytes 1179656 | tf_op jit(solution)/shard_map/ppermute | solution.py:36
  193.5 41.2 %copy-start.55 = (bf16[128,1536]{1,0:T(8,128)(2,1)}, bf16[128,1536]{1,0:T(8,128)(2,1)S(1)}, u32[]{:S(2)}) copy-start(bf16[128,1536]{1,0:T(8,128)(2,1)S(1)} %collective-permute-done) | copy-start | bytes 1179652
  193.5 17.1 %collective-permute-start.2 = (bf16[128,1536]{1,0:T(8,128)(2,1)S(1)}, bf16[128,1536]{1,0:T(8,128)(2,1)S(1)}, u32[]{:S(2)}, u32[]{:S(2)}) collective-permute-start(bf16[128,1536]{1,0:T(8,128)(2,1)S(1)} %collective-permute-done), channel_id=1, source_target_pairs={{0,4},{4,0},{1,5},{5,1},{2,6},{6,2},{3,7},{7,3},{8,12},{12,8},{9,1... | collective-permute-start | bytes 1179656 | tf_op jit(solution)/shard_map/ppermute | solution.py:36
  197.8 35.8 %collective-permute-start.16 = (bf16[128,1536]{1,0:T(8,128)(2,1)S(1)}, bf16[128,1536]{1,0:T(8,128)(2,1)S(1)}, u32[]{:S(2)}, u32[]{:S(2)}) collective-permute-start(bf16[128,1536]{1,0:T(8,128)(2,1)S(1)} %collective-permute-done.15), channel_id=1, source_target_pairs={{0,2},{2,0},{1,3},{3,1},{4,6},{6,4},{5,7},{7,5},{8,10},{10,8},{9,1... | collective-permute-start | bytes 1179656 | tf_op jit(solution)/shard_map/ppermute | solution.py:36
  202.2 32.5 %copy-start.56 = (bf16[128,1536]{1,0:T(8,128)(2,1)}, bf16[128,1536]{1,0:T(8,128)(2,1)S(1)}, u32[]{:S(2)}) copy-start(bf16[128,1536]{1,0:T(8,128)(2,1)S(1)} %collective-permute-done.1) | copy-start | bytes 1179652
  202.2 31.8 %collective-permute-start.17 = (bf16[128,1536]{1,0:T(8,128)(2,1)S(1)}, bf16[128,1536]{1,0:T(8,128)(2,1)S(1)}, u32[]{:S(2)}, u32[]{:S(2)}) collective-permute-start(bf16[128,1536]{1,0:T(8,128)(2,1)S(1)} %collective-permute-done.15), channel_id=1, source_target_pairs={{0,4},{4,0},{1,5},{5,1},{2,6},{6,2},{3,7},{7,3},{8,12},{12,8},{9,1... | collective-permute-start | bytes 1179656 | tf_op jit(solution)/shard_map/ppermute | solution.py:36
  210.6 24.1 %copy-start.57 = (bf16[128,1536]{1,0:T(8,128)(2,1)}, bf16[128,1536]{1,0:T(8,128)(2,1)S(1)}, u32[]{:S(2)}) copy-start(bf16[128,1536]{1,0:T(8,128)(2,1)S(1)} %collective-permute-done.2) | copy-start | bytes 1179652
  226.9 37.2 %collective-permute-start.27 = (bf16[128,1536]{1,0:T(8,128)(2,1)S(1)}, bf16[128,1536]{1,0:T(8,128)(2,1)S(1)}, u32[]{:S(2)}, u32[]{:S(2)}) collective-permute-start(bf16[128,1536]{1,0:T(8,128)(2,1)S(1)} %get-tuple-element.59), channel_id=1, source_target_pairs={{0,4},{4,0},{1,5},{5,1},{2,6},{6,2},{3,7},{7,3},{8,12},{12,8},{9,1... | collective-permute-start | bytes 1179656 | tf_op jit(solution)/shard_map/ppermute | solution.py:36
  228.1 81.3 %collective-permute-start.26 = (bf16[128,1536]{1,0:T(8,128)(2,1)S(1)}, bf16[128,1536]{1,0:T(8,128)(2,1)S(1)}, u32[]{:S(2)}, u32[]{:S(2)}) collective-permute-start(bf16[128,1536]{1,0:T(8,128)(2,1)S(1)} %get-tuple-element.58), channel_id=1, source_target_pairs={{0,4},{4,0},{1,5},{5,1},{2,6},{6,2},{3,7},{7,3},{8,12},{12,8},{9,1... | collective-permute-start | bytes 1179656 | tf_op jit(solution)/shard_map/ppermute | solution.py:36
  232.4 32.6 %collective-permute-start.13 = (bf16[128,1536]{1,0:T(8,128)(2,1)S(1)}, bf16[128,1536]{1,0:T(8,128)(2,1)S(1)}, u32[]{:S(2)}, u32[]{:S(2)}) collective-permute-start(bf16[128,1536]{1,0:T(8,128)(2,1)S(1)} %get-tuple-element.63), channel_id=1, source_target_pairs={{0,4},{4,0},{1,5},{5,1},{2,6},{6,2},{3,7},{7,3},{8,12},{12,8},{9,1... | collective-permute-start | bytes 1179656 | tf_op jit(solution)/shard_map/ppermute | solution.py:36
  233.6 104.3 %collective-permute-start.12 = (bf16[128,1536]{1,0:T(8,128)(2,1)S(1)}, bf16[128,1536]{1,0:T(8,128)(2,1)S(1)}, u32[]{:S(2)}, u32[]{:S(2)}) collective-permute-start(bf16[128,1536]{1,0:T(8,128)(2,1)S(1)} %get-tuple-element.62), channel_id=1, source_target_pairs={{0,4},{4,0},{1,5},{5,1},{2,6},{6,2},{3,7},{7,3},{8,12},{12,8},{9,1... | collective-permute-start | bytes 1179656 | tf_op jit(solution)/shard_map/ppermute | solution.py:36
  233.9 6.9 %collective-permute-start.18 = (bf16[128,1536]{1,0:T(8,128)(2,1)S(1)}, bf16[128,1536]{1,0:T(8,128)(2,1)S(1)}, u32[]{:S(2)}, u32[]{:S(2)}) collective-permute-start(bf16[128,1536]{1,0:T(8,128)(2,1)S(1)} %collective-permute-done.17), channel_id=1, source_target_pairs={{0,2},{2,0},{1,3},{3,1},{4,6},{6,4},{5,7},{7,5},{8,10},{10,8},{9,1... | collective-permute-start | bytes 1179656 | tf_op jit(solution)/shard_map/ppermute | solution.py:36
  259.2 6.7 %collective-permute-start.34 = (bf16[128,1536]{1,0:T(8,128)(2,1)S(1)}, bf16[128,1536]{1,0:T(8,128)(2,1)S(1)}, u32[]{:S(2)}, u32[]{:S(2)}) collective-permute-start(bf16[128,1536]{1,0:T(8,128)(2,1)S(1)} %get-tuple-element.61), channel_id=1, source_target_pairs={{0,2},{2,0},{1,3},{3,1},{4,6},{6,4},{5,7},{7,5},{8,10},{10,8},{9,1... | collective-permute-start | bytes 1179656 | tf_op jit(solution)/shard_map/ppermute | solution.py:36
  264.1 28.1 %collective-permute-start.33 = (bf16[128,1536]{1,0:T(8,128)(2,1)S(1)}, bf16[128,1536]{1,0:T(8,128)(2,1)S(1)}, u32[]{:S(2)}, u32[]{:S(2)}) collective-permute-start(bf16[128,1536]{1,0:T(8,128)(2,1)S(1)} %get-tuple-element.60), channel_id=1, source_target_pairs={{0,2},{2,0},{1,3},{3,1},{4,6},{6,4},{5,7},{7,5},{8,10},{10,8},{9,1... | collective-permute-start | bytes 1179656 | tf_op jit(solution)/shard_map/ppermute | solution.py:36
  265.0 46.8 %collective-permute-start.28 = (bf16[128,1536]{1,0:T(8,128)(2,1)S(1)}, bf16[128,1536]{1,0:T(8,128)(2,1)S(1)}, u32[]{:S(2)}, u32[]{:S(2)}) collective-permute-start(bf16[128,1536]{1,0:T(8,128)(2,1)S(1)} %fusion.42), channel_id=1, source_target_pairs={{0,2},{2,0},{1,3},{3,1},{4,6},{6,4},{5,7},{7,5},{8,10},{10,8},{9,1... | collective-permute-start | bytes 1179656 | tf_op jit(solution)/shard_map/ppermute | solution.py:36
  265.9 25.8 %collective-permute-start.20 = (bf16[128,1536]{1,0:T(8,128)(2,1)S(1)}, bf16[128,1536]{1,0:T(8,128)(2,1)S(1)}, u32[]{:S(2)}, u32[]{:S(2)}) collective-permute-start(bf16[128,1536]{1,0:T(8,128)(2,1)S(1)} %get-tuple-element.65), channel_id=1, source_target_pairs={{0,2},{2,0},{1,3},{3,1},{4,6},{6,4},{5,7},{7,5},{8,10},{10,8},{9,1... | collective-permute-start | bytes 1179656 | tf_op jit(solution)/shard_map/ppermute | solution.py:36
  291.7 6.6 %collective-permute-start.35 = (bf16[128,1536]{1,0:T(8,128)(2,1)S(1)}, bf16[128,1536]{1,0:T(8,128)(2,1)S(1)}, u32[]{:S(2)}, u32[]{:S(2)}) collective-permute-start(bf16[128,1536]{1,0:T(8,128)(2,1)S(1)} %fusion.39), channel_id=1, source_target_pairs={{0,4},{4,0},{1,5},{5,1},{2,6},{6,2},{3,7},{7,3},{8,12},{12,8},{9,1... | collective-permute-start | bytes 1179656 | tf_op jit(solution)/shard_map/ppermute | solution.py:36
  292.1 53.8 %copy-start.16 = (bf16[128,1536]{1,0:T(8,128)(2,1)S(1)}, bf16[128,1536]{1,0:T(8,128)(2,1)}, u32[]{:S(2)}) copy-start(bf16[128,1536]{1,0:T(8,128)(2,1)} %param.16) | copy-start | bytes 1179652
  292.1 8.1 %collective-permute-start.19 = (bf16[128,1536]{1,0:T(8,128)(2,1)S(1)}, bf16[128,1536]{1,0:T(8,128)(2,1)S(1)}, u32[]{:S(2)}, u32[]{:S(2)}) collective-permute-start(bf16[128,1536]{1,0:T(8,128)(2,1)S(1)} %get-tuple-element.64), channel_id=1, source_target_pairs={{0,2},{2,0},{1,3},{3,1},{4,6},{6,4},{5,7},{7,5},{8,10},{10,8},{9,1... | collective-permute-start | bytes 1179656 | tf_op jit(solution)/shard_map/ppermute | solution.py:36
  298.3 10.9 %collective-permute-start.21 = (bf16[128,1536]{1,0:T(8,128)(2,1)S(1)}, bf16[128,1536]{1,0:T(8,128)(2,1)S(1)}, u32[]{:S(2)}, u32[]{:S(2)}) collective-permute-start(bf16[128,1536]{1,0:T(8,128)(2,1)S(1)} %fusion.45), channel_id=1, source_target_pairs={{0,4},{4,0},{1,5},{5,1},{2,6},{6,2},{3,7},{7,3},{8,12},{12,8},{9,1... | collective-permute-start | bytes 1179656 | tf_op jit(solution)/shard_map/ppermute | solution.py:36
  300.3 37.7 %collective-permute-start.14 = (bf16[128,1536]{1,0:T(8,128)(2,1)S(1)}, bf16[128,1536]{1,0:T(8,128)(2,1)S(1)}, u32[]{:S(2)}, u32[]{:S(2)}) collective-permute-start(bf16[128,1536]{1,0:T(8,128)(2,1)S(1)} %fusion.48), channel_id=1, source_target_pairs={{0,2},{2,0},{1,3},{3,1},{4,6},{6,4},{5,7},{7,5},{8,10},{10,8},{9,1... | collective-permute-start | bytes 1179656 | tf_op jit(solution)/shard_map/ppermute | solution.py:36
  309.2 28.3 %collective-permute-start.36 = (bf16[128,1536]{1,0:T(8,128)(2,1)S(1)}, bf16[128,1536]{1,0:T(8,128)(2,1)S(1)}, u32[]{:S(2)}, u32[]{:S(2)}) collective-permute-start(bf16[128,1536]{1,0:T(8,128)(2,1)S(1)} %fusion.41), channel_id=1, source_target_pairs={{0,16},{16,0},{1,17},{17,1},{2,18},{18,2},{3,19},{19,3},{4,20},{20... | collective-permute-start | bytes 1179656 | tf_op jit(solution)/shard_map/ppermute | solution.py:36
  309.4 36.6 %collective-permute-start.22 = (bf16[128,1536]{1,0:T(8,128)(2,1)S(1)}, bf16[128,1536]{1,0:T(8,128)(2,1)S(1)}, u32[]{:S(2)}, u32[]{:S(2)}) collective-permute-start(bf16[128,1536]{1,0:T(8,128)(2,1)S(1)} %fusion.47), channel_id=1, source_target_pairs={{0,16},{16,0},{1,17},{17,1},{2,18},{18,2},{3,19},{19,3},{4,20},{20... | collective-permute-start | bytes 1179656 | tf_op jit(solution)/shard_map/ppermute | solution.py:36
  369.2 87.2 %all-gather.11.cloned.1.call-start = ((), (), s32[]{:S(2)}) async-start(), calls=%async_computation.9 | async-start | bytes 3538944 | tf_op jit(solution)/shard_map/all_gather | solution.py:312
  384.2 155.4 %all-gather.9.cloned.1.call-start = ((), (), s32[]{:S(2)}) async-start(), calls=%async_computation.7 | async-start | bytes 4718592 | tf_op jit(solution)/shard_map/all_gather | solution.py:337
  409.9 25.0 %collective-permute-start.37 = (bf16[3,2,280,1536]{3,2,0,1:T(8,128)(2,1)}, bf16[3,2,280,1536]{3,2,0,1:T(8,128)(2,1)}, u32[]{:S(2)}, u32[]{:S(2)}) collective-permute-start(bf16[3,2,280,1536]{3,2,0,1:T(8,128)(2,1)} %fusion.9), channel_id=1, source_target_pairs={{0,1},{1,0},{2,3},{3,2},{4,5},{5,4},{6,7},{7,6},{8,9},{9,8},{10,11... | collective-permute-start | bytes 15482888 | tf_op jit(solution)/shard_map/ppermute | solution.py:36
  417.7 16.4 %all-to-all-start = ((bf16[8,128,384]{1,2,0:T(8,128)(2,1)}), bf16[8,128,384]{1,2,0:T(8,128)(2,1)S(1)}, u32[]{:S(2)}, u32[]{:S(2)}) async-start(bf16[8,128,384]{1,2,0:T(8,128)(2,1)} %bitcast.44), calls=%async_computation.1 | async-start | bytes 1572864 | tf_op jit(solution)/shard_map/all_to_all | solution.py:254
  421.7 138.6 %reduce-scatter.8.cloned.1.call-start = ((), (), s32[]{:S(2)}) async-start(), calls=%async_computation.10 | async-start | bytes 737280 | tf_op jit(solution)/shard_map/reduce_scatter | solution.py:359
  450.6 93.7 %collective-permute-start.38 = (bf16[3,280,1536]{2,1,0:T(8,128)(2,1)}, bf16[3,280,1536]{2,1,0:T(8,128)(2,1)}, u32[]{:S(2)}, u32[]{:S(2)}) collective-permute-start(bf16[3,280,1536]{2,1,0:T(8,128)(2,1)} %fusion.17), channel_id=1, source_target_pairs={{0,8},{8,0},{1,9},{9,1},{2,10},{10,2},{3,11},{11,3},{4,12},{12,4},... | collective-permute-start | bytes 7741448 | tf_op jit(solution)/shard_map/ppermute | solution.py:36
  456.3 81.5 %copy-start.46 = (f32[8,20]{1,0:T(8,128)S(1)}, f32[8,20]{1,0:T(8,128)}, u32[]{:S(2)}) copy-start(f32[8,20]{1,0:T(8,128)} %param.21) | copy-start | bytes 1924
  456.3 81.5 %copy-start.49 = (f32[8,20]{1,0:T(8,128)S(1)}, f32[8,20]{1,0:T(8,128)}, u32[]{:S(2)}) copy-start(f32[8,20]{1,0:T(8,128)} %param.28) | copy-start | bytes 1924
  456.3 81.5 %copy-start.50 = (f32[8,20]{1,0:T(8,128)S(1)}, f32[8,20]{1,0:T(8,128)}, u32[]{:S(2)}) copy-start(f32[8,20]{1,0:T(8,128)} %param.29) | copy-start | bytes 1924
  456.3 82.2 %copy-start.7 = (f32[128,1536]{1,0:T(8,128)S(1)}, f32[128,1536]{1,0:T(8,128)}, u32[]{:S(2)}) copy-start(f32[128,1536]{1,0:T(8,128)} %get-tuple-element.47) | copy-start | bytes 2359300
  456.3 82.2 %copy-start.54 = (f32[128]{0:T(128)S(1)}, f32[128]{0:T(128)}, u32[]{:S(2)}) copy-start(f32[128]{0:T(128)} %get-tuple-element.86) | copy-start | bytes 1540
  459.9 107.9 %reduce-scatter.6.cloned.1.call-start = ((), (), s32[]{:S(2)}) async-start(), calls=%async_computation.8 | async-start | bytes 983040 | tf_op jit(solution)/shard_map/reduce_scatter | solution.py:358
  (46 other events, 333.6 us)
Sparse Core Ops, SparseCore 0:
  11.5 108.7 all-gather.4
  127.6 26.6 all-gather.6
  369.3 34.0 reduce-scatter.3
  405.1 36.8 all-gather.10
  444.3 36.6 all-gather.8
  483.2 29.8 reduce-scatter.7
  544.4 23.4 reduce-scatter.5

commit v2 on v1

v2 whole, which is shorter than its diff:
```python
import math

import jax
import jax.numpy as jnp
from jax import lax
from jax.experimental import pallas as pl
from jax.experimental.pallas import tpu as pltpu
from jax.sharding import Mesh
from jax.sharding import PartitionSpec as P

D = 1536
HEADS = 12
KV_HEADS = 2
HEAD_DIM = 128
FF = 8960
BLOCK = 256
STEP = 5
QW = 1536
KW = 256
QKV = 2048


NORM_EPS = 1e-06
ROPE_BASE = 1000000.0
BETA_ONE = 0.9
BETA_TWO = 0.95
ADAM_EPS = 1e-08
DECAY = 0.1


DP = ("zh", "zl")
SEQ = ("y", "x", "c")
ALL = DP + SEQ


def low(value):
    return value.astype(jnp.bfloat16)


def wide(value):
    return value.astype(jnp.float32)


def after(value, *others):
    return lax.optimization_barrier((value,) + others)[0]


def shift(value, axis, step):
    count = lax.axis_size(axis)
    return lax.ppermute(value, axis, [(i, (i + step) % count) for i in range(count)])


def rotations(value, axis):
    return [value] + [shift(value, axis, step) for step in range(1, lax.axis_size(axis))]


def plane_steps():
    return [(j, i) for j in range(lax.axis_size("y")) for i in range(lax.axis_size("x"))]


def plane_shift(value, down, right):
    tall, broad = lax.axis_size("y"), lax.axis_size("x")
    pairs = [
        (j * broad + i, (j + down) % tall * broad + (i + right) % broad)
        for j in range(tall)
        for i in range(broad)
    ]
    return lax.ppermute(value, ("y", "x"), pairs)


def plane_pieces(value, dim, cut):
    across, along = rotations(value, "x"), rotations(value, "y")
    size = value.shape[dim]
    pieces = []
    for j, i in plane_steps():
        if j == 0 or i == 0:
            pieces.append((across[i] if j == 0 else along[j],))
        else:
            head = lax.slice_in_dim(across[i], 0, cut, axis=dim)
            tail = lax.slice_in_dim(along[j], cut, size, axis=dim)
            pieces.append((shift(head, "y", j), shift(tail, "x", i)))
    return pieces


def seq_gather_small(value):
    mine = [value] + [plane_shift(value, j, i) for j, i in plane_steps()[1:]]
    return jnp.concatenate(rotations(jnp.concatenate(mine, axis=0), "c"), axis=0)


def seq_scatter_small(value, rows):
    part = value.shape[0] // lax.axis_size("c")
    total = add_back(
        [value[step * part : (step + 1) * part] for step in range(lax.axis_size("c"))], "c"
    )
    result = [total[:rows]]
    for number, (j, i) in enumerate(plane_steps()[1:], 1):
        term = low(total[number * rows : (number + 1) * rows])
        result.append(plane_shift(term, -j, -i))
    return result


def seq_sources():
    tall, broad, cores = (lax.axis_size(name) for name in SEQ)
    row, col, core = (lax.axis_index(name) for name in SEQ)
    return [
        ((row - j) % tall * broad + (col - i) % broad) * cores + (core - k) % cores
        for k in range(cores)
        for j, i in plane_steps()
    ]


def wanted_columns(columns, width):
    tall, broad, cores = (lax.axis_size(name) for name in SEQ)
    row, col, core = (lax.axis_index(name) for name in SEQ)
    depth, z = lax.axis_size(DP), lax.axis_index(DP)
    place = jnp.arange(columns, dtype=jnp.int32)
    inner, rest = place % width, place // width
    dp_step, rest = rest % depth, rest // depth
    c_step, rest = rest % cores, rest // cores
    x_step, y_step = rest % broad, rest // broad
    seq = ((row - y_step) % tall * broad + (col - x_step) % broad) * cores + (core - c_step) % cores
    source = ((z - dp_step) % depth * (tall * broad * cores) + seq) * width + inner
    return low(jnp.arange(columns, dtype=jnp.int32)[:, None] == source[None, :])


def token_gather(value, order):
    result = []
    for number, block in enumerate(rotations(order(1, value), "zh")):
        block = value if number == 0 else order(2, block)
        if number % 2 == 0:
            grid = [rotations(item, "y") for item in rotations(block, "x")]
            grid = [[grid[i][j] for i in range(len(grid))] for j in range(len(grid[0]))]
        else:
            grid = [rotations(item, "x") for item in rotations(block, "y")]
        result.append([item for line in grid for item in line])
    return result


def add_back(blocks, axis, early=(), log=None):
    total = wide(blocks[0])
    for step in range(1, len(blocks)):
        got = shift(low(blocks[step]), axis, -step)
        if log is not None:
            log.append(got)
        total = total + wide(after(got, *early) if early else got)
    return total


def token_scatter(parts, early=()):
    across, along = lax.axis_size("x"), lax.axis_size("y")
    lines, first, second = [], [], []
    for number, blocks in reversed(list(enumerate(parts))):
        grid = [blocks[j * across : (j + 1) * across] for j in range(along)]
        axes = ("y", "x") if number % 2 == 0 else ("x", "y")
        if number % 2 == 0:
            grid = [list(column) for column in zip(*grid)]
        sums = [add_back(line, axes[0], log=first) for line in grid]
        lines.append(add_back(sums, axes[1], early, log=second))
    lines = lines[::-1]
    last = lines.pop()
    sent = shift(low(last), "zh", -len(lines))
    return lines + [last], add_back(lines, "zh"), sent, first, second


VMEM_BYTES = 56 * 2**20
ANYWHERE = pl.BlockSpec(memory_space=pl.ANY)
SCALARS = pl.BlockSpec(memory_space=pltpu.SMEM)


def projection_pieces(block):
    rows, columns = block.shape
    depth = lax.axis_size(DP)
    tall, broad, cores = (lax.axis_size(name) for name in SEQ)
    if rows % 16:
        whole = lax.all_gather(block, ALL, axis=0, tiled=True)
        return ([whole], None, None), whole, whole
    line = rotations(block, DP)
    cut = columns // 2
    z = lax.axis_index(DP)
    z_sources = [(z - k) % depth for k in range(depth)]
    sources = seq_sources()
    own = plane_pieces(jnp.stack(line), 2, cut)
    pieces, plan, targets = [], [], []
    for k in range(cores):
        for number, piece in enumerate(own):
            for part, value in enumerate(piece):
                pieces.append(value if k == 0 else shift(value, "c", k))
                place = (part * cut, cut) if len(piece) == 2 else (0, columns)
                plan.append([(slot, len(targets) + slot, place) for slot in range(depth)])
                seq = sources[k * len(own) + number]
                targets += [(z_sources[slot] * tall * broad * cores + seq) * rows for slot in range(depth)]
    return (pieces, plan, jnp.stack(targets).astype(jnp.int32)), line[-1], own[-1][-1]


def start_pieces(plan, where_ref, pieces, whole, sems):
    if plan is None:
        copies = [pltpu.make_async_copy(pieces[0], whole, sems.at[0])]
    else:
        copies = []
        for piece, jobs in zip(pieces, plan):
            for slot, target, columns in jobs:
                first = pl.multiple_of(where_ref[target], 16)
                copies.append(
                    pltpu.make_async_copy(
                        piece.at[slot],
                        whole.at[pl.ds(first, piece.shape[1]), pl.ds(*columns)],
                        sems.at[len(copies)],
                    )
                )
    for copy in copies:
        copy.start()
    return copies


def call_with_pieces(kernel, projection, operands, outs, name, micros):
    pieces, plan, targets = projection
    count = 1 if plan is None else sum(len(jobs) for jobs in plan)
    if targets is None:
        targets = jnp.zeros((8,), jnp.int32)
    size = len(operands)

    def run(*refs):
        where_ref, rest = refs[0], refs[1:]
        whole, sems = rest[-2], rest[-1]
        copies = start_pieces(plan, where_ref, rest[size : size + len(pieces)], whole, sems)

        def ready():
            for copy in copies:
                copy.wait()

        kernel(ready, whole, *rest[:size], *rest[size + len(pieces) : -2])

    return pl.pallas_call(
        run,
        out_shape=outs,
        in_specs=[SCALARS]
        + [pl.BlockSpec(memory_space=pltpu.VMEM)] * size
        + [ANYWHERE] * len(pieces),
        scratch_shapes=[
            pltpu.VMEM((D, QKV), jnp.bfloat16),
            pltpu.SemaphoreType.DMA((count,)),
        ],
        compiler_params=pltpu.CompilerParams(vmem_limit_bytes=VMEM_BYTES),
        cost_estimate=cost(micros),
        name=name,
    )(targets, *operands, *pieces)


def local_call(kernel, operands, outs, name, micros, scratch=()):
    return pl.pallas_call(
        kernel,
        out_shape=outs,
        scratch_shapes=list(scratch),
        compiler_params=pltpu.CompilerParams(vmem_limit_bytes=VMEM_BYTES),
        cost_estimate=cost(micros),
        name=name,
    )(*operands)


def cost(micros):
    return pl.CostEstimate(flops=int(micros * 1.1e9), bytes_accessed=0, transcendentals=0)


def shaped(shape, dtype):
    return jax.ShapeDtypeStruct(shape, dtype)


def dot(left, right, left_dim, right_dim):
    return lax.dot_general(
        left, right, (((left_dim,), (right_dim,)), ((), ())), preferred_element_type=jnp.float32
    )


def swap_halves(values):
    return pltpu.roll(values, HEAD_DIM // 2, 1)


def turned(values, cosine, sine):
    return values * cosine + swap_halves(values) * sine


def turned_back(grads, cosine, sine):
    return grads * cosine + swap_halves(grads * sine)


def front_kernel(
    ready, whole, rows_ref, gain_ref, bias_ref, cosine_ref, sine_ref, normed_ref, query_ref, pair_ref
):
    rows = wide(rows_ref[...])
    normed_ref[...] = low(rows * norm_scale(rows) * gain_ref[...])
    normed = normed_ref[...]
    cosine, sine = cosine_ref[...], sine_ref[...]
    ready()
    for first in range(0, QKV, 256):
        mixed = dot(normed, whole[:, first : first + 256], 1, 0) + bias_ref[:, first : first + 256]
        for start in (0, HEAD_DIM):
            part = mixed[:, start : start + HEAD_DIM]
            column = first + start
            if column < QW + KW:
                part = turned(part, cosine, sine)
            if column < QW:
                query_ref[:, column : column + HEAD_DIM] = low(part)
            else:
                pair_ref[:, column - QW : column - QW + HEAD_DIM] = low(part)


TOGETHER = 2


def head_views(step):
    heads = step * TOGETHER
    kind = heads // (HEADS // KV_HEADS)
    queries = [pl.ds(pl.multiple_of((heads + i) * HEAD_DIM, HEAD_DIM), HEAD_DIM) for i in range(TOGETHER)]
    keys = pl.ds(pl.multiple_of(kind * HEAD_DIM, HEAD_DIM), HEAD_DIM)
    values = pl.ds(pl.multiple_of(KW + kind * HEAD_DIM, HEAD_DIM), HEAD_DIM)
    return queries, keys, values


def visible(key_marks_ref, query_marks_ref):
    seen = (key_marks_ref[:, 0:1] == query_marks_ref[0:1, :]) & (
        key_marks_ref[:, 1:2] <= query_marks_ref[1:2, :]
    )
    return jnp.concatenate([jnp.where(seen, 0.0, -1e30)] * TOGETHER, axis=1)


def probabilities(keys, query, hidden):
    scores = dot(keys, query, 1, 1) * (HEAD_DIM**-0.5) + hidden
    grown = jnp.exp(scores - jnp.max(scores, axis=0, keepdims=True))
    return grown * (1.0 / jnp.sum(grown, axis=0, keepdims=True))


def attend_kernel(
    query_ref, pair_ref, key_marks_ref, query_marks_ref, rows_ref, out_ref, gain_ref,
    attended_ref, middle_ref, normed_ref, hidden_ref,
):
    hidden_ref[...] = visible(key_marks_ref, query_marks_ref)

    def step(index, unused):
        queries, keys, values = head_views(index)
        query = jnp.concatenate([query_ref[:, view] for view in queries], axis=0)
        weights = low(probabilities(pair_ref[:, keys], query, hidden_ref[...]))
        result = low(dot(weights, pair_ref[:, values], 0, 0))
        count = query_ref.shape[0]
        for i, view in enumerate(queries):
            attended_ref[:, view] = result[i * count : (i + 1) * count]
        return unused

    lax.fori_loop(0, HEADS // TOGETHER, step, 0)
    middle = wide(rows_ref[...]) + dot(attended_ref[...], out_ref[...], 1, 0)
    middle_ref[...] = middle
    normed_ref[...] = low(middle * norm_scale(middle) * gain_ref[...])


def attend_back_kernel(
    normed_grad_ref, received_ref, middle_ref, back_ref, gain_ref, out_ref, query_ref, pair_ref,
    key_marks_ref, query_marks_ref, cosine_ref, sine_ref,
    middle_grad_ref, branch_ref, mixed_ref, pair_grad_ref, gain_grad_ref,
    hidden_ref, attended_grad_ref,
):
    hidden_ref[...] = visible(key_marks_ref, query_marks_ref)
    normed_grad = normed_grad_ref[...] + wide(received_ref[...])
    middle = middle_ref[...]
    scale = norm_scale(middle)
    weighted = gain_ref[...] * normed_grad
    middle_grad = (
        wide(back_ref[...])
        + scale * weighted
        - middle * scale**3 * jnp.mean(weighted * middle, axis=1, keepdims=True)
    )
    gain_grad_ref[...] = jnp.sum(normed_grad * middle * scale, axis=0, keepdims=True)
    middle_grad_ref[...] = middle_grad
    branch_ref[...] = low(middle_grad)
    attended_grad_ref[...] = low(dot(branch_ref[...], out_ref[...], 1, 1))
    pair_grad_ref[...] = jnp.zeros_like(pair_grad_ref)
    cosine, sine = cosine_ref[...], sine_ref[...]

    def step(index, unused):
        queries, keys, values = head_views(index)
        query = jnp.concatenate([query_ref[:, view] for view in queries], axis=0)
        grad = jnp.concatenate([attended_grad_ref[:, view] for view in queries], axis=0)
        key = pair_ref[:, keys]
        weights = probabilities(key, query, hidden_ref[...])
        pulled = dot(pair_ref[:, values], grad, 1, 1)
        delta = jnp.sum(weights * pulled, axis=0, keepdims=True)
        score_grad = low(weights * (pulled - delta))
        query_grad = dot(score_grad, key, 0, 0) * (HEAD_DIM**-0.5)
        count = query_ref.shape[0]
        for i, view in enumerate(queries):
            mixed_ref[:, view] = low(
                turned_back(query_grad[i * count : (i + 1) * count], cosine, sine)
            )
        pair_grad_ref[:, keys] += dot(score_grad, query, 1, 0) * (HEAD_DIM**-0.5)
        pair_grad_ref[:, values] += dot(low(weights), grad, 1, 0)
        return unused

    lax.fori_loop(0, HEADS // TOGETHER, step, 0)


def query_kernel(ready, whole, mixed_ref, normed_grad_ref, bias_grad_ref, pair_rows_ref):
    mixed = mixed_ref[...]
    bias_grad_ref[...] = jnp.sum(wide(mixed), axis=0, keepdims=True)
    ready()
    normed_grad_ref[...] = dot(mixed, whole[:, :QW], 1, 1)
    pair_rows_ref[...] = whole[:, QW:]


def finish_kernel(count, *refs):
    terms, refs = refs[:count], refs[count:]
    cosine_ref, sine_ref, part_ref, pair_rows_ref, rows_ref, gain_ref, middle_grad_ref = refs[:7]
    pair_ref, input_grad_ref, gain_grad_ref, bias_grad_ref = refs[7:]
    total = terms[0][...]
    for term in terms[1:]:
        total = total + wide(term[...])
    for first in range(0, 2 * KW, HEAD_DIM):
        part = total[:, first : first + HEAD_DIM]
        if first < KW:
            part = turned_back(part, cosine_ref[...], sine_ref[...])
        pair_ref[:, first : first + HEAD_DIM] = low(part)
    rows = wide(rows_ref[...])
    scale = norm_scale(rows)
    pair = pair_ref[...]
    bias_grad_ref[...] = jnp.sum(wide(pair), axis=0, keepdims=True)
    normed_grad = part_ref[...] + dot(pair, pair_rows_ref[...], 1, 1)
    weighted = gain_ref[...] * normed_grad
    input_grad_ref[...] = (
        middle_grad_ref[...]
        + scale * weighted
        - rows * scale**3 * jnp.mean(weighted * rows, axis=1, keepdims=True)
    )
    gain_grad_ref[...] = jnp.sum(normed_grad * rows * scale, axis=0, keepdims=True)


def unit_tile(units):
    return units // 2 if units % 32 == 0 else units


def units_kernel(size, *refs):
    normed_refs, back_refs, units_ref = refs[:size], refs[size : 2 * size], refs[2 * size]
    hidden_ref, gate_ref, up_ref, *out_refs = refs[2 * size + 1 : 3 * size + 4]
    normed_rows, back_rows, total = refs[3 * size + 4 :]
    count = normed_refs[0].shape[0]
    step = pl.program_id(0)

    @pl.when(step == 0)
    def _():
        for number in range(size):
            view = slice(number * count, (number + 1) * count)
            normed_rows[view, :] = normed_refs[number][...]
            back_rows[view, :] = back_refs[number][...]
        total[...] = jnp.zeros_like(total)

    normed = normed_rows[...]
    gate = dot(units_ref[0], normed, 1, 1)
    up = dot(units_ref[1], normed, 1, 1)
    pulled = dot(units_ref[2], back_rows[...], 1, 1)
    sigma = jax.nn.sigmoid(gate)
    active = gate * sigma
    hidden_ref[...] = low(active * up)
    gate_grad = low(pulled * up * sigma * (1.0 + gate * (1.0 - sigma)))
    up_grad = low(pulled * active)
    gate_ref[...] = gate_grad
    up_ref[...] = up_grad
    total[...] += dot(gate_grad, units_ref[0], 0, 0) + dot(up_grad, units_ref[1], 0, 0)

    @pl.when(step == pl.num_programs(0) - 1)
    def _():
        for number in range(size):
            out_refs[number][...] = low(total[number * count : (number + 1) * count])


def whole_block(shape):
    return pl.BlockSpec(shape, lambda i: (0,) * len(shape))


def units_forward(normed, back, units):
    size, count = len(normed), normed[0].shape[0]
    tile, tokens = unit_tile(units.shape[1]), size * count
    token_block = whole_block((count, D))
    by_unit = pl.BlockSpec((tile, tokens), lambda i: (i, 0))
    return pl.pallas_call(
        lambda *refs: units_kernel(size, *refs),
        grid=(units.shape[1] // tile,),
        in_specs=[token_block] * (2 * size) + [pl.BlockSpec((3, tile, D), lambda i: (0, i, 0))],
        out_specs=[by_unit] * 3 + [token_block] * size,
        out_shape=[shaped((units.shape[1], tokens), jnp.bfloat16)] * 3
        + [shaped((count, D), jnp.bfloat16)] * size,
        scratch_shapes=[
            pltpu.VMEM((tokens, D), jnp.bfloat16),
            pltpu.VMEM((tokens, D), jnp.bfloat16),
            pltpu.VMEM((tokens, D), jnp.float32),
        ],
        compiler_params=pltpu.CompilerParams(vmem_limit_bytes=VMEM_BYTES),
        cost_estimate=cost(10),
        name="units_forward",
    )(*normed, *back, units)


def gradient_kernel(parts, size, *refs):
    by_unit, refs = refs[: 3 * parts], refs[3 * parts :]
    normed_refs, back_refs, out_ref = refs[:size], refs[size : 2 * size], refs[2 * size]
    normed_rows, back_rows = refs[2 * size + 1 :]
    count = normed_refs[0].shape[0]

    @pl.when(pl.program_id(0) == 0)
    def _():
        for number in range(size):
            view = slice(number * count, (number + 1) * count)
            normed_rows[view, :] = normed_refs[number][...]
            back_rows[view, :] = back_refs[number][...]

    for kind, rows in ((0, normed_rows), (1, normed_rows), (2, back_rows)):
        place = (kind + 1) % 3
        values = [by_unit[3 * part + place][...] for part in range(parts)]
        out_ref[kind] = low(dot(jnp.concatenate(values, axis=1), rows[...], 1, 0))


def units_gradient(parts, normed, back):
    units, tokens = parts[0][0].shape
    size, count = len(normed), normed[0].shape[0]
    tile = unit_tile(units)
    token_block = whole_block((count, D))
    return pl.pallas_call(
        lambda *refs: gradient_kernel(len(parts), size, *refs),
        grid=(units // tile,),
        in_specs=[pl.BlockSpec((tile, tokens), lambda i: (i, 0))] * (3 * len(parts))
        + [token_block] * (2 * size),
        out_specs=pl.BlockSpec((3, tile, D), lambda i: (0, i, 0)),
        out_shape=shaped((3, units, D), jnp.bfloat16),
        scratch_shapes=[
            pltpu.VMEM((size * count, D), jnp.bfloat16),
            pltpu.VMEM((size * count, D), jnp.bfloat16),
        ],
        compiler_params=pltpu.CompilerParams(vmem_limit_bytes=VMEM_BYTES),
        cost_estimate=cost(11),
        name="units_gradient",
    )(*[item for part in parts for item in part], *normed, *back)


def branch_kernel(parts, *refs):
    hidden_refs, units_ref, out_refs, total = refs[:parts], refs[parts], refs[parts + 1 : -1], refs[-1]
    step = pl.program_id(0)

    @pl.when(step == 0)
    def _():
        total[...] = jnp.zeros_like(total)

    hidden = jnp.concatenate([ref[...] for ref in hidden_refs], axis=1)
    total[...] += dot(hidden, units_ref[0], 0, 0)

    @pl.when(step == pl.num_programs(0) - 1)
    def _():
        count = out_refs[0].shape[0]
        for number, out_ref in enumerate(out_refs):
            out_ref[...] = low(total[number * count : (number + 1) * count])


def units_branch(hidden, units, count):
    tokens = sum(item.shape[1] for item in hidden)
    tile = unit_tile(units.shape[1])
    size = tokens // count
    return pl.pallas_call(
        lambda *refs: branch_kernel(len(hidden), *refs),
        grid=(units.shape[1] // tile,),
        in_specs=[pl.BlockSpec((tile, item.shape[1]), lambda i: (i, 0)) for item in hidden]
        + [pl.BlockSpec((1, tile, D), lambda i: (2, i, 0))],
        out_specs=[whole_block((count, D))] * size,
        out_shape=[shaped((count, D), jnp.bfloat16)] * size,
        scratch_shapes=[pltpu.VMEM((tokens, D), jnp.float32)],
        compiler_params=pltpu.CompilerParams(vmem_limit_bytes=VMEM_BYTES),
        cost_estimate=cost(5),
        name="units_branch",
    )(*hidden, units)


def weight_kernel(plan, *refs):
    count = max(job[0] for job in plan) + 1
    lefts, rights = refs[:count], refs[count:-2]
    kept_ref, sent_ref = refs[-2:]
    left, right = [], []
    for number, first, size in plan:
        left.append(lefts[number][first : first + size, :])
        right.append(rights[len(right)][...])
    total = dot(jnp.concatenate(left, axis=0), jnp.concatenate(right, axis=0), 0, 0)
    half = total.shape[0] // 2
    kept_ref[...] = total[:half]
    sent_ref[...] = low(total[half:])


def weight_term(lefts, pieces, name):
    plan, rights = [], []
    for number, piece in enumerate(pieces):
        first = 0
        for value in piece:
            plan.append((number, first, value.shape[0]))
            first += value.shape[0]
            rights.append(value)
    shape = (lefts[0].shape[1] // 2, rights[0].shape[1])
    kept, sent = local_call(
        lambda *refs: weight_kernel(plan, *refs),
        list(lefts) + rights,
        [shaped(shape, jnp.float32), shaped(shape, jnp.bfloat16)],
        name,
        3,
    )
    return kept, shift(sent, "c", -1)


def dp_scatter(total, early=()):
    depth = lax.axis_size(DP)
    width = total.shape[0] // depth
    return add_back([total[i * width : (i + 1) * width] for i in range(depth)], DP, early)


def norm_scale(rows):
    return lax.rsqrt(jnp.mean(rows * rows, axis=1, keepdims=True) + NORM_EPS)


def unpack_small(small):
    gain_cols = D // KW
    group = HEADS // KV_HEADS
    gain_one = small[:, :gain_cols].reshape(D)
    gain_two = small[:, gain_cols : 2 * gain_cols].reshape(D)
    query_bias = small[:, 2 * gain_cols : 2 * gain_cols + group].reshape(KV_HEADS, HEAD_DIM, group)
    query_bias = jnp.transpose(query_bias, (0, 2, 1)).reshape(QW)
    key_bias = small[:, 2 * gain_cols + group]
    value_bias = small[:, 2 * gain_cols + group + 1]
    return (gain_one, gain_two, jnp.concatenate([query_bias, key_bias, value_bias]))


def pack_small(gain_one, gain_two, bias):
    gain_cols = D // KW
    group = HEADS // KV_HEADS
    query_part = jnp.transpose(bias[:QW].reshape(KV_HEADS, group, HEAD_DIM), (0, 2, 1)).reshape(
        KW, group
    )
    return jnp.concatenate(
        [
            gain_one.reshape(KW, gain_cols),
            gain_two.reshape(KW, gain_cols),
            query_part,
            bias[QW : QW + KW][:, None],
            bias[QW + KW :][:, None],
        ],
        axis=1,
    )


def layout(starts_row, places):
    before = starts_row[None, :] <= places[:, None]
    documents = jnp.sum(before.astype(jnp.int32), axis=1) - 1
    begin = jnp.max(jnp.where(before, starts_row[None, :], 0), axis=1)
    offset = places - begin
    return (documents, offset // BLOCK, offset)


def turning(offset):
    half = HEAD_DIM // 2
    frequency = ROPE_BASE ** (-(2.0 * jnp.arange(half, dtype=jnp.float32)) / HEAD_DIM)
    angle = offset.astype(jnp.float32)[:, None] * frequency[None, :]
    angle = jnp.concatenate([angle, angle], axis=1)
    return (jnp.cos(angle)[:, None, :], jnp.sin(angle)[:, None, :])


def optimizer_step(weight, grad, first, second, rate, decay):
    first = BETA_ONE * first + (1.0 - BETA_ONE) * grad
    second = BETA_TWO * second + (1.0 - BETA_TWO) * grad * grad
    fixed_first = first / (1.0 - BETA_ONE**STEP)
    fixed_second = second / (1.0 - BETA_TWO**STEP)
    weight = weight - rate * (fixed_first / (jnp.sqrt(fixed_second) + ADAM_EPS) + decay * weight)
    return (weight, first, second, weight.astype(jnp.bfloat16))


def body(
    inputs,
    output_grad,
    document_starts,
    joined_weight,
    out_weight,
    units_weight,
    small_params,
    joined_first,
    joined_second,
    out_first,
    out_second,
    units_first,
    units_second,
    small_first,
    small_second,
):
    count = inputs.shape[0]
    seq_count = lax.axis_size(SEQ)
    devices = seq_count * lax.axis_size(DP)
    seq_index = lax.axis_index(SEQ)
    group_len = count * seq_count
    first = seq_index * count
    starts_row = document_starts[0]
    feature_width = joined_weight.shape[0]
    unit_width = units_weight.shape[0]

    device = lax.axis_index(ALL)
    small_rows, small_cols = small_params.shape
    vector = lax.dynamic_update_slice_in_dim(
        jnp.zeros((devices * small_rows, small_cols), jnp.float32),
        wide(low(small_params)),
        device * small_rows,
        0,
    )
    vector = jnp.concatenate(unpack_small(vector)).reshape(1, -1)
    for axis in ("c", "x", "y", DP):
        vector = sum(rotations(vector, axis))
    gain_one, gain_two, bias = vector[:, :D], vector[:, D : 2 * D], vector[:, 2 * D :]

    projection, along_dp, at_last = projection_pieces(low(joined_weight))
    full_out = lax.all_gather(low(out_weight), ALL, axis=0, tiled=True)
    documents, blocks, offset = layout(starts_row, first + jnp.arange(count, dtype=jnp.int32))
    cosine, sine = turning(offset)
    cosine, sine = cosine[:, 0], sine[:, 0]
    sine = jnp.concatenate([-sine[:, : HEAD_DIM // 2], sine[:, HEAD_DIM // 2 :]], axis=1)
    sources = seq_sources()
    places = jnp.concatenate([i * count + jnp.arange(count, dtype=jnp.int32) for i in sources])
    all_documents, all_blocks, unused_offset = layout(starts_row, places)
    key_marks = jnp.stack([all_documents, all_blocks], axis=1)
    query_marks = jnp.stack([documents, blocks], axis=0)
    wanted = wanted_columns(D, feature_width)

    sharing = ("zl", "c")
    units_half = after(low(units_weight), along_dp)
    units_all = lax.all_gather(units_half, sharing, axis=0, tiled=True)
    units_all = jnp.transpose(units_all, (1, 0, 2))

    normed_one, query, pair = call_with_pieces(
        front_kernel,
        projection,
        [inputs, gain_one, bias, cosine, sine],
        [
            shaped((count, D), jnp.bfloat16),
            shaped((count, QW), jnp.bfloat16),
            shaped((count, 2 * KW), jnp.bfloat16),
        ],
        "front",
        6,
    )
    pair_all = seq_gather_small(pair)

    back_blocks = token_gather(
        output_grad,
        lambda stage, value: after(value, along_dp) if stage == 1 else after(value, at_last),
    )

    attended, middle, normed_two = local_call(
        attend_kernel,
        [after(query, *back_blocks[0], *back_blocks[-1]), pair_all, key_marks, query_marks, inputs, full_out, gain_two],
        [
            shaped((count, QW), jnp.bfloat16),
            shaped((count, D), jnp.float32),
            shaped((count, D), jnp.bfloat16),
        ],
        "attend",
        12,
        [pltpu.VMEM((group_len, TOGETHER * count), jnp.float32)],
    )

    steps = plane_steps()
    normed_sent = low(dot(after(normed_one, normed_two), wanted, 1, 0))
    attended_sent = low(dot(attended, wanted, 1, 0))
    chip_width = D // len(steps)
    normed_owned, attended_owned = [], []
    for number, (j, i) in enumerate(steps):
        view = slice(number * chip_width, (number + 1) * chip_width)
        both = [normed_sent[:, view], attended_sent[:, view]]
        if number:
            moved = plane_shift(jnp.concatenate(both, axis=1), -j, -i)
            both = [moved[:, :chip_width], moved[:, chip_width:]]
        normed_owned.append(both[0])
        attended_owned.append(both[1])

    normed_blocks = token_gather(normed_two, lambda stage, value: value)
    unit_parts = [
        units_forward(normed, back, units_all)
        for normed, back in zip(normed_blocks, back_blocks)
    ]
    grad_terms = [part[3:] for part in unit_parts]
    hidden_parts = [part[0] for part in unit_parts]
    units_term = units_gradient(
        [part[:3] for part in unit_parts],
        [block for line in normed_blocks for block in line],
        [block for line in back_blocks for block in line],
    )
    units_grad = wide(
        lax.psum_scatter(
            jnp.transpose(units_term, (1, 0, 2)), sharing, scatter_dimension=0, tiled=True
        )
    )
    plane_sums, normed_grad_own, normed_grad_received, grads_first, unused = token_scatter(grad_terms)
    branch_terms = units_branch(hidden_parts, after(units_all, units_term, *grads_first), count)
    normed_grad_own = after(normed_grad_own, *branch_terms)
    branch_terms = [after(item, *plane_sums) for item in branch_terms]
    line = len(normed_blocks[0])
    branch_terms = [branch_terms[k : k + line] for k in range(0, len(branch_terms), line)]
    unused, branch_own, branch_received, branch_first, branch_second = token_scatter(branch_terms)
    block_output = low(middle + branch_own + wide(branch_received))

    middle = after(middle, *normed_owned, *attended_owned)
    middle_grad, branch_grad, mixed_grad, pair_grad, gain_two_grad = local_call(
        attend_back_kernel,
        [
            normed_grad_own,
            normed_grad_received,
            middle,
            output_grad,
            gain_two,
            full_out,
            query,
            pair_all,
            key_marks,
            query_marks,
            cosine,
            sine,
        ],
        [
            shaped((count, D), jnp.float32),
            shaped((count, D), jnp.bfloat16),
            shaped((count, QW), jnp.bfloat16),
            shaped((group_len, 2 * KW), jnp.float32),
            shaped((1, D), jnp.float32),
        ],
        "attend_back",
        16,
        [
            pltpu.VMEM((group_len, TOGETHER * count), jnp.float32),
            pltpu.VMEM((count, QW), jnp.bfloat16),
        ],
    )
    pair_terms = seq_scatter_small(pair_grad, count)
    query_pieces = plane_pieces(mixed_grad, 0, count // 2)
    branch_pieces = plane_pieces(branch_grad, 0, count // 2)
    normed_grad_part, query_bias_grad, pair_rows = call_with_pieces(
        query_kernel,
        projection,
        [mixed_grad],
        [
            shaped((count, D), jnp.float32),
            shaped((1, QW), jnp.float32),
            shaped((D, 2 * KW), jnp.bfloat16),
        ],
        "query_back",
        7,
    )
    straight = [piece[0] for piece in query_pieces + branch_pieces if len(piece) == 1]
    pair_terms[0] = after(pair_terms[0], *straight, *branch_first)
    pair_mixed, input_grad, gain_one_grad, pair_bias_grad = local_call(
        lambda *refs: finish_kernel(len(pair_terms), *refs),
        pair_terms
        + [cosine, sine, normed_grad_part, pair_rows, inputs, gain_one, middle_grad],
        [
            shaped((count, 2 * KW), jnp.bfloat16),
            shaped((count, D), jnp.float32),
            shaped((1, D), jnp.float32),
            shaped((1, 2 * KW), jnp.float32),
        ],
        "finish",
        4,
    )
    pair_pieces = [(pair_mixed,)] + [(plane_shift(pair_mixed, j, i),) for j, i in steps[1:]]
    vector = jnp.concatenate([gain_one_grad, gain_two_grad, query_bias_grad, pair_bias_grad], axis=1)
    vector = sum(rotations(vector, "c"))
    attended_owned[0] = after(attended_owned[0], vector)
    kept, got = weight_term(attended_owned, branch_pieces, "out_weights")
    vector = sum(rotations(vector, "x"))
    normed_owned[0] = after(normed_owned[0], got, vector, *branch_second)
    outer_grad = dp_scatter(kept + wide(got))
    query_kept, query_got = weight_term(normed_owned, query_pieces, "query_weights")
    vector = sum(rotations(vector, "y"))
    pair_pieces[0] = (after(pair_mixed, query_got, vector),)
    pair_kept, pair_got = weight_term(normed_owned, pair_pieces, "pair_weights")
    units_new = optimizer_step(
        units_weight, units_grad, units_first, units_second, 2.0 / math.sqrt(D), DECAY
    )
    joined_grad = dp_scatter(
        jnp.concatenate([query_kept + wide(query_got), pair_kept + wide(pair_got)], axis=1),
        [units_new[3]],
    )
    vector = sum(rotations(vector, DP)).reshape(-1)
    small_grad = pack_small(vector[:D], vector[D : 2 * D], vector[2 * D :])
    small_grad = lax.dynamic_slice_in_dim(small_grad, device * small_rows, small_rows, 0)

    joined = optimizer_step(
        joined_weight, joined_grad, joined_first, joined_second, 2.0 / math.sqrt(D), DECAY
    )
    outer = optimizer_step(
        out_weight, outer_grad, out_first, out_second, 2.0 / math.sqrt(QW // 64), DECAY
    )
    small = optimizer_step(small_params, small_grad, small_first, small_second, 0.5, 0.0)
    return (block_output, input_grad) + joined + outer + units_new + small


def solution(mesh):
    groups, members = mesh.devices.shape
    fine = Mesh(mesh.devices.reshape(groups // 2, 2, members // 4, 2, 2), ALL)
    flat, cube = P(ALL, None), P(ALL, None, None)
    in_specs = (flat, flat, P(DP, None), flat, flat, cube, flat) + (flat,) * 4 + (cube,) * 2 + (flat,) * 2
    out_specs = (flat,) * 10 + (cube,) * 4 + (flat,) * 4
    return jax.shard_map(body, mesh=fine, in_specs=in_specs, out_specs=out_specs, check_vma=False)
```

time: 586 us -> 503 us (0.86)
  matrix products: 124 us -> 4.12 us
  Pallas kernels: 0 us -> 117 us
  blocking collectives: 77 us -> 0 us
  starting transfers between devices: 37.5 us -> 81.9 us
  other arithmetic: 61 us -> 35.7 us
  waiting for transfers between devices: 223 us -> 210 us
  local copies, waits for them, and re-layouts: 39 us -> 30.1 us
    dot_general x30 -> x2, matrix products: 124 us -> 4.12 us  [dot(): lax.dot_general(left, right, (((left_dim,), (right_dim,)), ((), ())), pre...]
    pallas_call x0 -> x12, Pallas kernels: none -> 117 us  [the longest x6 41.5 us: local_call(): pl.pallas_call(kernel, out_shape=outs, scratch_shapes=list(scratch), comp...]
    unnamed x1 -> x0, blocking collectives: 77 us -> none
    all_gather x4 -> x2, waiting for transfers between devices: 67.7 us -> 12 us  [the longest x1 12 us: body(): units_all = lax.all_gather(units_half, sharing, axis=0, tiled=True)]
    ppermute x39 -> x71, waiting for transfers between devices: 137 us -> 179 us  [shift(): lax.ppermute(value, axis, [(i, (i + step) % count) for i in range(count)])]
    ppermute x39 -> x71, starting transfers between devices: 32.7 us -> 70.8 us  [shift(): lax.ppermute(value, axis, [(i, (i + step) % count) for i in range(count)])]
    ppermute x0 -> x12, waiting for transfers between devices: none -> 18.7 us  [plane_shift(): return lax.ppermute(value, ('y', 'x'), pairs)]
    all_to_all x1 -> x0, waiting for transfers between devices: 12.1 us -> none  [body(): owned = lax.all_to_all(sent, SEQ, split_axis=0, concat_axis=0, tiled=True)]
  transfers between devices with their start and end apart: 47 -> 86, of which waited for: 16 -> 37; matrix products, arithmetic and copies ran while one was open for 33% -> 10% of each run, Pallas kernels for 0% -> 17%
where the time goes in v2:
time: 503 us; the launch traced here: 494 us
  waiting for transfers between devices  210 us (42%)
  Pallas kernels  117 us (23%)
  starting transfers between devices  81.9 us (16%)
  other arithmetic  35.7 us (7%)
  local copies, waits for them, and re-layouts  30.1 us (6%)
  between operations  15.2 us (3%)
    ppermute x71, waiting for transfers between devices, shift(): lax.ppermute(value, axis, [(i, (i + step) % count) for i in range(count)])  179 us
    ppermute x71, starting transfers between devices, shift(): lax.ppermute(value, axis, [(i, (i + step) % count) for i in range(count)])  70.8 us
    pallas_call x6, Pallas kernels, local_call(): pl.pallas_call(kernel, out_shape=outs, scratch_shapes=list(scratch), comp...  41.5 us
    pallas_call x2, Pallas kernels, units_forward(): pl.pallas_call(lambda *refs: units_kernel(size, *refs), grid=(units.shape...  34.3 us
    ppermute x12, waiting for transfers between devices, plane_shift(): return lax.ppermute(value, ('y', 'x'), pairs)  18.7 us
    pallas_call x1, Pallas kernels, units_gradient(): pl.pallas_call(lambda *refs: gradient_kernel(len(parts), size, *refs), gr...  18.2 us
    unnamed x154, local copies, waits for them, and re-layouts  17.4 us
    convert_element_type x4, other arithmetic, optimizer_step(): return (weight, first, second, weight.astype(jnp.bfloat16))  16.8 us
  transfers between devices with their start and end apart: 86, of which 37 were waited for; matrix products, arithmetic and copies ran while one was open for 10% of the time, Pallas kernels for 17%

profile of v2, /device:TPU:7, one launch (start us, length us, event | category | flops | bytes accessed | tf_op | source)
XLA Modules:
  0.0 494.0 jit_solution(1478507478676903903)
XLA Ops:
  7.2 1.6 convert_element_type.180
  10.0 3.4 collective-permute-start.8
  13.4 4.2 convert_element_type.181
  18.3 3.1 collective-permute-start.6
  22.5 2.2 collective-permute-start
  26.3 9.5 %collective-permute-done.7 = bf16[48,2048]{1,0:T(8,128)(2,1)S(1)} collective-permute-done((bf16[48,2048]{1,0:T(8,128)(2,1)S(1)}, bf16[48,2048]{1,0:T(8,128)(2,1)S(1)}, u32[]{:S(2)}, u32[]{:S(2)}) %collective-permute-start.7) | collective-permute-done | bytes 196640 | tf_op jit(solution)/shard_map/ppermute | solution.py:50
  38.6 19.4 %collective-permute-done.1 = f32[1,5120]{1,0:T(1,128)S(1)} collective-permute-done((f32[1,5120]{1,0:T(1,128)S(1)}, f32[1,5120]{1,0:T(1,128)S(1)}, u32[]{:S(2)}, u32[]{:S(2)}) %collective-permute-start.1) | collective-permute-done | bytes 20512 | tf_op jit(solution)/shard_map/ppermute | solution.py:50
  61.2 1.4 collective-permute-start.4
  66.0 3.9 collective-permute-start.13
  72.8 12.7 %collective-permute-done.12.refs_10_.refs_6_ = bf16[4,48,1024]{2,1,0:T(8,128)(2,1)S(1)} collective-permute-done((bf16[4,48,1024]{2,1,0:T(8,128)(2,1)S(1)}, bf16[4,48,1024]{2,1,0:T(8,128)(2,1)S(1)}, u32[]{:S(2)}, u32[]{:S(2)}) %collective-permute-start.12) | collective-permute-done | bytes 393248 | tf_op jit(solution)/shard_map/ppermute | solution.py:50
  89.6 6.1 %front.1 = (bf16[128,1536]{1,0:T(8,128)(2,1)}, bf16[128,1536]{1,0:T(8,128)(2,1)}, bf16[128,512]{1,0:T(8,128)(2,1)}) custom-call(s32[40]{0:T(128)} %stack.164.refs_0_, bf16[128,1536]{1,0:T(8,128)(2,1)} %refs_8_.1, f32[1,1536]{1,0:T(1,128)} %get-tuple-element.254.refs_2_.refs_9_, f32[1,2048]{1,0:T(1,128)} %slice.222.refs_3_, ...), custom_call_target="tpu_custom_call" | custom-call | flops 6600000000 | tf_op jit(solution)/shard_map/front/pallas_call | solution.py:233
  95.7 1.5 collective-permute-start.27
  98.4 2.6 collective-permute-done.27
  101.9 3.2 collective-permute-done.26
  111.8 8.4 %collective-permute-done.20.refs_7_.refs_17_ = bf16[128,1536]{1,0:T(8,128)(2,1)S(1)} collective-permute-done((bf16[128,1536]{1,0:T(8,128)(2,1)S(1)}, bf16[128,1536]{1,0:T(8,128)(2,1)S(1)}, u32[]{:S(2)}, u32[]{:S(2)}) %collective-permute-start.20) | collective-permute-done | bytes 393248 | tf_op jit(solution)/shard_map/ppermute | solution.py:50
  120.2 7.4 %collective-permute-done.24.refs_7_.refs_21_ = bf16[128,1536]{1,0:T(8,128)(2,1)S(1)} collective-permute-done((bf16[128,1536]{1,0:T(8,128)(2,1)S(1)}, bf16[128,1536]{1,0:T(8,128)(2,1)S(1)}, u32[]{:S(2)}, u32[]{:S(2)}) %collective-permute-start.24) | collective-permute-done | bytes 393248 | tf_op jit(solution)/shard_map/ppermute | solution.py:50
  128.7 12.1 %attend.1 = (bf16[128,1536]{1,0:T(8,128)(2,1)}, f32[128,1536]{1,0:T(8,128)}, bf16[128,1536]{1,0:T(8,128)(2,1)}) custom-call(bf16[128,1536]{1,0:T(8,128)(2,1)} %get-tuple-element.90.query_ref, bf16[1024,512]{1,0:T(8,128)(2,1)} %copy-done.24, s32[1024,2]{1,0:T(8,128)} %copy.104.key_marks_ref, s32[2,128]{1,0:T(2,128)} %pad_add_fusion.1.query_marks_ref, ...), custom_call_target="tpu_custom_call" | custom-call | flops 13200000000 | tf_op jit(solution)/shard_map/attend/pallas_call | solution.py:250
  140.8 2.2 collective-permute-start.32
  143.1 17.2 %collective-permute-done.32.refs_0_.refs_10_ = bf16[128,1536]{1,0:T(8,128)(2,1)S(1)} collective-permute-done((bf16[128,1536]{1,0:T(8,128)(2,1)}, bf16[128,1536]{1,0:T(8,128)(2,1)S(1)}, u32[]{:S(2)}, u32[]{:S(2)}) %collective-permute-start.32) | collective-permute-done | bytes 393248 | tf_op jit(solution)/shard_map/ppermute | solution.py:50
  162.0 7.3 %collective-permute-done.34.refs_2_.refs_12_ = bf16[128,1536]{1,0:T(8,128)(2,1)S(1)} collective-permute-done((bf16[128,1536]{1,0:T(8,128)(2,1)S(1)}, bf16[128,1536]{1,0:T(8,128)(2,1)S(1)}, u32[]{:S(2)}, u32[]{:S(2)}) %collective-permute-start.34) | collective-permute-done | bytes 393248 | tf_op jit(solution)/shard_map/ppermute | solution.py:50
  171.3 6.6 %collective-permute-done.33.refs_1_.refs_11_ = bf16[128,1536]{1,0:T(8,128)(2,1)S(1)} collective-permute-done((bf16[128,1536]{1,0:T(8,128)(2,1)S(1)}, bf16[128,1536]{1,0:T(8,128)(2,1)S(1)}, u32[]{:S(2)}, u32[]{:S(2)}) %collective-permute-start.33) | collective-permute-done | bytes 393248 | tf_op jit(solution)/shard_map/ppermute | solution.py:50
  177.9 8.4 %collective-permute-done.35.refs_3_.refs_13_ = bf16[128,1536]{1,0:T(8,128)(2,1)S(1)} collective-permute-done((bf16[128,1536]{1,0:T(8,128)(2,1)S(1)}, bf16[128,1536]{1,0:T(8,128)(2,1)S(1)}, u32[]{:S(2)}, u32[]{:S(2)}) %collective-permute-start.35) | collective-permute-done | bytes 393248 | tf_op jit(solution)/shard_map/ppermute | solution.py:50
  186.3 12.0 %all-gather.5.cloned.1.call-done = bf16[1120,3,1536]{2,0,1:T(8,128)(2,1)} async-done(((bf16[280,3,1536]{2,0,1:T(8,128)(2,1)}), bf16[1120,3,1536]{2,0,1:T(8,128)(2,1)}) %all-gather.5.cloned.1.call-update) | async-done | bytes 10321936 | tf_op jit(solution)/shard_map/all_gather | solution.py:728
  198.3 17.1 %units_forward.3 = (bf16[1120,512]{1,0:T(8,128)(2,1)}, bf16[1120,512]{1,0:T(8,128)(2,1)}, bf16[1120,512]{1,0:T(8,128)(2,1)}, bf16[128,1536]{1,0:T(8,128)(2,1)}, ...) custom-call(bf16[128,1536]{1,0:T(8,128)(2,1)} %copy-done.51, ...), custom_call_target="tpu_custom_call" | custom-call | flops 11000000512 | tf_op jit(solution)/shard_map/units_forward/pallas_call | solution.py:480
  217.0 17.1 %units_forward.2 = (bf16[1120,512]{1,0:T(8,128)(2,1)}, bf16[1120,512]{1,0:T(8,128)(2,1)}, bf16[1120,512]{1,0:T(8,128)(2,1)}, bf16[128,1536]{1,0:T(8,128)(2,1)}, ...) custom-call(bf16[128,1536]{1,0:T(8,128)(2,1)} %get-tuple-element.93.refs_0_.refs_6_, ...), custom_call_target="tpu_custom_call" | custom-call | flops 11000000512 | tf_op jit(solution)/shard_map/units_forward/pallas_call | solution.py:480
  234.1 18.2 %units_gradient.1 = bf16[3,1120,1536]{2,1,0:T(8,128)(2,1)} custom-call(bf16[1120,512]{1,0:T(8,128)(2,1)} %get-tuple-element.95.refs_0_, bf16[1120,512]{1,0:T(8,128)(2,1)} %get-tuple-element.97.refs_1_, bf16[1120,512]{1,0:T(8,128)(2,1)} %get-tuple-element.98.refs_2_, bf16[1120,512]{1,0:T(8,128)(2,1)} %get-tuple-element.96.refs_3_.refs_1_, ...), custom_call_target="tpu_custom_call" | custom-call | flops 12099999744 | tf_op jit(solution)/shard_map/units_gradient/pallas_call | solution.py:522
  252.3 8.5 %copy.112 = bf16[3,140,8,1536]{3,2,0,1:T(8,128)(2,1)} copy(bf16[3,140,8,1536]{3,2,1,0:T(8,128)(2,1)} %bitcast.89) | data formatting | bytes 20643840
  261.8 2.1 fusion.7
  264.6 2.1 fusion.6
  268.1 2.2 collective-permute-start.52
  270.2 4.2 collective-permute-done.50
  275.4 3.0 collective-permute-done.51
  282.5 4.4 collective-permute-done.37
  287.5 7.2 %collective-permute-done.36 = bf16[128,1536]{1,0:T(8,128)(2,1)S(1)} collective-permute-done((bf16[128,1536]{1,0:T(8,128)(2,1)S(1)}, bf16[128,1536]{1,0:T(8,128)(2,1)S(1)}, u32[]{:S(2)}, u32[]{:S(2)}) %collective-permute-start.36) | collective-permute-done | bytes 393248 | tf_op jit(solution)/shard_map/ppermute | solution.py:50
  294.7 5.6 %collective-permute-done.39 = bf16[128,1536]{1,0:T(8,128)(2,1)S(1)} collective-permute-done((bf16[128,1536]{1,0:T(8,128)(2,1)S(1)}, bf16[128,1536]{1,0:T(8,128)(2,1)S(1)}, u32[]{:S(2)}, u32[]{:S(2)}) %collective-permute-start.39) | collective-permute-done | bytes 393248 | tf_op jit(solution)/shard_map/ppermute | solution.py:50
  300.9 10.1 %units_branch.1 = (bf16[128,1536]{1,0:T(8,128)(2,1)}, bf16[128,1536]{1,0:T(8,128)(2,1)}, bf16[128,1536]{1,0:T(8,128)(2,1)}, bf16[128,1536]{1,0:T(8,128)(2,1)}, b...) custom-call(bf16[1120,512]{1,0:T(8,128)(2,1)} %get-tuple-element.95., ...), custom_call_target="tpu_custom_call" | custom-call | flops 5500000256 | tf_op jit(solution)/shard_map/units_branch/pallas_call | solution.py:561
  311.1 2.2 collective-permute-start.49
  314.4 15.9 %collective-permute-done.49.received_ref = bf16[128,1536]{1,0:T(8,128)(2,1)S(1)} collective-permute-done((bf16[128,1536]{1,0:T(8,128)(2,1)S(1)}, bf16[128,1536]{1,0:T(8,128)(2,1)S(1)}, u32[]{:S(2)}, u32[]{:S(2)}) %collective-permute-start.49) | collective-permute-done | bytes 393248 | tf_op jit(solution)/shard_map/ppermute | solution.py:50
  331.1 16.0 %attend_back.1 = (f32[128,1536]{1,0:T(8,128)}, bf16[128,1536]{1,0:T(8,128)(2,1)}, bf16[128,1536]{1,0:T(8,128)(2,1)}, f32[1024,512]{1,0:T(8,128)}, f32[1,1536]{1,0:T(1,128)}) custom-call(f32[128,1536]{1,0:T(8,128)} %convert_add_fusion.4.normed_grad_ref, bf16[128,1536]{1,0:T(8,128)(2,1)} %copy-done.59, f32[128,1536]{1,0:T(8,128)} %get-tuple-element.130.middle_ref, ...), custom_call_target="tpu_custom_call" | custom-call | flops 17600000000 | tf_op jit(solution)/shard_map/attend_back/pallas_call | solution.py:250
  348.4 1.7 collective-permute-start.53
  353.0 7.7 %collective-permute-done.42 = bf16[128,1536]{1,0:T(8,128)(2,1)S(1)} collective-permute-done((bf16[128,1536]{1,0:T(8,128)(2,1)S(1)}, bf16[128,1536]{1,0:T(8,128)(2,1)S(1)}, u32[]{:S(2)}, u32[]{:S(2)}) %collective-permute-start.42) | collective-permute-done | bytes 393248 | tf_op jit(solution)/shard_map/ppermute | solution.py:50
  362.2 1.4 fusion.61
  363.6 5.6 %collective-permute-done.43 = bf16[128,1536]{1,0:T(8,128)(2,1)S(1)} collective-permute-done((bf16[128,1536]{1,0:T(8,128)(2,1)S(1)}, bf16[128,1536]{1,0:T(8,128)(2,1)S(1)}, u32[]{:S(2)}, u32[]{:S(2)}) %collective-permute-start.43) | collective-permute-done | bytes 393248 | tf_op jit(solution)/shard_map/ppermute | solution.py:50
  371.9 5.8 %collective-permute-done.57.refs_6_ = bf16[128,1536]{1,0:T(8,128)(2,1)S(1)} collective-permute-done((bf16[128,1536]{1,0:T(8,128)(2,1)}, bf16[128,1536]{1,0:T(8,128)(2,1)S(1)}, u32[]{:S(2)}, u32[]{:S(2)}) %collective-permute-start.57) | collective-permute-done | bytes 393248 | tf_op jit(solution)/shard_map/ppermute | solution.py:50
  379.8 7.2 %query_back.1 = (f32[128,1536]{1,0:T(8,128)}, f32[1,1536]{1,0:T(1,128)}, bf16[1536,512]{1,0:T(8,128)(2,1)}) custom-call(s32[40]{0:T(128)} %stack.164.refs_0_, bf16[128,1536]{1,0:T(8,128)(2,1)} %get-tuple-element.132.refs_1_.refs_4_, bf16[4,48,2048]{2,1,0:T(8,128)(2,1)} %copy-done.3, bf16[4,48,2048]{2,1,0:T(8,128)(2,1)} %copy-done.18, ...), custom_call_target="tpu_custom_call" | custom-call | flops 7699999744 | tf_op jit(solution)/shard_map/query_back/pallas_call | solution.py:233
  387.8 1.7 collective-permute-done.60.refs_3_
  389.5 2.2 collective-permute-done.59.refs_2_
  393.2 4.1 finish.1
  398.7 1.5 collective-permute-start.61
  401.1 1.4 collective-permute-start.65
  402.8 1.4 collective-permute-start.63
  405.4 5.6 %collective-permute-done.47 = bf16[128,1536]{1,0:T(8,128)(2,1)S(1)} collective-permute-done((bf16[128,1536]{1,0:T(8,128)(2,1)S(1)}, bf16[128,1536]{1,0:T(8,128)(2,1)S(1)}, u32[]{:S(2)}, u32[]{:S(2)}) %collective-permute-start.47) | collective-permute-done | bytes 393248 | tf_op jit(solution)/shard_map/ppermute | solution.py:50
  412.0 3.7 collective-permute-done.69
  416.9 3.1 collective-permute-start.81
  420.7 3.5 out_weights.1
  425.6 3.6 collective-permute-start.64
  432.9 1.4 fusion.55
  434.4 1.7 collective-permute-start.77
  438.1 3.5 query_weights.1
  441.6 10.1 %collective-permute-done.48 = bf16[128,1536]{1,0:T(8,128)(2,1)} collective-permute-done((bf16[128,1536]{1,0:T(8,128)(2,1)S(1)}, bf16[128,1536]{1,0:T(8,128)(2,1)}, u32[]{:S(2)}, u32[]{:S(2)}) %collective-permute-start.48) | collective-permute-done | bytes 393248 | tf_op jit(solution)/shard_map/ppermute | solution.py:50
  452.7 2.0 add_convert_fusion
  461.1 2.4 pair_weights.1
  468.7 13.0 %fusion.58 = (bf16[280,3,1536]{2,0,1:T(8,128)(2,1)}, f32[280,3,1536]{2,0,1:T(8,128)}, f32[280,3,1536]{2,0,1:T(8,128)}, f32[280,3,1536]{2,0,1:T(8,128)}) fusion(f32[280,3,1536]{2,0,1:T(8,128)} %param.20, bf16[35,3,8,1536]{3,2,1,0:T(8,128)(2,1)} %bitcast.90, f32[280,3,1536]{2,0,1:T(8,128)} %param.26, f32[280,3,1536]{2,0,1:T(8,128)} %param.27), kind=kLoop, calls=%fused_computation.195 | loop fusion | flops 21934080 | bytes 36126720 | tf_op jit(solution)/shard_map/convert_element_type | solution.py:670
  481.7 4.3 collective-permute-done.75
  (390 shorter events, 87.2 us)
Async XLA Ops:
  7.2 120.5 %all-gather.3.cloned.1.call-start = ((), (), s32[]{:S(2)}) async-start(), calls=%async_computation.1 | async-start | bytes 4866048 | tf_op jit(solution)/shard_map/all_gather | solution.py:714
  8.9 189.4 %all-gather.5.cloned.1.call-start = ((), (), s32[]{:S(2)}) async-start(), calls=%async_computation.2 | async-start | bytes 12902400 | tf_op jit(solution)/shard_map/all_gather | solution.py:728
  17.7 451.0 %reduce-scatter.4.cloned.1.call-start = ((), (), s32[]{:S(2)}) async-start(), calls=%async_computation.3 | async-start | bytes 12902400
  17.7 18.1 %collective-permute-start.7 = (bf16[48,2048]{1,0:T(8,128)(2,1)S(1)}, bf16[48,2048]{1,0:T(8,128)(2,1)S(1)}, u32[]{:S(2)}, u32[]{:S(2)}) collective-permute-start(bf16[48,2048]{1,0:T(8,128)(2,1)S(1)} %convert_element_type.177), channel_id=1, source_target_pairs={{0,16},{8,24},{16,0},{24,8},{1,17},{9,25},{17,1},{25,9},{2,18},{10... | collective-permute-start | bytes 589832 | tf_op jit(solution)/shard_map/ppermute | solution.py:50
  18.3 17.5 %collective-permute-start.6 = (bf16[48,2048]{1,0:T(8,128)(2,1)S(1)}, bf16[48,2048]{1,0:T(8,128)(2,1)S(1)}, u32[]{:S(2)}, u32[]{:S(2)}) collective-permute-start(bf16[48,2048]{1,0:T(8,128)(2,1)S(1)} %convert_element_type.177), channel_id=1, source_target_pairs={{0,8},{8,16},{16,24},{24,0},{1,9},{9,17},{17,25},{25,1},{2,10},{10... | collective-permute-start | bytes 589832 | tf_op jit(solution)/shard_map/ppermute | solution.py:50
  22.5 13.9 %collective-permute-start = (f32[1,5120]{1,0:T(1,128)S(1)}, f32[1,5120]{1,0:T(1,128)S(1)}, u32[]{:S(2)}, u32[]{:S(2)}) collective-permute-start(f32[1,5120]{1,0:T(1,128)S(1)} %bitcast.96), channel_id=1, source_target_pairs={{0,1},{1,0},{2,3},{3,2},{4,5},{5,4},{6,7},{7,6},{8,9},{9,8},{10,11... | collective-permute-start | bytes 61448 | tf_op jit(solution)/shard_map/ppermute | solution.py:50
  35.9 26.7 %collective-permute-start.10 = (bf16[4,48,2048]{2,1,0:T(8,128)(2,1)S(1)}, bf16[4,48,2048]{2,1,0:T(8,128)(2,1)S(1)}, u32[]{:S(2)}, u32[]{:S(2)}) collective-permute-start(bf16[4,48,2048]{2,1,0:T(8,128)(2,1)S(1)} %pad_maximum_fusion.1.refs_6_.refs_2_), channel_id=1, source_target_pairs={{0,4},{4,0},{1,5},{5,1},{2,6},{6,2},{3,7},{7,3},{8,12},{12,8},{9,1... | collective-permute-start | bytes 2359304 | tf_op jit(solution)/shard_map/ppermute | solution.py:50
  36.2 29.8 %collective-permute-start.9 = (bf16[4,48,2048]{2,1,0:T(8,128)(2,1)S(1)}, bf16[4,48,2048]{2,1,0:T(8,128)(2,1)S(1)}, u32[]{:S(2)}, u32[]{:S(2)}) collective-permute-start(bf16[4,48,2048]{2,1,0:T(8,128)(2,1)S(1)} %pad_maximum_fusion.1.refs_6_.refs_2_), channel_id=1, source_target_pairs={{0,2},{2,0},{1,3},{3,1},{4,6},{6,4},{5,7},{7,5},{8,10},{10,8},{9,1... | collective-permute-start | bytes 2359304 | tf_op jit(solution)/shard_map/ppermute | solution.py:50
  36.5 21.4 %collective-permute-start.1 = (f32[1,5120]{1,0:T(1,128)S(1)}, f32[1,5120]{1,0:T(1,128)S(1)}, u32[]{:S(2)}, u32[]{:S(2)}) collective-permute-start(f32[1,5120]{1,0:T(1,128)S(1)} %add.759), channel_id=1, source_target_pairs={{0,2},{2,0},{1,3},{3,1},{4,6},{6,4},{5,7},{7,5},{8,10},{10,8},{9,1... | collective-permute-start | bytes 61448 | tf_op jit(solution)/shard_map/ppermute | solution.py:50
  37.8 34.2 %collective-permute-start.21 = (bf16[128,1536]{1,0:T(8,128)(2,1)}, bf16[128,1536]{1,0:T(8,128)(2,1)}, u32[]{:S(2)}, u32[]{:S(2)}) collective-permute-start(bf16[128,1536]{1,0:T(8,128)(2,1)} %back_ref.1), channel_id=1, source_target_pairs={{0,16},{16,0},{1,17},{17,1},{2,18},{18,2},{3,19},{19,3},{4,20},{20... | collective-permute-start | bytes 1179656 | tf_op jit(solution)/shard_map/ppermute | solution.py:50
  61.2 9.1 %collective-permute-start.4 = (f32[1,5120]{1,0:T(1,128)S(1)}, f32[1,5120]{1,0:T(1,128)S(1)}, u32[]{:S(2)}, u32[]{:S(2)}) collective-permute-start(f32[1,5120]{1,0:T(1,128)S(1)} %add.761), channel_id=1, source_target_pairs={{0,16},{8,24},{16,0},{24,8},{1,17},{9,25},{17,1},{25,9},{2,18},{10... | collective-permute-start | bytes 61448 | tf_op jit(solution)/shard_map/ppermute | solution.py:50
  66.0 20.8 %collective-permute-start.13 = (bf16[4,48,2048]{2,1,0:T(8,128)(2,1)S(1)}, bf16[4,48,2048]{2,1,0:T(8,128)(2,1)S(1)}, u32[]{:S(2)}, u32[]{:S(2)}) collective-permute-start(bf16[4,48,2048]{2,1,0:T(8,128)(2,1)S(1)} %pad_maximum_fusion.1.refs_6_.refs_2_), channel_id=1, source_target_pairs={{0,1},{1,0},{2,3},{3,2},{4,5},{5,4},{6,7},{7,6},{8,9},{9,8},{10,11... | collective-permute-start | bytes 2359304 | tf_op jit(solution)/shard_map/ppermute | solution.py:50
  69.9 15.6 %collective-permute-start.12 = (bf16[4,48,1024]{2,1,0:T(8,128)(2,1)S(1)}, bf16[4,48,1024]{2,1,0:T(8,128)(2,1)S(1)}, u32[]{:S(2)}, u32[]{:S(2)}) collective-permute-start(bf16[4,48,1024]{2,1,0:T(8,128)(2,1)S(1)} %slice.226), channel_id=1, source_target_pairs={{0,2},{2,0},{1,3},{3,1},{4,6},{6,4},{5,7},{7,5},{8,10},{10,8},{9,1... | collective-permute-start | bytes 1179656 | tf_op jit(solution)/shard_map/ppermute | solution.py:50
  70.2 15.8 %collective-permute-start.11 = (bf16[4,48,1024]{2,1,0:T(8,128)(2,1)S(1)}, bf16[4,48,1024]{2,1,0:T(8,128)(2,1)S(1)}, u32[]{:S(2)}, u32[]{:S(2)}) collective-permute-start(bf16[4,48,1024]{2,1,0:T(8,128)(2,1)S(1)} %slice.225), channel_id=1, source_target_pairs={{0,4},{4,0},{1,5},{5,1},{2,6},{6,2},{3,7},{7,3},{8,12},{12,8},{9,1... | collective-permute-start | bytes 1179656 | tf_op jit(solution)/shard_map/ppermute | solution.py:50
  71.5 16.7 %collective-permute-start.15 = (bf16[4,48,2048]{2,1,0:T(8,128)(2,1)S(1)}, bf16[4,48,2048]{2,1,0:T(8,128)(2,1)S(1)}, u32[]{:S(2)}, u32[]{:S(2)}) collective-permute-start(bf16[4,48,2048]{2,1,0:T(8,128)(2,1)S(1)} %collective-permute-done.10.refs_8_.refs_4_), channel_id=1, source_target_pairs={{0,1},{1,0},{2,3},{3,2},{4,5},{5,4},{6,7},{7,6},{8,9},{9,8},{10,11... | collective-permute-start | bytes 2359304 | tf_op jit(solution)/shard_map/ppermute | solution.py:50
  72.0 16.5 %collective-permute-start.14 = (bf16[4,48,2048]{2,1,0:T(8,128)(2,1)S(1)}, bf16[4,48,2048]{2,1,0:T(8,128)(2,1)S(1)}, u32[]{:S(2)}, u32[]{:S(2)}) collective-permute-start(bf16[4,48,2048]{2,1,0:T(8,128)(2,1)S(1)} %collective-permute-done.9.refs_7_.refs_3_), channel_id=1, source_target_pairs={{0,1},{1,0},{2,3},{3,2},{4,5},{5,4},{6,7},{7,6},{8,9},{9,8},{10,11... | collective-permute-start | bytes 2359304 | tf_op jit(solution)/shard_map/ppermute | solution.py:50
  86.7 20.5 %collective-permute-start.18 = (bf16[128,1536]{1,0:T(8,128)(2,1)}, bf16[128,1536]{1,0:T(8,128)(2,1)S(1)}, u32[]{:S(2)}, u32[]{:S(2)}) collective-permute-start(bf16[128,1536]{1,0:T(8,128)(2,1)} %back_ref.1), channel_id=1, source_target_pairs={{0,2},{2,0},{1,3},{3,1},{4,6},{6,4},{5,7},{7,5},{8,10},{10,8},{9,1... | collective-permute-start | bytes 1179656 | tf_op jit(solution)/shard_map/ppermute | solution.py:50
  87.9 21.0 %collective-permute-start.23 = (bf16[128,1536]{1,0:T(8,128)(2,1)}, bf16[128,1536]{1,0:T(8,128)(2,1)S(1)}, u32[]{:S(2)}, u32[]{:S(2)}) collective-permute-start(bf16[128,1536]{1,0:T(8,128)(2,1)} %collective-permute-done.21.refs_4_.refs_18_), channel_id=1, source_target_pairs={{0,4},{4,0},{1,5},{5,1},{2,6},{6,2},{3,7},{7,3},{8,12},{12,8},{9,1... | collective-permute-start | bytes 1179656 | tf_op jit(solution)/shard_map/ppermute | solution.py:50
  101.0 10.8 %collective-permute-start.19 = (bf16[128,1536]{1,0:T(8,128)(2,1)S(1)}, bf16[128,1536]{1,0:T(8,128)(2,1)S(1)}, u32[]{:S(2)}, u32[]{:S(2)}) collective-permute-start(bf16[128,1536]{1,0:T(8,128)(2,1)S(1)} %copy-done.33), channel_id=1, source_target_pairs={{0,4},{4,0},{1,5},{5,1},{2,6},{6,2},{3,7},{7,3},{8,12},{12,8},{9,1... | collective-permute-start | bytes 1179656 | tf_op jit(solution)/shard_map/ppermute | solution.py:50
  106.0 21.5 %collective-permute-start.28 = (bf16[512,512]{1,0:T(8,128)(2,1)S(1)}, bf16[512,512]{1,0:T(8,128)(2,1)S(1)}, u32[]{:S(2)}, u32[]{:S(2)}) collective-permute-start(bf16[512,512]{1,0:T(8,128)(2,1)S(1)} %pad_maximum_fusion.2), channel_id=1, source_target_pairs={{0,1},{1,0},{2,3},{3,2},{4,5},{5,4},{6,7},{7,6},{8,9},{9,8},{10,11... | collective-permute-start | bytes 1572872 | tf_op jit(solution)/shard_map/ppermute | solution.py:50
  107.3 12.9 %collective-permute-start.20 = (bf16[128,1536]{1,0:T(8,128)(2,1)S(1)}, bf16[128,1536]{1,0:T(8,128)(2,1)S(1)}, u32[]{:S(2)}, u32[]{:S(2)}) collective-permute-start(bf16[128,1536]{1,0:T(8,128)(2,1)S(1)} %collective-permute-done.18.refs_5_.refs_15_), channel_id=1, source_target_pairs={{0,4},{4,0},{1,5},{5,1},{2,6},{6,2},{3,7},{7,3},{8,12},{12,8},{9,1... | collective-permute-start | bytes 1179656 | tf_op jit(solution)/shard_map/ppermute | solution.py:50
  108.4 11.8 %collective-permute-start.22 = (bf16[128,1536]{1,0:T(8,128)(2,1)}, bf16[128,1536]{1,0:T(8,128)(2,1)S(1)}, u32[]{:S(2)}, u32[]{:S(2)}) collective-permute-start(bf16[128,1536]{1,0:T(8,128)(2,1)} %collective-permute-done.21.refs_4_.refs_18_), channel_id=1, source_target_pairs={{0,2},{2,0},{1,3},{3,1},{4,6},{6,4},{5,7},{7,5},{8,10},{10,8},{9,1... | collective-permute-start | bytes 1179656 | tf_op jit(solution)/shard_map/ppermute | solution.py:50
  109.0 18.6 %collective-permute-start.24 = (bf16[128,1536]{1,0:T(8,128)(2,1)S(1)}, bf16[128,1536]{1,0:T(8,128)(2,1)S(1)}, u32[]{:S(2)}, u32[]{:S(2)}) collective-permute-start(bf16[128,1536]{1,0:T(8,128)(2,1)S(1)} %collective-permute-done.23.refs_6_.refs_20_), channel_id=1, source_target_pairs={{0,2},{2,0},{1,3},{3,1},{4,6},{6,4},{5,7},{7,5},{8,10},{10,8},{9,1... | collective-permute-start | bytes 1179656 | tf_op jit(solution)/shard_map/ppermute | solution.py:50
  140.8 19.5 %collective-permute-start.32 = (bf16[128,1536]{1,0:T(8,128)(2,1)}, bf16[128,1536]{1,0:T(8,128)(2,1)S(1)}, u32[]{:S(2)}, u32[]{:S(2)}) collective-permute-start(bf16[128,1536]{1,0:T(8,128)(2,1)} %get-tuple-element.93.refs_0_.refs_6_), channel_id=1, source_target_pairs={{0,16},{16,0},{1,17},{17,1},{2,18},{18,2},{3,19},{19,3},{4,20},{20... | collective-permute-start | bytes 1179656 | tf_op jit(solution)/shard_map/ppermute | solution.py:50
  160.6 10.2 %collective-permute-start.29 = (bf16[128,1536]{1,0:T(8,128)(2,1)}, bf16[128,1536]{1,0:T(8,128)(2,1)S(1)}, u32[]{:S(2)}, u32[]{:S(2)}) collective-permute-start(bf16[128,1536]{1,0:T(8,128)(2,1)} %get-tuple-element.93.refs_0_.refs_6_), channel_id=1, source_target_pairs={{0,2},{2,0},{1,3},{3,1},{4,6},{6,4},{5,7},{7,5},{8,10},{10,8},{9,1... | collective-permute-start | bytes 1179656 | tf_op jit(solution)/shard_map/ppermute | solution.py:50
  161.8 16.1 %collective-permute-start.33 = (bf16[128,1536]{1,0:T(8,128)(2,1)S(1)}, bf16[128,1536]{1,0:T(8,128)(2,1)S(1)}, u32[]{:S(2)}, u32[]{:S(2)}) collective-permute-start(bf16[128,1536]{1,0:T(8,128)(2,1)S(1)} %collective-permute-done.32.refs_0_.refs_10_), channel_id=1, source_target_pairs={{0,2},{2,0},{1,3},{3,1},{4,6},{6,4},{5,7},{7,5},{8,10},{10,8},{9,1... | collective-permute-start | bytes 1179656 | tf_op jit(solution)/shard_map/ppermute | solution.py:50
  169.3 17.0 %collective-permute-start.35 = (bf16[128,1536]{1,0:T(8,128)(2,1)S(1)}, bf16[128,1536]{1,0:T(8,128)(2,1)S(1)}, u32[]{:S(2)}, u32[]{:S(2)}) collective-permute-start(bf16[128,1536]{1,0:T(8,128)(2,1)S(1)} %collective-permute-done.34.refs_2_.refs_12_), channel_id=1, source_target_pairs={{0,2},{2,0},{1,3},{3,1},{4,6},{6,4},{5,7},{7,5},{8,10},{10,8},{9,1... | collective-permute-start | bytes 1179656 | tf_op jit(solution)/shard_map/ppermute | solution.py:50
  169.8 45.7 %collective-permute-start.30 = (bf16[128,1536]{1,0:T(8,128)(2,1)}, bf16[128,1536]{1,0:T(8,128)(2,1)S(1)}, u32[]{:S(2)}, u32[]{:S(2)}) collective-permute-start(bf16[128,1536]{1,0:T(8,128)(2,1)} %get-tuple-element.93.refs_0_.refs_6_), channel_id=1, source_target_pairs={{0,4},{4,0},{1,5},{5,1},{2,6},{6,2},{3,7},{7,3},{8,12},{12,8},{9,1... | collective-permute-start | bytes 1179656 | tf_op jit(solution)/shard_map/ppermute | solution.py:50
  170.8 44.7 %collective-permute-start.31 = (bf16[128,1536]{1,0:T(8,128)(2,1)S(1)}, bf16[128,1536]{1,0:T(8,128)(2,1)S(1)}, u32[]{:S(2)}, u32[]{:S(2)}) collective-permute-start(bf16[128,1536]{1,0:T(8,128)(2,1)S(1)} %collective-permute-done.29.refs_1_.refs_7_), channel_id=1, source_target_pairs={{0,4},{4,0},{1,5},{5,1},{2,6},{6,2},{3,7},{7,3},{8,12},{12,8},{9,1... | collective-permute-start | bytes 1179656 | tf_op jit(solution)/shard_map/ppermute | solution.py:50
  267.7 10.7 %collective-permute-start.51 = (bf16[128,768]{1,0:T(8,128)(2,1)S(1)}, bf16[128,768]{1,0:T(8,128)(2,1)S(1)}, u32[]{:S(2)}, u32[]{:S(2)}) collective-permute-start(bf16[128,768]{1,0:T(8,128)(2,1)S(1)} %pad_maximum_fusion.4), channel_id=1, source_target_pairs={{0,4},{2,6},{4,0},{6,2},{1,5},{3,7},{5,1},{7,3},{8,12},{10,14},{12... | collective-permute-start | bytes 589832 | tf_op jit(solution)/shard_map/ppermute | solution.py:68
  268.1 11.0 %collective-permute-start.52 = (bf16[128,768]{1,0:T(8,128)(2,1)S(1)}, bf16[128,768]{1,0:T(8,128)(2,1)S(1)}, u32[]{:S(2)}, u32[]{:S(2)}) collective-permute-start(bf16[128,768]{1,0:T(8,128)(2,1)S(1)} %pad_maximum_fusion.5), channel_id=1, source_target_pairs={{0,6},{2,4},{4,2},{6,0},{1,7},{3,5},{5,3},{7,1},{8,14},{10,12},{12... | collective-permute-start | bytes 589832 | tf_op jit(solution)/shard_map/ppermute | solution.py:68
  275.1 11.8 %collective-permute-start.37 = (bf16[128,1536]{1,0:T(8,128)(2,1)S(1)}, bf16[128,1536]{1,0:T(8,128)(2,1)S(1)}, u32[]{:S(2)}, u32[]{:S(2)}) collective-permute-start(bf16[128,1536]{1,0:T(8,128)(2,1)S(1)} %copy-done.44), channel_id=1, source_target_pairs={{0,2},{2,0},{1,3},{3,1},{4,6},{6,4},{5,7},{7,5},{8,10},{10,8},{9,1... | collective-permute-start | bytes 1179656 | tf_op jit(solution)/shard_map/ppermute | solution.py:50
  279.7 14.9 %collective-permute-start.36 = (bf16[128,1536]{1,0:T(8,128)(2,1)S(1)}, bf16[128,1536]{1,0:T(8,128)(2,1)S(1)}, u32[]{:S(2)}, u32[]{:S(2)}) collective-permute-start(bf16[128,1536]{1,0:T(8,128)(2,1)S(1)} %copy-done.40), channel_id=1, source_target_pairs={{0,2},{2,0},{1,3},{3,1},{4,6},{6,4},{5,7},{7,5},{8,10},{10,8},{9,1... | collective-permute-start | bytes 1179656 | tf_op jit(solution)/shard_map/ppermute | solution.py:50
  281.1 13.6 %collective-permute-start.38 = (bf16[128,1536]{1,0:T(8,128)(2,1)S(1)}, bf16[128,1536]{1,0:T(8,128)(2,1)S(1)}, u32[]{:S(2)}, u32[]{:S(2)}) collective-permute-start(bf16[128,1536]{1,0:T(8,128)(2,1)S(1)} %copy-done.43), channel_id=1, source_target_pairs={{0,4},{4,0},{1,5},{5,1},{2,6},{6,2},{3,7},{7,3},{8,12},{12,8},{9,1... | collective-permute-start | bytes 1179656 | tf_op jit(solution)/shard_map/ppermute | solution.py:50
  281.2 19.1 %collective-permute-start.39 = (bf16[128,1536]{1,0:T(8,128)(2,1)S(1)}, bf16[128,1536]{1,0:T(8,128)(2,1)S(1)}, u32[]{:S(2)}, u32[]{:S(2)}) collective-permute-start(bf16[128,1536]{1,0:T(8,128)(2,1)S(1)} %copy-done.42), channel_id=1, source_target_pairs={{0,4},{4,0},{1,5},{5,1},{2,6},{6,2},{3,7},{7,3},{8,12},{12,8},{9,1... | collective-permute-start | bytes 1179656 | tf_op jit(solution)/shard_map/ppermute | solution.py:50
  287.0 23.9 %collective-permute-start.41 = (bf16[128,1536]{1,0:T(8,128)(2,1)S(1)}, bf16[128,1536]{1,0:T(8,128)(2,1)S(1)}, u32[]{:S(2)}, u32[]{:S(2)}) collective-permute-start(bf16[128,1536]{1,0:T(8,128)(2,1)S(1)} %add_convert_fusion.4), channel_id=1, source_target_pairs={{0,4},{4,0},{1,5},{5,1},{2,6},{6,2},{3,7},{7,3},{8,12},{12,8},{9,1... | collective-permute-start | bytes 1179656 | tf_op jit(solution)/shard_map/ppermute | solution.py:50
  300.4 13.0 %collective-permute-start.40 = (bf16[128,1536]{1,0:T(8,128)(2,1)S(1)}, bf16[128,1536]{1,0:T(8,128)(2,1)S(1)}, u32[]{:S(2)}, u32[]{:S(2)}) collective-permute-start(bf16[128,1536]{1,0:T(8,128)(2,1)S(1)} %add_convert_fusion.5), channel_id=1, source_target_pairs={{0,2},{2,0},{1,3},{3,1},{4,6},{6,4},{5,7},{7,5},{8,10},{10,8},{9,1... | collective-permute-start | bytes 1179656 | tf_op jit(solution)/shard_map/ppermute | solution.py:50
  311.1 19.2 %collective-permute-start.49 = (bf16[128,1536]{1,0:T(8,128)(2,1)S(1)}, bf16[128,1536]{1,0:T(8,128)(2,1)S(1)}, u32[]{:S(2)}, u32[]{:S(2)}) collective-permute-start(bf16[128,1536]{1,0:T(8,128)(2,1)S(1)} %convert_add_fusion.3), channel_id=1, source_target_pairs={{0,16},{16,0},{1,17},{17,1},{2,18},{18,2},{3,19},{19,3},{4,20},{20... | collective-permute-start | bytes 1179656 | tf_op jit(solution)/shard_map/ppermute | solution.py:50
  348.4 12.5 %collective-permute-start.53 = (bf16[512,512]{1,0:T(8,128)(2,1)S(1)}, bf16[512,512]{1,0:T(8,128)(2,1)S(1)}, u32[]{:S(2)}, u32[]{:S(2)}) collective-permute-start(bf16[512,512]{1,0:T(8,128)(2,1)S(1)} %slice.295), channel_id=1, source_target_pairs={{0,1},{1,0},{2,3},{3,2},{4,5},{5,4},{6,7},{7,6},{8,9},{9,8},{10,11... | collective-permute-start | bytes 1572872 | tf_op jit(solution)/shard_map/ppermute | solution.py:50
  350.1 10.7 %collective-permute-start.42 = (bf16[128,1536]{1,0:T(8,128)(2,1)S(1)}, bf16[128,1536]{1,0:T(8,128)(2,1)S(1)}, u32[]{:S(2)}, u32[]{:S(2)}) collective-permute-start(bf16[128,1536]{1,0:T(8,128)(2,1)S(1)} %copy-done.52), channel_id=1, source_target_pairs={{0,4},{4,0},{1,5},{5,1},{2,6},{6,2},{3,7},{7,3},{8,12},{12,8},{9,1... | collective-permute-start | bytes 1179656 | tf_op jit(solution)/shard_map/ppermute | solution.py:50
  350.2 19.0 %collective-permute-start.43 = (bf16[128,1536]{1,0:T(8,128)(2,1)S(1)}, bf16[128,1536]{1,0:T(8,128)(2,1)S(1)}, u32[]{:S(2)}, u32[]{:S(2)}) collective-permute-start(bf16[128,1536]{1,0:T(8,128)(2,1)S(1)} %copy-done.50), channel_id=1, source_target_pairs={{0,4},{4,0},{1,5},{5,1},{2,6},{6,2},{3,7},{7,3},{8,12},{12,8},{9,1... | collective-permute-start | bytes 1179656 | tf_op jit(solution)/shard_map/ppermute | solution.py:50
  351.6 17.7 %collective-permute-start.45 = (bf16[128,1536]{1,0:T(8,128)(2,1)S(1)}, bf16[128,1536]{1,0:T(8,128)(2,1)S(1)}, u32[]{:S(2)}, u32[]{:S(2)}) collective-permute-start(bf16[128,1536]{1,0:T(8,128)(2,1)S(1)} %copy-done.49), channel_id=1, source_target_pairs={{0,2},{2,0},{1,3},{3,1},{4,6},{6,4},{5,7},{7,5},{8,10},{10,8},{9,1... | collective-permute-start | bytes 1179656 | tf_op jit(solution)/shard_map/ppermute | solution.py:50
  352.9 17.6 %collective-permute-start.46 = (bf16[128,1536]{1,0:T(8,128)(2,1)S(1)}, bf16[128,1536]{1,0:T(8,128)(2,1)S(1)}, u32[]{:S(2)}, u32[]{:S(2)}) collective-permute-start(bf16[128,1536]{1,0:T(8,128)(2,1)S(1)} %copy-done.48), channel_id=1, source_target_pairs={{0,2},{2,0},{1,3},{3,1},{4,6},{6,4},{5,7},{7,5},{8,10},{10,8},{9,1... | collective-permute-start | bytes 1179656 | tf_op jit(solution)/shard_map/ppermute | solution.py:50
  360.8 16.9 %collective-permute-start.57 = (bf16[128,1536]{1,0:T(8,128)(2,1)}, bf16[128,1536]{1,0:T(8,128)(2,1)S(1)}, u32[]{:S(2)}, u32[]{:S(2)}) collective-permute-start(bf16[128,1536]{1,0:T(8,128)(2,1)} %get-tuple-element.133.refs_4_), channel_id=1, source_target_pairs={{0,4},{4,0},{1,5},{5,1},{2,6},{6,2},{3,7},{7,3},{8,12},{12,8},{9,1... | collective-permute-start | bytes 1179656 | tf_op jit(solution)/shard_map/ppermute | solution.py:50
  360.8 17.6 %collective-permute-start.56 = (bf16[128,1536]{1,0:T(8,128)(2,1)}, bf16[128,1536]{1,0:T(8,128)(2,1)S(1)}, u32[]{:S(2)}, u32[]{:S(2)}) collective-permute-start(bf16[128,1536]{1,0:T(8,128)(2,1)} %get-tuple-element.133.refs_4_), channel_id=1, source_target_pairs={{0,2},{2,0},{1,3},{3,1},{4,6},{6,4},{5,7},{7,5},{8,10},{10,8},{9,1... | collective-permute-start | bytes 1179656 | tf_op jit(solution)/shard_map/ppermute | solution.py:50
  369.2 18.6 %collective-permute-start.55 = (bf16[128,1536]{1,0:T(8,128)(2,1)}, bf16[128,1536]{1,0:T(8,128)(2,1)S(1)}, u32[]{:S(2)}, u32[]{:S(2)}) collective-permute-start(bf16[128,1536]{1,0:T(8,128)(2,1)} %get-tuple-element.132.refs_1_.refs_4_), channel_id=1, source_target_pairs={{0,4},{4,0},{1,5},{5,1},{2,6},{6,2},{3,7},{7,3},{8,12},{12,8},{9,1... | collective-permute-start | bytes 1179656 | tf_op jit(solution)/shard_map/ppermute | solution.py:50
  369.3 18.5 %collective-permute-start.54 = (bf16[128,1536]{1,0:T(8,128)(2,1)}, bf16[128,1536]{1,0:T(8,128)(2,1)S(1)}, u32[]{:S(2)}, u32[]{:S(2)}) collective-permute-start(bf16[128,1536]{1,0:T(8,128)(2,1)} %get-tuple-element.132.refs_1_.refs_4_), channel_id=1, source_target_pairs={{0,2},{2,0},{1,3},{3,1},{4,6},{6,4},{5,7},{7,5},{8,10},{10,8},{9,1... | collective-permute-start | bytes 1179656 | tf_op jit(solution)/shard_map/ppermute | solution.py:50
  370.6 18.9 %collective-permute-start.60 = (bf16[128,512]{1,0:T(8,128)(2,1)S(1)}, bf16[128,512]{1,0:T(8,128)(2,1)S(1)}, u32[]{:S(2)}, u32[]{:S(2)}) collective-permute-start(bf16[128,512]{1,0:T(8,128)(2,1)S(1)} %get-tuple-element.225), channel_id=1, source_target_pairs={{0,6},{2,4},{4,2},{6,0},{1,7},{3,5},{5,3},{7,1},{8,14},{10,12},{12... | collective-permute-start | bytes 393224 | tf_op jit(solution)/shard_map/ppermute | solution.py:68
  377.6 14.0 %collective-permute-start.59 = (bf16[128,512]{1,0:T(8,128)(2,1)S(1)}, bf16[128,512]{1,0:T(8,128)(2,1)S(1)}, u32[]{:S(2)}, u32[]{:S(2)}) collective-permute-start(bf16[128,512]{1,0:T(8,128)(2,1)S(1)} %get-tuple-element.226), channel_id=1, source_target_pairs={{0,4},{2,6},{4,0},{6,2},{1,5},{3,7},{5,1},{7,3},{8,12},{10,14},{12... | collective-permute-start | bytes 393224 | tf_op jit(solution)/shard_map/ppermute | solution.py:68
  378.5 14.0 %collective-permute-start.58 = (bf16[128,512]{1,0:T(8,128)(2,1)S(1)}, bf16[128,512]{1,0:T(8,128)(2,1)S(1)}, u32[]{:S(2)}, u32[]{:S(2)}) collective-permute-start(bf16[128,512]{1,0:T(8,128)(2,1)S(1)} %get-tuple-element.227), channel_id=1, source_target_pairs={{0,2},{2,0},{4,6},{6,4},{1,3},{3,1},{5,7},{7,5},{8,10},{10,8},{12,... | collective-permute-start | bytes 393224 | tf_op jit(solution)/shard_map/ppermute | solution.py:68
  400.3 10.8 %collective-permute-start.47 = (bf16[128,1536]{1,0:T(8,128)(2,1)S(1)}, bf16[128,1536]{1,0:T(8,128)(2,1)S(1)}, u32[]{:S(2)}, u32[]{:S(2)}) collective-permute-start(bf16[128,1536]{1,0:T(8,128)(2,1)S(1)} %add_convert_fusion.2), channel_id=1, source_target_pairs={{0,4},{4,0},{1,5},{5,1},{2,6},{6,2},{3,7},{7,3},{8,12},{12,8},{9,1... | collective-permute-start | bytes 1179656 | tf_op jit(solution)/shard_map/ppermute | solution.py:50
  402.6 31.8 %collective-permute-start.44 = (bf16[128,1536]{1,0:T(8,128)(2,1)S(1)}, bf16[128,1536]{1,0:T(8,128)(2,1)S(1)}, u32[]{:S(2)}, u32[]{:S(2)}) collective-permute-start(bf16[128,1536]{1,0:T(8,128)(2,1)S(1)} %add_convert_fusion.3), channel_id=1, source_target_pairs={{0,2},{2,0},{1,3},{3,1},{4,6},{6,4},{5,7},{7,5},{8,10},{10,8},{9,1... | collective-permute-start | bytes 1179656 | tf_op jit(solution)/shard_map/ppermute | solution.py:50
  402.8 14.1 %collective-permute-start.63 = (bf16[64,1536]{1,0:T(8,128)(2,1)S(1)}, bf16[64,1536]{1,0:T(8,128)(2,1)S(1)}, u32[]{:S(2)}, u32[]{:S(2)}) collective-permute-start(bf16[64,1536]{1,0:T(8,128)(2,1)S(1)} %slice.248), channel_id=1, source_target_pairs={{0,2},{2,0},{1,3},{3,1},{4,6},{6,4},{5,7},{7,5},{8,10},{10,8},{9,1... | collective-permute-start | bytes 589832 | tf_op jit(solution)/shard_map/ppermute | solution.py:50
  404.2 15.8 %collective-permute-start.62 = (bf16[64,1536]{1,0:T(8,128)(2,1)S(1)}, bf16[64,1536]{1,0:T(8,128)(2,1)S(1)}, u32[]{:S(2)}, u32[]{:S(2)}) collective-permute-start(bf16[64,1536]{1,0:T(8,128)(2,1)S(1)} %slice.247), channel_id=1, source_target_pairs={{0,4},{4,0},{1,5},{5,1},{2,6},{6,2},{3,7},{7,3},{8,12},{12,8},{9,1... | collective-permute-start | bytes 589832 | tf_op jit(solution)/shard_map/ppermute | solution.py:50
  405.1 31.0 %collective-permute-start.67 = (bf16[64,1536]{1,0:T(8,128)(2,1)S(1)}, bf16[64,1536]{1,0:T(8,128)(2,1)}, u32[]{:S(2)}, u32[]{:S(2)}) collective-permute-start(bf16[64,1536]{1,0:T(8,128)(2,1)S(1)} %slice.250), channel_id=1, source_target_pairs={{0,2},{2,0},{1,3},{3,1},{4,6},{6,4},{5,7},{7,5},{8,10},{10,8},{9,1... | collective-permute-start | bytes 589832 | tf_op jit(solution)/shard_map/ppermute | solution.py:50
  424.2 12.7 %collective-permute-start.66 = (bf16[64,1536]{1,0:T(8,128)(2,1)}, bf16[64,1536]{1,0:T(8,128)(2,1)}, u32[]{:S(2)}, u32[]{:S(2)}) collective-permute-start(bf16[64,1536]{1,0:T(8,128)(2,1)} %slice.249), channel_id=1, source_target_pairs={{0,4},{4,0},{1,5},{5,1},{2,6},{6,2},{3,7},{7,3},{8,12},{12,8},{9,1... | collective-permute-start | bytes 589832 | tf_op jit(solution)/shard_map/ppermute | solution.py:50
  425.0 26.6 %collective-permute-start.48 = (bf16[128,1536]{1,0:T(8,128)(2,1)S(1)}, bf16[128,1536]{1,0:T(8,128)(2,1)}, u32[]{:S(2)}, u32[]{:S(2)}) collective-permute-start(bf16[128,1536]{1,0:T(8,128)(2,1)S(1)} %add_convert_fusion.1), channel_id=1, source_target_pairs={{0,16},{16,0},{1,17},{17,1},{2,18},{18,2},{3,19},{19,3},{4,20},{20... | collective-permute-start | bytes 1179656 | tf_op jit(solution)/shard_map/ppermute | solution.py:50
  432.2 26.8 %collective-permute-start.72 = (bf16[128,512]{1,0:T(8,128)(2,1)}, bf16[128,512]{1,0:T(8,128)(2,1)S(1)}, u32[]{:S(2)}, u32[]{:S(2)}) collective-permute-start(bf16[128,512]{1,0:T(8,128)(2,1)} %get-tuple-element.149.refs_4_), channel_id=1, source_target_pairs={{0,6},{2,4},{4,2},{6,0},{1,7},{3,5},{5,3},{7,1},{8,14},{10,12},{12... | collective-permute-start | bytes 393224 | tf_op jit(solution)/shard_map/ppermute | solution.py:68
  434.4 20.2 %collective-permute-start.77 = (bf16[48,1536]{1,0:T(8,128)(2,1)S(1)}, bf16[48,1536]{1,0:T(8,128)(2,1)S(1)}, u32[]{:S(2)}, u32[]{:S(2)}) collective-permute-start(bf16[48,1536]{1,0:T(8,128)(2,1)S(1)} %get-tuple-element.222), channel_id=1, source_target_pairs={{0,24},{8,0},{16,8},{24,16},{1,25},{9,1},{17,9},{25,17},{2,26},{10... | collective-permute-start | bytes 442376 | tf_op jit(solution)/shard_map/ppermute | solution.py:50
  436.1 19.2 %collective-permute-start.79 = (bf16[48,1536]{1,0:T(8,128)(2,1)S(1)}, bf16[48,1536]{1,0:T(8,128)(2,1)S(1)}, u32[]{:S(2)}, u32[]{:S(2)}) collective-permute-start(bf16[48,1536]{1,0:T(8,128)(2,1)S(1)} %get-tuple-element.223), channel_id=1, source_target_pairs={{0,8},{8,16},{16,24},{24,0},{1,9},{9,17},{17,25},{25,1},{2,10},{10... | collective-permute-start | bytes 442376 | tf_op jit(solution)/shard_map/ppermute | solution.py:50
  436.9 20.9 %collective-permute-start.78 = (bf16[48,1536]{1,0:T(8,128)(2,1)S(1)}, bf16[48,1536]{1,0:T(8,128)(2,1)S(1)}, u32[]{:S(2)}, u32[]{:S(2)}) collective-permute-start(bf16[48,1536]{1,0:T(8,128)(2,1)S(1)} %get-tuple-element.224), channel_id=1, source_target_pairs={{0,16},{8,24},{16,0},{24,8},{1,17},{9,25},{17,1},{25,9},{2,18},{10... | collective-permute-start | bytes 442376 | tf_op jit(solution)/shard_map/ppermute | solution.py:50
  466.8 19.2 %collective-permute-start.74 = (bf16[48,2048]{1,0:T(8,128)(2,1)S(1)}, bf16[48,2048]{1,0:T(8,128)(2,1)S(1)}, u32[]{:S(2)}, u32[]{:S(2)}) collective-permute-start(bf16[48,2048]{1,0:T(8,128)(2,1)S(1)} %get-tuple-element.219), channel_id=1, source_target_pairs={{0,24},{8,0},{16,8},{24,16},{1,25},{9,1},{17,9},{25,17},{2,26},{10... | collective-permute-start | bytes 589832 | tf_op jit(solution)/shard_map/ppermute | solution.py:50
  468.0 13.7 %collective-permute-start.76 = (bf16[48,2048]{1,0:T(8,128)(2,1)S(1)}, bf16[48,2048]{1,0:T(8,128)(2,1)S(1)}, u32[]{:S(2)}, u32[]{:S(2)}) collective-permute-start(bf16[48,2048]{1,0:T(8,128)(2,1)S(1)} %get-tuple-element.220), channel_id=1, source_target_pairs={{0,8},{8,16},{16,24},{24,0},{1,9},{9,17},{17,25},{25,1},{2,10},{10... | collective-permute-start | bytes 589832 | tf_op jit(solution)/shard_map/ppermute | solution.py:50
  468.3 17.7 %collective-permute-start.75 = (bf16[48,2048]{1,0:T(8,128)(2,1)S(1)}, bf16[48,2048]{1,0:T(8,128)(2,1)S(1)}, u32[]{:S(2)}, u32[]{:S(2)}) collective-permute-start(bf16[48,2048]{1,0:T(8,128)(2,1)S(1)} %get-tuple-element.221), channel_id=1, source_target_pairs={{0,16},{8,24},{16,0},{24,8},{1,17},{9,25},{17,1},{25,9},{2,18},{10... | collective-permute-start | bytes 589832 | tf_op jit(solution)/shard_map/ppermute | solution.py:50
  (93 other events, 1193.0 us)
Sparse Core Ops, SparseCore 0:
  11.5 79.9 all-gather.2
  93.6 104.6 all-gather.4
  260.9 100.6 reduce-scatter.3

commit v3 on v2

v3 whole, which is shorter than its diff:
```python
import math

import jax
import jax.numpy as jnp
from jax import lax
from jax.experimental import pallas as pl
from jax.experimental.pallas import tpu as pltpu
from jax.sharding import Mesh
from jax.sharding import PartitionSpec as P

D = 1536
HEADS = 12
KV_HEADS = 2
HEAD_DIM = 128
FF = 8960
BLOCK = 256
STEP = 5
QW = 1536
KW = 256
QKV = 2048


NORM_EPS = 1e-06
ROPE_BASE = 1000000.0
BETA_ONE = 0.9
BETA_TWO = 0.95
ADAM_EPS = 1e-08
DECAY = 0.1


DP = ("zh", "zl")
SEQ = ("y", "x", "c")
ALL = DP + SEQ


def low(value):
    return value.astype(jnp.bfloat16)


def wide(value):
    return value.astype(jnp.float32)


def after(value, *others):
    return lax.optimization_barrier((value,) + others)[0]


def shift(value, axis, step):
    count = lax.axis_size(axis)
    return lax.ppermute(value, axis, [(i, (i + step) % count) for i in range(count)])


def rotations(value, axis):
    return [value] + [shift(value, axis, step) for step in range(1, lax.axis_size(axis))]


def plane_steps():
    return [(j, i) for j in range(lax.axis_size("y")) for i in range(lax.axis_size("x"))]


def plane_shift(value, down, right):
    tall, broad = lax.axis_size("y"), lax.axis_size("x")
    pairs = [
        (j * broad + i, (j + down) % tall * broad + (i + right) % broad)
        for j in range(tall)
        for i in range(broad)
    ]
    return lax.ppermute(value, ("y", "x"), pairs)


def plane_pieces(value, dim, cut, second):
    across, along = rotations(value, "x"), rotations(value, "y")
    size = value.shape[dim]
    pieces = []
    for j, i in plane_steps():
        if j == 0 or i == 0:
            pieces.append((across[i] if j == 0 else along[j],))
        else:
            head = after(lax.slice_in_dim(across[i], 0, cut, axis=dim), *second)
            tail = after(lax.slice_in_dim(along[j], cut, size, axis=dim), *second)
            pieces.append((shift(head, "y", j), shift(tail, "x", i)))
    return pieces


def plane_blocks(value):
    return [value] + [plane_shift(value, j, i) for j, i in plane_steps()[1:]]


def seq_gather_small(value):
    mine = jnp.concatenate(plane_blocks(value), axis=0)
    return jnp.concatenate(rotations(mine, "c"), axis=0)


def seq_scatter_small(value, rows):
    part = value.shape[0] // lax.axis_size("c")
    log = []
    total = add_back(
        [value[step * part : (step + 1) * part] for step in range(lax.axis_size("c"))], "c", log=log
    )
    result = [total[:rows]]
    for number, (j, i) in enumerate(plane_steps()[1:], 1):
        term = low(total[number * rows : (number + 1) * rows])
        result.append(plane_shift(term, -j, -i))
    return result, log


def seq_sources():
    tall, broad, cores = (lax.axis_size(name) for name in SEQ)
    row, col, core = (lax.axis_index(name) for name in SEQ)
    return [
        ((row - j) % tall * broad + (col - i) % broad) * cores + (core - k) % cores
        for k in range(cores)
        for j, i in plane_steps()
    ]


def wanted_columns(columns, width):
    tall, broad, cores = (lax.axis_size(name) for name in SEQ)
    row, col, core = (lax.axis_index(name) for name in SEQ)
    depth, z = lax.axis_size(DP), lax.axis_index(DP)
    place = jnp.arange(columns, dtype=jnp.int32)
    inner, rest = place % width, place // width
    dp_step, rest = rest % depth, rest // depth
    c_step, rest = rest % cores, rest // cores
    x_step, y_step = rest % broad, rest // broad
    seq = ((row - y_step) % tall * broad + (col - x_step) % broad) * cores + (core - c_step) % cores
    source = ((z - dp_step) % depth * (tall * broad * cores) + seq) * width + inner
    return low(jnp.arange(columns, dtype=jnp.int32)[:, None] == source[None, :])


def token_gather(value, order):
    result = []
    for number, block in enumerate(rotations(order(value), "zh")):
        block = value if number == 0 else block
        if number % 2 == 0:
            grid = [rotations(item, "y") for item in rotations(block, "x")]
            grid = [[grid[i][j] for i in range(len(grid))] for j in range(len(grid[0]))]
        else:
            grid = [rotations(item, "x") for item in rotations(block, "y")]
        result.append([item for line in grid for item in line])
    return result


def add_back(blocks, axis, early=(), log=None):
    total = wide(blocks[0])
    for step in range(1, len(blocks)):
        got = shift(low(blocks[step]), axis, -step)
        if log is not None:
            log.append(got)
        total = total + wide(after(got, *early) if early else got)
    return total


def token_scatter(parts, between=None):
    across, along = lax.axis_size("x"), lax.axis_size("y")
    lines, first, second = [], [], []
    for number, blocks in reversed(list(enumerate(parts))):
        grid = [blocks[j * across : (j + 1) * across] for j in range(along)]
        axis = "y" if number % 2 == 0 else "x"
        if number % 2 == 0:
            grid = [list(column) for column in zip(*grid)]
        lines.append([add_back(line, axis, log=first) for line in grid])
    early = between(first) if between else ()
    for number, sums in enumerate(lines):
        axis = "x" if (len(parts) - 1 - number) % 2 == 0 else "y"
        lines[number] = add_back(sums, axis, early, log=second)
    lines = lines[::-1]
    last = lines.pop()
    sent = low(last)
    sent = shift(sent, "zh", -len(lines))
    return lines + [last], add_back(lines, "zh"), sent, first, second


VMEM_BYTES = 56 * 2**20
COST_SHARE = 4
ANYWHERE = pl.BlockSpec(memory_space=pl.ANY)
SCALARS = pl.BlockSpec(memory_space=pltpu.SMEM)


def projection_pieces(block, line, first, second):
    rows, columns = block.shape
    depth = lax.axis_size(DP)
    tall, broad, cores = (lax.axis_size(name) for name in SEQ)
    if rows % 16:
        return [lax.all_gather(block, ALL, axis=0, tiled=True)], None, None
    cut = columns // 2
    z = lax.axis_index(DP)
    z_sources = [(z - k) % depth for k in range(depth)]
    sources = seq_sources()
    own = plane_pieces(after(jnp.stack(line), *first), 2, cut, second)
    pieces, plan, targets = [], [], []
    for k in range(cores):
        for number, piece in enumerate(own):
            for part, value in enumerate(piece):
                pieces.append(value if k == 0 else shift(value, "c", k))
                place = (part * cut, cut) if len(piece) == 2 else (0, columns)
                plan.append([(slot, len(targets) + slot, place) for slot in range(depth)])
                seq = sources[k * len(own) + number]
                targets += [(z_sources[slot] * tall * broad * cores + seq) * rows for slot in range(depth)]
    return pieces, plan, jnp.stack(targets).astype(jnp.int32)


def start_pieces(plan, where_ref, pieces, whole, sems):
    if plan is None:
        copies = [pltpu.make_async_copy(pieces[0], whole, sems.at[0])]
    else:
        copies = []
        for piece, jobs in zip(pieces, plan):
            for slot, target, columns in jobs:
                first = pl.multiple_of(where_ref[target], 16)
                copies.append(
                    pltpu.make_async_copy(
                        piece.at[slot],
                        whole.at[pl.ds(first, piece.shape[1]), pl.ds(*columns)],
                        sems.at[len(copies)],
                    )
                )
    for copy in copies:
        copy.start()
    return copies


def call_with_pieces(kernel, projection, operands, outs, name, micros, scratch=()):
    pieces, plan, targets = projection
    count = 1 if plan is None else sum(len(jobs) for jobs in plan)
    if targets is None:
        targets = jnp.zeros((8,), jnp.int32)
    size = len(operands)

    def run(*refs):
        where_ref, whole, sems = refs[0], refs[-2], refs[-1]
        rest = refs[1:]
        copies = start_pieces(plan, where_ref, rest[size : size + len(pieces)], whole, sems)

        def ready():
            for copy in copies:
                copy.wait()

        kernel(ready, whole, *rest[:size], *rest[size + len(pieces) : -2])

    return pl.pallas_call(
        run,
        out_shape=outs,
        in_specs=[SCALARS]
        + [pl.BlockSpec(memory_space=pltpu.VMEM)] * size
        + [ANYWHERE] * len(pieces),
        scratch_shapes=[
            *scratch,
            pltpu.VMEM((D, pieces[0].shape[-1]), jnp.bfloat16),
            pltpu.SemaphoreType.DMA((count,)),
        ],
        compiler_params=pltpu.CompilerParams(vmem_limit_bytes=VMEM_BYTES),
        cost_estimate=cost(micros),
        name=name,
    )(targets, *operands, *pieces)


def local_call(kernel, operands, outs, name, micros, scratch=()):
    return pl.pallas_call(
        kernel,
        out_shape=outs,
        scratch_shapes=list(scratch),
        compiler_params=pltpu.CompilerParams(vmem_limit_bytes=VMEM_BYTES),
        cost_estimate=cost(micros),
        name=name,
    )(*operands)


def cost(micros):
    return pl.CostEstimate(flops=int(micros * 1.1e9) // COST_SHARE, bytes_accessed=0, transcendentals=0)


def shaped(shape, dtype):
    return jax.ShapeDtypeStruct(shape, dtype)


def dot(left, right, left_dim, right_dim):
    return lax.dot_general(
        left, right, (((left_dim,), (right_dim,)), ((), ())), preferred_element_type=jnp.float32
    )


def swap_halves(values):
    return pltpu.roll(values, HEAD_DIM // 2, 1)


def turned(values, cosine, sine):
    return values * cosine + swap_halves(values) * sine


def turned_back(grads, cosine, sine):
    return grads * cosine + swap_halves(grads * sine)


def front_kernel(
    ready, whole, rows_ref, gain_ref, bias_ref, cosine_ref, sine_ref, normed_ref, query_ref, pair_ref
):
    rows = wide(rows_ref[...])
    normed_ref[...] = low(rows * norm_scale(rows) * gain_ref[...])
    normed = normed_ref[...]
    cosine, sine = cosine_ref[...], sine_ref[...]
    ready()
    for first in range(0, QKV, 256):
        mixed = dot(normed, whole[:, first : first + 256], 1, 0) + bias_ref[:, first : first + 256]
        for start in (0, HEAD_DIM):
            part = mixed[:, start : start + HEAD_DIM]
            column = first + start
            if column < QW + KW:
                part = turned(part, cosine, sine)
            if column < QW:
                query_ref[:, column : column + HEAD_DIM] = low(part)
            else:
                pair_ref[:, column - QW : column - QW + HEAD_DIM] = low(part)


TOGETHER = 2


def head_views(step):
    heads = step * TOGETHER
    kind = heads // (HEADS // KV_HEADS)
    queries = [pl.ds(pl.multiple_of((heads + i) * HEAD_DIM, HEAD_DIM), HEAD_DIM) for i in range(TOGETHER)]
    keys = pl.ds(pl.multiple_of(kind * HEAD_DIM, HEAD_DIM), HEAD_DIM)
    values = pl.ds(pl.multiple_of(KW + kind * HEAD_DIM, HEAD_DIM), HEAD_DIM)
    return queries, keys, values


def visible(key_marks_ref, query_marks_ref):
    seen = (key_marks_ref[:, 0:1] == query_marks_ref[0:1, :]) & (
        key_marks_ref[:, 1:2] <= query_marks_ref[1:2, :]
    )
    return jnp.concatenate([jnp.where(seen, 0.0, -1e30)] * TOGETHER, axis=1)


def probabilities(keys, query, hidden):
    scores = dot(keys, query, 1, 1) * (HEAD_DIM**-0.5) + hidden
    grown = jnp.exp(scores - jnp.max(scores, axis=0, keepdims=True))
    return grown * (1.0 / jnp.sum(grown, axis=0, keepdims=True))


def attend_kernel(
    ready, whole, query_ref, pair_ref, key_marks_ref, query_marks_ref, rows_ref, gain_ref,
    attended_ref, middle_ref, normed_ref, hidden_ref,
):
    hidden_ref[...] = visible(key_marks_ref, query_marks_ref)

    def step(index, unused):
        queries, keys, values = head_views(index)
        query = jnp.concatenate([query_ref[:, view] for view in queries], axis=0)
        weights = low(probabilities(pair_ref[:, keys], query, hidden_ref[...]))
        result = low(dot(weights, pair_ref[:, values], 0, 0))
        count = query_ref.shape[0]
        for i, view in enumerate(queries):
            attended_ref[:, view] = result[i * count : (i + 1) * count]
        return unused

    lax.fori_loop(0, HEADS // TOGETHER, step, 0)
    ready()
    middle = wide(rows_ref[...]) + dot(attended_ref[...], whole[...], 1, 0)
    middle_ref[...] = middle
    normed_ref[...] = low(middle * norm_scale(middle) * gain_ref[...])


def middle_back_kernel(
    ready, whole, normed_grad_ref, received_ref, middle_ref, back_ref, gain_ref,
    middle_grad_ref, branch_ref, gain_grad_ref, attended_grad_ref,
):
    normed_grad = normed_grad_ref[...] + wide(received_ref[...])
    middle = middle_ref[...]
    scale = norm_scale(middle)
    weighted = gain_ref[...] * normed_grad
    middle_grad = (
        wide(back_ref[...])
        + scale * weighted
        - middle * scale**3 * jnp.mean(weighted * middle, axis=1, keepdims=True)
    )
    gain_grad_ref[...] = jnp.sum(normed_grad * middle * scale, axis=0, keepdims=True)
    middle_grad_ref[...] = middle_grad
    branch_ref[...] = low(middle_grad)
    ready()
    attended_grad_ref[...] = low(dot(branch_ref[...], whole[...], 1, 1))


def attend_back_kernel(
    attended_grad_ref, query_ref, pair_ref, key_marks_ref, query_marks_ref, cosine_ref, sine_ref,
    mixed_ref, pair_grad_ref, hidden_ref,
):
    hidden_ref[...] = visible(key_marks_ref, query_marks_ref)
    pair_grad_ref[...] = jnp.zeros_like(pair_grad_ref)
    cosine, sine = cosine_ref[...], sine_ref[...]

    def step(index, unused):
        queries, keys, values = head_views(index)
        query = jnp.concatenate([query_ref[:, view] for view in queries], axis=0)
        grad = jnp.concatenate([attended_grad_ref[:, view] for view in queries], axis=0)
        key = pair_ref[:, keys]
        weights = probabilities(key, query, hidden_ref[...])
        pulled = dot(pair_ref[:, values], grad, 1, 1)
        delta = jnp.sum(weights * pulled, axis=0, keepdims=True)
        score_grad = low(weights * (pulled - delta))
        query_grad = dot(score_grad, key, 0, 0) * (HEAD_DIM**-0.5)
        count = query_ref.shape[0]
        for i, view in enumerate(queries):
            mixed_ref[:, view] = low(
                turned_back(query_grad[i * count : (i + 1) * count], cosine, sine)
            )
        pair_grad_ref[:, keys] += dot(score_grad, query, 1, 0) * (HEAD_DIM**-0.5)
        pair_grad_ref[:, values] += dot(low(weights), grad, 1, 0)
        return unused

    lax.fori_loop(0, HEADS // TOGETHER, step, 0)


def query_kernel(ready, whole, mixed_ref, normed_grad_ref, pair_rows_ref):
    ready()
    normed_grad_ref[...] = dot(mixed_ref[...], whole[:, :QW], 1, 1)
    pair_rows_ref[...] = whole[:, QW:]


def finish_kernel(size, *refs):
    terms, refs = refs[:size], refs[size:]
    cosine_ref, sine_ref, mixed_ref, part_ref, pair_rows_ref, rows_ref, gain_ref = refs[:7]
    middle_grad_ref, gain_two_grad_ref, block_ref, input_grad_ref = refs[7:]
    count = mixed_ref.shape[0]
    total = terms[0][...]
    for term in terms[1:]:
        total = total + wide(term[...])
    block_ref[:count, :QW] = mixed_ref[...]
    for first in range(0, 2 * KW, HEAD_DIM):
        part = total[:, first : first + HEAD_DIM]
        if first < KW:
            part = turned_back(part, cosine_ref[...], sine_ref[...])
        block_ref[:count, QW + first : QW + first + HEAD_DIM] = low(part)
    rows = wide(rows_ref[...])
    scale = norm_scale(rows)
    normed_grad = part_ref[...] + dot(block_ref[:count, QW:], pair_rows_ref[...], 1, 1)
    weighted = gain_ref[...] * normed_grad
    input_grad_ref[...] = (
        middle_grad_ref[...]
        + scale * weighted
        - rows * scale**3 * jnp.mean(weighted * rows, axis=1, keepdims=True)
    )
    gain_grad = jnp.sum(normed_grad * rows * scale, axis=0, keepdims=True)
    gains = jnp.concatenate([gain_grad, gain_two_grad_ref[...], jnp.zeros((14, D), jnp.float32)], axis=0)
    block_ref[count:, :D] = low(gains)
    block_ref[count:, D:] = jnp.zeros((16, QKV - D), jnp.bfloat16)


def gradient_kernel(parts, size, *refs):
    by_unit, blocks = refs[: 3 * parts], refs[3 * parts : 3 * parts + 2 * size]
    out_ref, values, rows, sems = refs[3 * parts + 2 * size :]
    count, tokens = blocks[0].shape[0], by_unit[0].shape[1]

    def copies(kind):
        result = []
        for part in range(parts):
            number = 3 * part + kind
            view = values.at[kind, :, pl.ds(part * tokens, tokens)]
            result.append(pltpu.make_async_copy(by_unit[number], view, sems.at[number]))
        if kind != 1:
            side = kind // 2
            for number in range(size):
                view = rows.at[side, pl.ds(number * count, count), :]
                place = 3 * parts + side * size + number
                result.append(pltpu.make_async_copy(blocks[side * size + number], view, sems.at[place]))
        return result

    step = pl.program_id(0)

    @pl.when(step == 0)
    def _():
        for kind in range(3):
            for copy in copies(kind):
                copy.start()

    for kind in range(3):

        @pl.when(step == 2 * kind)
        def _():
            for copy in copies(kind):
                copy.wait()

        for half in range(2):

            @pl.when(step == 2 * kind + half)
            def _():
                right = rows[kind // 2, :, half * (D // 2) : (half + 1) * (D // 2)]
                out_ref[...] = low(dot(values[kind], right, 1, 0))


def units_gradient(parts, normed, back):
    units, tokens = parts[0][0].shape
    size, count = len(normed), normed[0].shape[0]
    return pl.pallas_call(
        lambda *refs: gradient_kernel(len(parts), size, *refs),
        grid=(6,),
        in_specs=[ANYWHERE] * (3 * len(parts) + 2 * size),
        out_specs=pl.BlockSpec((units, D // 2), lambda i: (0, i)),
        out_shape=shaped((units, 3 * D), jnp.bfloat16),
        scratch_shapes=[
            pltpu.VMEM((3, units, tokens * len(parts)), jnp.bfloat16),
            pltpu.VMEM((2, size * count, D), jnp.bfloat16),
            pltpu.SemaphoreType.DMA((3 * len(parts) + 2 * size,)),
        ],
        compiler_params=pltpu.CompilerParams(vmem_limit_bytes=VMEM_BYTES),
        cost_estimate=cost(8),
        name="units_gradient",
    )(*[item for part in parts for item in part], *normed, *back)


def units_step_kernel(grad_ref, weight_ref, first_ref, second_ref, *out_refs):
    results = optimizer_step(
        weight_ref[...], wide(grad_ref[...])[None], first_ref[...], second_ref[...],
        2.0 / math.sqrt(D), DECAY,
    )
    for out_ref, result in zip(out_refs, results):
        out_ref[...] = result


def units_step(grad, weight, first, second):
    units = grad.shape[0]
    width = D // 2
    block = pl.BlockSpec((1, units, width), lambda i: (i // 2, 0, i % 2))
    turn = lambda value: jnp.transpose(value, (1, 0, 2))
    dtypes = [jnp.float32] * 3 + [jnp.bfloat16]
    results = pl.pallas_call(
        units_step_kernel,
        grid=(6,),
        in_specs=[pl.BlockSpec((units, width), lambda i: (0, i))] + [block] * 3,
        out_specs=[block] * 4,
        out_shape=[shaped((3, units, D), dtype) for dtype in dtypes],
        compiler_params=pltpu.CompilerParams(vmem_limit_bytes=VMEM_BYTES),
        cost_estimate=cost(12),
        name="units_step",
    )(grad, turn(weight), turn(first), turn(second))
    return tuple(turn(result) for result in results)


def weight_kernel(size, *refs):
    left = jnp.concatenate([ref[...] for ref in refs[:size]], axis=0)
    right = jnp.concatenate([ref[...] for ref in refs[size : 2 * size]], axis=0)
    kept_ref, sent_ref = refs[2 * size :]
    total = dot(left, right, 0, 0)
    half = total.shape[0] // 2
    kept_ref[...] = total[:half]
    sent_ref[...] = low(total[half:])


def joined_kernel(size, *refs):
    count = refs[0].shape[0]
    left = jnp.concatenate([ref[...] for ref in refs[:size]], axis=0)
    rights = refs[size : 2 * size]
    right = jnp.concatenate([ref[:count, :] for ref in rights], axis=0)
    kept_ref, vector_ref, sent_ref = refs[2 * size :]
    half = kept_ref.shape[0]
    gains = sum(wide(ref[count:, :]) for ref in rights)
    bias = jnp.sum(wide(right), axis=0, keepdims=True)
    vector = jnp.concatenate([gains[:2], bias, jnp.zeros((13, QKV), jnp.float32)], axis=0)
    vector_ref[...] = vector[:8]
    sent_ref[half:, :] = low(vector)
    total = dot(left, right, 0, 0)
    kept_ref[...] = total[:half]
    sent_ref[:half, :] = low(total[half:])


def dp_scatter(total, early=(), log=None):
    depth = lax.axis_size(DP)
    width = total.shape[0] // depth
    return add_back([total[i * width : (i + 1) * width] for i in range(depth)], DP, early, log)


def norm_scale(rows):
    return lax.rsqrt(jnp.mean(rows * rows, axis=1, keepdims=True) + NORM_EPS)


def unpack_small(small):
    gain_cols = D // KW
    group = HEADS // KV_HEADS
    gain_one = small[:, :gain_cols].reshape(D)
    gain_two = small[:, gain_cols : 2 * gain_cols].reshape(D)
    query_bias = small[:, 2 * gain_cols : 2 * gain_cols + group].reshape(KV_HEADS, HEAD_DIM, group)
    query_bias = jnp.transpose(query_bias, (0, 2, 1)).reshape(QW)
    key_bias = small[:, 2 * gain_cols + group]
    value_bias = small[:, 2 * gain_cols + group + 1]
    return (gain_one, gain_two, jnp.concatenate([query_bias, key_bias, value_bias]))


def pack_small(gain_one, gain_two, bias):
    gain_cols = D // KW
    group = HEADS // KV_HEADS
    query_part = jnp.transpose(bias[:QW].reshape(KV_HEADS, group, HEAD_DIM), (0, 2, 1)).reshape(
        KW, group
    )
    return jnp.concatenate(
        [
            gain_one.reshape(KW, gain_cols),
            gain_two.reshape(KW, gain_cols),
            query_part,
            bias[QW : QW + KW][:, None],
            bias[QW + KW :][:, None],
        ],
        axis=1,
    )


def layout(starts_row, places):
    before = starts_row[None, :] <= places[:, None]
    documents = jnp.sum(before.astype(jnp.int32), axis=1) - 1
    begin = jnp.max(jnp.where(before, starts_row[None, :], 0), axis=1)
    offset = places - begin
    return (documents, offset // BLOCK, offset)


def turning(offset):
    half = HEAD_DIM // 2
    frequency = ROPE_BASE ** (-(2.0 * jnp.arange(half, dtype=jnp.float32)) / HEAD_DIM)
    angle = offset.astype(jnp.float32)[:, None] * frequency[None, :]
    angle = jnp.concatenate([angle, angle], axis=1)
    return (jnp.cos(angle)[:, None, :], jnp.sin(angle)[:, None, :])


def optimizer_step(weight, grad, first, second, rate, decay):
    first = BETA_ONE * first + (1.0 - BETA_ONE) * grad
    second = BETA_TWO * second + (1.0 - BETA_TWO) * grad * grad
    fixed_first = first / (1.0 - BETA_ONE**STEP)
    fixed_second = second / (1.0 - BETA_TWO**STEP)
    weight = weight - rate * (fixed_first / (jnp.sqrt(fixed_second) + ADAM_EPS) + decay * weight)
    return (weight, first, second, weight.astype(jnp.bfloat16))


def body(
    inputs,
    output_grad,
    document_starts,
    joined_weight,
    out_weight,
    units_weight,
    small_params,
    joined_first,
    joined_second,
    out_first,
    out_second,
    units_first,
    units_second,
    small_first,
    small_second,
):
    count = inputs.shape[0]
    seq_count = lax.axis_size(SEQ)
    devices = seq_count * lax.axis_size(DP)
    seq_index = lax.axis_index(SEQ)
    group_len = count * seq_count
    first = seq_index * count
    starts_row = document_starts[0]
    feature_width = joined_weight.shape[0]
    unit_width = units_weight.shape[0]

    device = lax.axis_index(ALL)
    small_rows, small_cols = small_params.shape
    size = small_rows * small_cols
    vector = lax.dynamic_update_slice_in_dim(
        jnp.zeros((devices * size,), jnp.float32),
        wide(low(small_params)).reshape(-1),
        device * size,
        0,
    ).reshape(1, -1)
    for axis in (DP, "c", "x", "y"):
        vector = sum(rotations(vector, axis))
    vector = jnp.concatenate(unpack_small(vector.reshape(-1, small_cols))).reshape(1, -1)
    gain_one, gain_two, bias = vector[:, :D], vector[:, D : 2 * D], vector[:, 2 * D :]

    joined_half = low(joined_weight)
    line = rotations(joined_half, DP)
    back_blocks = token_gather(output_grad, lambda value: after(value, line[-1]))
    projection = projection_pieces(
        joined_half, line, back_blocks[0][1:3], [back_blocks[0][3], back_blocks[1][0]]
    )
    out_half = low(out_weight)
    out_line = rotations(after(out_half, line[-1]), DP)
    out_projection = projection_pieces(
        out_half, out_line, projection[0][1:3], projection[0][3:5]
    )
    documents, blocks, offset = layout(starts_row, first + jnp.arange(count, dtype=jnp.int32))
    cosine, sine = turning(offset)
    cosine, sine = cosine[:, 0], sine[:, 0]
    sine = jnp.concatenate([-sine[:, : HEAD_DIM // 2], sine[:, HEAD_DIM // 2 :]], axis=1)
    sources = seq_sources()
    places = jnp.concatenate([i * count + jnp.arange(count, dtype=jnp.int32) for i in sources])
    all_documents, all_blocks, unused_offset = layout(starts_row, places)
    key_marks = jnp.stack([all_documents, all_blocks], axis=1)
    query_marks = jnp.stack([documents, blocks], axis=0)
    wanted = wanted_columns(D, feature_width)

    sharing = ("zl", "c")
    units_half = low(units_weight)
    units_all = lax.all_gather(units_half, sharing, axis=0, tiled=True)
    units_all = jnp.transpose(units_all, (1, 0, 2))

    normed_one, query, pair = call_with_pieces(
        front_kernel,
        projection,
        [after(inputs, *back_blocks[1][1:3]), gain_one, bias, cosine, sine],
        [
            shaped((count, D), jnp.bfloat16),
            shaped((count, QW), jnp.bfloat16),
            shaped((count, 2 * KW), jnp.bfloat16),
        ],
        "front",
        6,
    )
    pair_all = seq_gather_small(pair)

    attended, middle, normed_two = call_with_pieces(
        attend_kernel,
        out_projection,
        [after(query, back_blocks[1][3]), pair_all, key_marks, query_marks, inputs, gain_two],
        [
            shaped((count, QW), jnp.bfloat16),
            shaped((count, D), jnp.float32),
            shaped((count, D), jnp.bfloat16),
        ],
        "attend",
        12,
        [pltpu.VMEM((group_len, TOGETHER * count), jnp.float32)],
    )

    steps = plane_steps()
    normed_sent = low(dot(after(normed_one, normed_two), wanted, 1, 0))
    attended_sent = low(dot(attended, wanted, 1, 0))
    chip_width = D // len(steps)
    normed_owned, attended_owned = [], []
    for number, (j, i) in enumerate(steps):
        view = slice(number * chip_width, (number + 1) * chip_width)
        both = [normed_sent[:, view], attended_sent[:, view]]
        if number:
            moved = plane_shift(jnp.concatenate(both, axis=1), -j, -i)
            both = [moved[:, :chip_width], moved[:, chip_width:]]
        normed_owned.append(both[0])
        attended_owned.append(both[1])

    normed_blocks = token_gather(normed_two, lambda value: value)
    by_unit = lambda rows, tokens: jnp.einsum(
        "ud,td->ut", rows, tokens, preferred_element_type=jnp.float32
    )
    by_token = lambda values, rows: jnp.einsum(
        "ut,ud->td", values, rows, preferred_element_type=jnp.float32
    )
    cut = lambda value: [value[i : i + count] for i in range(0, value.shape[0], count)]
    unit_parts, grad_terms = [], []
    for normed, back in zip(normed_blocks, back_blocks):
        pulled = by_unit(units_all[2], jnp.concatenate(back, axis=0))
        if unit_parts:
            normed = [after(normed[0], *normed_owned, *attended_owned)] + normed[1:]
        normed = jnp.concatenate(normed, axis=0)
        gate = by_unit(units_all[0], normed)
        up = by_unit(units_all[1], normed)
        sigma = jax.nn.sigmoid(gate)
        active = gate * sigma
        gate_grad = low(pulled * up * sigma * (1.0 + gate * (1.0 - sigma)))
        up_grad = low(pulled * active)
        unit_parts.append((gate_grad, up_grad, low(active * up)))
        grad_terms.append(by_token(gate_grad, units_all[0]) + by_token(up_grad, units_all[1]))
    branch_terms = []

    def between(received):
        branch_terms.extend(
            cut(low(by_token(after(part[2], received[0]), units_all[2]))) for part in unit_parts
        )
        return sum(branch_terms, [])

    plane_sums, normed_grad_own, normed_grad_received, *unused = token_scatter(
        [cut(item) for item in grad_terms], between
    )
    parts = [unit_parts[0][:2] + (after(unit_parts[0][2], *plane_sums),)] + unit_parts[1:]
    units_term = units_gradient(
        parts,
        [block for blocks in normed_blocks for block in blocks],
        [block for blocks in back_blocks for block in blocks],
    )
    units_sum = lax.psum_scatter(units_term, sharing, scatter_dimension=0, tiled=True)
    branch_terms = [[after(item, *plane_sums) for item in blocks] for blocks in branch_terms]
    unused, branch_own, branch_received, branch_first, branch_second = token_scatter(branch_terms)
    block_output = low(middle + branch_own + wide(branch_received))

    middle_grad, branch_grad, gain_two_grad, attended_grad = call_with_pieces(
        middle_back_kernel,
        out_projection,
        [normed_grad_own, normed_grad_received, middle, output_grad, gain_two],
        [
            shaped((count, D), jnp.float32),
            shaped((count, D), jnp.bfloat16),
            shaped((1, D), jnp.float32),
            shaped((count, QW), jnp.bfloat16),
        ],
        "middle_back",
        4,
    )
    branch_pieces = plane_blocks(branch_grad)
    mixed_grad, pair_grad = local_call(
        attend_back_kernel,
        [attended_grad, query, pair_all, key_marks, query_marks, cosine, sine],
        [shaped((count, QW), jnp.bfloat16), shaped((group_len, 2 * KW), jnp.float32)],
        "attend_back",
        800,
        [pltpu.VMEM((group_len, TOGETHER * count), jnp.float32)],
    )
    pair_terms, pair_got = seq_scatter_small(after(pair_grad, *branch_pieces[1:3]), count)
    query_operand = after(mixed_grad, *pair_got)
    normed_grad_part, pair_rows = call_with_pieces(
        query_kernel,
        projection,
        [query_operand],
        [shaped((count, D), jnp.float32), shaped((D, 2 * KW), jnp.bfloat16)],
        "query_back",
        7,
    )
    mixed_block, input_grad = local_call(
        lambda *refs: finish_kernel(len(pair_terms), *refs),
        pair_terms
        + [cosine, sine, mixed_grad, normed_grad_part, pair_rows, inputs, gain_one, middle_grad]
        + [gain_two_grad],
        [shaped((count + 16, QKV), jnp.bfloat16), shaped((count, D), jnp.float32)],
        "finish",
        4,
    )
    mixed_pieces = plane_blocks(mixed_block)
    attended_owned[0] = after(attended_owned[0], mixed_block, *branch_first)
    half = attended_owned[0].shape[1] // 2
    kept, sent = local_call(
        lambda *refs: weight_kernel(len(steps), *refs),
        attended_owned + branch_pieces,
        [shaped((half, D), jnp.float32), shaped((half, D), jnp.bfloat16)],
        "out_weights",
        3,
    )
    outer_sum = kept + wide(shift(sent, "c", -1))
    normed_owned[0] = after(normed_owned[0], *branch_second)
    kept, kept_vector, sent = local_call(
        lambda *refs: joined_kernel(len(steps), *refs),
        normed_owned + mixed_pieces,
        [
            shaped((half, QKV), jnp.float32),
            shaped((8, QKV), jnp.float32),
            shaped((half + 16, QKV), jnp.bfloat16),
        ],
        "joined_weights",
        5,
    )
    got = shift(sent, "c", -1)
    units_new = units_step(units_sum, units_weight, units_first, units_second)
    outer_grad = dp_scatter(outer_sum, [units_new[3]])
    joined_grad = dp_scatter(kept + wide(got[:half]), [units_new[3]])
    vector = sum(rotations(kept_vector + wide(got[half : half + 8]), DP))
    small_grad = pack_small(vector[0, :D], vector[1, :D], vector[2])
    small_grad = lax.dynamic_slice_in_dim(small_grad, device * small_rows, small_rows, 0)

    joined = optimizer_step(
        joined_weight, joined_grad, joined_first, joined_second, 2.0 / math.sqrt(D), DECAY
    )
    outer = optimizer_step(
        out_weight, outer_grad, out_first, out_second, 2.0 / math.sqrt(QW // 64), DECAY
    )
    small = optimizer_step(small_params, small_grad, small_first, small_second, 0.5, 0.0)
    return (block_output, input_grad) + joined + outer + units_new + small


def solution(mesh):
    groups, members = mesh.devices.shape
    fine = Mesh(mesh.devices.reshape(groups // 2, 2, members // 4, 2, 2), ALL)
    flat, cube = P(ALL, None), P(ALL, None, None)
    in_specs = (flat, flat, P(DP, None), flat, flat, cube, flat) + (flat,) * 4 + (cube,) * 2 + (flat,) * 2
    out_specs = (flat,) * 10 + (cube,) * 4 + (flat,) * 4
    return jax.shard_map(body, mesh=fine, in_specs=in_specs, out_specs=out_specs, check_vma=False)
```

time: 503 us -> 439 us (0.87)
  the two profiles are of different devices: /device:TPU:7 before, /device:TPU:0 now
where the time goes in v3:
time: 439 us; the launch traced here: 432 us
  waiting for transfers between devices  141 us (32%)
  starting transfers between devices  96.1 us (22%)
  Pallas kernels  86.9 us (20%)
  matrix products  38.5 us (9%)
  local copies, waits for them, and re-layouts  29.8 us (7%)
  other arithmetic  23.2 us (5%)
  between operations  15.9 us (4%)
    ppermute x71, waiting for transfers between devices, shift(): lax.ppermute(value, axis, [(i, (i + step) % count) for i in range(count)])  104 us
    ppermute x71, starting transfers between devices, shift(): lax.ppermute(value, axis, [(i, (i + step) % count) for i in range(count)])  79.2 us
    ppermute x15, waiting for transfers between devices, plane_shift(): return lax.ppermute(value, ('y', 'x'), pairs)  37 us
    pallas_call x4, Pallas kernels, call_with_pieces(): pl.pallas_call(run, out_shape=outs, in_specs=[SCALARS] + [pl.BlockSpec(me...  31.5 us
    pallas_call x4, Pallas kernels, local_call(): pl.pallas_call(kernel, out_shape=outs, scratch_shapes=list(scratch), comp...  24.8 us
    dot_general x6, matrix products, body(): jnp.einsum('ud,td->ut', rows, tokens, preferred_element_type=jnp.float32)  20.5 us
    ppermute x15, starting transfers between devices, plane_shift(): return lax.ppermute(value, ('y', 'x'), pairs)  16.9 us
    pallas_call x1, Pallas kernels, units_gradient(): pl.pallas_call(lambda *refs: gradient_kernel(len(parts), size, *refs), gr...  16.3 us
  transfers between devices with their start and end apart: 88, of which 32 were waited for; matrix products, arithmetic and copies ran while one was open for 13% of the time, Pallas kernels for 20%

profile of v3, /device:TPU:0, one launch (start us, length us, event | category | flops | bytes accessed | tf_op | source)
XLA Modules:
  0.0 431.5 jit_solution(9142994800168633377)
XLA Ops:
  7.2 4.3 convert_element_type.188
  12.4 3.1 collective-permute-start.4
  15.5 2.6 collective-permute-start.5
  23.7 1.9 collective-permute-start.12
  28.4 3.0 collective-permute-done
  32.5 1.8 collective-permute-done.10
  34.2 6.9 %collective-permute-done.11 = bf16[48,2048]{1,0:T(8,128)(2,1)S(1)} collective-permute-done((bf16[48,2048]{1,0:T(8,128)(2,1)S(1)}, bf16[48,2048]{1,0:T(8,128)(2,1)S(1)}, u32[]{:S(2)}, u32[]{:S(2)}) %collective-permute-start.11) | collective-permute-done | bytes 196640 | tf_op jit(solution)/shard_map/ppermute | solution.py:50
  46.9 3.4 collective-permute-start.1
  51.9 10.0 %collective-permute-done.9 = f32[1,5120]{1,0:T(1,128)S(1)} collective-permute-done((f32[1,5120]{1,0:T(1,128)S(1)}, f32[1,5120]{1,0:T(1,128)S(1)}, u32[]{:S(2)}, u32[]{:S(2)}) %collective-permute-start.9) | collective-permute-done | bytes 20512 | tf_op jit(solution)/shard_map/ppermute | solution.py:50
  62.0 2.3 collective-permute-start.29
  64.8 8.2 %collective-permute-done.29 = bf16[48,1536]{1,0:T(8,128)(2,1)} collective-permute-done((bf16[48,1536]{1,0:T(8,128)(2,1)S(1)}, bf16[48,1536]{1,0:T(8,128)(2,1)}, u32[]{:S(2)}, u32[]{:S(2)}) %collective-permute-start.29) | collective-permute-done | bytes 147488 | tf_op jit(solution)/shard_map/ppermute | solution.py:50
  75.8 3.7 collective-permute-start.31
  79.9 6.3 %collective-permute-done.30 = bf16[48,1536]{1,0:T(8,128)(2,1)S(1)} collective-permute-done((bf16[48,1536]{1,0:T(8,128)(2,1)S(1)}, bf16[48,1536]{1,0:T(8,128)(2,1)S(1)}, u32[]{:S(2)}, u32[]{:S(2)}) %collective-permute-start.30) | collective-permute-done | bytes 147488 | tf_op jit(solution)/shard_map/ppermute | solution.py:50
  86.6 2.5 collective-permute-done.31
  94.0 5.6 %collective-permute-done.18.refs_10_.refs_6_ = bf16[4,48,1024]{2,1,0:T(8,128)(2,1)S(1)} collective-permute-done((bf16[4,48,1024]{2,1,0:T(8,128)(2,1)S(1)}, bf16[4,48,1024]{2,1,0:T(8,128)(2,1)S(1)}, u32[]{:S(2)}, u32[]{:S(2)}) %collective-permute-start.18) | collective-permute-done | bytes 393248 | tf_op jit(solution)/shard_map/ppermute | solution.py:50
  102.7 6.1 %front.1 = (bf16[128,1536]{1,0:T(8,128)(2,1)}, bf16[128,1536]{1,0:T(8,128)(2,1)}, bf16[128,512]{1,0:T(8,128)(2,1)}) custom-call(s32[40]{0:T(128)} %stack.220.refs_0_, bf16[128,1536]{1,0:T(8,128)(2,1)} %refs_9_.1, f32[1,1536]{1,0:T(1,128)} %get-tuple-element.252.refs_2_.refs_10_, f32[1,2048]{1,0:T(1,128)} %slice.308.refs_3_, ...), custom_call_target="tpu_custom_call" | custom-call | flops 1650000000 | tf_op jit(solution)/shard_map/front/pallas_call | solution.py:241
  110.3 2.0 collective-permute-start.27
  113.5 5.7 %collective-permute-done.25 = bf16[128,512]{1,0:T(8,128)(2,1)S(1)} collective-permute-done((bf16[128,512]{1,0:T(8,128)(2,1)}, bf16[128,512]{1,0:T(8,128)(2,1)S(1)}, u32[]{:S(2)}, u32[]{:S(2)}) %collective-permute-start.25) | collective-permute-done | bytes 131104 | tf_op jit(solution)/shard_map/ppermute | solution.py:68
  120.1 1.8 collective-permute-done.27
  127.4 3.1 collective-permute-done.24.refs_21_
  130.5 5.8 %collective-permute-done.35.refs_11_.refs_10_ = bf16[4,48,768]{2,1,0:T(8,128)(2,1)S(1)} collective-permute-done((bf16[4,48,768]{2,1,0:T(8,128)(2,1)S(1)}, bf16[4,48,768]{2,1,0:T(8,128)(2,1)S(1)}, u32[]{:S(2)}, u32[]{:S(2)}) %collective-permute-start.35) | collective-permute-done | bytes 294944 | tf_op jit(solution)/shard_map/ppermute | solution.py:50
  142.0 11.4 %attend.1 = (bf16[128,1536]{1,0:T(8,128)(2,1)}, f32[128,1536]{1,0:T(8,128)}, bf16[128,1536]{1,0:T(8,128)(2,1)}) custom-call(s32[40]{0:T(128)} %stack.220.refs_0_, bf16[128,1536]{1,0:T(8,128)(2,1)} %get-tuple-element.84.refs_1_.query_ref, bf16[1024,512]{1,0:T(8,128)(2,1)} %copy-done.59, s32[1024,2]{1,0:T(8,128)} %copy.89.refs_3_.key_marks_ref, ...), custom_call_target="tpu_custom_call" | custom-call | flops 3300000000 | tf_op jit(solution)/shard_map/attend/pallas_call | solution.py:241
  153.4 4.6 %collective-permute-start.44 = (bf16[128,1536]{1,0:T(8,128)(2,1)}, bf16[128,1536]{1,0:T(8,128)(2,1)S(1)}, u32[]{:S(2)}, u32[]{:S(2)}) collective-permute-start(bf16[128,1536]{1,0:T(8,128)(2,1)} %get-tuple-element.91.refs_6_), channel_id=1, source_target_pairs={{0,16},{16,0},{1,17},{17,1},{2,18},{18,2},{3,19},{19,3},{4,20},{20... | collective-permute-start | bytes 1179656 | tf_op jit(solution)/shard_map/ppermute | solution.py:50
  160.0 2.1 fusion.4
  162.0 2.1 fusion.5
  167.4 6.5 %collective-permute-done.47 = bf16[128,768]{1,0:T(8,128)(2,1)S(1)} collective-permute-done((bf16[128,768]{1,0:T(8,128)(2,1)S(1)}, bf16[128,768]{1,0:T(8,128)(2,1)S(1)}, u32[]{:S(2)}, u32[]{:S(2)}) %collective-permute-start.47) | collective-permute-done | bytes 196640 | tf_op jit(solution)/shard_map/ppermute | solution.py:68
  175.8 3.2 collective-permute-done.46
  184.8 9.2 %collective-permute-done.49.refs_12_ = bf16[128,1536]{1,0:T(8,128)(2,1)S(1)} collective-permute-done((bf16[128,1536]{1,0:T(8,128)(2,1)S(1)}, bf16[128,1536]{1,0:T(8,128)(2,1)S(1)}, u32[]{:S(2)}, u32[]{:S(2)}) %collective-permute-start.49) | collective-permute-done | bytes 393248 | tf_op jit(solution)/shard_map/ppermute | solution.py:50
  196.4 3.1 collective-permute-done.43.refs_9_
  199.5 2.3 collective-permute-done.50.refs_13_
  202.6 4.6 %convolution_bitcast_fusion.1 = f32[1120,512]{1,0:T(8,128)S(1)} fusion(bf16[512,1536]{1,0:T(8,128)(2,1)} %constant_dynamic-update-slice_fusion.19, bf16[3,1120,1536]{2,1,0:T(8,128)(2,1)} %bitcast.136), kind=kOutput, calls=%fused_computation.9 | convolution fusion | flops 1761607680 | bytes 7307264 | tf_op jit(solution)/shard_map/ud,td->ut/dot_general | solution.py:742
  208.0 3.4 convolution_bitcast_fusion.2
  211.4 4.2 multiply_convert_fusion.3
  215.7 2.3 fusion.9
  218.0 2.4 fusion.93
  221.4 2.0 convolution_bitcast_fusion.5
  224.7 3.2 convolution_bitcast_fusion
  227.9 3.1 multiply_convert_fusion.5
  231.0 2.3 fusion.8
  233.3 2.3 fusion.94
  239.5 2.3 convolution_convert_fusion.1
  241.8 2.3 convolution_convert_fusion
  245.2 2.6 collective-permute-done.53
  250.0 9.2 %collective-permute-done.56 = bf16[128,1536]{1,0:T(8,128)(2,1)S(1)} collective-permute-done((bf16[128,1536]{1,0:T(8,128)(2,1)S(1)}, bf16[128,1536]{1,0:T(8,128)(2,1)S(1)}, u32[]{:S(2)}, u32[]{:S(2)}) %collective-permute-start.56) | collective-permute-done | bytes 393248 | tf_op jit(solution)/shard_map/ppermute | solution.py:50
  264.8 16.3 %units_gradient.1 = bf16[1120,4608]{1,0:T(8,128)(2,1)} custom-call(bf16[1120,512]{1,0:T(8,128)(2,1)} %copy-done.1, bf16[1120,512]{1,0:T(8,128)(2,1)} %copy-done.32, bf16[1120,512]{1,0:T(8,128)(2,1)} %copy-done.31, bf16[1120,512]{1,0:T(8,128)(2,1)} %copy-done, bf16[1120,512]{1,0:T(8,128)(2,1)} %copy-done.29, bf16[1120,512]{1,0:T(8,128)(2,1)} %copy-done.30, ...), custom_call_target="tpu_custom_call" | custom-call | flops 2200000000 | tf_op jit(solution)/shard_map/units_gradient/pallas_call | solution.py:494
  281.9 6.9 %middle_back.1 = (f32[128,1536]{1,0:T(8,128)}, bf16[128,1536]{1,0:T(8,128)(2,1)}, f32[1,1536]{1,0:T(1,128)}, bf16[128,1536]{1,0:T(8,128)(2,1)}) custom-call(s32[40]{0:T(128)} %stack.220.refs_0_, f32[128,1536]{1,0:T(8,128)} %fusion.27.refs_1_, bf16[128,1536]{1,0:T(8,128)(2,1)} %copy-done.46, f32[128,1536]{1,0:T(8,128)} %get-tuple-element.90.refs_3_, ...), custom_call_target="tpu_custom_call" | custom-call | flops 1100000000 | tf_op jit(solution)/shard_map/middle_back/pallas_call | solution.py:241
  291.3 12.8 %attend_back.1 = (bf16[128,1536]{1,0:T(8,128)(2,1)}, f32[1024,512]{1,0:T(8,128)}) custom-call(bf16[128,1536]{1,0:T(8,128)(2,1)} %get-tuple-element.108.attended_grad_ref, bf16[128,1536]{1,0:T(8,128)(2,1)} %get-tuple-element.84.refs_1_.query_ref, bf16[1024,512]{1,0:T(8,128)(2,1)} %copy-done.59, s32[1024,2]{1,0:T(8,128)} %copy.89.refs_3_.key_marks_ref, ...), custom_call_target="tpu_custom_call" | custom-call | flops 219999993856 | tf_op jit(solution)/shard_map/attend_back/pallas_call | solution.py:259
  312.2 2.8 collective-permute-done.60
  315.0 11.0 %collective-permute-done.62 = bf16[128,1536]{1,0:T(8,128)(2,1)S(1)} collective-permute-done((bf16[128,1536]{1,0:T(8,128)(2,1)S(1)}, bf16[128,1536]{1,0:T(8,128)(2,1)S(1)}, u32[]{:S(2)}, u32[]{:S(2)}) %collective-permute-start.62) | collective-permute-done | bytes 393248 | tf_op jit(solution)/shard_map/ppermute | solution.py:50
  326.2 2.2 collective-permute-start.63
  331.3 7.2 %query_back.1 = (f32[128,1536]{1,0:T(8,128)}, bf16[1536,512]{1,0:T(8,128)(2,1)}) custom-call(s32[40]{0:T(128)} %stack.220.refs_0_, bf16[128,1536]{1,0:T(8,128)(2,1)} %get-tuple-element.113.refs_1_.refs_6_, bf16[4,48,2048]{2,1,0:T(8,128)(2,1)} %copy-done.5, bf16[4,48,2048]{2,1,0:T(8,128)(2,1)} %copy-done.8, bf16[4,48,2048]{2,1,0:T(8,128)(2,1)} %copy-done.9, ...), custom_call_target="tpu_custom_call" | custom-call | flops 1924999936 | tf_op jit(solution)/shard_map/query_back/pallas_call | solution.py:241
  339.3 4.3 %finish.1 = (bf16[144,2048]{1,0:T(8,128)(2,1)}, f32[128,1536]{1,0:T(8,128)}) custom-call(f32[128,512]{1,0:T(8,128)} %slice.350.refs_0_, bf16[128,512]{1,0:T(8,128)(2,1)} %copy-done.52, bf16[128,512]{1,0:T(8,128)(2,1)} %copy-done.53, bf16[128,512]{1,0:T(8,128)(2,1)} %copy-done.54, f32[128,128]{1,0:T(8,128)} %get-tuple-element.250.refs_4_.cosine_ref, ...), custom_call_target="tpu_custom_call" | custom-call | flops 1100000000 | tf_op jit(solution)/shard_map/finish/pallas_call | solution.py:259
  347.2 3.5 out_weights.1
  350.7 2.0 add_convert_fusion
  352.7 7.5 %collective-permute-done.71.refs_5_ = bf16[144,2048]{1,0:T(8,128)(2,1)S(1)} collective-permute-done((bf16[144,2048]{1,0:T(8,128)(2,1)}, bf16[144,2048]{1,0:T(8,128)(2,1)S(1)}, u32[]{:S(2)}, u32[]{:S(2)}) %collective-permute-start.71) | collective-permute-done | bytes 589856 | tf_op jit(solution)/shard_map/ppermute | solution.py:68
  360.2 12.1 %collective-permute-done.72.refs_6_ = bf16[144,2048]{1,0:T(8,128)(2,1)S(1)} collective-permute-done((bf16[144,2048]{1,0:T(8,128)(2,1)}, bf16[144,2048]{1,0:T(8,128)(2,1)S(1)}, u32[]{:S(2)}, u32[]{:S(2)}) %collective-permute-start.72) | collective-permute-done | bytes 589856 | tf_op jit(solution)/shard_map/ppermute | solution.py:68
  373.9 4.1 joined_weights.1
  381.1 2.9 collective-permute-start.84
  386.1 3.8 collective-permute-done.83
  389.9 5.4 %collective-permute-start.82 = (bf16[48,1536]{1,0:T(8,128)(2,1)S(1)}, bf16[48,1536]{1,0:T(8,128)(2,1)}, u32[]{:S(2)}, u32[]{:S(2)}) collective-permute-start(bf16[48,1536]{1,0:T(8,128)(2,1)S(1)} %get-tuple-element.223), channel_id=1, source_target_pairs={{0,8},{8,16},{16,24},{24,0},{1,9},{9,17},{17,25},{25,1},{2,10},{10... | collective-permute-start | bytes 442376 | tf_op jit(solution)/shard_map/ppermute | solution.py:50
  395.3 3.6 collective-permute-done.84
  405.2 14.3 %units_step.1 = (f32[3,280,1536]{2,1,0:T(8,128)}, f32[3,280,1536]{2,1,0:T(8,128)}, f32[3,280,1536]{2,1,0:T(8,128)}, bf16[3,280,1536]{2,1,0:T(8,128)(2,1)}) custom-call(bf16[280,4608]{1,0:T(8,128)(2,1)} %reduce-scatter.2.cloned.1.call-done.grad_ref, f32[3,280,1536]{2,1,0:T(8,128)} %bitcast.133, f32[3,280,1536]{2,1,0:T(8,128)} %bitcast.134, ...), custom_call_target="tpu_custom_call" | custom-call | flops 3300000000 | tf_op jit(solution)/shard_map/units_step/pallas_call | solution.py:526
  419.6 2.3 fusion.72
  421.9 2.3 fusion.75
  (399 shorter events, 107.7 us)
Async XLA Ops:
  7.2 195.4 %all-gather.2.cloned.1.call-start = ((), (), s32[]{:S(2)}) async-start(), calls=%async_computation.1 | async-start | bytes 12902400 | tf_op jit(solution)/shard_map/all_gather | solution.py:696
  11.5 393.7 %reduce-scatter.2.cloned.1.call-start = ((), (), s32[]{:S(2)}) async-start(), calls=%async_computation.2 | async-start | bytes 12902400 | tf_op jit(solution)/shard_map/reduce_scatter | solution.py:780
  19.5 12.0 %collective-permute-start = (bf16[48,2048]{1,0:T(8,128)(2,1)S(1)}, bf16[48,2048]{1,0:T(8,128)(2,1)S(1)}, u32[]{:S(2)}, u32[]{:S(2)}) collective-permute-start(bf16[48,2048]{1,0:T(8,128)(2,1)S(1)} %convert_element_type.182), channel_id=1, source_target_pairs={{0,24},{8,0},{16,8},{24,16},{1,25},{9,1},{17,9},{25,17},{2,26},{10... | collective-permute-start | bytes 589832 | tf_op jit(solution)/shard_map/ppermute | solution.py:50
  20.0 14.3 %collective-permute-start.10 = (bf16[48,2048]{1,0:T(8,128)(2,1)S(1)}, bf16[48,2048]{1,0:T(8,128)(2,1)S(1)}, u32[]{:S(2)}, u32[]{:S(2)}) collective-permute-start(bf16[48,2048]{1,0:T(8,128)(2,1)S(1)} %convert_element_type.182), channel_id=1, source_target_pairs={{0,8},{8,16},{16,24},{24,0},{1,9},{9,17},{17,25},{25,1},{2,10},{10... | collective-permute-start | bytes 589832 | tf_op jit(solution)/shard_map/ppermute | solution.py:50
  23.2 18.0 %collective-permute-start.11 = (bf16[48,2048]{1,0:T(8,128)(2,1)S(1)}, bf16[48,2048]{1,0:T(8,128)(2,1)S(1)}, u32[]{:S(2)}, u32[]{:S(2)}) collective-permute-start(bf16[48,2048]{1,0:T(8,128)(2,1)S(1)} %convert_element_type.182), channel_id=1, source_target_pairs={{0,16},{8,24},{16,0},{24,8},{1,17},{9,25},{17,1},{25,9},{2,18},{10... | collective-permute-start | bytes 589832 | tf_op jit(solution)/shard_map/ppermute | solution.py:50
  23.7 17.6 %collective-permute-start.12 = (bf16[128,1536]{1,0:T(8,128)(2,1)S(1)}, bf16[128,1536]{1,0:T(8,128)(2,1)}, u32[]{:S(2)}, u32[]{:S(2)}) collective-permute-start(bf16[128,1536]{1,0:T(8,128)(2,1)S(1)} %copy-done.23), channel_id=1, source_target_pairs={{0,2},{2,0},{1,3},{3,1},{4,6},{6,4},{5,7},{7,5},{8,10},{10,8},{9,1... | collective-permute-start | bytes 1179656 | tf_op jit(solution)/shard_map/ppermute | solution.py:50
  26.9 14.4 %collective-permute-start.13 = (bf16[128,1536]{1,0:T(8,128)(2,1)S(1)}, bf16[128,1536]{1,0:T(8,128)(2,1)}, u32[]{:S(2)}, u32[]{:S(2)}) collective-permute-start(bf16[128,1536]{1,0:T(8,128)(2,1)S(1)} %copy-done.23), channel_id=1, source_target_pairs={{0,4},{4,0},{1,5},{5,1},{2,6},{6,2},{3,7},{7,3},{8,12},{12,8},{9,1... | collective-permute-start | bytes 1179656 | tf_op jit(solution)/shard_map/ppermute | solution.py:50
  31.5 13.5 %collective-permute-start.8 = (f32[1,5120]{1,0:T(1,128)S(1)}, f32[1,5120]{1,0:T(1,128)S(1)}, u32[]{:S(2)}, u32[]{:S(2)}) collective-permute-start(f32[1,5120]{1,0:T(1,128)S(1)} %add.844), channel_id=1, source_target_pairs={{0,2},{2,0},{1,3},{3,1},{4,6},{6,4},{5,7},{7,5},{8,10},{10,8},{9,1... | collective-permute-start | bytes 61448 | tf_op jit(solution)/shard_map/ppermute | solution.py:50
  41.3 34.4 %collective-permute-start.14 = (bf16[4,48,2048]{2,1,0:T(8,128)(2,1)S(1)}, bf16[4,48,2048]{2,1,0:T(8,128)(2,1)S(1)}, u32[]{:S(2)}, u32[]{:S(2)}) collective-permute-start(bf16[4,48,2048]{2,1,0:T(8,128)(2,1)S(1)} %pad_maximum_fusion.refs_6_.refs_2_), channel_id=1, source_target_pairs={{0,2},{2,0},{1,3},{3,1},{4,6},{6,4},{5,7},{7,5},{8,10},{10,8},{9,1... | collective-permute-start | bytes 2359304 | tf_op jit(solution)/shard_map/ppermute | solution.py:50
  42.7 33.1 %collective-permute-start.15 = (bf16[4,48,2048]{2,1,0:T(8,128)(2,1)S(1)}, bf16[4,48,2048]{2,1,0:T(8,128)(2,1)S(1)}, u32[]{:S(2)}, u32[]{:S(2)}) collective-permute-start(bf16[4,48,2048]{2,1,0:T(8,128)(2,1)S(1)} %pad_maximum_fusion.refs_6_.refs_2_), channel_id=1, source_target_pairs={{0,4},{4,0},{1,5},{5,1},{2,6},{6,2},{3,7},{7,3},{8,12},{12,8},{9,1... | collective-permute-start | bytes 2359304 | tf_op jit(solution)/shard_map/ppermute | solution.py:50
  45.0 16.8 %collective-permute-start.9 = (f32[1,5120]{1,0:T(1,128)S(1)}, f32[1,5120]{1,0:T(1,128)S(1)}, u32[]{:S(2)}, u32[]{:S(2)}) collective-permute-start(f32[1,5120]{1,0:T(1,128)S(1)} %add.845), channel_id=1, source_target_pairs={{0,4},{4,0},{1,5},{5,1},{2,6},{6,2},{3,7},{7,3},{8,12},{12,8},{9,1... | collective-permute-start | bytes 61448 | tf_op jit(solution)/shard_map/ppermute | solution.py:50
  46.9 26.1 %collective-permute-start.1 = (bf16[128,1536]{1,0:T(8,128)(2,1)S(1)}, bf16[128,1536]{1,0:T(8,128)(2,1)}, u32[]{:S(2)}, u32[]{:S(2)}) collective-permute-start(bf16[128,1536]{1,0:T(8,128)(2,1)S(1)} %copy-done.23), channel_id=1, source_target_pairs={{0,16},{16,0},{1,17},{17,1},{2,18},{18,2},{3,19},{19,3},{4,20},{20... | collective-permute-start | bytes 1179656 | tf_op jit(solution)/shard_map/ppermute | solution.py:50
  50.3 24.2 %collective-permute-start.16 = (bf16[128,1536]{1,0:T(8,128)(2,1)}, bf16[128,1536]{1,0:T(8,128)(2,1)}, u32[]{:S(2)}, u32[]{:S(2)}) collective-permute-start(bf16[128,1536]{1,0:T(8,128)(2,1)} %collective-permute-done.12.refs_15_), channel_id=1, source_target_pairs={{0,4},{4,0},{1,5},{5,1},{2,6},{6,2},{3,7},{7,3},{8,12},{12,8},{9,1... | collective-permute-start | bytes 1179656 | tf_op jit(solution)/shard_map/ppermute | solution.py:50
  62.0 10.9 %collective-permute-start.29 = (bf16[48,1536]{1,0:T(8,128)(2,1)S(1)}, bf16[48,1536]{1,0:T(8,128)(2,1)}, u32[]{:S(2)}, u32[]{:S(2)}) collective-permute-start(bf16[48,1536]{1,0:T(8,128)(2,1)S(1)} %convert_element_type.187), channel_id=1, source_target_pairs={{0,8},{8,16},{16,24},{24,0},{1,9},{9,17},{17,25},{25,1},{2,10},{10... | collective-permute-start | bytes 442376 | tf_op jit(solution)/shard_map/ppermute | solution.py:50
  73.0 19.5 %collective-permute-start.19 = (bf16[4,48,2048]{2,1,0:T(8,128)(2,1)S(1)}, bf16[4,48,2048]{2,1,0:T(8,128)(2,1)}, u32[]{:S(2)}, u32[]{:S(2)}) collective-permute-start(bf16[4,48,2048]{2,1,0:T(8,128)(2,1)S(1)} %pad_maximum_fusion.refs_6_.refs_2_), channel_id=1, source_target_pairs={{0,1},{1,0},{2,3},{3,2},{4,5},{5,4},{6,7},{7,6},{8,9},{9,8},{10,11... | collective-permute-start | bytes 2359304 | tf_op jit(solution)/shard_map/ppermute | solution.py:50
  73.0 17.2 %collective-permute-start.3 = (bf16[128,1536]{1,0:T(8,128)(2,1)}, bf16[128,1536]{1,0:T(8,128)(2,1)}, u32[]{:S(2)}, u32[]{:S(2)}) collective-permute-start(bf16[128,1536]{1,0:T(8,128)(2,1)} %collective-permute-done.1.refs_18_), channel_id=1, source_target_pairs={{0,4},{4,0},{1,5},{5,1},{2,6},{6,2},{3,7},{7,3},{8,12},{12,8},{9,1... | collective-permute-start | bytes 1179656 | tf_op jit(solution)/shard_map/ppermute | solution.py:50
  74.5 15.7 %collective-permute-start.2 = (bf16[128,1536]{1,0:T(8,128)(2,1)}, bf16[128,1536]{1,0:T(8,128)(2,1)}, u32[]{:S(2)}, u32[]{:S(2)}) collective-permute-start(bf16[128,1536]{1,0:T(8,128)(2,1)} %collective-permute-done.1.refs_18_), channel_id=1, source_target_pairs={{0,2},{2,0},{1,3},{3,1},{4,6},{6,4},{5,7},{7,5},{8,10},{10,8},{9,1... | collective-permute-start | bytes 1179656 | tf_op jit(solution)/shard_map/ppermute | solution.py:50
  75.8 13.4 %collective-permute-start.31 = (bf16[48,1536]{1,0:T(8,128)(2,1)S(1)}, bf16[48,1536]{1,0:T(8,128)(2,1)S(1)}, u32[]{:S(2)}, u32[]{:S(2)}) collective-permute-start(bf16[48,1536]{1,0:T(8,128)(2,1)S(1)} %convert_element_type.187), channel_id=1, source_target_pairs={{0,24},{8,0},{16,8},{24,16},{1,25},{9,1},{17,9},{25,17},{2,26},{10... | collective-permute-start | bytes 442376 | tf_op jit(solution)/shard_map/ppermute | solution.py:50
  90.1 11.2 %collective-permute-start.20 = (bf16[4,48,2048]{2,1,0:T(8,128)(2,1)S(1)}, bf16[4,48,2048]{2,1,0:T(8,128)(2,1)S(1)}, u32[]{:S(2)}, u32[]{:S(2)}) collective-permute-start(bf16[4,48,2048]{2,1,0:T(8,128)(2,1)S(1)} %collective-permute-done.14.refs_7_.refs_3_), channel_id=1, source_target_pairs={{0,1},{1,0},{2,3},{3,2},{4,5},{5,4},{6,7},{7,6},{8,9},{9,8},{10,11... | collective-permute-start | bytes 2359304 | tf_op jit(solution)/shard_map/ppermute | solution.py:50
  90.2 11.1 %collective-permute-start.21 = (bf16[4,48,2048]{2,1,0:T(8,128)(2,1)S(1)}, bf16[4,48,2048]{2,1,0:T(8,128)(2,1)S(1)}, u32[]{:S(2)}, u32[]{:S(2)}) collective-permute-start(bf16[4,48,2048]{2,1,0:T(8,128)(2,1)S(1)} %collective-permute-done.15.refs_8_.refs_4_), channel_id=1, source_target_pairs={{0,1},{1,0},{2,3},{3,2},{4,5},{5,4},{6,7},{7,6},{8,9},{9,8},{10,11... | collective-permute-start | bytes 2359304 | tf_op jit(solution)/shard_map/ppermute | solution.py:50
  92.4 19.9 %collective-permute-start.33 = (bf16[4,48,1536]{2,1,0:T(8,128)(2,1)S(1)}, bf16[4,48,1536]{2,1,0:T(8,128)(2,1)S(1)}, u32[]{:S(2)}, u32[]{:S(2)}) collective-permute-start(bf16[4,48,1536]{2,1,0:T(8,128)(2,1)S(1)} %pad_maximum_fusion.1.refs_7_.refs_6_), channel_id=1, source_target_pairs={{0,4},{4,0},{1,5},{5,1},{2,6},{6,2},{3,7},{7,3},{8,12},{12,8},{9,1... | collective-permute-start | bytes 1769480 | tf_op jit(solution)/shard_map/ppermute | solution.py:50
  100.3 23.9 %collective-permute-start.32 = (bf16[4,48,1536]{2,1,0:T(8,128)(2,1)S(1)}, bf16[4,48,1536]{2,1,0:T(8,128)(2,1)}, u32[]{:S(2)}, u32[]{:S(2)}) collective-permute-start(bf16[4,48,1536]{2,1,0:T(8,128)(2,1)S(1)} %pad_maximum_fusion.1.refs_7_.refs_6_), channel_id=1, source_target_pairs={{0,2},{2,0},{1,3},{3,1},{4,6},{6,4},{5,7},{7,5},{8,10},{10,8},{9,1... | collective-permute-start | bytes 1769480 | tf_op jit(solution)/shard_map/ppermute | solution.py:50
  110.3 11.6 %collective-permute-start.27 = (bf16[128,512]{1,0:T(8,128)(2,1)}, bf16[128,512]{1,0:T(8,128)(2,1)S(1)}, u32[]{:S(2)}, u32[]{:S(2)}) collective-permute-start(bf16[128,512]{1,0:T(8,128)(2,1)} %get-tuple-element.85), channel_id=1, source_target_pairs={{0,6},{2,4},{4,2},{6,0},{1,7},{3,5},{5,3},{7,1},{8,14},{10,12},{12... | collective-permute-start | bytes 393224 | tf_op jit(solution)/shard_map/ppermute | solution.py:68
  112.4 18.2 %collective-permute-start.24 = (bf16[128,1536]{1,0:T(8,128)(2,1)}, bf16[128,1536]{1,0:T(8,128)(2,1)}, u32[]{:S(2)}, u32[]{:S(2)}) collective-permute-start(bf16[128,1536]{1,0:T(8,128)(2,1)} %collective-permute-done.3.refs_20_), channel_id=1, source_target_pairs={{0,2},{2,0},{1,3},{3,1},{4,6},{6,4},{5,7},{7,5},{8,10},{10,8},{9,1... | collective-permute-start | bytes 1179656 | tf_op jit(solution)/shard_map/ppermute | solution.py:50
  119.2 17.1 %collective-permute-start.35 = (bf16[4,48,768]{2,1,0:T(8,128)(2,1)S(1)}, bf16[4,48,768]{2,1,0:T(8,128)(2,1)S(1)}, u32[]{:S(2)}, u32[]{:S(2)}) collective-permute-start(bf16[4,48,768]{2,1,0:T(8,128)(2,1)S(1)} %slice.315), channel_id=1, source_target_pairs={{0,2},{2,0},{1,3},{3,1},{4,6},{6,4},{5,7},{7,5},{8,10},{10,8},{9,1... | collective-permute-start | bytes 884744 | tf_op jit(solution)/shard_map/ppermute | solution.py:50
  123.7 15.6 %collective-permute-start.28 = (bf16[512,512]{1,0:T(8,128)(2,1)}, bf16[512,512]{1,0:T(8,128)(2,1)}, u32[]{:S(2)}, u32[]{:S(2)}) collective-permute-start(bf16[512,512]{1,0:T(8,128)(2,1)} %pad_maximum_fusion.2), channel_id=1, source_target_pairs={{0,1},{1,0},{2,3},{3,2},{4,5},{5,4},{6,7},{7,6},{8,9},{9,8},{10,11... | collective-permute-start | bytes 1572872 | tf_op jit(solution)/shard_map/ppermute | solution.py:50
  123.7 16.8 %collective-permute-start.36 = (bf16[4,48,1536]{2,1,0:T(8,128)(2,1)S(1)}, bf16[4,48,1536]{2,1,0:T(8,128)(2,1)S(1)}, u32[]{:S(2)}, u32[]{:S(2)}) collective-permute-start(bf16[4,48,1536]{2,1,0:T(8,128)(2,1)S(1)} %pad_maximum_fusion.1.refs_7_.refs_6_), channel_id=1, source_target_pairs={{0,1},{1,0},{2,3},{3,2},{4,5},{5,4},{6,7},{7,6},{8,9},{9,8},{10,11... | collective-permute-start | bytes 1769480 | tf_op jit(solution)/shard_map/ppermute | solution.py:50
  125.9 12.8 %collective-permute-start.34 = (bf16[4,48,768]{2,1,0:T(8,128)(2,1)}, bf16[4,48,768]{2,1,0:T(8,128)(2,1)}, u32[]{:S(2)}, u32[]{:S(2)}) collective-permute-start(bf16[4,48,768]{2,1,0:T(8,128)(2,1)} %slice.314), channel_id=1, source_target_pairs={{0,4},{4,0},{1,5},{5,1},{2,6},{6,2},{3,7},{7,3},{8,12},{12,8},{9,1... | collective-permute-start | bytes 884744 | tf_op jit(solution)/shard_map/ppermute | solution.py:50
  153.4 27.3 %collective-permute-start.44 = (bf16[128,1536]{1,0:T(8,128)(2,1)}, bf16[128,1536]{1,0:T(8,128)(2,1)S(1)}, u32[]{:S(2)}, u32[]{:S(2)}) collective-permute-start(bf16[128,1536]{1,0:T(8,128)(2,1)} %get-tuple-element.91.refs_6_), channel_id=1, source_target_pairs={{0,16},{16,0},{1,17},{17,1},{2,18},{18,2},{3,19},{19,3},{4,20},{20... | collective-permute-start | bytes 1179656 | tf_op jit(solution)/shard_map/ppermute | solution.py:50
  158.0 25.5 %collective-permute-start.41 = (bf16[128,1536]{1,0:T(8,128)(2,1)}, bf16[128,1536]{1,0:T(8,128)(2,1)S(1)}, u32[]{:S(2)}, u32[]{:S(2)}) collective-permute-start(bf16[128,1536]{1,0:T(8,128)(2,1)} %get-tuple-element.91.refs_6_), channel_id=1, source_target_pairs={{0,2},{2,0},{1,3},{3,1},{4,6},{6,4},{5,7},{7,5},{8,10},{10,8},{9,1... | collective-permute-start | bytes 1179656 | tf_op jit(solution)/shard_map/ppermute | solution.py:50
  159.5 25.3 %collective-permute-start.42 = (bf16[128,1536]{1,0:T(8,128)(2,1)}, bf16[128,1536]{1,0:T(8,128)(2,1)S(1)}, u32[]{:S(2)}, u32[]{:S(2)}) collective-permute-start(bf16[128,1536]{1,0:T(8,128)(2,1)} %get-tuple-element.91.refs_6_), channel_id=1, source_target_pairs={{0,4},{4,0},{1,5},{5,1},{2,6},{6,2},{3,7},{7,3},{8,12},{12,8},{9,1... | collective-permute-start | bytes 1179656 | tf_op jit(solution)/shard_map/ppermute | solution.py:50
  166.5 12.5 %collective-permute-start.46 = (bf16[128,768]{1,0:T(8,128)(2,1)S(1)}, bf16[128,768]{1,0:T(8,128)(2,1)S(1)}, u32[]{:S(2)}, u32[]{:S(2)}) collective-permute-start(bf16[128,768]{1,0:T(8,128)(2,1)S(1)} %pad_maximum_fusion.4), channel_id=1, source_target_pairs={{0,4},{2,6},{4,0},{6,2},{1,5},{3,7},{5,1},{7,3},{8,12},{10,14},{12... | collective-permute-start | bytes 589832 | tf_op jit(solution)/shard_map/ppermute | solution.py:68
  180.7 14.1 %collective-permute-start.48 = (bf16[128,1536]{1,0:T(8,128)(2,1)S(1)}, bf16[128,1536]{1,0:T(8,128)(2,1)S(1)}, u32[]{:S(2)}, u32[]{:S(2)}) collective-permute-start(bf16[128,1536]{1,0:T(8,128)(2,1)S(1)} %collective-permute-done.44.refs_10_), channel_id=1, source_target_pairs={{0,2},{2,0},{1,3},{3,1},{4,6},{6,4},{5,7},{7,5},{8,10},{10,8},{9,1... | collective-permute-start | bytes 1179656 | tf_op jit(solution)/shard_map/ppermute | solution.py:50
  181.9 12.1 %collective-permute-start.49 = (bf16[128,1536]{1,0:T(8,128)(2,1)S(1)}, bf16[128,1536]{1,0:T(8,128)(2,1)S(1)}, u32[]{:S(2)}, u32[]{:S(2)}) collective-permute-start(bf16[128,1536]{1,0:T(8,128)(2,1)S(1)} %collective-permute-done.44.refs_10_), channel_id=1, source_target_pairs={{0,4},{4,0},{1,5},{5,1},{2,6},{6,2},{3,7},{7,3},{8,12},{12,8},{9,1... | collective-permute-start | bytes 1179656 | tf_op jit(solution)/shard_map/ppermute | solution.py:50
  183.5 15.9 %collective-permute-start.43 = (bf16[128,1536]{1,0:T(8,128)(2,1)S(1)}, bf16[128,1536]{1,0:T(8,128)(2,1)S(1)}, u32[]{:S(2)}, u32[]{:S(2)}) collective-permute-start(bf16[128,1536]{1,0:T(8,128)(2,1)S(1)} %collective-permute-done.41.refs_7_), channel_id=1, source_target_pairs={{0,4},{4,0},{1,5},{5,1},{2,6},{6,2},{3,7},{7,3},{8,12},{12,8},{9,1... | collective-permute-start | bytes 1179656 | tf_op jit(solution)/shard_map/ppermute | solution.py:50
  220.5 17.3 %collective-permute-start.55 = (bf16[128,1536]{1,0:T(8,128)(2,1)S(1)}, bf16[128,1536]{1,0:T(8,128)(2,1)S(1)}, u32[]{:S(2)}, u32[]{:S(2)}) collective-permute-start(bf16[128,1536]{1,0:T(8,128)(2,1)S(1)} %get-tuple-element.207), channel_id=1, source_target_pairs={{0,2},{2,0},{1,3},{3,1},{4,6},{6,4},{5,7},{7,5},{8,10},{10,8},{9,1... | collective-permute-start | bytes 1179656 | tf_op jit(solution)/shard_map/ppermute | solution.py:50
  223.4 16.2 %collective-permute-start.51 = (bf16[128,1536]{1,0:T(8,128)(2,1)S(1)}, bf16[128,1536]{1,0:T(8,128)(2,1)S(1)}, u32[]{:S(2)}, u32[]{:S(2)}) collective-permute-start(bf16[128,1536]{1,0:T(8,128)(2,1)S(1)} %get-tuple-element.208), channel_id=1, source_target_pairs={{0,2},{2,0},{1,3},{3,1},{4,6},{6,4},{5,7},{7,5},{8,10},{10,8},{9,1... | collective-permute-start | bytes 1179656 | tf_op jit(solution)/shard_map/ppermute | solution.py:50
  235.7 12.1 %collective-permute-start.53 = (bf16[128,1536]{1,0:T(8,128)(2,1)S(1)}, bf16[128,1536]{1,0:T(8,128)(2,1)S(1)}, u32[]{:S(2)}, u32[]{:S(2)}) collective-permute-start(bf16[128,1536]{1,0:T(8,128)(2,1)S(1)} %get-tuple-element.210), channel_id=1, source_target_pairs={{0,4},{4,0},{1,5},{5,1},{2,6},{6,2},{3,7},{7,3},{8,12},{12,8},{9,1... | collective-permute-start | bytes 1179656 | tf_op jit(solution)/shard_map/ppermute | solution.py:50
  237.4 23.4 %collective-permute-start.52 = (bf16[128,1536]{1,0:T(8,128)(2,1)S(1)}, bf16[128,1536]{1,0:T(8,128)(2,1)S(1)}, u32[]{:S(2)}, u32[]{:S(2)}) collective-permute-start(bf16[128,1536]{1,0:T(8,128)(2,1)S(1)} %get-tuple-element.209), channel_id=1, source_target_pairs={{0,4},{4,0},{1,5},{5,1},{2,6},{6,2},{3,7},{7,3},{8,12},{12,8},{9,1... | collective-permute-start | bytes 1179656 | tf_op jit(solution)/shard_map/ppermute | solution.py:50
  237.9 21.3 %collective-permute-start.56 = (bf16[128,1536]{1,0:T(8,128)(2,1)S(1)}, bf16[128,1536]{1,0:T(8,128)(2,1)S(1)}, u32[]{:S(2)}, u32[]{:S(2)}) collective-permute-start(bf16[128,1536]{1,0:T(8,128)(2,1)S(1)} %fusion.24), channel_id=1, source_target_pairs={{0,4},{4,0},{1,5},{5,1},{2,6},{6,2},{3,7},{7,3},{8,12},{12,8},{9,1... | collective-permute-start | bytes 1179656 | tf_op jit(solution)/shard_map/ppermute | solution.py:50
  247.9 12.8 %collective-permute-start.54 = (bf16[128,1536]{1,0:T(8,128)(2,1)S(1)}, bf16[128,1536]{1,0:T(8,128)(2,1)S(1)}, u32[]{:S(2)}, u32[]{:S(2)}) collective-permute-start(bf16[128,1536]{1,0:T(8,128)(2,1)S(1)} %fusion.26), channel_id=1, source_target_pairs={{0,2},{2,0},{1,3},{3,1},{4,6},{6,4},{5,7},{7,5},{8,10},{10,8},{9,1... | collective-permute-start | bytes 1179656 | tf_op jit(solution)/shard_map/ppermute | solution.py:50
  259.3 21.8 %collective-permute-start.64 = (bf16[128,1536]{1,0:T(8,128)(2,1)S(1)}, bf16[128,1536]{1,0:T(8,128)(2,1)S(1)}, u32[]{:S(2)}, u32[]{:S(2)}) collective-permute-start(bf16[128,1536]{1,0:T(8,128)(2,1)S(1)} %fusion.25), channel_id=1, source_target_pairs={{0,16},{16,0},{1,17},{17,1},{2,18},{18,2},{3,19},{19,3},{4,20},{20... | collective-permute-start | bytes 1179656 | tf_op jit(solution)/shard_map/ppermute | solution.py:50
  261.8 45.6 %collective-permute-start.58 = (bf16[128,1536]{1,0:T(8,128)(2,1)}, bf16[128,1536]{1,0:T(8,128)(2,1)}, u32[]{:S(2)}, u32[]{:S(2)}) collective-permute-start(bf16[128,1536]{1,0:T(8,128)(2,1)} %get-tuple-element.103), channel_id=1, source_target_pairs={{0,4},{4,0},{1,5},{5,1},{2,6},{6,2},{3,7},{7,3},{8,12},{12,8},{9,1... | collective-permute-start | bytes 1179656 | tf_op jit(solution)/shard_map/ppermute | solution.py:50
  263.3 45.3 %collective-permute-start.61 = (bf16[128,1536]{1,0:T(8,128)(2,1)}, bf16[128,1536]{1,0:T(8,128)(2,1)}, u32[]{:S(2)}, u32[]{:S(2)}) collective-permute-start(bf16[128,1536]{1,0:T(8,128)(2,1)} %get-tuple-element.107), channel_id=1, source_target_pairs={{0,2},{2,0},{1,3},{3,1},{4,6},{6,4},{5,7},{7,5},{8,10},{10,8},{9,1... | collective-permute-start | bytes 1179656 | tf_op jit(solution)/shard_map/ppermute | solution.py:50
  263.8 81.8 %collective-permute-start.57 = (bf16[128,1536]{1,0:T(8,128)(2,1)}, bf16[128,1536]{1,0:T(8,128)(2,1)}, u32[]{:S(2)}, u32[]{:S(2)}) collective-permute-start(bf16[128,1536]{1,0:T(8,128)(2,1)} %get-tuple-element.101), channel_id=1, source_target_pairs={{0,4},{4,0},{1,5},{5,1},{2,6},{6,2},{3,7},{7,3},{8,12},{12,8},{9,1... | collective-permute-start | bytes 1179656 | tf_op jit(solution)/shard_map/ppermute | solution.py:50
  288.8 15.4 %collective-permute-start.65 = (bf16[128,1536]{1,0:T(8,128)(2,1)}, bf16[128,1536]{1,0:T(8,128)(2,1)}, u32[]{:S(2)}, u32[]{:S(2)}) collective-permute-start(bf16[128,1536]{1,0:T(8,128)(2,1)} %get-tuple-element.110.refs_4_), channel_id=1, source_target_pairs={{0,2},{2,0},{4,6},{6,4},{1,3},{3,1},{5,7},{7,5},{8,10},{10,8},{12,... | collective-permute-start | bytes 1179656 | tf_op jit(solution)/shard_map/ppermute | solution.py:68
  289.7 15.0 %collective-permute-start.66 = (bf16[128,1536]{1,0:T(8,128)(2,1)}, bf16[128,1536]{1,0:T(8,128)(2,1)}, u32[]{:S(2)}, u32[]{:S(2)}) collective-permute-start(bf16[128,1536]{1,0:T(8,128)(2,1)} %get-tuple-element.110.refs_4_), channel_id=1, source_target_pairs={{0,4},{2,6},{4,0},{6,2},{1,5},{3,7},{5,1},{7,3},{8,12},{10,14},{12... | collective-permute-start | bytes 1179656 | tf_op jit(solution)/shard_map/ppermute | solution.py:68
  304.7 42.5 %collective-permute-start.78 = (bf16[128,1536]{1,0:T(8,128)(2,1)S(1)}, bf16[128,1536]{1,0:T(8,128)(2,1)}, u32[]{:S(2)}, u32[]{:S(2)}) collective-permute-start(bf16[128,1536]{1,0:T(8,128)(2,1)S(1)} %copy-done.65), channel_id=1, source_target_pairs={{0,6},{2,4},{4,2},{6,0},{1,7},{3,5},{5,3},{7,1},{8,14},{10,12},{12... | collective-permute-start | bytes 1179656 | tf_op jit(solution)/shard_map/ppermute | solution.py:68
  308.6 19.8 %collective-permute-start.59 = (bf16[128,1536]{1,0:T(8,128)(2,1)S(1)}, bf16[128,1536]{1,0:T(8,128)(2,1)S(1)}, u32[]{:S(2)}, u32[]{:S(2)}) collective-permute-start(bf16[128,1536]{1,0:T(8,128)(2,1)S(1)} %add_convert_fusion.3), channel_id=1, source_target_pairs={{0,2},{2,0},{1,3},{3,1},{4,6},{6,4},{5,7},{7,5},{8,10},{10,8},{9,1... | collective-permute-start | bytes 1179656 | tf_op jit(solution)/shard_map/ppermute | solution.py:50
  310.9 15.1 %collective-permute-start.62 = (bf16[128,1536]{1,0:T(8,128)(2,1)S(1)}, bf16[128,1536]{1,0:T(8,128)(2,1)S(1)}, u32[]{:S(2)}, u32[]{:S(2)}) collective-permute-start(bf16[128,1536]{1,0:T(8,128)(2,1)S(1)} %add_convert_fusion.2), channel_id=1, source_target_pairs={{0,4},{4,0},{1,5},{5,1},{2,6},{6,2},{3,7},{7,3},{8,12},{12,8},{9,1... | collective-permute-start | bytes 1179656 | tf_op jit(solution)/shard_map/ppermute | solution.py:50
  315.0 14.7 %collective-permute-start.68 = (bf16[128,512]{1,0:T(8,128)(2,1)S(1)}, bf16[128,512]{1,0:T(8,128)(2,1)S(1)}, u32[]{:S(2)}, u32[]{:S(2)}) collective-permute-start(bf16[128,512]{1,0:T(8,128)(2,1)S(1)} %get-tuple-element.227), channel_id=1, source_target_pairs={{0,2},{2,0},{4,6},{6,4},{1,3},{3,1},{5,7},{7,5},{8,10},{10,8},{12,... | collective-permute-start | bytes 393224 | tf_op jit(solution)/shard_map/ppermute | solution.py:68
  326.2 24.5 %collective-permute-start.63 = (bf16[128,1536]{1,0:T(8,128)(2,1)S(1)}, bf16[128,1536]{1,0:T(8,128)(2,1)S(1)}, u32[]{:S(2)}, u32[]{:S(2)}) collective-permute-start(bf16[128,1536]{1,0:T(8,128)(2,1)S(1)} %add_convert_fusion.1), channel_id=1, source_target_pairs={{0,16},{16,0},{1,17},{17,1},{2,18},{18,2},{3,19},{19,3},{4,20},{20... | collective-permute-start | bytes 1179656 | tf_op jit(solution)/shard_map/ppermute | solution.py:50
  343.6 16.5 %collective-permute-start.71 = (bf16[144,2048]{1,0:T(8,128)(2,1)}, bf16[144,2048]{1,0:T(8,128)(2,1)S(1)}, u32[]{:S(2)}, u32[]{:S(2)}) collective-permute-start(bf16[144,2048]{1,0:T(8,128)(2,1)} %get-tuple-element.120.refs_4_), channel_id=1, source_target_pairs={{0,2},{2,0},{4,6},{6,4},{1,3},{3,1},{5,7},{7,5},{8,10},{10,8},{12,... | collective-permute-start | bytes 1769480 | tf_op jit(solution)/shard_map/ppermute | solution.py:68
  345.0 27.3 %collective-permute-start.72 = (bf16[144,2048]{1,0:T(8,128)(2,1)}, bf16[144,2048]{1,0:T(8,128)(2,1)S(1)}, u32[]{:S(2)}, u32[]{:S(2)}) collective-permute-start(bf16[144,2048]{1,0:T(8,128)(2,1)} %get-tuple-element.120.refs_4_), channel_id=1, source_target_pairs={{0,4},{2,6},{4,0},{6,2},{1,5},{3,7},{5,1},{7,3},{8,12},{10,14},{12... | collective-permute-start | bytes 1769480 | tf_op jit(solution)/shard_map/ppermute | solution.py:68
  345.7 26.6 %collective-permute-start.73 = (bf16[144,2048]{1,0:T(8,128)(2,1)}, bf16[144,2048]{1,0:T(8,128)(2,1)S(1)}, u32[]{:S(2)}, u32[]{:S(2)}) collective-permute-start(bf16[144,2048]{1,0:T(8,128)(2,1)} %get-tuple-element.120.refs_4_), channel_id=1, source_target_pairs={{0,6},{2,4},{4,2},{6,0},{1,7},{3,5},{5,3},{7,1},{8,14},{10,12},{12... | collective-permute-start | bytes 1769480 | tf_op jit(solution)/shard_map/ppermute | solution.py:68
  350.7 27.4 %collective-permute-start.79 = (bf16[192,1536]{1,0:T(8,128)(2,1)}, bf16[192,1536]{1,0:T(8,128)(2,1)S(1)}, u32[]{:S(2)}, u32[]{:S(2)}) collective-permute-start(bf16[192,1536]{1,0:T(8,128)(2,1)} %get-tuple-element.130), channel_id=1, source_target_pairs={{0,1},{1,0},{2,3},{3,2},{4,5},{5,4},{6,7},{7,6},{8,9},{9,8},{10,11... | collective-permute-start | bytes 1769480 | tf_op jit(solution)/shard_map/ppermute | solution.py:50
  379.0 24.7 %collective-permute-start.80 = (bf16[48,1536]{1,0:T(8,128)(2,1)}, bf16[48,1536]{1,0:T(8,128)(2,1)}, u32[]{:S(2)}, u32[]{:S(2)}) collective-permute-start(bf16[48,1536]{1,0:T(8,128)(2,1)} %get-tuple-element.222), channel_id=1, source_target_pairs={{0,24},{8,0},{16,8},{24,16},{1,25},{9,1},{17,9},{25,17},{2,26},{10... | collective-permute-start | bytes 442376 | tf_op jit(solution)/shard_map/ppermute | solution.py:50
  379.0 40.5 %collective-permute-start.81 = (bf16[48,1536]{1,0:T(8,128)(2,1)}, bf16[48,1536]{1,0:T(8,128)(2,1)}, u32[]{:S(2)}, u32[]{:S(2)}) collective-permute-start(bf16[48,1536]{1,0:T(8,128)(2,1)} %get-tuple-element.224), channel_id=1, source_target_pairs={{0,16},{8,24},{16,0},{24,8},{1,17},{9,25},{17,1},{25,9},{2,18},{10... | collective-permute-start | bytes 442376 | tf_op jit(solution)/shard_map/ppermute | solution.py:50
  381.1 17.8 %collective-permute-start.84 = (f32[8,2048]{1,0:T(8,128)S(1)}, f32[8,2048]{1,0:T(8,128)S(1)}, u32[]{:S(2)}, u32[]{:S(2)}) collective-permute-start(f32[8,2048]{1,0:T(8,128)S(1)} %convert_add_fusion.3), channel_id=1, source_target_pairs={{0,16},{8,24},{16,0},{24,8},{1,17},{9,25},{17,1},{25,9},{2,18},{10... | collective-permute-start | bytes 196616 | tf_op jit(solution)/shard_map/ppermute | solution.py:50
  384.0 15.4 %collective-permute-start.85 = (f32[8,2048]{1,0:T(8,128)S(1)}, f32[8,2048]{1,0:T(8,128)S(1)}, u32[]{:S(2)}, u32[]{:S(2)}) collective-permute-start(f32[8,2048]{1,0:T(8,128)S(1)} %convert_add_fusion.3), channel_id=1, source_target_pairs={{0,24},{8,0},{16,8},{24,16},{1,25},{9,1},{17,9},{25,17},{2,26},{10... | collective-permute-start | bytes 196616 | tf_op jit(solution)/shard_map/ppermute | solution.py:50
  389.9 29.7 %collective-permute-start.82 = (bf16[48,1536]{1,0:T(8,128)(2,1)S(1)}, bf16[48,1536]{1,0:T(8,128)(2,1)}, u32[]{:S(2)}, u32[]{:S(2)}) collective-permute-start(bf16[48,1536]{1,0:T(8,128)(2,1)S(1)} %get-tuple-element.223), channel_id=1, source_target_pairs={{0,8},{8,16},{16,24},{24,0},{1,9},{9,17},{17,25},{25,1},{2,10},{10... | collective-permute-start | bytes 442376 | tf_op jit(solution)/shard_map/ppermute | solution.py:50
  398.9 20.7 %collective-permute-start.75 = (bf16[48,2048]{1,0:T(8,128)(2,1)}, bf16[48,2048]{1,0:T(8,128)(2,1)}, u32[]{:S(2)}, u32[]{:S(2)}) collective-permute-start(bf16[48,2048]{1,0:T(8,128)(2,1)} %get-tuple-element.219), channel_id=1, source_target_pairs={{0,24},{8,0},{16,8},{24,16},{1,25},{9,1},{17,9},{25,17},{2,26},{10... | collective-permute-start | bytes 589832 | tf_op jit(solution)/shard_map/ppermute | solution.py:50
  399.5 20.1 %collective-permute-start.76 = (bf16[48,2048]{1,0:T(8,128)(2,1)}, bf16[48,2048]{1,0:T(8,128)(2,1)}, u32[]{:S(2)}, u32[]{:S(2)}) collective-permute-start(bf16[48,2048]{1,0:T(8,128)(2,1)} %get-tuple-element.221), channel_id=1, source_target_pairs={{0,16},{8,24},{16,0},{24,8},{1,17},{9,25},{17,1},{25,9},{2,18},{10... | collective-permute-start | bytes 589832 | tf_op jit(solution)/shard_map/ppermute | solution.py:50
  403.7 15.8 %collective-permute-start.77 = (bf16[48,2048]{1,0:T(8,128)(2,1)}, bf16[48,2048]{1,0:T(8,128)(2,1)S(1)}, u32[]{:S(2)}, u32[]{:S(2)}) collective-permute-start(bf16[48,2048]{1,0:T(8,128)(2,1)} %get-tuple-element.220), channel_id=1, source_target_pairs={{0,8},{8,16},{16,24},{24,0},{1,9},{9,17},{17,25},{25,1},{2,10},{10... | collective-permute-start | bytes 589832 | tf_op jit(solution)/shard_map/ppermute | solution.py:50
  (92 other events, 865.9 us)
Sparse Core Ops, SparseCore 0:
  11.6 123.4 all-gather.1
  281.3 99.5 reduce-scatter.1

commit v4 on v3

--- a/solution.py
+++ b/solution.py
@@ -137,6 +137,7 @@
             grid = [[grid[i][j] for i in range(len(grid))] for j in range(len(grid[0]))]
         else:
             grid = [rotations(item, "x") for item in rotations(block, "y")]
+            grid = [list(column) for column in zip(*grid)]
         result.append([item for line in grid for item in line])
     return result
 
@@ -151,24 +152,27 @@
     return total
 
 
-def token_scatter(parts, between=None):
-    across, along = lax.axis_size("x"), lax.axis_size("y")
-    lines, first, second = [], [], []
-    for number, blocks in reversed(list(enumerate(parts))):
-        grid = [blocks[j * across : (j + 1) * across] for j in range(along)]
-        axis = "y" if number % 2 == 0 else "x"
-        if number % 2 == 0:
-            grid = [list(column) for column in zip(*grid)]
-        lines.append([add_back(line, axis, log=first) for line in grid])
-    early = between(first) if between else ()
-    for number, sums in enumerate(lines):
-        axis = "x" if (len(parts) - 1 - number) % 2 == 0 else "y"
-        lines[number] = add_back(sums, axis, early, log=second)
-    lines = lines[::-1]
-    last = lines.pop()
-    sent = low(last)
-    sent = shift(sent, "zh", -len(lines))
-    return lines + [last], add_back(lines, "zh"), sent, first, second
+def slabs_back(value, axis, early=(), log=None):
+    size = value.shape[0] // lax.axis_size(axis)
+    slabs = [value[first : first + size] for first in range(0, value.shape[0], size)]
+    return add_back(slabs, axis, early, log)
+
+
+def scatter_first(parts, early=()):
+    log = []
+    order = reversed(list(enumerate(parts)))
+    lines = [
+        slabs_back(part, "yx"[number % 2], () if number else early, log) for number, part in order
+    ]
+    return lines[::-1], log
+
+
+def scatter_second(lines, early):
+    return [slabs_back(line, "xy"[number % 2], early) for number, line in enumerate(lines)]
+
+
+def scatter_last(lines):
+    return add_back(lines[:-1], "zh"), shift(low(lines[-1]), "zh", 1 - len(lines))
 
 
 VMEM_BYTES = 56 * 2**20
@@ -551,16 +555,17 @@
     left = jnp.concatenate([ref[...] for ref in refs[:size]], axis=0)
     rights = refs[size : 2 * size]
     right = jnp.concatenate([ref[:count, :] for ref in rights], axis=0)
-    kept_ref, vector_ref, sent_ref = refs[2 * size :]
-    half = kept_ref.shape[0]
+    kept_ref, sent_ref = refs[2 * size :]
     gains = sum(wide(ref[count:, :]) for ref in rights)
     bias = jnp.sum(wide(right), axis=0, keepdims=True)
-    vector = jnp.concatenate([gains[:2], bias, jnp.zeros((13, QKV), jnp.float32)], axis=0)
-    vector_ref[...] = vector[:8]
-    sent_ref[half:, :] = low(vector)
+    vector = jnp.concatenate([gains[:2], bias, jnp.zeros((5, QKV), jnp.float32)], axis=0)
     total = dot(left, right, 0, 0)
-    kept_ref[...] = total[:half]
-    sent_ref[:half, :] = low(total[half:])
+    depth, width = kept_ref.shape[0], kept_ref.shape[1] - 8
+    for slot in range(depth):
+        first, second = slot * width, (depth + slot) * width
+        kept_ref[slot, :width, :] = total[first : first + width]
+        kept_ref[slot, width:, :] = vector
+        sent_ref[slot] = low(jnp.concatenate([total[second : second + width], vector], axis=0))
 
 
 def dp_scatter(total, early=(), log=None):
@@ -585,22 +590,14 @@
     return (gain_one, gain_two, jnp.concatenate([query_bias, key_bias, value_bias]))
 
 
-def pack_small(gain_one, gain_two, bias):
-    gain_cols = D // KW
-    group = HEADS // KV_HEADS
-    query_part = jnp.transpose(bias[:QW].reshape(KV_HEADS, group, HEAD_DIM), (0, 2, 1)).reshape(
-        KW, group
-    )
-    return jnp.concatenate(
-        [
-            gain_one.reshape(KW, gain_cols),
-            gain_two.reshape(KW, gain_cols),
-            query_part,
-            bias[QW : QW + KW][:, None],
-            bias[QW + KW :][:, None],
-        ],
-        axis=1,
-    )
+def own_small(vector, first, rows):
+    group, width = HEADS // KV_HEADS, D // KW
+    cut = lambda row, start, size: lax.dynamic_slice(vector, (row, start), (1, size))
+    gains = [cut(row, first * width, rows * width).reshape(rows, width) for row in (0, 1)]
+    head, place = first // HEAD_DIM * group * HEAD_DIM, first % HEAD_DIM
+    queries = [cut(2, head + j * HEAD_DIM + place, rows) for j in range(group)]
+    keys = [cut(2, start + first, rows) for start in (QW, QW + KW)]
+    return jnp.concatenate(gains + [jnp.concatenate(queries + keys, axis=0).T], axis=1)
 
 
 def layout(starts_row, places):
@@ -760,17 +757,12 @@
         up_grad = low(pulled * active)
         unit_parts.append((gate_grad, up_grad, low(active * up)))
         grad_terms.append(by_token(gate_grad, units_all[0]) + by_token(up_grad, units_all[1]))
-    branch_terms = []
-
-    def between(received):
-        branch_terms.extend(
-            cut(low(by_token(after(part[2], received[0]), units_all[2]))) for part in unit_parts
-        )
-        return sum(branch_terms, [])
-
-    plane_sums, normed_grad_own, normed_grad_received, *unused = token_scatter(
-        [cut(item) for item in grad_terms], between
-    )
+    branch_terms = [
+        low(by_token(after(part[2], *grad_terms), units_all[2])) for part in unit_parts
+    ]
+    first_sums, received = scatter_first(grad_terms, branch_terms)
+    plane_sums = scatter_second(first_sums, ())
+    normed_grad_own, normed_grad_received = scatter_last(plane_sums)
     parts = [unit_parts[0][:2] + (after(unit_parts[0][2], *plane_sums),)] + unit_parts[1:]
     units_term = units_gradient(
         parts,
@@ -778,10 +770,9 @@
         [block for blocks in back_blocks for block in blocks],
     )
     units_sum = lax.psum_scatter(units_term, sharing, scatter_dimension=0, tiled=True)
-    branch_terms = [[after(item, *plane_sums) for item in blocks] for blocks in branch_terms]
-    unused, branch_own, branch_received, branch_first, branch_second = token_scatter(branch_terms)
-    block_output = low(middle + branch_own + wide(branch_received))
-
+    branch_sums, branch_first = scatter_first(
+        [after(item, *plane_sums) for item in branch_terms]
+    )
     middle_grad, branch_grad, gain_two_grad, attended_grad = call_with_pieces(
         middle_back_kernel,
         out_projection,
@@ -824,7 +815,10 @@
         4,
     )
     mixed_pieces = plane_blocks(mixed_block)
-    attended_owned[0] = after(attended_owned[0], mixed_block, *branch_first)
+    branch_sums = scatter_second(branch_sums, [mixed_block])
+    branch_own, branch_received = scatter_last(branch_sums)
+    block_output = low(middle + branch_own + wide(branch_received))
+    attended_owned[0] = after(attended_owned[0], mixed_block)
     half = attended_owned[0].shape[1] // 2
     kept, sent = local_call(
         lambda *refs: weight_kernel(len(steps), *refs),
@@ -834,25 +828,22 @@
         3,
     )
     outer_sum = kept + wide(shift(sent, "c", -1))
-    normed_owned[0] = after(normed_owned[0], *branch_second)
-    kept, kept_vector, sent = local_call(
+    depth = lax.axis_size(DP)
+    shape = (depth, half // depth + 8, QKV)
+    kept, sent = local_call(
         lambda *refs: joined_kernel(len(steps), *refs),
         normed_owned + mixed_pieces,
-        [
-            shaped((half, QKV), jnp.float32),
-            shaped((8, QKV), jnp.float32),
-            shaped((half + 16, QKV), jnp.bfloat16),
-        ],
+        [shaped(shape, jnp.float32), shaped(shape, jnp.bfloat16)],
         "joined_weights",
         5,
     )
     got = shift(sent, "c", -1)
     units_new = units_step(units_sum, units_weight, units_first, units_second)
     outer_grad = dp_scatter(outer_sum, [units_new[3]])
-    joined_grad = dp_scatter(kept + wide(got[:half]), [units_new[3]])
-    vector = sum(rotations(kept_vector + wide(got[half : half + 8]), DP))
-    small_grad = pack_small(vector[0, :D], vector[1, :D], vector[2])
-    small_grad = lax.dynamic_slice_in_dim(small_grad, device * small_rows, small_rows, 0)
+    total = kept + wide(got)
+    total = add_back([total[i] for i in range(depth)], DP, [units_new[3]])
+    joined_grad, vector = total[:-8], total[-8:]
+    small_grad = own_small(vector, device * small_rows, small_rows)
 
     joined = optimizer_step(
         joined_weight, joined_grad, joined_first, joined_second, 2.0 / math.sqrt(D), DECAY

time: 439 us -> 432 us (0.984)
  the two profiles are of different devices: /device:TPU:0 before, /device:TPU:7 now
where the time goes in v4:
time: 432 us; the launch traced here: 425 us
  waiting for transfers between devices  142 us (33%)
  starting transfers between devices  94 us (22%)
  Pallas kernels  87.3 us (20%)
  matrix products  36.5 us (8%)
  local copies, waits for them, and re-layouts  25 us (6%)
  other arithmetic  24.4 us (6%)
  between operations  15.9 us (4%)
    ppermute x64, waiting for transfers between devices, shift(): lax.ppermute(value, axis, [(i, (i + step) % count) for i in range(count)])  102 us
    ppermute x64, starting transfers between devices, shift(): lax.ppermute(value, axis, [(i, (i + step) % count) for i in range(count)])  80.3 us
    pallas_call x4, Pallas kernels, call_with_pieces(): pl.pallas_call(run, out_shape=outs, in_specs=[SCALARS] + [pl.BlockSpec(me...  31.9 us
    ppermute x15, waiting for transfers between devices, plane_shift(): return lax.ppermute(value, ('y', 'x'), pairs)  30.5 us
    pallas_call x4, Pallas kernels, local_call(): pl.pallas_call(kernel, out_shape=outs, scratch_shapes=list(scratch), comp...  25 us
    dot_general x6, matrix products, body(): jnp.einsum('ud,td->ut', rows, tokens, preferred_element_type=jnp.float32)  18.6 us
    pallas_call x1, Pallas kernels, units_gradient(): pl.pallas_call(lambda *refs: gradient_kernel(len(parts), size, *refs), gr...  16.3 us
    pallas_call x1, Pallas kernels, units_step(): pl.pallas_call(units_step_kernel, grid=(6,), in_specs=[pl.BlockSpec((unit...  14.3 us
  transfers between devices with their start and end apart: 81, of which 29 were waited for; matrix products, arithmetic and copies ran while one was open for 11% of the time, Pallas kernels for 21%

profile of v4, /device:TPU:7, one launch (start us, length us, event | category | flops | bytes accessed | tf_op | source)
XLA Modules:
  0.0 424.8 jit_solution(10318056269271790532)
XLA Ops:
  7.2 4.3 %convert_element_type.166 = bf16[280,3,1536]{2,0,1:T(8,128)(2,1)} convert(f32[280,3,1536]{2,0,1:T(8,128)} %param.20) | non-fusion elementwise | flops 1290240 | bytes 7741440 | tf_op jit(solution)/shard_map/convert_element_type | solution.py:37
  13.9 2.3 collective-permute-start.5
  21.4 2.4 collective-permute-start.7
  27.4 7.7 %collective-permute-done.11 = bf16[48,2048]{1,0:T(8,128)(2,1)S(1)} collective-permute-done((bf16[48,2048]{1,0:T(8,128)(2,1)S(1)}, bf16[48,2048]{1,0:T(8,128)(2,1)S(1)}, u32[]{:S(2)}, u32[]{:S(2)}) %collective-permute-start.11) | collective-permute-done | bytes 196640 | tf_op jit(solution)/shard_map/ppermute | solution.py:50
  40.0 3.1 collective-permute-start.1
  43.6 7.3 %collective-permute-done.9 = f32[1,5120]{1,0:T(1,128)S(1)} collective-permute-done((f32[1,5120]{1,0:T(1,128)S(1)}, f32[1,5120]{1,0:T(1,128)S(1)}, u32[]{:S(2)}, u32[]{:S(2)}) %collective-permute-start.9) | collective-permute-done | bytes 20512 | tf_op jit(solution)/shard_map/ppermute | solution.py:50
  51.0 4.3 %collective-permute-start.29 = (bf16[48,1536]{1,0:T(8,128)(2,1)S(1)}, bf16[48,1536]{1,0:T(8,128)(2,1)}, u32[]{:S(2)}, u32[]{:S(2)}) collective-permute-start(bf16[48,1536]{1,0:T(8,128)(2,1)S(1)} %convert_element_type.165), channel_id=1, source_target_pairs={{0,8},{8,16},{16,24},{24,0},{1,9},{9,17},{17,25},{25,1},{2,10},{10... | collective-permute-start | bytes 442376 | tf_op jit(solution)/shard_map/ppermute | solution.py:50
  55.8 11.6 %collective-permute-done.29 = bf16[48,1536]{1,0:T(8,128)(2,1)} collective-permute-done((bf16[48,1536]{1,0:T(8,128)(2,1)S(1)}, bf16[48,1536]{1,0:T(8,128)(2,1)}, u32[]{:S(2)}, u32[]{:S(2)}) %collective-permute-start.29) | collective-permute-done | bytes 147488 | tf_op jit(solution)/shard_map/ppermute | solution.py:50
  67.4 4.5 %collective-permute-start.19 = (bf16[4,48,2048]{2,1,0:T(8,128)(2,1)S(1)}, bf16[4,48,2048]{2,1,0:T(8,128)(2,1)}, u32[]{:S(2)}, u32[]{:S(2)}) collective-permute-start(bf16[4,48,2048]{2,1,0:T(8,128)(2,1)S(1)} %pad_maximum_fusion.refs_6_.refs_2_), channel_id=1, source_target_pairs={{0,1},{1,0},{2,3},{3,2},{4,5},{5,4},{6,7},{7,6},{8,9},{9,8},{10,11... | collective-permute-start | bytes 2359304 | tf_op jit(solution)/shard_map/ppermute | solution.py:50
  73.3 4.0 collective-permute-start.31
  77.6 2.2 collective-permute-done.30
  81.0 5.1 %collective-permute-done.31 = bf16[48,1536]{1,0:T(8,128)(2,1)S(1)} collective-permute-done((bf16[48,1536]{1,0:T(8,128)(2,1)S(1)}, bf16[48,1536]{1,0:T(8,128)(2,1)S(1)}, u32[]{:S(2)}, u32[]{:S(2)}) %collective-permute-start.31) | collective-permute-done | bytes 147488 | tf_op jit(solution)/shard_map/ppermute | solution.py:50
  92.1 3.6 collective-permute-done.18.refs_10_.refs_6_
  95.7 1.9 collective-permute-start.23
  100.3 6.1 %front.1 = (bf16[128,1536]{1,0:T(8,128)(2,1)}, bf16[128,1536]{1,0:T(8,128)(2,1)}, bf16[128,512]{1,0:T(8,128)(2,1)}) custom-call(s32[40]{0:T(128)} %stack.220.refs_0_, bf16[128,1536]{1,0:T(8,128)(2,1)} %refs_9_.1, f32[1,1536]{1,0:T(1,128)} %get-tuple-element.231.refs_2_.refs_10_, f32[1,2048]{1,0:T(1,128)} %slice.283.refs_3_, ...), custom_call_target="tpu_custom_call" | custom-call | flops 1650000000 | tf_op jit(solution)/shard_map/front/pallas_call | solution.py:245
  110.1 6.0 %collective-permute-done.25 = bf16[128,512]{1,0:T(8,128)(2,1)S(1)} collective-permute-done((bf16[128,512]{1,0:T(8,128)(2,1)}, bf16[128,512]{1,0:T(8,128)(2,1)S(1)}, u32[]{:S(2)}, u32[]{:S(2)}) %collective-permute-start.25) | collective-permute-done | bytes 131104 | tf_op jit(solution)/shard_map/ppermute | solution.py:68
  116.6 3.1 collective-permute-done.27
  119.7 1.7 pad_maximum_fusion.2
  123.8 3.5 collective-permute-done.24.refs_21_
  128.6 5.0 %collective-permute-done.35.refs_11_.refs_10_ = bf16[4,48,768]{2,1,0:T(8,128)(2,1)S(1)} collective-permute-done((bf16[4,48,768]{2,1,0:T(8,128)(2,1)S(1)}, bf16[4,48,768]{2,1,0:T(8,128)(2,1)S(1)}, u32[]{:S(2)}, u32[]{:S(2)}) %collective-permute-start.35) | collective-permute-done | bytes 294944 | tf_op jit(solution)/shard_map/ppermute | solution.py:50
  140.0 11.4 %attend.1 = (bf16[128,1536]{1,0:T(8,128)(2,1)}, f32[128,1536]{1,0:T(8,128)}, bf16[128,1536]{1,0:T(8,128)(2,1)}) custom-call(s32[40]{0:T(128)} %stack.220.refs_0_, bf16[128,1536]{1,0:T(8,128)(2,1)} %get-tuple-element.77.refs_1_.query_ref, bf16[1024,512]{1,0:T(8,128)(2,1)} %copy-done.60, s32[1024,2]{1,0:T(8,128)} %copy.77.refs_3_.key_marks_ref, ...), custom_call_target="tpu_custom_call" | custom-call | flops 3300000000 | tf_op jit(solution)/shard_map/attend/pallas_call | solution.py:245
  151.4 5.1 %collective-permute-start.44 = (bf16[128,1536]{1,0:T(8,128)(2,1)}, bf16[128,1536]{1,0:T(8,128)(2,1)S(1)}, u32[]{:S(2)}, u32[]{:S(2)}) collective-permute-start(bf16[128,1536]{1,0:T(8,128)(2,1)} %get-tuple-element.84.refs_6_), channel_id=1, source_target_pairs={{0,16},{16,0},{1,17},{17,1},{2,18},{18,2},{3,19},{19,3},{4,20},{20... | collective-permute-start | bytes 1179656 | tf_op jit(solution)/shard_map/ppermute | solution.py:50
  158.0 2.1 fusion.4
  160.1 2.1 fusion.5
  165.6 6.7 %collective-permute-done.47 = bf16[128,768]{1,0:T(8,128)(2,1)S(1)} collective-permute-done((bf16[128,768]{1,0:T(8,128)(2,1)S(1)}, bf16[128,768]{1,0:T(8,128)(2,1)S(1)}, u32[]{:S(2)}, u32[]{:S(2)}) %collective-permute-start.47) | collective-permute-done | bytes 196640 | tf_op jit(solution)/shard_map/ppermute | solution.py:68
  173.2 2.4 collective-permute-done.46
  180.0 6.7 %collective-permute-done.48.refs_11_ = bf16[128,1536]{1,0:T(8,128)(2,1)S(1)} collective-permute-done((bf16[128,1536]{1,0:T(8,128)(2,1)S(1)}, bf16[128,1536]{1,0:T(8,128)(2,1)S(1)}, u32[]{:S(2)}, u32[]{:S(2)}) %collective-permute-start.48) | collective-permute-done | bytes 393248 | tf_op jit(solution)/shard_map/ppermute | solution.py:50
  186.9 8.1 %collective-permute-done.43.refs_9_ = bf16[128,1536]{1,0:T(8,128)(2,1)S(1)} collective-permute-done((bf16[128,1536]{1,0:T(8,128)(2,1)S(1)}, bf16[128,1536]{1,0:T(8,128)(2,1)S(1)}, u32[]{:S(2)}, u32[]{:S(2)}) %collective-permute-start.43) | collective-permute-done | bytes 393248 | tf_op jit(solution)/shard_map/ppermute | solution.py:50
  196.7 4.1 convolution_bitcast_fusion.4
  201.6 2.0 convolution_bitcast_fusion.5
  203.6 2.0 convolution_bitcast_fusion
  205.7 3.2 convolution_bitcast_fusion.2
  208.9 3.2 multiply_convert_fusion
  212.2 2.3 fusion.8
  214.5 2.3 convolution_add_fusion
  217.1 4.0 multiply_convert_fusion.3
  221.2 2.2 fusion.9
  223.5 2.2 convolution_add_fusion.1
  225.7 2.3 convolution_convert_fusion
  229.6 2.5 convolution_convert_fusion.1
  232.5 10.2 %collective-permute-done.51 = bf16[256,1536]{1,0:T(8,128)(2,1)S(1)} collective-permute-done((bf16[256,1536]{1,0:T(8,128)(2,1)S(1)}, bf16[256,1536]{1,0:T(8,128)(2,1)S(1)}, u32[]{:S(2)}, u32[]{:S(2)}) %collective-permute-start.51) | collective-permute-done | bytes 786464 | tf_op jit(solution)/shard_map/ppermute | solution.py:50
  244.1 7.0 %collective-permute-done.54 = bf16[128,1536]{1,0:T(8,128)(2,1)S(1)} collective-permute-done((bf16[128,1536]{1,0:T(8,128)(2,1)S(1)}, bf16[128,1536]{1,0:T(8,128)(2,1)S(1)}, u32[]{:S(2)}, u32[]{:S(2)}) %collective-permute-start.54) | collective-permute-done | bytes 393248 | tf_op jit(solution)/shard_map/ppermute | solution.py:50
  253.8 16.3 %units_gradient.1 = bf16[1120,4608]{1,0:T(8,128)(2,1)} custom-call(bf16[1120,512]{1,0:T(8,128)(2,1)} %copy-done.4, bf16[1120,512]{1,0:T(8,128)(2,1)} %copy-done.3, bf16[1120,512]{1,0:T(8,128)(2,1)} %copy-done.35, bf16[1120,512]{1,0:T(8,128)(2,1)} %copy-done.1, bf16[1120,512]{1,0:T(8,128)(2,1)} %copy-done.2, bf16[1120,512]{1,0:T(8,128)(2,1)} %copy-done.34, ...), custom_call_target="tpu_custom_call" | custom-call | flops 2200000000 | tf_op jit(solution)/shard_map/units_gradient/pallas_call | solution.py:498
  273.5 6.8 %middle_back.1 = (f32[128,1536]{1,0:T(8,128)}, bf16[128,1536]{1,0:T(8,128)(2,1)}, f32[1,1536]{1,0:T(1,128)}, bf16[128,1536]{1,0:T(8,128)(2,1)}) custom-call(s32[40]{0:T(128)} %stack.220.refs_0_, f32[128,1536]{1,0:T(8,128)} %slice_add_fusion.5.refs_1_, bf16[128,1536]{1,0:T(8,128)(2,1)} %collective-permute-done.57.refs_2_, ...), custom_call_target="tpu_custom_call" | custom-call | flops 1100000000 | tf_op jit(solution)/shard_map/middle_back/pallas_call | solution.py:245
  283.0 12.8 %attend_back.1 = (bf16[128,1536]{1,0:T(8,128)(2,1)}, f32[1024,512]{1,0:T(8,128)}) custom-call(bf16[128,1536]{1,0:T(8,128)(2,1)} %get-tuple-element.93.attended_grad_ref, bf16[128,1536]{1,0:T(8,128)(2,1)} %get-tuple-element.77.refs_1_.query_ref, bf16[1024,512]{1,0:T(8,128)(2,1)} %copy-done.60, s32[1024,2]{1,0:T(8,128)} %copy.77.refs_3_.key_marks_ref, ...), custom_call_target="tpu_custom_call" | custom-call | flops 219999993856 | tf_op jit(solution)/shard_map/attend_back/pallas_call | solution.py:263
  297.3 10.2 %collective-permute-start.60 = (bf16[512,512]{1,0:T(8,128)(2,1)S(1)}, bf16[512,512]{1,0:T(8,128)(2,1)S(1)}, u32[]{:S(2)}, u32[]{:S(2)}) collective-permute-start(bf16[512,512]{1,0:T(8,128)(2,1)S(1)} %slice.400), channel_id=1, source_target_pairs={{0,1},{1,0},{2,3},{3,2},{4,5},{5,4},{6,7},{7,6},{8,9},{9,8},{10,11... | collective-permute-start | bytes 1572872 | tf_op jit(solution)/shard_map/ppermute | solution.py:50
  314.6 7.6 %query_back.1 = (f32[128,1536]{1,0:T(8,128)}, bf16[1536,512]{1,0:T(8,128)(2,1)}) custom-call(s32[40]{0:T(128)} %stack.220.refs_0_, bf16[128,1536]{1,0:T(8,128)(2,1)} %get-tuple-element.98.refs_1_.refs_6_, bf16[4,48,2048]{2,1,0:T(8,128)(2,1)} %copy-done.7, bf16[4,48,2048]{2,1,0:T(8,128)(2,1)} %copy-done.12, bf16[4,48,2048]{2,1,0:T(8,128)(2,1)} %copy-done.13, ...), custom_call_target="tpu_custom_call" | custom-call | flops 1924999936 | tf_op jit(solution)/shard_map/query_back/pallas_call | solution.py:245
  323.5 3.4 collective-permute-done.62.refs_2_
  327.6 4.4 %finish.1 = (bf16[144,2048]{1,0:T(8,128)(2,1)}, f32[128,1536]{1,0:T(8,128)}) custom-call(f32[128,512]{1,0:T(8,128)} %slice.319.refs_0_, bf16[128,512]{1,0:T(8,128)(2,1)} %copy-done.55, bf16[128,512]{1,0:T(8,128)(2,1)} %copy-done.56, bf16[128,512]{1,0:T(8,128)(2,1)} %copy-done.57, f32[128,128]{1,0:T(8,128)} %get-tuple-element.229.refs_4_.cosine_ref, ...), custom_call_target="tpu_custom_call" | custom-call | flops 1100000000 | tf_op jit(solution)/shard_map/finish/pallas_call | solution.py:263
  332.1 2.1 collective-permute-start.66
  334.7 2.2 collective-permute-start.69
  336.9 3.5 out_weights.1
  342.1 9.3 %collective-permute-done.66 = bf16[128,1536]{1,0:T(8,128)(2,1)S(1)} collective-permute-done((bf16[128,1536]{1,0:T(8,128)(2,1)S(1)}, bf16[128,1536]{1,0:T(8,128)(2,1)S(1)}, u32[]{:S(2)}, u32[]{:S(2)}) %collective-permute-start.66) | collective-permute-done | bytes 393248 | tf_op jit(solution)/shard_map/ppermute | solution.py:50
  351.4 1.9 fusion.27
  353.3 7.7 %collective-permute-done.69.refs_7_ = bf16[144,2048]{1,0:T(8,128)(2,1)S(1)} collective-permute-done((bf16[144,2048]{1,0:T(8,128)(2,1)}, bf16[144,2048]{1,0:T(8,128)(2,1)S(1)}, u32[]{:S(2)}, u32[]{:S(2)}) %collective-permute-start.69) | collective-permute-done | bytes 589856 | tf_op jit(solution)/shard_map/ppermute | solution.py:68
  361.9 4.3 %joined_weights.1 = (f32[4,56,2048]{2,1,0:T(8,128)}, bf16[4,56,2048]{2,1,0:T(8,128)(2,1)}) custom-call(bf16[128,384]{1,0:T(8,128)(2,1)} %get-tuple-element.232.refs_0_, bf16[128,384]{1,0:T(8,128)(2,1)} %get-tuple-element.214.refs_1_, bf16[128,384]{1,0:T(8,128)(2,1)} %get-tuple-element.212.refs_2_, bf16[128,384]{1,0:T(8,128)(2,1)} %get-tuple-element.210.refs_3_, ...), custom_call_target="tpu_custom_call" | custom-call | flops 1375000064 | tf_op jit(solution)/shard_map/joined_weights/pallas_call | solution.py:263
  366.2 2.7 collective-permute-start.70
  372.3 2.2 collective-permute-start.71
  375.0 8.9 %reduce-scatter.2.cloned.1.call-done.grad_ref = bf16[280,4608]{1,0:T(8,128)(2,1)} async-done(((bf16[1120,4608]{1,0:T(8,128)(2,1)}), bf16[280,4608]{1,0:T(8,128)(2,1)}) %reduce-scatter.2.cloned.1.call-update) | async-done | bytes 2580496 | tf_op jit(solution)/shard_map/reduce_scatter | solution.py:772
  383.9 14.3 %units_step.1 = (f32[3,280,1536]{2,1,0:T(8,128)}, f32[3,280,1536]{2,1,0:T(8,128)}, f32[3,280,1536]{2,1,0:T(8,128)}, bf16[3,280,1536]{2,1,0:T(8,128)(2,1)}) custom-call(bf16[280,4608]{1,0:T(8,128)(2,1)} %reduce-scatter.2.cloned.1.call-done.grad_ref, f32[3,280,1536]{2,1,0:T(8,128)} %bitcast.138, f32[3,280,1536]{2,1,0:T(8,128)} %bitcast.151, ...), custom_call_target="tpu_custom_call" | custom-call | flops 3300000000 | tf_op jit(solution)/shard_map/units_step/pallas_call | solution.py:530
  398.2 2.7 collective-permute-done.72
  403.4 8.7 %collective-permute-done.78 = bf16[48,1536]{1,0:T(8,128)(2,1)} collective-permute-done((bf16[48,1536]{1,0:T(8,128)(2,1)S(1)}, bf16[48,1536]{1,0:T(8,128)(2,1)}, u32[]{:S(2)}, u32[]{:S(2)}) %collective-permute-start.78) | collective-permute-done | bytes 147488 | tf_op jit(solution)/shard_map/ppermute | solution.py:50
  412.1 2.5 fusion.76
  415.3 2.2 fusion.73
  (390 shorter events, 88.6 us)
Async XLA Ops:
  7.2 189.5 %all-gather.2.cloned.1.call-start = ((), (), s32[]{:S(2)}) async-start(), calls=%async_computation.1 | async-start | bytes 12902400 | tf_op jit(solution)/shard_map/all_gather | solution.py:693
  11.5 372.3 %reduce-scatter.2.cloned.1.call-start = ((), (), s32[]{:S(2)}) async-start(), calls=%async_computation.2 | async-start | bytes 12902400 | tf_op jit(solution)/shard_map/reduce_scatter | solution.py:772
  17.5 9.8 %collective-permute-start.10 = (bf16[48,2048]{1,0:T(8,128)(2,1)S(1)}, bf16[48,2048]{1,0:T(8,128)(2,1)S(1)}, u32[]{:S(2)}, u32[]{:S(2)}) collective-permute-start(bf16[48,2048]{1,0:T(8,128)(2,1)S(1)} %convert_element_type.160), channel_id=1, source_target_pairs={{0,8},{8,16},{16,24},{24,0},{1,9},{9,17},{17,25},{25,1},{2,10},{10... | collective-permute-start | bytes 589832 | tf_op jit(solution)/shard_map/ppermute | solution.py:50
  20.5 14.6 %collective-permute-start.11 = (bf16[48,2048]{1,0:T(8,128)(2,1)S(1)}, bf16[48,2048]{1,0:T(8,128)(2,1)S(1)}, u32[]{:S(2)}, u32[]{:S(2)}) collective-permute-start(bf16[48,2048]{1,0:T(8,128)(2,1)S(1)} %convert_element_type.160), channel_id=1, source_target_pairs={{0,16},{8,24},{16,0},{24,8},{1,17},{9,25},{17,1},{25,9},{2,18},{10... | collective-permute-start | bytes 589832 | tf_op jit(solution)/shard_map/ppermute | solution.py:50
  21.0 14.2 %collective-permute-start.12 = (bf16[128,1536]{1,0:T(8,128)(2,1)S(1)}, bf16[128,1536]{1,0:T(8,128)(2,1)S(1)}, u32[]{:S(2)}, u32[]{:S(2)}) collective-permute-start(bf16[128,1536]{1,0:T(8,128)(2,1)S(1)} %copy-done.26), channel_id=1, source_target_pairs={{0,2},{2,0},{1,3},{3,1},{4,6},{6,4},{5,7},{7,5},{8,10},{10,8},{9,1... | collective-permute-start | bytes 1179656 | tf_op jit(solution)/shard_map/ppermute | solution.py:50
  24.6 11.4 %collective-permute-start.13 = (bf16[128,1536]{1,0:T(8,128)(2,1)S(1)}, bf16[128,1536]{1,0:T(8,128)(2,1)}, u32[]{:S(2)}, u32[]{:S(2)}) collective-permute-start(bf16[128,1536]{1,0:T(8,128)(2,1)S(1)} %copy-done.26), channel_id=1, source_target_pairs={{0,4},{4,0},{1,5},{5,1},{2,6},{6,2},{3,7},{7,3},{8,12},{12,8},{9,1... | collective-permute-start | bytes 1179656 | tf_op jit(solution)/shard_map/ppermute | solution.py:50
  24.7 12.8 %collective-permute-start.8 = (f32[1,5120]{1,0:T(1,128)S(1)}, f32[1,5120]{1,0:T(1,128)S(1)}, u32[]{:S(2)}, u32[]{:S(2)}) collective-permute-start(f32[1,5120]{1,0:T(1,128)S(1)} %add.886), channel_id=1, source_target_pairs={{0,2},{2,0},{1,3},{3,1},{4,6},{6,4},{5,7},{7,5},{8,10},{10,8},{9,1... | collective-permute-start | bytes 61448 | tf_op jit(solution)/shard_map/ppermute | solution.py:50
  36.0 37.2 %collective-permute-start.14 = (bf16[4,48,2048]{2,1,0:T(8,128)(2,1)S(1)}, bf16[4,48,2048]{2,1,0:T(8,128)(2,1)S(1)}, u32[]{:S(2)}, u32[]{:S(2)}) collective-permute-start(bf16[4,48,2048]{2,1,0:T(8,128)(2,1)S(1)} %pad_maximum_fusion.refs_6_.refs_2_), channel_id=1, source_target_pairs={{0,2},{2,0},{1,3},{3,1},{4,6},{6,4},{5,7},{7,5},{8,10},{10,8},{9,1... | collective-permute-start | bytes 2359304 | tf_op jit(solution)/shard_map/ppermute | solution.py:50
  36.4 36.8 %collective-permute-start.15 = (bf16[4,48,2048]{2,1,0:T(8,128)(2,1)S(1)}, bf16[4,48,2048]{2,1,0:T(8,128)(2,1)S(1)}, u32[]{:S(2)}, u32[]{:S(2)}) collective-permute-start(bf16[4,48,2048]{2,1,0:T(8,128)(2,1)S(1)} %pad_maximum_fusion.refs_6_.refs_2_), channel_id=1, source_target_pairs={{0,4},{4,0},{1,5},{5,1},{2,6},{6,2},{3,7},{7,3},{8,12},{12,8},{9,1... | collective-permute-start | bytes 2359304 | tf_op jit(solution)/shard_map/ppermute | solution.py:50
  37.5 13.3 %collective-permute-start.9 = (f32[1,5120]{1,0:T(1,128)S(1)}, f32[1,5120]{1,0:T(1,128)S(1)}, u32[]{:S(2)}, u32[]{:S(2)}) collective-permute-start(f32[1,5120]{1,0:T(1,128)S(1)} %add.887), channel_id=1, source_target_pairs={{0,4},{4,0},{1,5},{5,1},{2,6},{6,2},{3,7},{7,3},{8,12},{12,8},{9,1... | collective-permute-start | bytes 61448 | tf_op jit(solution)/shard_map/ppermute | solution.py:50
  40.0 31.9 %collective-permute-start.1 = (bf16[128,1536]{1,0:T(8,128)(2,1)S(1)}, bf16[128,1536]{1,0:T(8,128)(2,1)}, u32[]{:S(2)}, u32[]{:S(2)}) collective-permute-start(bf16[128,1536]{1,0:T(8,128)(2,1)S(1)} %copy-done.26), channel_id=1, source_target_pairs={{0,16},{16,0},{1,17},{17,1},{2,18},{18,2},{3,19},{19,3},{4,20},{20... | collective-permute-start | bytes 1179656 | tf_op jit(solution)/shard_map/ppermute | solution.py:50
  43.1 29.1 %collective-permute-start.16 = (bf16[128,1536]{1,0:T(8,128)(2,1)}, bf16[128,1536]{1,0:T(8,128)(2,1)}, u32[]{:S(2)}, u32[]{:S(2)}) collective-permute-start(bf16[128,1536]{1,0:T(8,128)(2,1)} %copy-done.45), channel_id=1, source_target_pairs={{0,4},{4,0},{1,5},{5,1},{2,6},{6,2},{3,7},{7,3},{8,12},{12,8},{9,1... | collective-permute-start | bytes 1179656 | tf_op jit(solution)/shard_map/ppermute | solution.py:50
  51.0 16.4 %collective-permute-start.29 = (bf16[48,1536]{1,0:T(8,128)(2,1)S(1)}, bf16[48,1536]{1,0:T(8,128)(2,1)}, u32[]{:S(2)}, u32[]{:S(2)}) collective-permute-start(bf16[48,1536]{1,0:T(8,128)(2,1)S(1)} %convert_element_type.165), channel_id=1, source_target_pairs={{0,8},{8,16},{16,24},{24,0},{1,9},{9,17},{17,25},{25,1},{2,10},{10... | collective-permute-start | bytes 442376 | tf_op jit(solution)/shard_map/ppermute | solution.py:50
  67.4 22.5 %collective-permute-start.19 = (bf16[4,48,2048]{2,1,0:T(8,128)(2,1)S(1)}, bf16[4,48,2048]{2,1,0:T(8,128)(2,1)}, u32[]{:S(2)}, u32[]{:S(2)}) collective-permute-start(bf16[4,48,2048]{2,1,0:T(8,128)(2,1)S(1)} %pad_maximum_fusion.refs_6_.refs_2_), channel_id=1, source_target_pairs={{0,1},{1,0},{2,3},{3,2},{4,5},{5,4},{6,7},{7,6},{8,9},{9,8},{10,11... | collective-permute-start | bytes 2359304 | tf_op jit(solution)/shard_map/ppermute | solution.py:50
  71.9 14.8 %collective-permute-start.2 = (bf16[128,1536]{1,0:T(8,128)(2,1)}, bf16[128,1536]{1,0:T(8,128)(2,1)S(1)}, u32[]{:S(2)}, u32[]{:S(2)}) collective-permute-start(bf16[128,1536]{1,0:T(8,128)(2,1)} %collective-permute-done.1.refs_18_), channel_id=1, source_target_pairs={{0,4},{4,0},{1,5},{5,1},{2,6},{6,2},{3,7},{7,3},{8,12},{12,8},{9,1... | collective-permute-start | bytes 1179656 | tf_op jit(solution)/shard_map/ppermute | solution.py:50
  72.1 16.0 %collective-permute-start.3 = (bf16[128,1536]{1,0:T(8,128)(2,1)}, bf16[128,1536]{1,0:T(8,128)(2,1)}, u32[]{:S(2)}, u32[]{:S(2)}) collective-permute-start(bf16[128,1536]{1,0:T(8,128)(2,1)} %collective-permute-done.1.refs_18_), channel_id=1, source_target_pairs={{0,2},{2,0},{1,3},{3,1},{4,6},{6,4},{5,7},{7,5},{8,10},{10,8},{9,1... | collective-permute-start | bytes 1179656 | tf_op jit(solution)/shard_map/ppermute | solution.py:50
  73.3 12.8 %collective-permute-start.31 = (bf16[48,1536]{1,0:T(8,128)(2,1)S(1)}, bf16[48,1536]{1,0:T(8,128)(2,1)S(1)}, u32[]{:S(2)}, u32[]{:S(2)}) collective-permute-start(bf16[48,1536]{1,0:T(8,128)(2,1)S(1)} %convert_element_type.165), channel_id=1, source_target_pairs={{0,24},{8,0},{16,8},{24,16},{1,25},{9,1},{17,9},{25,17},{2,26},{10... | collective-permute-start | bytes 442376 | tf_op jit(solution)/shard_map/ppermute | solution.py:50
  79.8 11.3 %collective-permute-start.17 = (bf16[4,48,1024]{2,1,0:T(8,128)(2,1)S(1)}, bf16[4,48,1024]{2,1,0:T(8,128)(2,1)S(1)}, u32[]{:S(2)}, u32[]{:S(2)}) collective-permute-start(bf16[4,48,1024]{2,1,0:T(8,128)(2,1)S(1)} %slice.286), channel_id=1, source_target_pairs={{0,4},{4,0},{1,5},{5,1},{2,6},{6,2},{3,7},{7,3},{8,12},{12,8},{9,1... | collective-permute-start | bytes 1179656 | tf_op jit(solution)/shard_map/ppermute | solution.py:50
  86.1 9.6 %collective-permute-start.18 = (bf16[4,48,1024]{2,1,0:T(8,128)(2,1)S(1)}, bf16[4,48,1024]{2,1,0:T(8,128)(2,1)S(1)}, u32[]{:S(2)}, u32[]{:S(2)}) collective-permute-start(bf16[4,48,1024]{2,1,0:T(8,128)(2,1)S(1)} %slice.287), channel_id=1, source_target_pairs={{0,2},{2,0},{1,3},{3,1},{4,6},{6,4},{5,7},{7,5},{8,10},{10,8},{9,1... | collective-permute-start | bytes 1179656 | tf_op jit(solution)/shard_map/ppermute | solution.py:50
  86.7 12.3 %collective-permute-start.20 = (bf16[4,48,2048]{2,1,0:T(8,128)(2,1)S(1)}, bf16[4,48,2048]{2,1,0:T(8,128)(2,1)S(1)}, u32[]{:S(2)}, u32[]{:S(2)}) collective-permute-start(bf16[4,48,2048]{2,1,0:T(8,128)(2,1)S(1)} %collective-permute-done.14.refs_7_.refs_3_), channel_id=1, source_target_pairs={{0,1},{1,0},{2,3},{3,2},{4,5},{5,4},{6,7},{7,6},{8,9},{9,8},{10,11... | collective-permute-start | bytes 2359304 | tf_op jit(solution)/shard_map/ppermute | solution.py:50
  88.1 10.9 %collective-permute-start.21 = (bf16[4,48,2048]{2,1,0:T(8,128)(2,1)S(1)}, bf16[4,48,2048]{2,1,0:T(8,128)(2,1)S(1)}, u32[]{:S(2)}, u32[]{:S(2)}) collective-permute-start(bf16[4,48,2048]{2,1,0:T(8,128)(2,1)S(1)} %collective-permute-done.15.refs_8_.refs_4_), channel_id=1, source_target_pairs={{0,1},{1,0},{2,3},{3,2},{4,5},{5,4},{6,7},{7,6},{8,9},{9,8},{10,11... | collective-permute-start | bytes 2359304 | tf_op jit(solution)/shard_map/ppermute | solution.py:50
  89.9 19.4 %collective-permute-start.33 = (bf16[4,48,1536]{2,1,0:T(8,128)(2,1)S(1)}, bf16[4,48,1536]{2,1,0:T(8,128)(2,1)S(1)}, u32[]{:S(2)}, u32[]{:S(2)}) collective-permute-start(bf16[4,48,1536]{2,1,0:T(8,128)(2,1)S(1)} %pad_maximum_fusion.1.refs_7_.refs_6_), channel_id=1, source_target_pairs={{0,4},{4,0},{1,5},{5,1},{2,6},{6,2},{3,7},{7,3},{8,12},{12,8},{9,1... | collective-permute-start | bytes 1769480 | tf_op jit(solution)/shard_map/ppermute | solution.py:50
  98.3 24.6 %collective-permute-start.32 = (bf16[4,48,1536]{2,1,0:T(8,128)(2,1)S(1)}, bf16[4,48,1536]{2,1,0:T(8,128)(2,1)S(1)}, u32[]{:S(2)}, u32[]{:S(2)}) collective-permute-start(bf16[4,48,1536]{2,1,0:T(8,128)(2,1)S(1)} %pad_maximum_fusion.1.refs_7_.refs_6_), channel_id=1, source_target_pairs={{0,2},{2,0},{1,3},{3,1},{4,6},{6,4},{5,7},{7,5},{8,10},{10,8},{9,1... | collective-permute-start | bytes 1769480 | tf_op jit(solution)/shard_map/ppermute | solution.py:50
  106.4 9.6 %collective-permute-start.25 = (bf16[128,512]{1,0:T(8,128)(2,1)}, bf16[128,512]{1,0:T(8,128)(2,1)S(1)}, u32[]{:S(2)}, u32[]{:S(2)}) collective-permute-start(bf16[128,512]{1,0:T(8,128)(2,1)} %get-tuple-element.78), channel_id=1, source_target_pairs={{0,2},{2,0},{4,6},{6,4},{1,3},{3,1},{5,7},{7,5},{8,10},{10,8},{12,... | collective-permute-start | bytes 393224 | tf_op jit(solution)/shard_map/ppermute | solution.py:68
  107.2 9.4 %collective-permute-start.26 = (bf16[128,512]{1,0:T(8,128)(2,1)}, bf16[128,512]{1,0:T(8,128)(2,1)S(1)}, u32[]{:S(2)}, u32[]{:S(2)}) collective-permute-start(bf16[128,512]{1,0:T(8,128)(2,1)} %get-tuple-element.78), channel_id=1, source_target_pairs={{0,4},{2,6},{4,0},{6,2},{1,5},{3,7},{5,1},{7,3},{8,12},{10,14},{12... | collective-permute-start | bytes 393224 | tf_op jit(solution)/shard_map/ppermute | solution.py:68
  108.4 11.3 %collective-permute-start.27 = (bf16[128,512]{1,0:T(8,128)(2,1)}, bf16[128,512]{1,0:T(8,128)(2,1)S(1)}, u32[]{:S(2)}, u32[]{:S(2)}) collective-permute-start(bf16[128,512]{1,0:T(8,128)(2,1)} %get-tuple-element.78), channel_id=1, source_target_pairs={{0,6},{2,4},{4,2},{6,0},{1,7},{3,5},{5,3},{7,1},{8,14},{10,12},{12... | collective-permute-start | bytes 393224 | tf_op jit(solution)/shard_map/ppermute | solution.py:68
  109.2 18.1 %collective-permute-start.24 = (bf16[128,1536]{1,0:T(8,128)(2,1)S(1)}, bf16[128,1536]{1,0:T(8,128)(2,1)}, u32[]{:S(2)}, u32[]{:S(2)}) collective-permute-start(bf16[128,1536]{1,0:T(8,128)(2,1)S(1)} %copy-done.48), channel_id=1, source_target_pairs={{0,2},{2,0},{1,3},{3,1},{4,6},{6,4},{5,7},{7,5},{8,10},{10,8},{9,1... | collective-permute-start | bytes 1179656 | tf_op jit(solution)/shard_map/ppermute | solution.py:50
  116.1 17.6 %collective-permute-start.35 = (bf16[4,48,768]{2,1,0:T(8,128)(2,1)S(1)}, bf16[4,48,768]{2,1,0:T(8,128)(2,1)S(1)}, u32[]{:S(2)}, u32[]{:S(2)}) collective-permute-start(bf16[4,48,768]{2,1,0:T(8,128)(2,1)S(1)} %slice.290), channel_id=1, source_target_pairs={{0,2},{2,0},{1,3},{3,1},{4,6},{6,4},{5,7},{7,5},{8,10},{10,8},{9,1... | collective-permute-start | bytes 884744 | tf_op jit(solution)/shard_map/ppermute | solution.py:50
  121.5 15.4 %collective-permute-start.28 = (bf16[512,512]{1,0:T(8,128)(2,1)}, bf16[512,512]{1,0:T(8,128)(2,1)}, u32[]{:S(2)}, u32[]{:S(2)}) collective-permute-start(bf16[512,512]{1,0:T(8,128)(2,1)} %pad_maximum_fusion.2), channel_id=1, source_target_pairs={{0,1},{1,0},{2,3},{3,2},{4,5},{5,4},{6,7},{7,6},{8,9},{9,8},{10,11... | collective-permute-start | bytes 1572872 | tf_op jit(solution)/shard_map/ppermute | solution.py:50
  122.8 15.7 %collective-permute-start.36 = (bf16[4,48,1536]{2,1,0:T(8,128)(2,1)S(1)}, bf16[4,48,1536]{2,1,0:T(8,128)(2,1)S(1)}, u32[]{:S(2)}, u32[]{:S(2)}) collective-permute-start(bf16[4,48,1536]{2,1,0:T(8,128)(2,1)S(1)} %pad_maximum_fusion.1.refs_7_.refs_6_), channel_id=1, source_target_pairs={{0,1},{1,0},{2,3},{3,2},{4,5},{5,4},{6,7},{7,6},{8,9},{9,8},{10,11... | collective-permute-start | bytes 1769480 | tf_op jit(solution)/shard_map/ppermute | solution.py:50
  123.6 13.1 %collective-permute-start.34 = (bf16[4,48,768]{2,1,0:T(8,128)(2,1)}, bf16[4,48,768]{2,1,0:T(8,128)(2,1)}, u32[]{:S(2)}, u32[]{:S(2)}) collective-permute-start(bf16[4,48,768]{2,1,0:T(8,128)(2,1)} %slice.289), channel_id=1, source_target_pairs={{0,4},{4,0},{1,5},{5,1},{2,6},{6,2},{3,7},{7,3},{8,12},{12,8},{9,1... | collective-permute-start | bytes 884744 | tf_op jit(solution)/shard_map/ppermute | solution.py:50
  127.3 11.7 %collective-permute-start.37 = (bf16[4,48,1536]{2,1,0:T(8,128)(2,1)S(1)}, bf16[4,48,1536]{2,1,0:T(8,128)(2,1)S(1)}, u32[]{:S(2)}, u32[]{:S(2)}) collective-permute-start(bf16[4,48,1536]{2,1,0:T(8,128)(2,1)S(1)} %collective-permute-done.32.refs_8_.refs_7_), channel_id=1, source_target_pairs={{0,1},{1,0},{2,3},{3,2},{4,5},{5,4},{6,7},{7,6},{8,9},{9,8},{10,11... | collective-permute-start | bytes 1769480 | tf_op jit(solution)/shard_map/ppermute | solution.py:50
  151.4 26.8 %collective-permute-start.44 = (bf16[128,1536]{1,0:T(8,128)(2,1)}, bf16[128,1536]{1,0:T(8,128)(2,1)S(1)}, u32[]{:S(2)}, u32[]{:S(2)}) collective-permute-start(bf16[128,1536]{1,0:T(8,128)(2,1)} %get-tuple-element.84.refs_6_), channel_id=1, source_target_pairs={{0,16},{16,0},{1,17},{17,1},{2,18},{18,2},{3,19},{19,3},{4,20},{20... | collective-permute-start | bytes 1179656 | tf_op jit(solution)/shard_map/ppermute | solution.py:50
  156.5 22.9 %collective-permute-start.41 = (bf16[128,1536]{1,0:T(8,128)(2,1)}, bf16[128,1536]{1,0:T(8,128)(2,1)S(1)}, u32[]{:S(2)}, u32[]{:S(2)}) collective-permute-start(bf16[128,1536]{1,0:T(8,128)(2,1)} %get-tuple-element.84.refs_6_), channel_id=1, source_target_pairs={{0,2},{2,0},{1,3},{3,1},{4,6},{6,4},{5,7},{7,5},{8,10},{10,8},{9,1... | collective-permute-start | bytes 1179656 | tf_op jit(solution)/shard_map/ppermute | solution.py:50
  157.0 22.9 %collective-permute-start.42 = (bf16[128,1536]{1,0:T(8,128)(2,1)}, bf16[128,1536]{1,0:T(8,128)(2,1)S(1)}, u32[]{:S(2)}, u32[]{:S(2)}) collective-permute-start(bf16[128,1536]{1,0:T(8,128)(2,1)} %get-tuple-element.84.refs_6_), channel_id=1, source_target_pairs={{0,4},{4,0},{1,5},{5,1},{2,6},{6,2},{3,7},{7,3},{8,12},{12,8},{9,1... | collective-permute-start | bytes 1179656 | tf_op jit(solution)/shard_map/ppermute | solution.py:50
  164.2 11.5 %collective-permute-start.46 = (bf16[128,768]{1,0:T(8,128)(2,1)S(1)}, bf16[128,768]{1,0:T(8,128)(2,1)S(1)}, u32[]{:S(2)}, u32[]{:S(2)}) collective-permute-start(bf16[128,768]{1,0:T(8,128)(2,1)S(1)} %pad_maximum_fusion.4), channel_id=1, source_target_pairs={{0,4},{2,6},{4,0},{6,2},{1,5},{3,7},{5,1},{7,3},{8,12},{10,14},{12... | collective-permute-start | bytes 589832 | tf_op jit(solution)/shard_map/ppermute | solution.py:68
  179.3 15.7 %collective-permute-start.43 = (bf16[128,1536]{1,0:T(8,128)(2,1)S(1)}, bf16[128,1536]{1,0:T(8,128)(2,1)S(1)}, u32[]{:S(2)}, u32[]{:S(2)}) collective-permute-start(bf16[128,1536]{1,0:T(8,128)(2,1)S(1)} %collective-permute-done.41.refs_7_), channel_id=1, source_target_pairs={{0,4},{4,0},{1,5},{5,1},{2,6},{6,2},{3,7},{7,3},{8,12},{12,8},{9,1... | collective-permute-start | bytes 1179656 | tf_op jit(solution)/shard_map/ppermute | solution.py:50
  216.9 15.2 %collective-permute-start.53 = (bf16[256,1536]{1,0:T(8,128)(2,1)S(1)}, bf16[256,1536]{1,0:T(8,128)(2,1)S(1)}, u32[]{:S(2)}, u32[]{:S(2)}) collective-permute-start(bf16[256,1536]{1,0:T(8,128)(2,1)S(1)} %slice.398), channel_id=1, source_target_pairs={{0,2},{2,0},{1,3},{3,1},{4,6},{6,4},{5,7},{7,5},{8,10},{10,8},{9,1... | collective-permute-start | bytes 2359304 | tf_op jit(solution)/shard_map/ppermute | solution.py:50
  228.1 14.6 %collective-permute-start.51 = (bf16[256,1536]{1,0:T(8,128)(2,1)S(1)}, bf16[256,1536]{1,0:T(8,128)(2,1)S(1)}, u32[]{:S(2)}, u32[]{:S(2)}) collective-permute-start(bf16[256,1536]{1,0:T(8,128)(2,1)S(1)} %slice.399), channel_id=1, source_target_pairs={{0,4},{4,0},{1,5},{5,1},{2,6},{6,2},{3,7},{7,3},{8,12},{12,8},{9,1... | collective-permute-start | bytes 2359304 | tf_op jit(solution)/shard_map/ppermute | solution.py:50
  232.3 18.8 %collective-permute-start.54 = (bf16[128,1536]{1,0:T(8,128)(2,1)S(1)}, bf16[128,1536]{1,0:T(8,128)(2,1)S(1)}, u32[]{:S(2)}, u32[]{:S(2)}) collective-permute-start(bf16[128,1536]{1,0:T(8,128)(2,1)S(1)} %slice.403), channel_id=1, source_target_pairs={{0,4},{4,0},{1,5},{5,1},{2,6},{6,2},{3,7},{7,3},{8,12},{12,8},{9,1... | collective-permute-start | bytes 1179656 | tf_op jit(solution)/shard_map/ppermute | solution.py:50
  242.9 9.9 %collective-permute-start.52 = (bf16[128,1536]{1,0:T(8,128)(2,1)S(1)}, bf16[128,1536]{1,0:T(8,128)(2,1)S(1)}, u32[]{:S(2)}, u32[]{:S(2)}) collective-permute-start(bf16[128,1536]{1,0:T(8,128)(2,1)S(1)} %slice.404), channel_id=1, source_target_pairs={{0,2},{2,0},{1,3},{3,1},{4,6},{6,4},{5,7},{7,5},{8,10},{10,8},{9,1... | collective-permute-start | bytes 1179656 | tf_op jit(solution)/shard_map/ppermute | solution.py:50
  251.2 22.3 %collective-permute-start.57 = (bf16[128,1536]{1,0:T(8,128)(2,1)S(1)}, bf16[128,1536]{1,0:T(8,128)(2,1)}, u32[]{:S(2)}, u32[]{:S(2)}) collective-permute-start(bf16[128,1536]{1,0:T(8,128)(2,1)S(1)} %slice_add_fusion.4), channel_id=1, source_target_pairs={{0,16},{16,0},{1,17},{17,1},{2,18},{18,2},{3,19},{19,3},{4,20},{20... | collective-permute-start | bytes 1179656 | tf_op jit(solution)/shard_map/ppermute | solution.py:50
  271.0 36.4 %collective-permute-start.55 = (bf16[256,1536]{1,0:T(8,128)(2,1)}, bf16[256,1536]{1,0:T(8,128)(2,1)}, u32[]{:S(2)}, u32[]{:S(2)}) collective-permute-start(bf16[256,1536]{1,0:T(8,128)(2,1)} %slice.254), channel_id=1, source_target_pairs={{0,4},{4,0},{1,5},{5,1},{2,6},{6,2},{3,7},{7,3},{8,12},{12,8},{9,1... | collective-permute-start | bytes 2359304 | tf_op jit(solution)/shard_map/ppermute | solution.py:50
  273.0 35.8 %collective-permute-start.64 = (bf16[256,1536]{1,0:T(8,128)(2,1)}, bf16[256,1536]{1,0:T(8,128)(2,1)}, u32[]{:S(2)}, u32[]{:S(2)}) collective-permute-start(bf16[256,1536]{1,0:T(8,128)(2,1)} %slice.264), channel_id=1, source_target_pairs={{0,2},{2,0},{1,3},{3,1},{4,6},{6,4},{5,7},{7,5},{8,10},{10,8},{9,1... | collective-permute-start | bytes 2359304 | tf_op jit(solution)/shard_map/ppermute | solution.py:50
  280.3 15.5 %collective-permute-start.58 = (bf16[128,1536]{1,0:T(8,128)(2,1)}, bf16[128,1536]{1,0:T(8,128)(2,1)}, u32[]{:S(2)}, u32[]{:S(2)}) collective-permute-start(bf16[128,1536]{1,0:T(8,128)(2,1)} %get-tuple-element.95.refs_4_), channel_id=1, source_target_pairs={{0,2},{2,0},{4,6},{6,4},{1,3},{3,1},{5,7},{7,5},{8,10},{10,8},{12,... | collective-permute-start | bytes 1179656 | tf_op jit(solution)/shard_map/ppermute | solution.py:68
  281.4 14.4 %collective-permute-start.59 = (bf16[128,1536]{1,0:T(8,128)(2,1)}, bf16[128,1536]{1,0:T(8,128)(2,1)}, u32[]{:S(2)}, u32[]{:S(2)}) collective-permute-start(bf16[128,1536]{1,0:T(8,128)(2,1)} %get-tuple-element.95.refs_4_), channel_id=1, source_target_pairs={{0,4},{2,6},{4,0},{6,2},{1,5},{3,7},{5,1},{7,3},{8,12},{10,14},{12... | collective-permute-start | bytes 1179656 | tf_op jit(solution)/shard_map/ppermute | solution.py:68
  281.8 52.9 %collective-permute-start.74 = (bf16[128,1536]{1,0:T(8,128)(2,1)}, bf16[128,1536]{1,0:T(8,128)(2,1)}, u32[]{:S(2)}, u32[]{:S(2)}) collective-permute-start(bf16[128,1536]{1,0:T(8,128)(2,1)} %get-tuple-element.95.refs_4_), channel_id=1, source_target_pairs={{0,6},{2,4},{4,2},{6,0},{1,7},{3,5},{5,3},{7,1},{8,14},{10,12},{12... | collective-permute-start | bytes 1179656 | tf_op jit(solution)/shard_map/ppermute | solution.py:68
  297.3 13.6 %collective-permute-start.60 = (bf16[512,512]{1,0:T(8,128)(2,1)S(1)}, bf16[512,512]{1,0:T(8,128)(2,1)S(1)}, u32[]{:S(2)}, u32[]{:S(2)}) collective-permute-start(bf16[512,512]{1,0:T(8,128)(2,1)S(1)} %slice.400), channel_id=1, source_target_pairs={{0,1},{1,0},{2,3},{3,2},{4,5},{5,4},{6,7},{7,6},{8,9},{9,8},{10,11... | collective-permute-start | bytes 1572872 | tf_op jit(solution)/shard_map/ppermute | solution.py:50
  310.4 21.6 %collective-permute-start.65 = (bf16[128,1536]{1,0:T(8,128)(2,1)S(1)}, bf16[128,1536]{1,0:T(8,128)(2,1)S(1)}, u32[]{:S(2)}, u32[]{:S(2)}) collective-permute-start(bf16[128,1536]{1,0:T(8,128)(2,1)S(1)} %slice.401), channel_id=1, source_target_pairs={{0,4},{4,0},{1,5},{5,1},{2,6},{6,2},{3,7},{7,3},{8,12},{12,8},{9,1... | collective-permute-start | bytes 1179656 | tf_op jit(solution)/shard_map/ppermute | solution.py:50
  311.1 11.0 %collective-permute-start.61 = (bf16[128,512]{1,0:T(8,128)(2,1)S(1)}, bf16[128,512]{1,0:T(8,128)(2,1)S(1)}, u32[]{:S(2)}, u32[]{:S(2)}) collective-permute-start(bf16[128,512]{1,0:T(8,128)(2,1)S(1)} %get-tuple-element.200), channel_id=1, source_target_pairs={{0,2},{2,0},{4,6},{6,4},{1,3},{3,1},{5,7},{7,5},{8,10},{10,8},{12,... | collective-permute-start | bytes 393224 | tf_op jit(solution)/shard_map/ppermute | solution.py:68
  312.6 14.3 %collective-permute-start.62 = (bf16[128,512]{1,0:T(8,128)(2,1)S(1)}, bf16[128,512]{1,0:T(8,128)(2,1)S(1)}, u32[]{:S(2)}, u32[]{:S(2)}) collective-permute-start(bf16[128,512]{1,0:T(8,128)(2,1)S(1)} %get-tuple-element.199), channel_id=1, source_target_pairs={{0,4},{2,6},{4,0},{6,2},{1,5},{3,7},{5,1},{7,3},{8,12},{10,14},{12... | collective-permute-start | bytes 393224 | tf_op jit(solution)/shard_map/ppermute | solution.py:68
  312.8 14.1 %collective-permute-start.63 = (bf16[128,512]{1,0:T(8,128)(2,1)S(1)}, bf16[128,512]{1,0:T(8,128)(2,1)S(1)}, u32[]{:S(2)}, u32[]{:S(2)}) collective-permute-start(bf16[128,512]{1,0:T(8,128)(2,1)S(1)} %get-tuple-element.198), channel_id=1, source_target_pairs={{0,6},{2,4},{4,2},{6,0},{1,7},{3,5},{5,3},{7,1},{8,14},{10,12},{12... | collective-permute-start | bytes 393224 | tf_op jit(solution)/shard_map/ppermute | solution.py:68
  322.2 18.2 %collective-permute-start.56 = (bf16[128,1536]{1,0:T(8,128)(2,1)S(1)}, bf16[128,1536]{1,0:T(8,128)(2,1)}, u32[]{:S(2)}, u32[]{:S(2)}) collective-permute-start(bf16[128,1536]{1,0:T(8,128)(2,1)S(1)} %slice.402), channel_id=1, source_target_pairs={{0,2},{2,0},{1,3},{3,1},{4,6},{6,4},{5,7},{7,5},{8,10},{10,8},{9,1... | collective-permute-start | bytes 1179656 | tf_op jit(solution)/shard_map/ppermute | solution.py:50
  332.1 19.3 %collective-permute-start.66 = (bf16[128,1536]{1,0:T(8,128)(2,1)S(1)}, bf16[128,1536]{1,0:T(8,128)(2,1)S(1)}, u32[]{:S(2)}, u32[]{:S(2)}) collective-permute-start(bf16[128,1536]{1,0:T(8,128)(2,1)S(1)} %fusion.24), channel_id=1, source_target_pairs={{0,16},{16,0},{1,17},{17,1},{2,18},{18,2},{3,19},{19,3},{4,20},{20... | collective-permute-start | bytes 1179656 | tf_op jit(solution)/shard_map/ppermute | solution.py:50
  334.2 19.1 %collective-permute-start.67 = (bf16[144,2048]{1,0:T(8,128)(2,1)}, bf16[144,2048]{1,0:T(8,128)(2,1)S(1)}, u32[]{:S(2)}, u32[]{:S(2)}) collective-permute-start(bf16[144,2048]{1,0:T(8,128)(2,1)} %get-tuple-element.103.refs_4_), channel_id=1, source_target_pairs={{0,2},{2,0},{4,6},{6,4},{1,3},{3,1},{5,7},{7,5},{8,10},{10,8},{12,... | collective-permute-start | bytes 1769480 | tf_op jit(solution)/shard_map/ppermute | solution.py:68
  334.4 19.0 %collective-permute-start.68 = (bf16[144,2048]{1,0:T(8,128)(2,1)}, bf16[144,2048]{1,0:T(8,128)(2,1)S(1)}, u32[]{:S(2)}, u32[]{:S(2)}) collective-permute-start(bf16[144,2048]{1,0:T(8,128)(2,1)} %get-tuple-element.103.refs_4_), channel_id=1, source_target_pairs={{0,4},{2,6},{4,0},{6,2},{1,5},{3,7},{5,1},{7,3},{8,12},{10,14},{12... | collective-permute-start | bytes 1769480 | tf_op jit(solution)/shard_map/ppermute | solution.py:68
  334.7 26.4 %collective-permute-start.69 = (bf16[144,2048]{1,0:T(8,128)(2,1)}, bf16[144,2048]{1,0:T(8,128)(2,1)S(1)}, u32[]{:S(2)}, u32[]{:S(2)}) collective-permute-start(bf16[144,2048]{1,0:T(8,128)(2,1)} %get-tuple-element.103.refs_4_), channel_id=1, source_target_pairs={{0,6},{2,4},{4,2},{6,0},{1,7},{3,5},{5,3},{7,1},{8,14},{10,12},{12... | collective-permute-start | bytes 1769480 | tf_op jit(solution)/shard_map/ppermute | solution.py:68
  340.4 28.5 %collective-permute-start.75 = (bf16[192,1536]{1,0:T(8,128)(2,1)}, bf16[192,1536]{1,0:T(8,128)(2,1)S(1)}, u32[]{:S(2)}, u32[]{:S(2)}) collective-permute-start(bf16[192,1536]{1,0:T(8,128)(2,1)} %get-tuple-element.117), channel_id=1, source_target_pairs={{0,1},{1,0},{2,3},{3,2},{4,5},{5,4},{6,7},{7,6},{8,9},{9,8},{10,11... | collective-permute-start | bytes 1769480 | tf_op jit(solution)/shard_map/ppermute | solution.py:50
  369.8 33.6 %collective-permute-start.76 = (bf16[48,1536]{1,0:T(8,128)(2,1)}, bf16[48,1536]{1,0:T(8,128)(2,1)}, u32[]{:S(2)}, u32[]{:S(2)}) collective-permute-start(bf16[48,1536]{1,0:T(8,128)(2,1)} %get-tuple-element.195), channel_id=1, source_target_pairs={{0,24},{8,0},{16,8},{24,16},{1,25},{9,1},{17,9},{25,17},{2,26},{10... | collective-permute-start | bytes 442376 | tf_op jit(solution)/shard_map/ppermute | solution.py:50
  370.0 33.5 %collective-permute-start.77 = (bf16[48,1536]{1,0:T(8,128)(2,1)}, bf16[48,1536]{1,0:T(8,128)(2,1)}, u32[]{:S(2)}, u32[]{:S(2)}) collective-permute-start(bf16[48,1536]{1,0:T(8,128)(2,1)} %get-tuple-element.197), channel_id=1, source_target_pairs={{0,16},{8,24},{16,0},{24,8},{1,17},{9,25},{17,1},{25,9},{2,18},{10... | collective-permute-start | bytes 442376 | tf_op jit(solution)/shard_map/ppermute | solution.py:50
  372.3 25.8 %collective-permute-start.71 = (bf16[56,2048]{1,0:T(8,128)(2,1)}, bf16[56,2048]{1,0:T(8,128)(2,1)}, u32[]{:S(2)}, u32[]{:S(2)}) collective-permute-start(bf16[56,2048]{1,0:T(8,128)(2,1)} %get-tuple-element.192), channel_id=1, source_target_pairs={{0,24},{8,0},{16,8},{24,16},{1,25},{9,1},{17,9},{25,17},{2,26},{10... | collective-permute-start | bytes 688136 | tf_op jit(solution)/shard_map/ppermute | solution.py:50
  374.5 26.3 %collective-permute-start.72 = (bf16[56,2048]{1,0:T(8,128)(2,1)}, bf16[56,2048]{1,0:T(8,128)(2,1)}, u32[]{:S(2)}, u32[]{:S(2)}) collective-permute-start(bf16[56,2048]{1,0:T(8,128)(2,1)} %get-tuple-element.194), channel_id=1, source_target_pairs={{0,16},{8,24},{16,0},{24,8},{1,17},{9,25},{17,1},{25,9},{2,18},{10... | collective-permute-start | bytes 688136 | tf_op jit(solution)/shard_map/ppermute | solution.py:50
  374.5 26.3 %collective-permute-start.73 = (bf16[56,2048]{1,0:T(8,128)(2,1)}, bf16[56,2048]{1,0:T(8,128)(2,1)}, u32[]{:S(2)}, u32[]{:S(2)}) collective-permute-start(bf16[56,2048]{1,0:T(8,128)(2,1)} %get-tuple-element.193), channel_id=1, source_target_pairs={{0,8},{8,16},{16,24},{24,0},{1,9},{9,17},{17,25},{25,1},{2,10},{10... | collective-permute-start | bytes 688136 | tf_op jit(solution)/shard_map/ppermute | solution.py:50
  398.1 14.0 %collective-permute-start.78 = (bf16[48,1536]{1,0:T(8,128)(2,1)S(1)}, bf16[48,1536]{1,0:T(8,128)(2,1)}, u32[]{:S(2)}, u32[]{:S(2)}) collective-permute-start(bf16[48,1536]{1,0:T(8,128)(2,1)S(1)} %get-tuple-element.196), channel_id=1, source_target_pairs={{0,8},{8,16},{16,24},{24,0},{1,9},{9,17},{17,25},{25,1},{2,10},{10... | collective-permute-start | bytes 442376 | tf_op jit(solution)/shard_map/ppermute | solution.py:50
  (87 other events, 859.3 us)
Sparse Core Ops, SparseCore 0:
  11.6 122.2 all-gather.1
  270.2 113.5 reduce-scatter.1

commit v5 on v4

--- a/solution.py
+++ b/solution.py
@@ -317,7 +317,7 @@
                 pair_ref[:, column - QW : column - QW + HEAD_DIM] = low(part)
 
 
-TOGETHER = 2
+TOGETHER = 3
 
 
 def head_views(step):

time: 432 us -> 431 us (level)
  transfers between devices with their start and end apart: 81 -> 81, of which waited for: 29 -> 29; matrix products, arithmetic and copies ran while one was open for 11% -> 11% of each run, Pallas kernels for 21% -> 20%
where the time goes in v5:
time: 431 us; the launch traced here: 424 us
  waiting for transfers between devices  142 us (33%)
  starting transfers between devices  95.7 us (22%)
  Pallas kernels  84.6 us (20%)
  matrix products  36.5 us (8%)
  local copies, waits for them, and re-layouts  24.9 us (6%)
  other arithmetic  24.4 us (6%)
  between operations  15.9 us (4%)
    ppermute x64, waiting for transfers between devices, shift(): lax.ppermute(value, axis, [(i, (i + step) % count) for i in range(count)])  102 us
    ppermute x64, starting transfers between devices, shift(): lax.ppermute(value, axis, [(i, (i + step) % count) for i in range(count)])  82 us
    pallas_call x4, Pallas kernels, call_with_pieces(): pl.pallas_call(run, out_shape=outs, in_specs=[SCALARS] + [pl.BlockSpec(me...  30.8 us
    ppermute x15, waiting for transfers between devices, plane_shift(): return lax.ppermute(value, ('y', 'x'), pairs)  30.5 us
    pallas_call x4, Pallas kernels, local_call(): pl.pallas_call(kernel, out_shape=outs, scratch_shapes=list(scratch), comp...  23.2 us
    dot_general x6, matrix products, body(): jnp.einsum('ud,td->ut', rows, tokens, preferred_element_type=jnp.float32)  18.6 us
    pallas_call x1, Pallas kernels, units_gradient(): pl.pallas_call(lambda *refs: gradient_kernel(len(parts), size, *refs), gr...  16.3 us
    pallas_call x1, Pallas kernels, units_step(): pl.pallas_call(units_step_kernel, grid=(6,), in_specs=[pl.BlockSpec((unit...  14.3 us
  transfers between devices with their start and end apart: 81, of which 29 were waited for; matrix products, arithmetic and copies ran while one was open for 11% of the time, Pallas kernels for 20%

profile of v5, /device:TPU:7, one launch (start us, length us, event | category | flops | bytes accessed | tf_op | source)
XLA Modules:
  0.0 423.9 jit_solution(3517120819432338423)
XLA Ops:
  7.2 4.3 %convert_element_type.166 = bf16[280,3,1536]{2,0,1:T(8,128)(2,1)} convert(f32[280,3,1536]{2,0,1:T(8,128)} %param.20) | non-fusion elementwise | flops 1290240 | bytes 7741440 | tf_op jit(solution)/shard_map/convert_element_type | solution.py:37
  13.9 2.3 collective-permute-start.5
  21.4 2.4 collective-permute-start.7
  27.4 7.7 %collective-permute-done.11 = bf16[48,2048]{1,0:T(8,128)(2,1)S(1)} collective-permute-done((bf16[48,2048]{1,0:T(8,128)(2,1)S(1)}, bf16[48,2048]{1,0:T(8,128)(2,1)S(1)}, u32[]{:S(2)}, u32[]{:S(2)}) %collective-permute-start.11) | collective-permute-done | bytes 196640 | tf_op jit(solution)/shard_map/ppermute | solution.py:50
  40.0 3.1 collective-permute-start.1
  43.6 7.3 %collective-permute-done.9 = f32[1,5120]{1,0:T(1,128)S(1)} collective-permute-done((f32[1,5120]{1,0:T(1,128)S(1)}, f32[1,5120]{1,0:T(1,128)S(1)}, u32[]{:S(2)}, u32[]{:S(2)}) %collective-permute-start.9) | collective-permute-done | bytes 20512 | tf_op jit(solution)/shard_map/ppermute | solution.py:50
  51.0 4.3 %collective-permute-start.29 = (bf16[48,1536]{1,0:T(8,128)(2,1)S(1)}, bf16[48,1536]{1,0:T(8,128)(2,1)}, u32[]{:S(2)}, u32[]{:S(2)}) collective-permute-start(bf16[48,1536]{1,0:T(8,128)(2,1)S(1)} %convert_element_type.165), channel_id=1, source_target_pairs={{0,8},{8,16},{16,24},{24,0},{1,9},{9,17},{17,25},{25,1},{2,10},{10... | collective-permute-start | bytes 442376 | tf_op jit(solution)/shard_map/ppermute | solution.py:50
  55.8 11.6 %collective-permute-done.29 = bf16[48,1536]{1,0:T(8,128)(2,1)} collective-permute-done((bf16[48,1536]{1,0:T(8,128)(2,1)S(1)}, bf16[48,1536]{1,0:T(8,128)(2,1)}, u32[]{:S(2)}, u32[]{:S(2)}) %collective-permute-start.29) | collective-permute-done | bytes 147488 | tf_op jit(solution)/shard_map/ppermute | solution.py:50
  67.4 4.5 %collective-permute-start.19 = (bf16[4,48,2048]{2,1,0:T(8,128)(2,1)S(1)}, bf16[4,48,2048]{2,1,0:T(8,128)(2,1)}, u32[]{:S(2)}, u32[]{:S(2)}) collective-permute-start(bf16[4,48,2048]{2,1,0:T(8,128)(2,1)S(1)} %pad_maximum_fusion.refs_6_.refs_2_), channel_id=1, source_target_pairs={{0,1},{1,0},{2,3},{3,2},{4,5},{5,4},{6,7},{7,6},{8,9},{9,8},{10,11... | collective-permute-start | bytes 2359304 | tf_op jit(solution)/shard_map/ppermute | solution.py:50
  73.3 4.0 collective-permute-start.31
  77.6 2.2 collective-permute-done.30
  81.0 5.1 %collective-permute-done.31 = bf16[48,1536]{1,0:T(8,128)(2,1)S(1)} collective-permute-done((bf16[48,1536]{1,0:T(8,128)(2,1)S(1)}, bf16[48,1536]{1,0:T(8,128)(2,1)S(1)}, u32[]{:S(2)}, u32[]{:S(2)}) %collective-permute-start.31) | collective-permute-done | bytes 147488 | tf_op jit(solution)/shard_map/ppermute | solution.py:50
  92.1 3.6 collective-permute-done.18.refs_10_.refs_6_
  95.7 1.9 collective-permute-start.23
  100.3 6.1 %front.1 = (bf16[128,1536]{1,0:T(8,128)(2,1)}, bf16[128,1536]{1,0:T(8,128)(2,1)}, bf16[128,512]{1,0:T(8,128)(2,1)}) custom-call(s32[40]{0:T(128)} %stack.220.refs_0_, bf16[128,1536]{1,0:T(8,128)(2,1)} %refs_9_.1, f32[1,1536]{1,0:T(1,128)} %get-tuple-element.231.refs_2_.refs_10_, f32[1,2048]{1,0:T(1,128)} %slice.283.refs_3_, ...), custom_call_target="tpu_custom_call" | custom-call | flops 1650000000 | tf_op jit(solution)/shard_map/front/pallas_call | solution.py:245
  110.1 6.0 %collective-permute-done.25 = bf16[128,512]{1,0:T(8,128)(2,1)S(1)} collective-permute-done((bf16[128,512]{1,0:T(8,128)(2,1)}, bf16[128,512]{1,0:T(8,128)(2,1)S(1)}, u32[]{:S(2)}, u32[]{:S(2)}) %collective-permute-start.25) | collective-permute-done | bytes 131104 | tf_op jit(solution)/shard_map/ppermute | solution.py:68
  116.6 3.1 collective-permute-done.27
  119.7 1.7 pad_maximum_fusion.2
  123.8 3.5 collective-permute-done.24.refs_21_
  128.6 5.0 %collective-permute-done.35.refs_11_.refs_10_ = bf16[4,48,768]{2,1,0:T(8,128)(2,1)S(1)} collective-permute-done((bf16[4,48,768]{2,1,0:T(8,128)(2,1)S(1)}, bf16[4,48,768]{2,1,0:T(8,128)(2,1)S(1)}, u32[]{:S(2)}, u32[]{:S(2)}) %collective-permute-start.35) | collective-permute-done | bytes 294944 | tf_op jit(solution)/shard_map/ppermute | solution.py:50
  140.0 10.3 %attend.1 = (bf16[128,1536]{1,0:T(8,128)(2,1)}, f32[128,1536]{1,0:T(8,128)}, bf16[128,1536]{1,0:T(8,128)(2,1)}) custom-call(s32[40]{0:T(128)} %stack.220.refs_0_, bf16[128,1536]{1,0:T(8,128)(2,1)} %get-tuple-element.77.refs_1_.query_ref, bf16[1024,512]{1,0:T(8,128)(2,1)} %copy-done.60, s32[1024,2]{1,0:T(8,128)} %copy.77.refs_3_.key_marks_ref, ...), custom_call_target="tpu_custom_call" | custom-call | flops 3300000000 | tf_op jit(solution)/shard_map/attend/pallas_call | solution.py:245
  150.3 5.1 %collective-permute-start.44 = (bf16[128,1536]{1,0:T(8,128)(2,1)}, bf16[128,1536]{1,0:T(8,128)(2,1)S(1)}, u32[]{:S(2)}, u32[]{:S(2)}) collective-permute-start(bf16[128,1536]{1,0:T(8,128)(2,1)} %get-tuple-element.84.refs_6_), channel_id=1, source_target_pairs={{0,16},{16,0},{1,17},{17,1},{2,18},{18,2},{3,19},{19,3},{4,20},{20... | collective-permute-start | bytes 1179656 | tf_op jit(solution)/shard_map/ppermute | solution.py:50
  156.9 2.1 fusion.4
  159.0 2.1 fusion.5
  164.5 6.7 %collective-permute-done.47 = bf16[128,768]{1,0:T(8,128)(2,1)S(1)} collective-permute-done((bf16[128,768]{1,0:T(8,128)(2,1)S(1)}, bf16[128,768]{1,0:T(8,128)(2,1)S(1)}, u32[]{:S(2)}, u32[]{:S(2)}) %collective-permute-start.47) | collective-permute-done | bytes 196640 | tf_op jit(solution)/shard_map/ppermute | solution.py:68
  172.2 2.4 collective-permute-done.46
  178.9 6.6 %collective-permute-done.48.refs_11_ = bf16[128,1536]{1,0:T(8,128)(2,1)S(1)} collective-permute-done((bf16[128,1536]{1,0:T(8,128)(2,1)S(1)}, bf16[128,1536]{1,0:T(8,128)(2,1)S(1)}, u32[]{:S(2)}, u32[]{:S(2)}) %collective-permute-start.48) | collective-permute-done | bytes 393248 | tf_op jit(solution)/shard_map/ppermute | solution.py:50
  185.9 8.1 %collective-permute-done.43.refs_9_ = bf16[128,1536]{1,0:T(8,128)(2,1)S(1)} collective-permute-done((bf16[128,1536]{1,0:T(8,128)(2,1)S(1)}, bf16[128,1536]{1,0:T(8,128)(2,1)S(1)}, u32[]{:S(2)}, u32[]{:S(2)}) %collective-permute-start.43) | collective-permute-done | bytes 393248 | tf_op jit(solution)/shard_map/ppermute | solution.py:50
  195.6 4.1 convolution_bitcast_fusion.4
  200.6 2.0 convolution_bitcast_fusion.5
  202.6 2.0 convolution_bitcast_fusion
  204.6 3.2 convolution_bitcast_fusion.2
  207.9 3.2 multiply_convert_fusion
  211.1 2.3 fusion.8
  213.4 2.3 convolution_add_fusion
  216.1 4.0 multiply_convert_fusion.3
  220.2 2.2 fusion.9
  222.4 2.2 convolution_add_fusion.1
  224.7 2.3 convolution_convert_fusion
  228.5 2.5 convolution_convert_fusion.1
  231.4 10.2 %collective-permute-done.51 = bf16[256,1536]{1,0:T(8,128)(2,1)S(1)} collective-permute-done((bf16[256,1536]{1,0:T(8,128)(2,1)S(1)}, bf16[256,1536]{1,0:T(8,128)(2,1)S(1)}, u32[]{:S(2)}, u32[]{:S(2)}) %collective-permute-start.51) | collective-permute-done | bytes 786464 | tf_op jit(solution)/shard_map/ppermute | solution.py:50
  243.1 7.0 %collective-permute-done.54 = bf16[128,1536]{1,0:T(8,128)(2,1)S(1)} collective-permute-done((bf16[128,1536]{1,0:T(8,128)(2,1)S(1)}, bf16[128,1536]{1,0:T(8,128)(2,1)S(1)}, u32[]{:S(2)}, u32[]{:S(2)}) %collective-permute-start.54) | collective-permute-done | bytes 393248 | tf_op jit(solution)/shard_map/ppermute | solution.py:50
  252.8 16.3 %units_gradient.1 = bf16[1120,4608]{1,0:T(8,128)(2,1)} custom-call(bf16[1120,512]{1,0:T(8,128)(2,1)} %copy-done.4, bf16[1120,512]{1,0:T(8,128)(2,1)} %copy-done.3, bf16[1120,512]{1,0:T(8,128)(2,1)} %copy-done.35, bf16[1120,512]{1,0:T(8,128)(2,1)} %copy-done.1, bf16[1120,512]{1,0:T(8,128)(2,1)} %copy-done.2, bf16[1120,512]{1,0:T(8,128)(2,1)} %copy-done.34, ...), custom_call_target="tpu_custom_call" | custom-call | flops 2200000000 | tf_op jit(solution)/shard_map/units_gradient/pallas_call | solution.py:498
  272.4 6.8 %middle_back.1 = (f32[128,1536]{1,0:T(8,128)}, bf16[128,1536]{1,0:T(8,128)(2,1)}, f32[1,1536]{1,0:T(1,128)}, bf16[128,1536]{1,0:T(8,128)(2,1)}) custom-call(s32[40]{0:T(128)} %stack.220.refs_0_, f32[128,1536]{1,0:T(8,128)} %slice_add_fusion.5.refs_1_, bf16[128,1536]{1,0:T(8,128)(2,1)} %collective-permute-done.57.refs_2_, ...), custom_call_target="tpu_custom_call" | custom-call | flops 1100000000 | tf_op jit(solution)/shard_map/middle_back/pallas_call | solution.py:245
  282.0 11.1 %attend_back.1 = (bf16[128,1536]{1,0:T(8,128)(2,1)}, f32[1024,512]{1,0:T(8,128)}) custom-call(bf16[128,1536]{1,0:T(8,128)(2,1)} %get-tuple-element.93.attended_grad_ref, bf16[128,1536]{1,0:T(8,128)(2,1)} %get-tuple-element.77.refs_1_.query_ref, bf16[1024,512]{1,0:T(8,128)(2,1)} %copy-done.60, s32[1024,2]{1,0:T(8,128)} %copy.77.refs_3_.key_marks_ref, ...), custom_call_target="tpu_custom_call" | custom-call | flops 219999993856 | tf_op jit(solution)/shard_map/attend_back/pallas_call | solution.py:263
  294.5 11.9 %collective-permute-start.60 = (bf16[512,512]{1,0:T(8,128)(2,1)S(1)}, bf16[512,512]{1,0:T(8,128)(2,1)S(1)}, u32[]{:S(2)}, u32[]{:S(2)}) collective-permute-start(bf16[512,512]{1,0:T(8,128)(2,1)S(1)} %slice.400), channel_id=1, source_target_pairs={{0,1},{1,0},{2,3},{3,2},{4,5},{5,4},{6,7},{7,6},{8,9},{9,8},{10,11... | collective-permute-start | bytes 1572872 | tf_op jit(solution)/shard_map/ppermute | solution.py:50
  313.6 7.6 %query_back.1 = (f32[128,1536]{1,0:T(8,128)}, bf16[1536,512]{1,0:T(8,128)(2,1)}) custom-call(s32[40]{0:T(128)} %stack.220.refs_0_, bf16[128,1536]{1,0:T(8,128)(2,1)} %get-tuple-element.98.refs_1_.refs_6_, bf16[4,48,2048]{2,1,0:T(8,128)(2,1)} %copy-done.7, bf16[4,48,2048]{2,1,0:T(8,128)(2,1)} %copy-done.12, bf16[4,48,2048]{2,1,0:T(8,128)(2,1)} %copy-done.13, ...), custom_call_target="tpu_custom_call" | custom-call | flops 1924999936 | tf_op jit(solution)/shard_map/query_back/pallas_call | solution.py:245
  322.4 3.4 collective-permute-done.62.refs_2_
  326.5 4.4 %finish.1 = (bf16[144,2048]{1,0:T(8,128)(2,1)}, f32[128,1536]{1,0:T(8,128)}) custom-call(f32[128,512]{1,0:T(8,128)} %slice.319.refs_0_, bf16[128,512]{1,0:T(8,128)(2,1)} %copy-done.55, bf16[128,512]{1,0:T(8,128)(2,1)} %copy-done.56, bf16[128,512]{1,0:T(8,128)(2,1)} %copy-done.57, f32[128,128]{1,0:T(8,128)} %get-tuple-element.229.refs_4_.cosine_ref, ...), custom_call_target="tpu_custom_call" | custom-call | flops 1100000000 | tf_op jit(solution)/shard_map/finish/pallas_call | solution.py:263
  331.0 2.1 collective-permute-start.66
  333.6 2.2 collective-permute-start.69
  335.8 3.5 out_weights.1
  341.0 9.3 %collective-permute-done.66 = bf16[128,1536]{1,0:T(8,128)(2,1)S(1)} collective-permute-done((bf16[128,1536]{1,0:T(8,128)(2,1)S(1)}, bf16[128,1536]{1,0:T(8,128)(2,1)S(1)}, u32[]{:S(2)}, u32[]{:S(2)}) %collective-permute-start.66) | collective-permute-done | bytes 393248 | tf_op jit(solution)/shard_map/ppermute | solution.py:50
  350.3 1.9 fusion.27
  352.3 7.7 %collective-permute-done.69.refs_7_ = bf16[144,2048]{1,0:T(8,128)(2,1)S(1)} collective-permute-done((bf16[144,2048]{1,0:T(8,128)(2,1)}, bf16[144,2048]{1,0:T(8,128)(2,1)S(1)}, u32[]{:S(2)}, u32[]{:S(2)}) %collective-permute-start.69) | collective-permute-done | bytes 589856 | tf_op jit(solution)/shard_map/ppermute | solution.py:68
  360.8 4.3 %joined_weights.1 = (f32[4,56,2048]{2,1,0:T(8,128)}, bf16[4,56,2048]{2,1,0:T(8,128)(2,1)}) custom-call(bf16[128,384]{1,0:T(8,128)(2,1)} %get-tuple-element.232.refs_0_, bf16[128,384]{1,0:T(8,128)(2,1)} %get-tuple-element.214.refs_1_, bf16[128,384]{1,0:T(8,128)(2,1)} %get-tuple-element.212.refs_2_, bf16[128,384]{1,0:T(8,128)(2,1)} %get-tuple-element.210.refs_3_, ...), custom_call_target="tpu_custom_call" | custom-call | flops 1375000064 | tf_op jit(solution)/shard_map/joined_weights/pallas_call | solution.py:263
  365.1 2.7 collective-permute-start.70
  371.3 2.2 collective-permute-start.71
  373.7 9.1 %reduce-scatter.2.cloned.1.call-done.grad_ref = bf16[280,4608]{1,0:T(8,128)(2,1)} async-done(((bf16[1120,4608]{1,0:T(8,128)(2,1)}), bf16[280,4608]{1,0:T(8,128)(2,1)}) %reduce-scatter.2.cloned.1.call-update) | async-done | bytes 2580496 | tf_op jit(solution)/shard_map/reduce_scatter | solution.py:772
  382.8 14.3 %units_step.1 = (f32[3,280,1536]{2,1,0:T(8,128)}, f32[3,280,1536]{2,1,0:T(8,128)}, f32[3,280,1536]{2,1,0:T(8,128)}, bf16[3,280,1536]{2,1,0:T(8,128)(2,1)}) custom-call(bf16[280,4608]{1,0:T(8,128)(2,1)} %reduce-scatter.2.cloned.1.call-done.grad_ref, f32[3,280,1536]{2,1,0:T(8,128)} %bitcast.138, f32[3,280,1536]{2,1,0:T(8,128)} %bitcast.151, ...), custom_call_target="tpu_custom_call" | custom-call | flops 3300000000 | tf_op jit(solution)/shard_map/units_step/pallas_call | solution.py:530
  397.1 2.7 collective-permute-done.72
  402.4 8.9 %collective-permute-done.78 = bf16[48,1536]{1,0:T(8,128)(2,1)} collective-permute-done((bf16[48,1536]{1,0:T(8,128)(2,1)S(1)}, bf16[48,1536]{1,0:T(8,128)(2,1)}, u32[]{:S(2)}, u32[]{:S(2)}) %collective-permute-start.78) | collective-permute-done | bytes 147488 | tf_op jit(solution)/shard_map/ppermute | solution.py:50
  411.2 2.5 fusion.76
  414.5 2.2 fusion.73
  (390 shorter events, 88.5 us)
Async XLA Ops:
  7.2 188.4 %all-gather.2.cloned.1.call-start = ((), (), s32[]{:S(2)}) async-start(), calls=%async_computation.1 | async-start | bytes 12902400 | tf_op jit(solution)/shard_map/all_gather | solution.py:693
  11.5 371.3 %reduce-scatter.2.cloned.1.call-start = ((), (), s32[]{:S(2)}) async-start(), calls=%async_computation.2 | async-start | bytes 12902400 | tf_op jit(solution)/shard_map/reduce_scatter | solution.py:772
  17.5 9.8 %collective-permute-start.10 = (bf16[48,2048]{1,0:T(8,128)(2,1)S(1)}, bf16[48,2048]{1,0:T(8,128)(2,1)S(1)}, u32[]{:S(2)}, u32[]{:S(2)}) collective-permute-start(bf16[48,2048]{1,0:T(8,128)(2,1)S(1)} %convert_element_type.160), channel_id=1, source_target_pairs={{0,8},{8,16},{16,24},{24,0},{1,9},{9,17},{17,25},{25,1},{2,10},{10... | collective-permute-start | bytes 589832 | tf_op jit(solution)/shard_map/ppermute | solution.py:50
  20.5 14.6 %collective-permute-start.11 = (bf16[48,2048]{1,0:T(8,128)(2,1)S(1)}, bf16[48,2048]{1,0:T(8,128)(2,1)S(1)}, u32[]{:S(2)}, u32[]{:S(2)}) collective-permute-start(bf16[48,2048]{1,0:T(8,128)(2,1)S(1)} %convert_element_type.160), channel_id=1, source_target_pairs={{0,16},{8,24},{16,0},{24,8},{1,17},{9,25},{17,1},{25,9},{2,18},{10... | collective-permute-start | bytes 589832 | tf_op jit(solution)/shard_map/ppermute | solution.py:50
  21.0 14.2 %collective-permute-start.12 = (bf16[128,1536]{1,0:T(8,128)(2,1)S(1)}, bf16[128,1536]{1,0:T(8,128)(2,1)S(1)}, u32[]{:S(2)}, u32[]{:S(2)}) collective-permute-start(bf16[128,1536]{1,0:T(8,128)(2,1)S(1)} %copy-done.26), channel_id=1, source_target_pairs={{0,2},{2,0},{1,3},{3,1},{4,6},{6,4},{5,7},{7,5},{8,10},{10,8},{9,1... | collective-permute-start | bytes 1179656 | tf_op jit(solution)/shard_map/ppermute | solution.py:50
  24.6 11.4 %collective-permute-start.13 = (bf16[128,1536]{1,0:T(8,128)(2,1)S(1)}, bf16[128,1536]{1,0:T(8,128)(2,1)}, u32[]{:S(2)}, u32[]{:S(2)}) collective-permute-start(bf16[128,1536]{1,0:T(8,128)(2,1)S(1)} %copy-done.26), channel_id=1, source_target_pairs={{0,4},{4,0},{1,5},{5,1},{2,6},{6,2},{3,7},{7,3},{8,12},{12,8},{9,1... | collective-permute-start | bytes 1179656 | tf_op jit(solution)/shard_map/ppermute | solution.py:50
  24.7 12.8 %collective-permute-start.8 = (f32[1,5120]{1,0:T(1,128)S(1)}, f32[1,5120]{1,0:T(1,128)S(1)}, u32[]{:S(2)}, u32[]{:S(2)}) collective-permute-start(f32[1,5120]{1,0:T(1,128)S(1)} %add.886), channel_id=1, source_target_pairs={{0,2},{2,0},{1,3},{3,1},{4,6},{6,4},{5,7},{7,5},{8,10},{10,8},{9,1... | collective-permute-start | bytes 61448 | tf_op jit(solution)/shard_map/ppermute | solution.py:50
  36.0 37.2 %collective-permute-start.14 = (bf16[4,48,2048]{2,1,0:T(8,128)(2,1)S(1)}, bf16[4,48,2048]{2,1,0:T(8,128)(2,1)S(1)}, u32[]{:S(2)}, u32[]{:S(2)}) collective-permute-start(bf16[4,48,2048]{2,1,0:T(8,128)(2,1)S(1)} %pad_maximum_fusion.refs_6_.refs_2_), channel_id=1, source_target_pairs={{0,2},{2,0},{1,3},{3,1},{4,6},{6,4},{5,7},{7,5},{8,10},{10,8},{9,1... | collective-permute-start | bytes 2359304 | tf_op jit(solution)/shard_map/ppermute | solution.py:50
  36.4 36.8 %collective-permute-start.15 = (bf16[4,48,2048]{2,1,0:T(8,128)(2,1)S(1)}, bf16[4,48,2048]{2,1,0:T(8,128)(2,1)S(1)}, u32[]{:S(2)}, u32[]{:S(2)}) collective-permute-start(bf16[4,48,2048]{2,1,0:T(8,128)(2,1)S(1)} %pad_maximum_fusion.refs_6_.refs_2_), channel_id=1, source_target_pairs={{0,4},{4,0},{1,5},{5,1},{2,6},{6,2},{3,7},{7,3},{8,12},{12,8},{9,1... | collective-permute-start | bytes 2359304 | tf_op jit(solution)/shard_map/ppermute | solution.py:50
  37.5 13.3 %collective-permute-start.9 = (f32[1,5120]{1,0:T(1,128)S(1)}, f32[1,5120]{1,0:T(1,128)S(1)}, u32[]{:S(2)}, u32[]{:S(2)}) collective-permute-start(f32[1,5120]{1,0:T(1,128)S(1)} %add.887), channel_id=1, source_target_pairs={{0,4},{4,0},{1,5},{5,1},{2,6},{6,2},{3,7},{7,3},{8,12},{12,8},{9,1... | collective-permute-start | bytes 61448 | tf_op jit(solution)/shard_map/ppermute | solution.py:50
  40.0 31.9 %collective-permute-start.1 = (bf16[128,1536]{1,0:T(8,128)(2,1)S(1)}, bf16[128,1536]{1,0:T(8,128)(2,1)}, u32[]{:S(2)}, u32[]{:S(2)}) collective-permute-start(bf16[128,1536]{1,0:T(8,128)(2,1)S(1)} %copy-done.26), channel_id=1, source_target_pairs={{0,16},{16,0},{1,17},{17,1},{2,18},{18,2},{3,19},{19,3},{4,20},{20... | collective-permute-start | bytes 1179656 | tf_op jit(solution)/shard_map/ppermute | solution.py:50
  43.1 29.1 %collective-permute-start.16 = (bf16[128,1536]{1,0:T(8,128)(2,1)}, bf16[128,1536]{1,0:T(8,128)(2,1)}, u32[]{:S(2)}, u32[]{:S(2)}) collective-permute-start(bf16[128,1536]{1,0:T(8,128)(2,1)} %copy-done.45), channel_id=1, source_target_pairs={{0,4},{4,0},{1,5},{5,1},{2,6},{6,2},{3,7},{7,3},{8,12},{12,8},{9,1... | collective-permute-start | bytes 1179656 | tf_op jit(solution)/shard_map/ppermute | solution.py:50
  51.0 16.4 %collective-permute-start.29 = (bf16[48,1536]{1,0:T(8,128)(2,1)S(1)}, bf16[48,1536]{1,0:T(8,128)(2,1)}, u32[]{:S(2)}, u32[]{:S(2)}) collective-permute-start(bf16[48,1536]{1,0:T(8,128)(2,1)S(1)} %convert_element_type.165), channel_id=1, source_target_pairs={{0,8},{8,16},{16,24},{24,0},{1,9},{9,17},{17,25},{25,1},{2,10},{10... | collective-permute-start | bytes 442376 | tf_op jit(solution)/shard_map/ppermute | solution.py:50
  67.4 22.5 %collective-permute-start.19 = (bf16[4,48,2048]{2,1,0:T(8,128)(2,1)S(1)}, bf16[4,48,2048]{2,1,0:T(8,128)(2,1)}, u32[]{:S(2)}, u32[]{:S(2)}) collective-permute-start(bf16[4,48,2048]{2,1,0:T(8,128)(2,1)S(1)} %pad_maximum_fusion.refs_6_.refs_2_), channel_id=1, source_target_pairs={{0,1},{1,0},{2,3},{3,2},{4,5},{5,4},{6,7},{7,6},{8,9},{9,8},{10,11... | collective-permute-start | bytes 2359304 | tf_op jit(solution)/shard_map/ppermute | solution.py:50
  71.9 14.8 %collective-permute-start.2 = (bf16[128,1536]{1,0:T(8,128)(2,1)}, bf16[128,1536]{1,0:T(8,128)(2,1)S(1)}, u32[]{:S(2)}, u32[]{:S(2)}) collective-permute-start(bf16[128,1536]{1,0:T(8,128)(2,1)} %collective-permute-done.1.refs_18_), channel_id=1, source_target_pairs={{0,4},{4,0},{1,5},{5,1},{2,6},{6,2},{3,7},{7,3},{8,12},{12,8},{9,1... | collective-permute-start | bytes 1179656 | tf_op jit(solution)/shard_map/ppermute | solution.py:50
  72.1 16.0 %collective-permute-start.3 = (bf16[128,1536]{1,0:T(8,128)(2,1)}, bf16[128,1536]{1,0:T(8,128)(2,1)}, u32[]{:S(2)}, u32[]{:S(2)}) collective-permute-start(bf16[128,1536]{1,0:T(8,128)(2,1)} %collective-permute-done.1.refs_18_), channel_id=1, source_target_pairs={{0,2},{2,0},{1,3},{3,1},{4,6},{6,4},{5,7},{7,5},{8,10},{10,8},{9,1... | collective-permute-start | bytes 1179656 | tf_op jit(solution)/shard_map/ppermute | solution.py:50
  73.3 12.8 %collective-permute-start.31 = (bf16[48,1536]{1,0:T(8,128)(2,1)S(1)}, bf16[48,1536]{1,0:T(8,128)(2,1)S(1)}, u32[]{:S(2)}, u32[]{:S(2)}) collective-permute-start(bf16[48,1536]{1,0:T(8,128)(2,1)S(1)} %convert_element_type.165), channel_id=1, source_target_pairs={{0,24},{8,0},{16,8},{24,16},{1,25},{9,1},{17,9},{25,17},{2,26},{10... | collective-permute-start | bytes 442376 | tf_op jit(solution)/shard_map/ppermute | solution.py:50
  79.8 11.3 %collective-permute-start.17 = (bf16[4,48,1024]{2,1,0:T(8,128)(2,1)S(1)}, bf16[4,48,1024]{2,1,0:T(8,128)(2,1)S(1)}, u32[]{:S(2)}, u32[]{:S(2)}) collective-permute-start(bf16[4,48,1024]{2,1,0:T(8,128)(2,1)S(1)} %slice.286), channel_id=1, source_target_pairs={{0,4},{4,0},{1,5},{5,1},{2,6},{6,2},{3,7},{7,3},{8,12},{12,8},{9,1... | collective-permute-start | bytes 1179656 | tf_op jit(solution)/shard_map/ppermute | solution.py:50
  86.1 9.6 %collective-permute-start.18 = (bf16[4,48,1024]{2,1,0:T(8,128)(2,1)S(1)}, bf16[4,48,1024]{2,1,0:T(8,128)(2,1)S(1)}, u32[]{:S(2)}, u32[]{:S(2)}) collective-permute-start(bf16[4,48,1024]{2,1,0:T(8,128)(2,1)S(1)} %slice.287), channel_id=1, source_target_pairs={{0,2},{2,0},{1,3},{3,1},{4,6},{6,4},{5,7},{7,5},{8,10},{10,8},{9,1... | collective-permute-start | bytes 1179656 | tf_op jit(solution)/shard_map/ppermute | solution.py:50
  86.7 12.3 %collective-permute-start.20 = (bf16[4,48,2048]{2,1,0:T(8,128)(2,1)S(1)}, bf16[4,48,2048]{2,1,0:T(8,128)(2,1)S(1)}, u32[]{:S(2)}, u32[]{:S(2)}) collective-permute-start(bf16[4,48,2048]{2,1,0:T(8,128)(2,1)S(1)} %collective-permute-done.14.refs_7_.refs_3_), channel_id=1, source_target_pairs={{0,1},{1,0},{2,3},{3,2},{4,5},{5,4},{6,7},{7,6},{8,9},{9,8},{10,11... | collective-permute-start | bytes 2359304 | tf_op jit(solution)/shard_map/ppermute | solution.py:50
  88.1 10.9 %collective-permute-start.21 = (bf16[4,48,2048]{2,1,0:T(8,128)(2,1)S(1)}, bf16[4,48,2048]{2,1,0:T(8,128)(2,1)S(1)}, u32[]{:S(2)}, u32[]{:S(2)}) collective-permute-start(bf16[4,48,2048]{2,1,0:T(8,128)(2,1)S(1)} %collective-permute-done.15.refs_8_.refs_4_), channel_id=1, source_target_pairs={{0,1},{1,0},{2,3},{3,2},{4,5},{5,4},{6,7},{7,6},{8,9},{9,8},{10,11... | collective-permute-start | bytes 2359304 | tf_op jit(solution)/shard_map/ppermute | solution.py:50
  89.9 19.4 %collective-permute-start.33 = (bf16[4,48,1536]{2,1,0:T(8,128)(2,1)S(1)}, bf16[4,48,1536]{2,1,0:T(8,128)(2,1)S(1)}, u32[]{:S(2)}, u32[]{:S(2)}) collective-permute-start(bf16[4,48,1536]{2,1,0:T(8,128)(2,1)S(1)} %pad_maximum_fusion.1.refs_7_.refs_6_), channel_id=1, source_target_pairs={{0,4},{4,0},{1,5},{5,1},{2,6},{6,2},{3,7},{7,3},{8,12},{12,8},{9,1... | collective-permute-start | bytes 1769480 | tf_op jit(solution)/shard_map/ppermute | solution.py:50
  98.3 24.6 %collective-permute-start.32 = (bf16[4,48,1536]{2,1,0:T(8,128)(2,1)S(1)}, bf16[4,48,1536]{2,1,0:T(8,128)(2,1)S(1)}, u32[]{:S(2)}, u32[]{:S(2)}) collective-permute-start(bf16[4,48,1536]{2,1,0:T(8,128)(2,1)S(1)} %pad_maximum_fusion.1.refs_7_.refs_6_), channel_id=1, source_target_pairs={{0,2},{2,0},{1,3},{3,1},{4,6},{6,4},{5,7},{7,5},{8,10},{10,8},{9,1... | collective-permute-start | bytes 1769480 | tf_op jit(solution)/shard_map/ppermute | solution.py:50
  106.4 9.6 %collective-permute-start.25 = (bf16[128,512]{1,0:T(8,128)(2,1)}, bf16[128,512]{1,0:T(8,128)(2,1)S(1)}, u32[]{:S(2)}, u32[]{:S(2)}) collective-permute-start(bf16[128,512]{1,0:T(8,128)(2,1)} %get-tuple-element.78), channel_id=1, source_target_pairs={{0,2},{2,0},{4,6},{6,4},{1,3},{3,1},{5,7},{7,5},{8,10},{10,8},{12,... | collective-permute-start | bytes 393224 | tf_op jit(solution)/shard_map/ppermute | solution.py:68
  107.2 9.4 %collective-permute-start.26 = (bf16[128,512]{1,0:T(8,128)(2,1)}, bf16[128,512]{1,0:T(8,128)(2,1)S(1)}, u32[]{:S(2)}, u32[]{:S(2)}) collective-permute-start(bf16[128,512]{1,0:T(8,128)(2,1)} %get-tuple-element.78), channel_id=1, source_target_pairs={{0,4},{2,6},{4,0},{6,2},{1,5},{3,7},{5,1},{7,3},{8,12},{10,14},{12... | collective-permute-start | bytes 393224 | tf_op jit(solution)/shard_map/ppermute | solution.py:68
  108.4 11.3 %collective-permute-start.27 = (bf16[128,512]{1,0:T(8,128)(2,1)}, bf16[128,512]{1,0:T(8,128)(2,1)S(1)}, u32[]{:S(2)}, u32[]{:S(2)}) collective-permute-start(bf16[128,512]{1,0:T(8,128)(2,1)} %get-tuple-element.78), channel_id=1, source_target_pairs={{0,6},{2,4},{4,2},{6,0},{1,7},{3,5},{5,3},{7,1},{8,14},{10,12},{12... | collective-permute-start | bytes 393224 | tf_op jit(solution)/shard_map/ppermute | solution.py:68
  109.2 18.1 %collective-permute-start.24 = (bf16[128,1536]{1,0:T(8,128)(2,1)S(1)}, bf16[128,1536]{1,0:T(8,128)(2,1)}, u32[]{:S(2)}, u32[]{:S(2)}) collective-permute-start(bf16[128,1536]{1,0:T(8,128)(2,1)S(1)} %copy-done.48), channel_id=1, source_target_pairs={{0,2},{2,0},{1,3},{3,1},{4,6},{6,4},{5,7},{7,5},{8,10},{10,8},{9,1... | collective-permute-start | bytes 1179656 | tf_op jit(solution)/shard_map/ppermute | solution.py:50
  116.1 17.6 %collective-permute-start.35 = (bf16[4,48,768]{2,1,0:T(8,128)(2,1)S(1)}, bf16[4,48,768]{2,1,0:T(8,128)(2,1)S(1)}, u32[]{:S(2)}, u32[]{:S(2)}) collective-permute-start(bf16[4,48,768]{2,1,0:T(8,128)(2,1)S(1)} %slice.290), channel_id=1, source_target_pairs={{0,2},{2,0},{1,3},{3,1},{4,6},{6,4},{5,7},{7,5},{8,10},{10,8},{9,1... | collective-permute-start | bytes 884744 | tf_op jit(solution)/shard_map/ppermute | solution.py:50
  121.5 15.4 %collective-permute-start.28 = (bf16[512,512]{1,0:T(8,128)(2,1)}, bf16[512,512]{1,0:T(8,128)(2,1)}, u32[]{:S(2)}, u32[]{:S(2)}) collective-permute-start(bf16[512,512]{1,0:T(8,128)(2,1)} %pad_maximum_fusion.2), channel_id=1, source_target_pairs={{0,1},{1,0},{2,3},{3,2},{4,5},{5,4},{6,7},{7,6},{8,9},{9,8},{10,11... | collective-permute-start | bytes 1572872 | tf_op jit(solution)/shard_map/ppermute | solution.py:50
  122.8 15.7 %collective-permute-start.36 = (bf16[4,48,1536]{2,1,0:T(8,128)(2,1)S(1)}, bf16[4,48,1536]{2,1,0:T(8,128)(2,1)S(1)}, u32[]{:S(2)}, u32[]{:S(2)}) collective-permute-start(bf16[4,48,1536]{2,1,0:T(8,128)(2,1)S(1)} %pad_maximum_fusion.1.refs_7_.refs_6_), channel_id=1, source_target_pairs={{0,1},{1,0},{2,3},{3,2},{4,5},{5,4},{6,7},{7,6},{8,9},{9,8},{10,11... | collective-permute-start | bytes 1769480 | tf_op jit(solution)/shard_map/ppermute | solution.py:50
  123.6 13.1 %collective-permute-start.34 = (bf16[4,48,768]{2,1,0:T(8,128)(2,1)}, bf16[4,48,768]{2,1,0:T(8,128)(2,1)}, u32[]{:S(2)}, u32[]{:S(2)}) collective-permute-start(bf16[4,48,768]{2,1,0:T(8,128)(2,1)} %slice.289), channel_id=1, source_target_pairs={{0,4},{4,0},{1,5},{5,1},{2,6},{6,2},{3,7},{7,3},{8,12},{12,8},{9,1... | collective-permute-start | bytes 884744 | tf_op jit(solution)/shard_map/ppermute | solution.py:50
  127.3 11.7 %collective-permute-start.37 = (bf16[4,48,1536]{2,1,0:T(8,128)(2,1)S(1)}, bf16[4,48,1536]{2,1,0:T(8,128)(2,1)S(1)}, u32[]{:S(2)}, u32[]{:S(2)}) collective-permute-start(bf16[4,48,1536]{2,1,0:T(8,128)(2,1)S(1)} %collective-permute-done.32.refs_8_.refs_7_), channel_id=1, source_target_pairs={{0,1},{1,0},{2,3},{3,2},{4,5},{5,4},{6,7},{7,6},{8,9},{9,8},{10,11... | collective-permute-start | bytes 1769480 | tf_op jit(solution)/shard_map/ppermute | solution.py:50
  150.3 26.8 %collective-permute-start.44 = (bf16[128,1536]{1,0:T(8,128)(2,1)}, bf16[128,1536]{1,0:T(8,128)(2,1)S(1)}, u32[]{:S(2)}, u32[]{:S(2)}) collective-permute-start(bf16[128,1536]{1,0:T(8,128)(2,1)} %get-tuple-element.84.refs_6_), channel_id=1, source_target_pairs={{0,16},{16,0},{1,17},{17,1},{2,18},{18,2},{3,19},{19,3},{4,20},{20... | collective-permute-start | bytes 1179656 | tf_op jit(solution)/shard_map/ppermute | solution.py:50
  155.4 22.9 %collective-permute-start.41 = (bf16[128,1536]{1,0:T(8,128)(2,1)}, bf16[128,1536]{1,0:T(8,128)(2,1)S(1)}, u32[]{:S(2)}, u32[]{:S(2)}) collective-permute-start(bf16[128,1536]{1,0:T(8,128)(2,1)} %get-tuple-element.84.refs_6_), channel_id=1, source_target_pairs={{0,2},{2,0},{1,3},{3,1},{4,6},{6,4},{5,7},{7,5},{8,10},{10,8},{9,1... | collective-permute-start | bytes 1179656 | tf_op jit(solution)/shard_map/ppermute | solution.py:50
  155.9 22.9 %collective-permute-start.42 = (bf16[128,1536]{1,0:T(8,128)(2,1)}, bf16[128,1536]{1,0:T(8,128)(2,1)S(1)}, u32[]{:S(2)}, u32[]{:S(2)}) collective-permute-start(bf16[128,1536]{1,0:T(8,128)(2,1)} %get-tuple-element.84.refs_6_), channel_id=1, source_target_pairs={{0,4},{4,0},{1,5},{5,1},{2,6},{6,2},{3,7},{7,3},{8,12},{12,8},{9,1... | collective-permute-start | bytes 1179656 | tf_op jit(solution)/shard_map/ppermute | solution.py:50
  163.1 11.5 %collective-permute-start.46 = (bf16[128,768]{1,0:T(8,128)(2,1)S(1)}, bf16[128,768]{1,0:T(8,128)(2,1)S(1)}, u32[]{:S(2)}, u32[]{:S(2)}) collective-permute-start(bf16[128,768]{1,0:T(8,128)(2,1)S(1)} %pad_maximum_fusion.4), channel_id=1, source_target_pairs={{0,4},{2,6},{4,0},{6,2},{1,5},{3,7},{5,1},{7,3},{8,12},{10,14},{12... | collective-permute-start | bytes 589832 | tf_op jit(solution)/shard_map/ppermute | solution.py:68
  178.3 15.7 %collective-permute-start.43 = (bf16[128,1536]{1,0:T(8,128)(2,1)S(1)}, bf16[128,1536]{1,0:T(8,128)(2,1)S(1)}, u32[]{:S(2)}, u32[]{:S(2)}) collective-permute-start(bf16[128,1536]{1,0:T(8,128)(2,1)S(1)} %collective-permute-done.41.refs_7_), channel_id=1, source_target_pairs={{0,4},{4,0},{1,5},{5,1},{2,6},{6,2},{3,7},{7,3},{8,12},{12,8},{9,1... | collective-permute-start | bytes 1179656 | tf_op jit(solution)/shard_map/ppermute | solution.py:50
  215.8 15.2 %collective-permute-start.53 = (bf16[256,1536]{1,0:T(8,128)(2,1)S(1)}, bf16[256,1536]{1,0:T(8,128)(2,1)S(1)}, u32[]{:S(2)}, u32[]{:S(2)}) collective-permute-start(bf16[256,1536]{1,0:T(8,128)(2,1)S(1)} %slice.398), channel_id=1, source_target_pairs={{0,2},{2,0},{1,3},{3,1},{4,6},{6,4},{5,7},{7,5},{8,10},{10,8},{9,1... | collective-permute-start | bytes 2359304 | tf_op jit(solution)/shard_map/ppermute | solution.py:50
  227.0 14.6 %collective-permute-start.51 = (bf16[256,1536]{1,0:T(8,128)(2,1)S(1)}, bf16[256,1536]{1,0:T(8,128)(2,1)S(1)}, u32[]{:S(2)}, u32[]{:S(2)}) collective-permute-start(bf16[256,1536]{1,0:T(8,128)(2,1)S(1)} %slice.399), channel_id=1, source_target_pairs={{0,4},{4,0},{1,5},{5,1},{2,6},{6,2},{3,7},{7,3},{8,12},{12,8},{9,1... | collective-permute-start | bytes 2359304 | tf_op jit(solution)/shard_map/ppermute | solution.py:50
  231.3 18.8 %collective-permute-start.54 = (bf16[128,1536]{1,0:T(8,128)(2,1)S(1)}, bf16[128,1536]{1,0:T(8,128)(2,1)S(1)}, u32[]{:S(2)}, u32[]{:S(2)}) collective-permute-start(bf16[128,1536]{1,0:T(8,128)(2,1)S(1)} %slice.403), channel_id=1, source_target_pairs={{0,4},{4,0},{1,5},{5,1},{2,6},{6,2},{3,7},{7,3},{8,12},{12,8},{9,1... | collective-permute-start | bytes 1179656 | tf_op jit(solution)/shard_map/ppermute | solution.py:50
  241.9 10.0 %collective-permute-start.52 = (bf16[128,1536]{1,0:T(8,128)(2,1)S(1)}, bf16[128,1536]{1,0:T(8,128)(2,1)S(1)}, u32[]{:S(2)}, u32[]{:S(2)}) collective-permute-start(bf16[128,1536]{1,0:T(8,128)(2,1)S(1)} %slice.404), channel_id=1, source_target_pairs={{0,2},{2,0},{1,3},{3,1},{4,6},{6,4},{5,7},{7,5},{8,10},{10,8},{9,1... | collective-permute-start | bytes 1179656 | tf_op jit(solution)/shard_map/ppermute | solution.py:50
  250.1 22.3 %collective-permute-start.57 = (bf16[128,1536]{1,0:T(8,128)(2,1)S(1)}, bf16[128,1536]{1,0:T(8,128)(2,1)}, u32[]{:S(2)}, u32[]{:S(2)}) collective-permute-start(bf16[128,1536]{1,0:T(8,128)(2,1)S(1)} %slice_add_fusion.4), channel_id=1, source_target_pairs={{0,16},{16,0},{1,17},{17,1},{2,18},{18,2},{3,19},{19,3},{4,20},{20... | collective-permute-start | bytes 1179656 | tf_op jit(solution)/shard_map/ppermute | solution.py:50
  270.0 36.3 %collective-permute-start.55 = (bf16[256,1536]{1,0:T(8,128)(2,1)}, bf16[256,1536]{1,0:T(8,128)(2,1)}, u32[]{:S(2)}, u32[]{:S(2)}) collective-permute-start(bf16[256,1536]{1,0:T(8,128)(2,1)} %slice.254), channel_id=1, source_target_pairs={{0,4},{4,0},{1,5},{5,1},{2,6},{6,2},{3,7},{7,3},{8,12},{12,8},{9,1... | collective-permute-start | bytes 2359304 | tf_op jit(solution)/shard_map/ppermute | solution.py:50
  271.9 35.8 %collective-permute-start.64 = (bf16[256,1536]{1,0:T(8,128)(2,1)}, bf16[256,1536]{1,0:T(8,128)(2,1)}, u32[]{:S(2)}, u32[]{:S(2)}) collective-permute-start(bf16[256,1536]{1,0:T(8,128)(2,1)} %slice.264), channel_id=1, source_target_pairs={{0,2},{2,0},{1,3},{3,1},{4,6},{6,4},{5,7},{7,5},{8,10},{10,8},{9,1... | collective-permute-start | bytes 2359304 | tf_op jit(solution)/shard_map/ppermute | solution.py:50
  279.3 13.8 %collective-permute-start.58 = (bf16[128,1536]{1,0:T(8,128)(2,1)}, bf16[128,1536]{1,0:T(8,128)(2,1)}, u32[]{:S(2)}, u32[]{:S(2)}) collective-permute-start(bf16[128,1536]{1,0:T(8,128)(2,1)} %get-tuple-element.95.refs_4_), channel_id=1, source_target_pairs={{0,2},{2,0},{4,6},{6,4},{1,3},{3,1},{5,7},{7,5},{8,10},{10,8},{12,... | collective-permute-start | bytes 1179656 | tf_op jit(solution)/shard_map/ppermute | solution.py:68
  280.3 12.8 %collective-permute-start.59 = (bf16[128,1536]{1,0:T(8,128)(2,1)}, bf16[128,1536]{1,0:T(8,128)(2,1)}, u32[]{:S(2)}, u32[]{:S(2)}) collective-permute-start(bf16[128,1536]{1,0:T(8,128)(2,1)} %get-tuple-element.95.refs_4_), channel_id=1, source_target_pairs={{0,4},{2,6},{4,0},{6,2},{1,5},{3,7},{5,1},{7,3},{8,12},{10,14},{12... | collective-permute-start | bytes 1179656 | tf_op jit(solution)/shard_map/ppermute | solution.py:68
  280.8 52.8 %collective-permute-start.74 = (bf16[128,1536]{1,0:T(8,128)(2,1)}, bf16[128,1536]{1,0:T(8,128)(2,1)}, u32[]{:S(2)}, u32[]{:S(2)}) collective-permute-start(bf16[128,1536]{1,0:T(8,128)(2,1)} %get-tuple-element.95.refs_4_), channel_id=1, source_target_pairs={{0,6},{2,4},{4,2},{6,0},{1,7},{3,5},{5,3},{7,1},{8,14},{10,12},{12... | collective-permute-start | bytes 1179656 | tf_op jit(solution)/shard_map/ppermute | solution.py:68
  294.5 15.4 %collective-permute-start.60 = (bf16[512,512]{1,0:T(8,128)(2,1)S(1)}, bf16[512,512]{1,0:T(8,128)(2,1)S(1)}, u32[]{:S(2)}, u32[]{:S(2)}) collective-permute-start(bf16[512,512]{1,0:T(8,128)(2,1)S(1)} %slice.400), channel_id=1, source_target_pairs={{0,1},{1,0},{2,3},{3,2},{4,5},{5,4},{6,7},{7,6},{8,9},{9,8},{10,11... | collective-permute-start | bytes 1572872 | tf_op jit(solution)/shard_map/ppermute | solution.py:50
  309.3 21.6 %collective-permute-start.65 = (bf16[128,1536]{1,0:T(8,128)(2,1)S(1)}, bf16[128,1536]{1,0:T(8,128)(2,1)S(1)}, u32[]{:S(2)}, u32[]{:S(2)}) collective-permute-start(bf16[128,1536]{1,0:T(8,128)(2,1)S(1)} %slice.401), channel_id=1, source_target_pairs={{0,4},{4,0},{1,5},{5,1},{2,6},{6,2},{3,7},{7,3},{8,12},{12,8},{9,1... | collective-permute-start | bytes 1179656 | tf_op jit(solution)/shard_map/ppermute | solution.py:50
  310.1 11.0 %collective-permute-start.61 = (bf16[128,512]{1,0:T(8,128)(2,1)S(1)}, bf16[128,512]{1,0:T(8,128)(2,1)S(1)}, u32[]{:S(2)}, u32[]{:S(2)}) collective-permute-start(bf16[128,512]{1,0:T(8,128)(2,1)S(1)} %get-tuple-element.200), channel_id=1, source_target_pairs={{0,2},{2,0},{4,6},{6,4},{1,3},{3,1},{5,7},{7,5},{8,10},{10,8},{12,... | collective-permute-start | bytes 393224 | tf_op jit(solution)/shard_map/ppermute | solution.py:68
  311.5 14.3 %collective-permute-start.62 = (bf16[128,512]{1,0:T(8,128)(2,1)S(1)}, bf16[128,512]{1,0:T(8,128)(2,1)S(1)}, u32[]{:S(2)}, u32[]{:S(2)}) collective-permute-start(bf16[128,512]{1,0:T(8,128)(2,1)S(1)} %get-tuple-element.199), channel_id=1, source_target_pairs={{0,4},{2,6},{4,0},{6,2},{1,5},{3,7},{5,1},{7,3},{8,12},{10,14},{12... | collective-permute-start | bytes 393224 | tf_op jit(solution)/shard_map/ppermute | solution.py:68
  311.7 14.1 %collective-permute-start.63 = (bf16[128,512]{1,0:T(8,128)(2,1)S(1)}, bf16[128,512]{1,0:T(8,128)(2,1)S(1)}, u32[]{:S(2)}, u32[]{:S(2)}) collective-permute-start(bf16[128,512]{1,0:T(8,128)(2,1)S(1)} %get-tuple-element.198), channel_id=1, source_target_pairs={{0,6},{2,4},{4,2},{6,0},{1,7},{3,5},{5,3},{7,1},{8,14},{10,12},{12... | collective-permute-start | bytes 393224 | tf_op jit(solution)/shard_map/ppermute | solution.py:68
  321.2 18.1 %collective-permute-start.56 = (bf16[128,1536]{1,0:T(8,128)(2,1)S(1)}, bf16[128,1536]{1,0:T(8,128)(2,1)}, u32[]{:S(2)}, u32[]{:S(2)}) collective-permute-start(bf16[128,1536]{1,0:T(8,128)(2,1)S(1)} %slice.402), channel_id=1, source_target_pairs={{0,2},{2,0},{1,3},{3,1},{4,6},{6,4},{5,7},{7,5},{8,10},{10,8},{9,1... | collective-permute-start | bytes 1179656 | tf_op jit(solution)/shard_map/ppermute | solution.py:50
  331.0 19.3 %collective-permute-start.66 = (bf16[128,1536]{1,0:T(8,128)(2,1)S(1)}, bf16[128,1536]{1,0:T(8,128)(2,1)S(1)}, u32[]{:S(2)}, u32[]{:S(2)}) collective-permute-start(bf16[128,1536]{1,0:T(8,128)(2,1)S(1)} %fusion.24), channel_id=1, source_target_pairs={{0,16},{16,0},{1,17},{17,1},{2,18},{18,2},{3,19},{19,3},{4,20},{20... | collective-permute-start | bytes 1179656 | tf_op jit(solution)/shard_map/ppermute | solution.py:50
  333.1 19.1 %collective-permute-start.67 = (bf16[144,2048]{1,0:T(8,128)(2,1)}, bf16[144,2048]{1,0:T(8,128)(2,1)S(1)}, u32[]{:S(2)}, u32[]{:S(2)}) collective-permute-start(bf16[144,2048]{1,0:T(8,128)(2,1)} %get-tuple-element.103.refs_4_), channel_id=1, source_target_pairs={{0,2},{2,0},{4,6},{6,4},{1,3},{3,1},{5,7},{7,5},{8,10},{10,8},{12,... | collective-permute-start | bytes 1769480 | tf_op jit(solution)/shard_map/ppermute | solution.py:68
  333.3 19.0 %collective-permute-start.68 = (bf16[144,2048]{1,0:T(8,128)(2,1)}, bf16[144,2048]{1,0:T(8,128)(2,1)S(1)}, u32[]{:S(2)}, u32[]{:S(2)}) collective-permute-start(bf16[144,2048]{1,0:T(8,128)(2,1)} %get-tuple-element.103.refs_4_), channel_id=1, source_target_pairs={{0,4},{2,6},{4,0},{6,2},{1,5},{3,7},{5,1},{7,3},{8,12},{10,14},{12... | collective-permute-start | bytes 1769480 | tf_op jit(solution)/shard_map/ppermute | solution.py:68
  333.6 26.4 %collective-permute-start.69 = (bf16[144,2048]{1,0:T(8,128)(2,1)}, bf16[144,2048]{1,0:T(8,128)(2,1)S(1)}, u32[]{:S(2)}, u32[]{:S(2)}) collective-permute-start(bf16[144,2048]{1,0:T(8,128)(2,1)} %get-tuple-element.103.refs_4_), channel_id=1, source_target_pairs={{0,6},{2,4},{4,2},{6,0},{1,7},{3,5},{5,3},{7,1},{8,14},{10,12},{12... | collective-permute-start | bytes 1769480 | tf_op jit(solution)/shard_map/ppermute | solution.py:68
  339.3 28.5 %collective-permute-start.75 = (bf16[192,1536]{1,0:T(8,128)(2,1)}, bf16[192,1536]{1,0:T(8,128)(2,1)S(1)}, u32[]{:S(2)}, u32[]{:S(2)}) collective-permute-start(bf16[192,1536]{1,0:T(8,128)(2,1)} %get-tuple-element.117), channel_id=1, source_target_pairs={{0,1},{1,0},{2,3},{3,2},{4,5},{5,4},{6,7},{7,6},{8,9},{9,8},{10,11... | collective-permute-start | bytes 1769480 | tf_op jit(solution)/shard_map/ppermute | solution.py:50
  368.7 33.6 %collective-permute-start.76 = (bf16[48,1536]{1,0:T(8,128)(2,1)}, bf16[48,1536]{1,0:T(8,128)(2,1)}, u32[]{:S(2)}, u32[]{:S(2)}) collective-permute-start(bf16[48,1536]{1,0:T(8,128)(2,1)} %get-tuple-element.195), channel_id=1, source_target_pairs={{0,24},{8,0},{16,8},{24,16},{1,25},{9,1},{17,9},{25,17},{2,26},{10... | collective-permute-start | bytes 442376 | tf_op jit(solution)/shard_map/ppermute | solution.py:50
  368.7 33.6 %collective-permute-start.77 = (bf16[48,1536]{1,0:T(8,128)(2,1)}, bf16[48,1536]{1,0:T(8,128)(2,1)}, u32[]{:S(2)}, u32[]{:S(2)}) collective-permute-start(bf16[48,1536]{1,0:T(8,128)(2,1)} %get-tuple-element.197), channel_id=1, source_target_pairs={{0,16},{8,24},{16,0},{24,8},{1,17},{9,25},{17,1},{25,9},{2,18},{10... | collective-permute-start | bytes 442376 | tf_op jit(solution)/shard_map/ppermute | solution.py:50
  371.3 25.8 %collective-permute-start.71 = (bf16[56,2048]{1,0:T(8,128)(2,1)}, bf16[56,2048]{1,0:T(8,128)(2,1)}, u32[]{:S(2)}, u32[]{:S(2)}) collective-permute-start(bf16[56,2048]{1,0:T(8,128)(2,1)} %get-tuple-element.192), channel_id=1, source_target_pairs={{0,24},{8,0},{16,8},{24,16},{1,25},{9,1},{17,9},{25,17},{2,26},{10... | collective-permute-start | bytes 688136 | tf_op jit(solution)/shard_map/ppermute | solution.py:50
  373.5 26.4 %collective-permute-start.72 = (bf16[56,2048]{1,0:T(8,128)(2,1)}, bf16[56,2048]{1,0:T(8,128)(2,1)}, u32[]{:S(2)}, u32[]{:S(2)}) collective-permute-start(bf16[56,2048]{1,0:T(8,128)(2,1)} %get-tuple-element.194), channel_id=1, source_target_pairs={{0,16},{8,24},{16,0},{24,8},{1,17},{9,25},{17,1},{25,9},{2,18},{10... | collective-permute-start | bytes 688136 | tf_op jit(solution)/shard_map/ppermute | solution.py:50
  373.5 26.4 %collective-permute-start.73 = (bf16[56,2048]{1,0:T(8,128)(2,1)}, bf16[56,2048]{1,0:T(8,128)(2,1)}, u32[]{:S(2)}, u32[]{:S(2)}) collective-permute-start(bf16[56,2048]{1,0:T(8,128)(2,1)} %get-tuple-element.193), channel_id=1, source_target_pairs={{0,8},{8,16},{16,24},{24,0},{1,9},{9,17},{17,25},{25,1},{2,10},{10... | collective-permute-start | bytes 688136 | tf_op jit(solution)/shard_map/ppermute | solution.py:50
  397.1 14.2 %collective-permute-start.78 = (bf16[48,1536]{1,0:T(8,128)(2,1)S(1)}, bf16[48,1536]{1,0:T(8,128)(2,1)}, u32[]{:S(2)}, u32[]{:S(2)}) collective-permute-start(bf16[48,1536]{1,0:T(8,128)(2,1)S(1)} %get-tuple-element.196), channel_id=1, source_target_pairs={{0,8},{8,16},{16,24},{24,0},{1,9},{9,17},{17,25},{25,1},{2,10},{10... | collective-permute-start | bytes 442376 | tf_op jit(solution)/shard_map/ppermute | solution.py:50
  (87 other events, 861.3 us)
Sparse Core Ops, SparseCore 0:
  11.6 122.2 all-gather.1
  269.2 113.5 reduce-scatter.1

commit v6 on v5

--- a/solution.py
+++ b/solution.py
@@ -523,13 +523,13 @@
 
 def units_step(grad, weight, first, second):
     units = grad.shape[0]
-    width = D // 2
-    block = pl.BlockSpec((1, units, width), lambda i: (i // 2, 0, i % 2))
+    width = D // 4
+    block = pl.BlockSpec((1, units, width), lambda i: (i // 4, 0, i % 4))
     turn = lambda value: jnp.transpose(value, (1, 0, 2))
     dtypes = [jnp.float32] * 3 + [jnp.bfloat16]
     results = pl.pallas_call(
         units_step_kernel,
-        grid=(6,),
+        grid=(12,),
         in_specs=[pl.BlockSpec((units, width), lambda i: (0, i))] + [block] * 3,
         out_specs=[block] * 4,
         out_shape=[shaped((3, units, D), dtype) for dtype in dtypes],

time: 431 us -> 434 us (level)
  transfers between devices with their start and end apart: 81 -> 81, of which waited for: 29 -> 28; matrix products, arithmetic and copies ran while one was open for 11% -> 11% of each run, Pallas kernels for 20% -> 21%
where the time goes in v6:
time: 434 us; the launch traced here: 427 us
  waiting for transfers between devices  142 us (33%)
  starting transfers between devices  95.7 us (22%)
  Pallas kernels  87.8 us (20%)
  matrix products  36.5 us (8%)
  local copies, waits for them, and re-layouts  24.9 us (6%)
  other arithmetic  24.4 us (6%)
  between operations  15.9 us (4%)
    ppermute x64, waiting for transfers between devices, shift(): lax.ppermute(value, axis, [(i, (i + step) % count) for i in range(count)])  102 us
    ppermute x64, starting transfers between devices, shift(): lax.ppermute(value, axis, [(i, (i + step) % count) for i in range(count)])  82 us
    pallas_call x4, Pallas kernels, call_with_pieces(): pl.pallas_call(run, out_shape=outs, in_specs=[SCALARS] + [pl.BlockSpec(me...  30.8 us
    ppermute x15, waiting for transfers between devices, plane_shift(): return lax.ppermute(value, ('y', 'x'), pairs)  30.5 us
    pallas_call x4, Pallas kernels, local_call(): pl.pallas_call(kernel, out_shape=outs, scratch_shapes=list(scratch), comp...  23.2 us
    dot_general x6, matrix products, body(): jnp.einsum('ud,td->ut', rows, tokens, preferred_element_type=jnp.float32)  18.6 us
    pallas_call x1, Pallas kernels, units_step(): pl.pallas_call(units_step_kernel, grid=(12,), in_specs=[pl.BlockSpec((uni...  17.4 us
    pallas_call x1, Pallas kernels, units_gradient(): pl.pallas_call(lambda *refs: gradient_kernel(len(parts), size, *refs), gr...  16.3 us
  transfers between devices with their start and end apart: 81, of which 28 were waited for; matrix products, arithmetic and copies ran while one was open for 11% of the time, Pallas kernels for 21%

profile of v6, /device:TPU:7, one launch (start us, length us, event | category | flops | bytes accessed | tf_op | source)
XLA Modules:
  0.0 427.1 jit_solution(443029679706112017)
XLA Ops:
  7.2 4.3 convert_element_type.166
  13.9 2.3 collective-permute-start.5
  21.4 2.4 collective-permute-start.7
  27.4 7.7 %collective-permute-done.11 = bf16[48,2048]{1,0:T(8,128)(2,1)S(1)} collective-permute-done((bf16[48,2048]{1,0:T(8,128)(2,1)S(1)}, bf16[48,2048]{1,0:T(8,128)(2,1)S(1)}, u32[]{:S(2)}, u32[]{:S(2)}) %collective-permute-start.11) | collective-permute-done | bytes 196640 | tf_op jit(solution)/shard_map/ppermute | solution.py:50
  40.0 3.1 collective-permute-start.1
  43.6 7.3 %collective-permute-done.9 = f32[1,5120]{1,0:T(1,128)S(1)} collective-permute-done((f32[1,5120]{1,0:T(1,128)S(1)}, f32[1,5120]{1,0:T(1,128)S(1)}, u32[]{:S(2)}, u32[]{:S(2)}) %collective-permute-start.9) | collective-permute-done | bytes 20512 | tf_op jit(solution)/shard_map/ppermute | solution.py:50
  51.0 4.3 %collective-permute-start.29 = (bf16[48,1536]{1,0:T(8,128)(2,1)S(1)}, bf16[48,1536]{1,0:T(8,128)(2,1)}, u32[]{:S(2)}, u32[]{:S(2)}) collective-permute-start(bf16[48,1536]{1,0:T(8,128)(2,1)S(1)} %convert_element_type.165), channel_id=1, source_target_pairs={{0,8},{8,16},{16,24},{24,0},{1,9},{9,17},{17,25},{25,1},{2,10},{10... | collective-permute-start | bytes 442376 | tf_op jit(solution)/shard_map/ppermute | solution.py:50
  55.8 11.6 %collective-permute-done.29 = bf16[48,1536]{1,0:T(8,128)(2,1)} collective-permute-done((bf16[48,1536]{1,0:T(8,128)(2,1)S(1)}, bf16[48,1536]{1,0:T(8,128)(2,1)}, u32[]{:S(2)}, u32[]{:S(2)}) %collective-permute-start.29) | collective-permute-done | bytes 147488 | tf_op jit(solution)/shard_map/ppermute | solution.py:50
  67.4 4.5 %collective-permute-start.19 = (bf16[4,48,2048]{2,1,0:T(8,128)(2,1)S(1)}, bf16[4,48,2048]{2,1,0:T(8,128)(2,1)}, u32[]{:S(2)}, u32[]{:S(2)}) collective-permute-start(bf16[4,48,2048]{2,1,0:T(8,128)(2,1)S(1)} %pad_maximum_fusion.refs_6_.refs_2_), channel_id=1, source_target_pairs={{0,1},{1,0},{2,3},{3,2},{4,5},{5,4},{6,7},{7,6},{8,9},{9,8},{10,11... | collective-permute-start | bytes 2359304 | tf_op jit(solution)/shard_map/ppermute | solution.py:50
  73.3 4.0 collective-permute-start.31
  77.6 2.2 collective-permute-done.30
  81.0 5.1 %collective-permute-done.31 = bf16[48,1536]{1,0:T(8,128)(2,1)S(1)} collective-permute-done((bf16[48,1536]{1,0:T(8,128)(2,1)S(1)}, bf16[48,1536]{1,0:T(8,128)(2,1)S(1)}, u32[]{:S(2)}, u32[]{:S(2)}) %collective-permute-start.31) | collective-permute-done | bytes 147488 | tf_op jit(solution)/shard_map/ppermute | solution.py:50
  92.1 3.6 collective-permute-done.18.refs_10_.refs_6_
  95.7 1.9 collective-permute-start.23
  100.3 6.1 %front.1 = (bf16[128,1536]{1,0:T(8,128)(2,1)}, bf16[128,1536]{1,0:T(8,128)(2,1)}, bf16[128,512]{1,0:T(8,128)(2,1)}) custom-call(s32[40]{0:T(128)} %stack.220.refs_0_, bf16[128,1536]{1,0:T(8,128)(2,1)} %refs_9_.1, f32[1,1536]{1,0:T(1,128)} %get-tuple-element.231.refs_2_.refs_10_, f32[1,2048]{1,0:T(1,128)} %slice.283.refs_3_, ...), custom_call_target="tpu_custom_call" | custom-call | flops 1650000000 | tf_op jit(solution)/shard_map/front/pallas_call | solution.py:245
  110.1 6.0 %collective-permute-done.25 = bf16[128,512]{1,0:T(8,128)(2,1)S(1)} collective-permute-done((bf16[128,512]{1,0:T(8,128)(2,1)}, bf16[128,512]{1,0:T(8,128)(2,1)S(1)}, u32[]{:S(2)}, u32[]{:S(2)}) %collective-permute-start.25) | collective-permute-done | bytes 131104 | tf_op jit(solution)/shard_map/ppermute | solution.py:68
  116.6 3.1 collective-permute-done.27
  119.7 1.7 pad_maximum_fusion.2
  123.8 3.5 collective-permute-done.24.refs_21_
  128.6 5.0 %collective-permute-done.35.refs_11_.refs_10_ = bf16[4,48,768]{2,1,0:T(8,128)(2,1)S(1)} collective-permute-done((bf16[4,48,768]{2,1,0:T(8,128)(2,1)S(1)}, bf16[4,48,768]{2,1,0:T(8,128)(2,1)S(1)}, u32[]{:S(2)}, u32[]{:S(2)}) %collective-permute-start.35) | collective-permute-done | bytes 294944 | tf_op jit(solution)/shard_map/ppermute | solution.py:50
  140.0 10.3 %attend.1 = (bf16[128,1536]{1,0:T(8,128)(2,1)}, f32[128,1536]{1,0:T(8,128)}, bf16[128,1536]{1,0:T(8,128)(2,1)}) custom-call(s32[40]{0:T(128)} %stack.220.refs_0_, bf16[128,1536]{1,0:T(8,128)(2,1)} %get-tuple-element.77.refs_1_.query_ref, bf16[1024,512]{1,0:T(8,128)(2,1)} %copy-done.60, s32[1024,2]{1,0:T(8,128)} %copy.77.refs_3_.key_marks_ref, ...), custom_call_target="tpu_custom_call" | custom-call | flops 3300000000 | tf_op jit(solution)/shard_map/attend/pallas_call | solution.py:245
  150.3 5.1 %collective-permute-start.44 = (bf16[128,1536]{1,0:T(8,128)(2,1)}, bf16[128,1536]{1,0:T(8,128)(2,1)S(1)}, u32[]{:S(2)}, u32[]{:S(2)}) collective-permute-start(bf16[128,1536]{1,0:T(8,128)(2,1)} %get-tuple-element.84.refs_6_), channel_id=1, source_target_pairs={{0,16},{16,0},{1,17},{17,1},{2,18},{18,2},{3,19},{19,3},{4,20},{20... | collective-permute-start | bytes 1179656 | tf_op jit(solution)/shard_map/ppermute | solution.py:50
  156.9 2.1 fusion.4
  159.0 2.1 fusion.5
  164.5 6.7 %collective-permute-done.47 = bf16[128,768]{1,0:T(8,128)(2,1)S(1)} collective-permute-done((bf16[128,768]{1,0:T(8,128)(2,1)S(1)}, bf16[128,768]{1,0:T(8,128)(2,1)S(1)}, u32[]{:S(2)}, u32[]{:S(2)}) %collective-permute-start.47) | collective-permute-done | bytes 196640 | tf_op jit(solution)/shard_map/ppermute | solution.py:68
  172.2 2.4 collective-permute-done.46
  178.9 6.6 %collective-permute-done.48.refs_11_ = bf16[128,1536]{1,0:T(8,128)(2,1)S(1)} collective-permute-done((bf16[128,1536]{1,0:T(8,128)(2,1)S(1)}, bf16[128,1536]{1,0:T(8,128)(2,1)S(1)}, u32[]{:S(2)}, u32[]{:S(2)}) %collective-permute-start.48) | collective-permute-done | bytes 393248 | tf_op jit(solution)/shard_map/ppermute | solution.py:50
  185.9 8.1 %collective-permute-done.43.refs_9_ = bf16[128,1536]{1,0:T(8,128)(2,1)S(1)} collective-permute-done((bf16[128,1536]{1,0:T(8,128)(2,1)S(1)}, bf16[128,1536]{1,0:T(8,128)(2,1)S(1)}, u32[]{:S(2)}, u32[]{:S(2)}) %collective-permute-start.43) | collective-permute-done | bytes 393248 | tf_op jit(solution)/shard_map/ppermute | solution.py:50
  195.6 4.1 convolution_bitcast_fusion.4
  200.6 2.0 convolution_bitcast_fusion.5
  202.6 2.0 convolution_bitcast_fusion
  204.6 3.2 convolution_bitcast_fusion.2
  207.9 3.2 multiply_convert_fusion
  211.1 2.3 fusion.8
  213.4 2.3 convolution_add_fusion
  216.1 4.0 multiply_convert_fusion.3
  220.2 2.2 fusion.9
  222.4 2.2 convolution_add_fusion.1
  224.7 2.3 convolution_convert_fusion
  228.5 2.5 convolution_convert_fusion.1
  231.4 10.2 %collective-permute-done.51 = bf16[256,1536]{1,0:T(8,128)(2,1)S(1)} collective-permute-done((bf16[256,1536]{1,0:T(8,128)(2,1)S(1)}, bf16[256,1536]{1,0:T(8,128)(2,1)S(1)}, u32[]{:S(2)}, u32[]{:S(2)}) %collective-permute-start.51) | collective-permute-done | bytes 786464 | tf_op jit(solution)/shard_map/ppermute | solution.py:50
  243.1 7.0 %collective-permute-done.54 = bf16[128,1536]{1,0:T(8,128)(2,1)S(1)} collective-permute-done((bf16[128,1536]{1,0:T(8,128)(2,1)S(1)}, bf16[128,1536]{1,0:T(8,128)(2,1)S(1)}, u32[]{:S(2)}, u32[]{:S(2)}) %collective-permute-start.54) | collective-permute-done | bytes 393248 | tf_op jit(solution)/shard_map/ppermute | solution.py:50
  252.8 16.3 %units_gradient.1 = bf16[1120,4608]{1,0:T(8,128)(2,1)} custom-call(bf16[1120,512]{1,0:T(8,128)(2,1)} %copy-done.4, bf16[1120,512]{1,0:T(8,128)(2,1)} %copy-done.3, bf16[1120,512]{1,0:T(8,128)(2,1)} %copy-done.35, bf16[1120,512]{1,0:T(8,128)(2,1)} %copy-done.1, bf16[1120,512]{1,0:T(8,128)(2,1)} %copy-done.2, bf16[1120,512]{1,0:T(8,128)(2,1)} %copy-done.34, ...), custom_call_target="tpu_custom_call" | custom-call | flops 2200000000 | tf_op jit(solution)/shard_map/units_gradient/pallas_call | solution.py:498
  272.4 6.8 %middle_back.1 = (f32[128,1536]{1,0:T(8,128)}, bf16[128,1536]{1,0:T(8,128)(2,1)}, f32[1,1536]{1,0:T(1,128)}, bf16[128,1536]{1,0:T(8,128)(2,1)}) custom-call(s32[40]{0:T(128)} %stack.220.refs_0_, f32[128,1536]{1,0:T(8,128)} %slice_add_fusion.5.refs_1_, bf16[128,1536]{1,0:T(8,128)(2,1)} %collective-permute-done.57.refs_2_, ...), custom_call_target="tpu_custom_call" | custom-call | flops 1100000000 | tf_op jit(solution)/shard_map/middle_back/pallas_call | solution.py:245
  282.0 11.1 %attend_back.1 = (bf16[128,1536]{1,0:T(8,128)(2,1)}, f32[1024,512]{1,0:T(8,128)}) custom-call(bf16[128,1536]{1,0:T(8,128)(2,1)} %get-tuple-element.93.attended_grad_ref, bf16[128,1536]{1,0:T(8,128)(2,1)} %get-tuple-element.77.refs_1_.query_ref, bf16[1024,512]{1,0:T(8,128)(2,1)} %copy-done.60, s32[1024,2]{1,0:T(8,128)} %copy.77.refs_3_.key_marks_ref, ...), custom_call_target="tpu_custom_call" | custom-call | flops 219999993856 | tf_op jit(solution)/shard_map/attend_back/pallas_call | solution.py:263
  294.5 11.9 %collective-permute-start.60 = (bf16[512,512]{1,0:T(8,128)(2,1)S(1)}, bf16[512,512]{1,0:T(8,128)(2,1)S(1)}, u32[]{:S(2)}, u32[]{:S(2)}) collective-permute-start(bf16[512,512]{1,0:T(8,128)(2,1)S(1)} %slice.400), channel_id=1, source_target_pairs={{0,1},{1,0},{2,3},{3,2},{4,5},{5,4},{6,7},{7,6},{8,9},{9,8},{10,11... | collective-permute-start | bytes 1572872 | tf_op jit(solution)/shard_map/ppermute | solution.py:50
  313.6 7.6 %query_back.1 = (f32[128,1536]{1,0:T(8,128)}, bf16[1536,512]{1,0:T(8,128)(2,1)}) custom-call(s32[40]{0:T(128)} %stack.220.refs_0_, bf16[128,1536]{1,0:T(8,128)(2,1)} %get-tuple-element.98.refs_1_.refs_6_, bf16[4,48,2048]{2,1,0:T(8,128)(2,1)} %copy-done.7, bf16[4,48,2048]{2,1,0:T(8,128)(2,1)} %copy-done.12, bf16[4,48,2048]{2,1,0:T(8,128)(2,1)} %copy-done.13, ...), custom_call_target="tpu_custom_call" | custom-call | flops 1924999936 | tf_op jit(solution)/shard_map/query_back/pallas_call | solution.py:245
  322.4 3.4 collective-permute-done.62.refs_2_
  326.5 4.4 %finish.1 = (bf16[144,2048]{1,0:T(8,128)(2,1)}, f32[128,1536]{1,0:T(8,128)}) custom-call(f32[128,512]{1,0:T(8,128)} %slice.319.refs_0_, bf16[128,512]{1,0:T(8,128)(2,1)} %copy-done.55, bf16[128,512]{1,0:T(8,128)(2,1)} %copy-done.56, bf16[128,512]{1,0:T(8,128)(2,1)} %copy-done.57, f32[128,128]{1,0:T(8,128)} %get-tuple-element.229.refs_4_.cosine_ref, ...), custom_call_target="tpu_custom_call" | custom-call | flops 1100000000 | tf_op jit(solution)/shard_map/finish/pallas_call | solution.py:263
  331.0 2.1 collective-permute-start.66
  333.6 2.2 collective-permute-start.69
  335.8 3.5 out_weights.1
  339.3 1.7 collective-permute-start.75
  341.0 9.3 %collective-permute-done.66 = bf16[128,1536]{1,0:T(8,128)(2,1)S(1)} collective-permute-done((bf16[128,1536]{1,0:T(8,128)(2,1)S(1)}, bf16[128,1536]{1,0:T(8,128)(2,1)S(1)}, u32[]{:S(2)}, u32[]{:S(2)}) %collective-permute-start.66) | collective-permute-done | bytes 393248 | tf_op jit(solution)/shard_map/ppermute | solution.py:50
  350.3 1.9 fusion.27
  352.3 7.7 %collective-permute-done.69.refs_7_ = bf16[144,2048]{1,0:T(8,128)(2,1)S(1)} collective-permute-done((bf16[144,2048]{1,0:T(8,128)(2,1)}, bf16[144,2048]{1,0:T(8,128)(2,1)S(1)}, u32[]{:S(2)}, u32[]{:S(2)}) %collective-permute-start.69) | collective-permute-done | bytes 589856 | tf_op jit(solution)/shard_map/ppermute | solution.py:68
  360.8 4.3 joined_weights.1
  365.1 2.7 collective-permute-start.70
  371.3 2.2 collective-permute-start.71
  373.7 9.1 %reduce-scatter.2.cloned.1.call-done.grad_ref = bf16[280,4608]{1,0:T(8,128)(2,1)} async-done(((bf16[1120,4608]{1,0:T(8,128)(2,1)}), bf16[280,4608]{1,0:T(8,128)(2,1)}) %reduce-scatter.2.cloned.1.call-update) | async-done | bytes 2580496 | tf_op jit(solution)/shard_map/reduce_scatter | solution.py:772
  382.8 17.4 %units_step.1 = (f32[3,280,1536]{2,1,0:T(8,128)}, f32[3,280,1536]{2,1,0:T(8,128)}, f32[3,280,1536]{2,1,0:T(8,128)}, bf16[3,280,1536]{2,1,0:T(8,128)(2,1)}) custom-call(bf16[280,4608]{1,0:T(8,128)(2,1)} %reduce-scatter.2.cloned.1.call-done.grad_ref, f32[3,280,1536]{2,1,0:T(8,128)} %bitcast.138, f32[3,280,1536]{2,1,0:T(8,128)} %bitcast.151, ...), custom_call_target="tpu_custom_call" | custom-call | flops 3300000000 | tf_op jit(solution)/shard_map/units_step/pallas_call | solution.py:530
  402.9 11.5 %collective-permute-done.78 = bf16[48,1536]{1,0:T(8,128)(2,1)} collective-permute-done((bf16[48,1536]{1,0:T(8,128)(2,1)S(1)}, bf16[48,1536]{1,0:T(8,128)(2,1)}, u32[]{:S(2)}, u32[]{:S(2)}) %collective-permute-start.78) | collective-permute-done | bytes 147488 | tf_op jit(solution)/shard_map/ppermute | solution.py:50
  414.4 2.5 fusion.76
  417.6 2.2 fusion.73
  (390 shorter events, 86.8 us)
Async XLA Ops:
  7.2 188.4 %all-gather.2.cloned.1.call-start = ((), (), s32[]{:S(2)}) async-start(), calls=%async_computation.1 | async-start | bytes 12902400 | tf_op jit(solution)/shard_map/all_gather | solution.py:693
  11.5 371.3 %reduce-scatter.2.cloned.1.call-start = ((), (), s32[]{:S(2)}) async-start(), calls=%async_computation.2 | async-start | bytes 12902400 | tf_op jit(solution)/shard_map/reduce_scatter | solution.py:772
  17.5 9.8 %collective-permute-start.10 = (bf16[48,2048]{1,0:T(8,128)(2,1)S(1)}, bf16[48,2048]{1,0:T(8,128)(2,1)S(1)}, u32[]{:S(2)}, u32[]{:S(2)}) collective-permute-start(bf16[48,2048]{1,0:T(8,128)(2,1)S(1)} %convert_element_type.160), channel_id=1, source_target_pairs={{0,8},{8,16},{16,24},{24,0},{1,9},{9,17},{17,25},{25,1},{2,10},{10... | collective-permute-start | bytes 589832 | tf_op jit(solution)/shard_map/ppermute | solution.py:50
  20.5 14.6 %collective-permute-start.11 = (bf16[48,2048]{1,0:T(8,128)(2,1)S(1)}, bf16[48,2048]{1,0:T(8,128)(2,1)S(1)}, u32[]{:S(2)}, u32[]{:S(2)}) collective-permute-start(bf16[48,2048]{1,0:T(8,128)(2,1)S(1)} %convert_element_type.160), channel_id=1, source_target_pairs={{0,16},{8,24},{16,0},{24,8},{1,17},{9,25},{17,1},{25,9},{2,18},{10... | collective-permute-start | bytes 589832 | tf_op jit(solution)/shard_map/ppermute | solution.py:50
  21.0 14.2 %collective-permute-start.12 = (bf16[128,1536]{1,0:T(8,128)(2,1)S(1)}, bf16[128,1536]{1,0:T(8,128)(2,1)S(1)}, u32[]{:S(2)}, u32[]{:S(2)}) collective-permute-start(bf16[128,1536]{1,0:T(8,128)(2,1)S(1)} %copy-done.26), channel_id=1, source_target_pairs={{0,2},{2,0},{1,3},{3,1},{4,6},{6,4},{5,7},{7,5},{8,10},{10,8},{9,1... | collective-permute-start | bytes 1179656 | tf_op jit(solution)/shard_map/ppermute | solution.py:50
  24.6 11.4 %collective-permute-start.13 = (bf16[128,1536]{1,0:T(8,128)(2,1)S(1)}, bf16[128,1536]{1,0:T(8,128)(2,1)}, u32[]{:S(2)}, u32[]{:S(2)}) collective-permute-start(bf16[128,1536]{1,0:T(8,128)(2,1)S(1)} %copy-done.26), channel_id=1, source_target_pairs={{0,4},{4,0},{1,5},{5,1},{2,6},{6,2},{3,7},{7,3},{8,12},{12,8},{9,1... | collective-permute-start | bytes 1179656 | tf_op jit(solution)/shard_map/ppermute | solution.py:50
  24.7 12.8 %collective-permute-start.8 = (f32[1,5120]{1,0:T(1,128)S(1)}, f32[1,5120]{1,0:T(1,128)S(1)}, u32[]{:S(2)}, u32[]{:S(2)}) collective-permute-start(f32[1,5120]{1,0:T(1,128)S(1)} %add.886), channel_id=1, source_target_pairs={{0,2},{2,0},{1,3},{3,1},{4,6},{6,4},{5,7},{7,5},{8,10},{10,8},{9,1... | collective-permute-start | bytes 61448 | tf_op jit(solution)/shard_map/ppermute | solution.py:50
  36.0 37.2 %collective-permute-start.14 = (bf16[4,48,2048]{2,1,0:T(8,128)(2,1)S(1)}, bf16[4,48,2048]{2,1,0:T(8,128)(2,1)S(1)}, u32[]{:S(2)}, u32[]{:S(2)}) collective-permute-start(bf16[4,48,2048]{2,1,0:T(8,128)(2,1)S(1)} %pad_maximum_fusion.refs_6_.refs_2_), channel_id=1, source_target_pairs={{0,2},{2,0},{1,3},{3,1},{4,6},{6,4},{5,7},{7,5},{8,10},{10,8},{9,1... | collective-permute-start | bytes 2359304 | tf_op jit(solution)/shard_map/ppermute | solution.py:50
  36.4 36.8 %collective-permute-start.15 = (bf16[4,48,2048]{2,1,0:T(8,128)(2,1)S(1)}, bf16[4,48,2048]{2,1,0:T(8,128)(2,1)S(1)}, u32[]{:S(2)}, u32[]{:S(2)}) collective-permute-start(bf16[4,48,2048]{2,1,0:T(8,128)(2,1)S(1)} %pad_maximum_fusion.refs_6_.refs_2_), channel_id=1, source_target_pairs={{0,4},{4,0},{1,5},{5,1},{2,6},{6,2},{3,7},{7,3},{8,12},{12,8},{9,1... | collective-permute-start | bytes 2359304 | tf_op jit(solution)/shard_map/ppermute | solution.py:50
  37.5 13.3 %collective-permute-start.9 = (f32[1,5120]{1,0:T(1,128)S(1)}, f32[1,5120]{1,0:T(1,128)S(1)}, u32[]{:S(2)}, u32[]{:S(2)}) collective-permute-start(f32[1,5120]{1,0:T(1,128)S(1)} %add.887), channel_id=1, source_target_pairs={{0,4},{4,0},{1,5},{5,1},{2,6},{6,2},{3,7},{7,3},{8,12},{12,8},{9,1... | collective-permute-start | bytes 61448 | tf_op jit(solution)/shard_map/ppermute | solution.py:50
  40.0 31.9 %collective-permute-start.1 = (bf16[128,1536]{1,0:T(8,128)(2,1)S(1)}, bf16[128,1536]{1,0:T(8,128)(2,1)}, u32[]{:S(2)}, u32[]{:S(2)}) collective-permute-start(bf16[128,1536]{1,0:T(8,128)(2,1)S(1)} %copy-done.26), channel_id=1, source_target_pairs={{0,16},{16,0},{1,17},{17,1},{2,18},{18,2},{3,19},{19,3},{4,20},{20... | collective-permute-start | bytes 1179656 | tf_op jit(solution)/shard_map/ppermute | solution.py:50
  43.1 29.1 %collective-permute-start.16 = (bf16[128,1536]{1,0:T(8,128)(2,1)}, bf16[128,1536]{1,0:T(8,128)(2,1)}, u32[]{:S(2)}, u32[]{:S(2)}) collective-permute-start(bf16[128,1536]{1,0:T(8,128)(2,1)} %copy-done.45), channel_id=1, source_target_pairs={{0,4},{4,0},{1,5},{5,1},{2,6},{6,2},{3,7},{7,3},{8,12},{12,8},{9,1... | collective-permute-start | bytes 1179656 | tf_op jit(solution)/shard_map/ppermute | solution.py:50
  51.0 16.4 %collective-permute-start.29 = (bf16[48,1536]{1,0:T(8,128)(2,1)S(1)}, bf16[48,1536]{1,0:T(8,128)(2,1)}, u32[]{:S(2)}, u32[]{:S(2)}) collective-permute-start(bf16[48,1536]{1,0:T(8,128)(2,1)S(1)} %convert_element_type.165), channel_id=1, source_target_pairs={{0,8},{8,16},{16,24},{24,0},{1,9},{9,17},{17,25},{25,1},{2,10},{10... | collective-permute-start | bytes 442376 | tf_op jit(solution)/shard_map/ppermute | solution.py:50
  67.4 22.5 %collective-permute-start.19 = (bf16[4,48,2048]{2,1,0:T(8,128)(2,1)S(1)}, bf16[4,48,2048]{2,1,0:T(8,128)(2,1)}, u32[]{:S(2)}, u32[]{:S(2)}) collective-permute-start(bf16[4,48,2048]{2,1,0:T(8,128)(2,1)S(1)} %pad_maximum_fusion.refs_6_.refs_2_), channel_id=1, source_target_pairs={{0,1},{1,0},{2,3},{3,2},{4,5},{5,4},{6,7},{7,6},{8,9},{9,8},{10,11... | collective-permute-start | bytes 2359304 | tf_op jit(solution)/shard_map/ppermute | solution.py:50
  71.9 14.8 %collective-permute-start.2 = (bf16[128,1536]{1,0:T(8,128)(2,1)}, bf16[128,1536]{1,0:T(8,128)(2,1)S(1)}, u32[]{:S(2)}, u32[]{:S(2)}) collective-permute-start(bf16[128,1536]{1,0:T(8,128)(2,1)} %collective-permute-done.1.refs_18_), channel_id=1, source_target_pairs={{0,4},{4,0},{1,5},{5,1},{2,6},{6,2},{3,7},{7,3},{8,12},{12,8},{9,1... | collective-permute-start | bytes 1179656 | tf_op jit(solution)/shard_map/ppermute | solution.py:50
  72.1 16.0 %collective-permute-start.3 = (bf16[128,1536]{1,0:T(8,128)(2,1)}, bf16[128,1536]{1,0:T(8,128)(2,1)}, u32[]{:S(2)}, u32[]{:S(2)}) collective-permute-start(bf16[128,1536]{1,0:T(8,128)(2,1)} %collective-permute-done.1.refs_18_), channel_id=1, source_target_pairs={{0,2},{2,0},{1,3},{3,1},{4,6},{6,4},{5,7},{7,5},{8,10},{10,8},{9,1... | collective-permute-start | bytes 1179656 | tf_op jit(solution)/shard_map/ppermute | solution.py:50
  73.3 12.8 %collective-permute-start.31 = (bf16[48,1536]{1,0:T(8,128)(2,1)S(1)}, bf16[48,1536]{1,0:T(8,128)(2,1)S(1)}, u32[]{:S(2)}, u32[]{:S(2)}) collective-permute-start(bf16[48,1536]{1,0:T(8,128)(2,1)S(1)} %convert_element_type.165), channel_id=1, source_target_pairs={{0,24},{8,0},{16,8},{24,16},{1,25},{9,1},{17,9},{25,17},{2,26},{10... | collective-permute-start | bytes 442376 | tf_op jit(solution)/shard_map/ppermute | solution.py:50
  79.8 11.3 %collective-permute-start.17 = (bf16[4,48,1024]{2,1,0:T(8,128)(2,1)S(1)}, bf16[4,48,1024]{2,1,0:T(8,128)(2,1)S(1)}, u32[]{:S(2)}, u32[]{:S(2)}) collective-permute-start(bf16[4,48,1024]{2,1,0:T(8,128)(2,1)S(1)} %slice.286), channel_id=1, source_target_pairs={{0,4},{4,0},{1,5},{5,1},{2,6},{6,2},{3,7},{7,3},{8,12},{12,8},{9,1... | collective-permute-start | bytes 1179656 | tf_op jit(solution)/shard_map/ppermute | solution.py:50
  86.1 9.6 %collective-permute-start.18 = (bf16[4,48,1024]{2,1,0:T(8,128)(2,1)S(1)}, bf16[4,48,1024]{2,1,0:T(8,128)(2,1)S(1)}, u32[]{:S(2)}, u32[]{:S(2)}) collective-permute-start(bf16[4,48,1024]{2,1,0:T(8,128)(2,1)S(1)} %slice.287), channel_id=1, source_target_pairs={{0,2},{2,0},{1,3},{3,1},{4,6},{6,4},{5,7},{7,5},{8,10},{10,8},{9,1... | collective-permute-start | bytes 1179656 | tf_op jit(solution)/shard_map/ppermute | solution.py:50
  86.7 12.3 %collective-permute-start.20 = (bf16[4,48,2048]{2,1,0:T(8,128)(2,1)S(1)}, bf16[4,48,2048]{2,1,0:T(8,128)(2,1)S(1)}, u32[]{:S(2)}, u32[]{:S(2)}) collective-permute-start(bf16[4,48,2048]{2,1,0:T(8,128)(2,1)S(1)} %collective-permute-done.14.refs_7_.refs_3_), channel_id=1, source_target_pairs={{0,1},{1,0},{2,3},{3,2},{4,5},{5,4},{6,7},{7,6},{8,9},{9,8},{10,11... | collective-permute-start | bytes 2359304 | tf_op jit(solution)/shard_map/ppermute | solution.py:50
  88.1 10.9 %collective-permute-start.21 = (bf16[4,48,2048]{2,1,0:T(8,128)(2,1)S(1)}, bf16[4,48,2048]{2,1,0:T(8,128)(2,1)S(1)}, u32[]{:S(2)}, u32[]{:S(2)}) collective-permute-start(bf16[4,48,2048]{2,1,0:T(8,128)(2,1)S(1)} %collective-permute-done.15.refs_8_.refs_4_), channel_id=1, source_target_pairs={{0,1},{1,0},{2,3},{3,2},{4,5},{5,4},{6,7},{7,6},{8,9},{9,8},{10,11... | collective-permute-start | bytes 2359304 | tf_op jit(solution)/shard_map/ppermute | solution.py:50
  89.9 19.4 %collective-permute-start.33 = (bf16[4,48,1536]{2,1,0:T(8,128)(2,1)S(1)}, bf16[4,48,1536]{2,1,0:T(8,128)(2,1)S(1)}, u32[]{:S(2)}, u32[]{:S(2)}) collective-permute-start(bf16[4,48,1536]{2,1,0:T(8,128)(2,1)S(1)} %pad_maximum_fusion.1.refs_7_.refs_6_), channel_id=1, source_target_pairs={{0,4},{4,0},{1,5},{5,1},{2,6},{6,2},{3,7},{7,3},{8,12},{12,8},{9,1... | collective-permute-start | bytes 1769480 | tf_op jit(solution)/shard_map/ppermute | solution.py:50
  98.3 24.6 %collective-permute-start.32 = (bf16[4,48,1536]{2,1,0:T(8,128)(2,1)S(1)}, bf16[4,48,1536]{2,1,0:T(8,128)(2,1)S(1)}, u32[]{:S(2)}, u32[]{:S(2)}) collective-permute-start(bf16[4,48,1536]{2,1,0:T(8,128)(2,1)S(1)} %pad_maximum_fusion.1.refs_7_.refs_6_), channel_id=1, source_target_pairs={{0,2},{2,0},{1,3},{3,1},{4,6},{6,4},{5,7},{7,5},{8,10},{10,8},{9,1... | collective-permute-start | bytes 1769480 | tf_op jit(solution)/shard_map/ppermute | solution.py:50
  106.4 9.6 %collective-permute-start.25 = (bf16[128,512]{1,0:T(8,128)(2,1)}, bf16[128,512]{1,0:T(8,128)(2,1)S(1)}, u32[]{:S(2)}, u32[]{:S(2)}) collective-permute-start(bf16[128,512]{1,0:T(8,128)(2,1)} %get-tuple-element.78), channel_id=1, source_target_pairs={{0,2},{2,0},{4,6},{6,4},{1,3},{3,1},{5,7},{7,5},{8,10},{10,8},{12,... | collective-permute-start | bytes 393224 | tf_op jit(solution)/shard_map/ppermute | solution.py:68
  107.2 9.4 %collective-permute-start.26 = (bf16[128,512]{1,0:T(8,128)(2,1)}, bf16[128,512]{1,0:T(8,128)(2,1)S(1)}, u32[]{:S(2)}, u32[]{:S(2)}) collective-permute-start(bf16[128,512]{1,0:T(8,128)(2,1)} %get-tuple-element.78), channel_id=1, source_target_pairs={{0,4},{2,6},{4,0},{6,2},{1,5},{3,7},{5,1},{7,3},{8,12},{10,14},{12... | collective-permute-start | bytes 393224 | tf_op jit(solution)/shard_map/ppermute | solution.py:68
  108.4 11.3 %collective-permute-start.27 = (bf16[128,512]{1,0:T(8,128)(2,1)}, bf16[128,512]{1,0:T(8,128)(2,1)S(1)}, u32[]{:S(2)}, u32[]{:S(2)}) collective-permute-start(bf16[128,512]{1,0:T(8,128)(2,1)} %get-tuple-element.78), channel_id=1, source_target_pairs={{0,6},{2,4},{4,2},{6,0},{1,7},{3,5},{5,3},{7,1},{8,14},{10,12},{12... | collective-permute-start | bytes 393224 | tf_op jit(solution)/shard_map/ppermute | solution.py:68
  109.2 18.1 %collective-permute-start.24 = (bf16[128,1536]{1,0:T(8,128)(2,1)S(1)}, bf16[128,1536]{1,0:T(8,128)(2,1)}, u32[]{:S(2)}, u32[]{:S(2)}) collective-permute-start(bf16[128,1536]{1,0:T(8,128)(2,1)S(1)} %copy-done.48), channel_id=1, source_target_pairs={{0,2},{2,0},{1,3},{3,1},{4,6},{6,4},{5,7},{7,5},{8,10},{10,8},{9,1... | collective-permute-start | bytes 1179656 | tf_op jit(solution)/shard_map/ppermute | solution.py:50
  116.1 17.6 %collective-permute-start.35 = (bf16[4,48,768]{2,1,0:T(8,128)(2,1)S(1)}, bf16[4,48,768]{2,1,0:T(8,128)(2,1)S(1)}, u32[]{:S(2)}, u32[]{:S(2)}) collective-permute-start(bf16[4,48,768]{2,1,0:T(8,128)(2,1)S(1)} %slice.290), channel_id=1, source_target_pairs={{0,2},{2,0},{1,3},{3,1},{4,6},{6,4},{5,7},{7,5},{8,10},{10,8},{9,1... | collective-permute-start | bytes 884744 | tf_op jit(solution)/shard_map/ppermute | solution.py:50
  121.5 15.4 %collective-permute-start.28 = (bf16[512,512]{1,0:T(8,128)(2,1)}, bf16[512,512]{1,0:T(8,128)(2,1)}, u32[]{:S(2)}, u32[]{:S(2)}) collective-permute-start(bf16[512,512]{1,0:T(8,128)(2,1)} %pad_maximum_fusion.2), channel_id=1, source_target_pairs={{0,1},{1,0},{2,3},{3,2},{4,5},{5,4},{6,7},{7,6},{8,9},{9,8},{10,11... | collective-permute-start | bytes 1572872 | tf_op jit(solution)/shard_map/ppermute | solution.py:50
  122.8 15.7 %collective-permute-start.36 = (bf16[4,48,1536]{2,1,0:T(8,128)(2,1)S(1)}, bf16[4,48,1536]{2,1,0:T(8,128)(2,1)S(1)}, u32[]{:S(2)}, u32[]{:S(2)}) collective-permute-start(bf16[4,48,1536]{2,1,0:T(8,128)(2,1)S(1)} %pad_maximum_fusion.1.refs_7_.refs_6_), channel_id=1, source_target_pairs={{0,1},{1,0},{2,3},{3,2},{4,5},{5,4},{6,7},{7,6},{8,9},{9,8},{10,11... | collective-permute-start | bytes 1769480 | tf_op jit(solution)/shard_map/ppermute | solution.py:50
  123.6 13.1 %collective-permute-start.34 = (bf16[4,48,768]{2,1,0:T(8,128)(2,1)}, bf16[4,48,768]{2,1,0:T(8,128)(2,1)}, u32[]{:S(2)}, u32[]{:S(2)}) collective-permute-start(bf16[4,48,768]{2,1,0:T(8,128)(2,1)} %slice.289), channel_id=1, source_target_pairs={{0,4},{4,0},{1,5},{5,1},{2,6},{6,2},{3,7},{7,3},{8,12},{12,8},{9,1... | collective-permute-start | bytes 884744 | tf_op jit(solution)/shard_map/ppermute | solution.py:50
  127.3 11.7 %collective-permute-start.37 = (bf16[4,48,1536]{2,1,0:T(8,128)(2,1)S(1)}, bf16[4,48,1536]{2,1,0:T(8,128)(2,1)S(1)}, u32[]{:S(2)}, u32[]{:S(2)}) collective-permute-start(bf16[4,48,1536]{2,1,0:T(8,128)(2,1)S(1)} %collective-permute-done.32.refs_8_.refs_7_), channel_id=1, source_target_pairs={{0,1},{1,0},{2,3},{3,2},{4,5},{5,4},{6,7},{7,6},{8,9},{9,8},{10,11... | collective-permute-start | bytes 1769480 | tf_op jit(solution)/shard_map/ppermute | solution.py:50
  150.3 26.8 %collective-permute-start.44 = (bf16[128,1536]{1,0:T(8,128)(2,1)}, bf16[128,1536]{1,0:T(8,128)(2,1)S(1)}, u32[]{:S(2)}, u32[]{:S(2)}) collective-permute-start(bf16[128,1536]{1,0:T(8,128)(2,1)} %get-tuple-element.84.refs_6_), channel_id=1, source_target_pairs={{0,16},{16,0},{1,17},{17,1},{2,18},{18,2},{3,19},{19,3},{4,20},{20... | collective-permute-start | bytes 1179656 | tf_op jit(solution)/shard_map/ppermute | solution.py:50
  155.4 22.9 %collective-permute-start.41 = (bf16[128,1536]{1,0:T(8,128)(2,1)}, bf16[128,1536]{1,0:T(8,128)(2,1)S(1)}, u32[]{:S(2)}, u32[]{:S(2)}) collective-permute-start(bf16[128,1536]{1,0:T(8,128)(2,1)} %get-tuple-element.84.refs_6_), channel_id=1, source_target_pairs={{0,2},{2,0},{1,3},{3,1},{4,6},{6,4},{5,7},{7,5},{8,10},{10,8},{9,1... | collective-permute-start | bytes 1179656 | tf_op jit(solution)/shard_map/ppermute | solution.py:50
  155.9 22.9 %collective-permute-start.42 = (bf16[128,1536]{1,0:T(8,128)(2,1)}, bf16[128,1536]{1,0:T(8,128)(2,1)S(1)}, u32[]{:S(2)}, u32[]{:S(2)}) collective-permute-start(bf16[128,1536]{1,0:T(8,128)(2,1)} %get-tuple-element.84.refs_6_), channel_id=1, source_target_pairs={{0,4},{4,0},{1,5},{5,1},{2,6},{6,2},{3,7},{7,3},{8,12},{12,8},{9,1... | collective-permute-start | bytes 1179656 | tf_op jit(solution)/shard_map/ppermute | solution.py:50
  163.1 11.5 %collective-permute-start.46 = (bf16[128,768]{1,0:T(8,128)(2,1)S(1)}, bf16[128,768]{1,0:T(8,128)(2,1)S(1)}, u32[]{:S(2)}, u32[]{:S(2)}) collective-permute-start(bf16[128,768]{1,0:T(8,128)(2,1)S(1)} %pad_maximum_fusion.4), channel_id=1, source_target_pairs={{0,4},{2,6},{4,0},{6,2},{1,5},{3,7},{5,1},{7,3},{8,12},{10,14},{12... | collective-permute-start | bytes 589832 | tf_op jit(solution)/shard_map/ppermute | solution.py:68
  178.3 15.7 %collective-permute-start.43 = (bf16[128,1536]{1,0:T(8,128)(2,1)S(1)}, bf16[128,1536]{1,0:T(8,128)(2,1)S(1)}, u32[]{:S(2)}, u32[]{:S(2)}) collective-permute-start(bf16[128,1536]{1,0:T(8,128)(2,1)S(1)} %collective-permute-done.41.refs_7_), channel_id=1, source_target_pairs={{0,4},{4,0},{1,5},{5,1},{2,6},{6,2},{3,7},{7,3},{8,12},{12,8},{9,1... | collective-permute-start | bytes 1179656 | tf_op jit(solution)/shard_map/ppermute | solution.py:50
  215.8 15.2 %collective-permute-start.53 = (bf16[256,1536]{1,0:T(8,128)(2,1)S(1)}, bf16[256,1536]{1,0:T(8,128)(2,1)S(1)}, u32[]{:S(2)}, u32[]{:S(2)}) collective-permute-start(bf16[256,1536]{1,0:T(8,128)(2,1)S(1)} %slice.398), channel_id=1, source_target_pairs={{0,2},{2,0},{1,3},{3,1},{4,6},{6,4},{5,7},{7,5},{8,10},{10,8},{9,1... | collective-permute-start | bytes 2359304 | tf_op jit(solution)/shard_map/ppermute | solution.py:50
  227.0 14.6 %collective-permute-start.51 = (bf16[256,1536]{1,0:T(8,128)(2,1)S(1)}, bf16[256,1536]{1,0:T(8,128)(2,1)S(1)}, u32[]{:S(2)}, u32[]{:S(2)}) collective-permute-start(bf16[256,1536]{1,0:T(8,128)(2,1)S(1)} %slice.399), channel_id=1, source_target_pairs={{0,4},{4,0},{1,5},{5,1},{2,6},{6,2},{3,7},{7,3},{8,12},{12,8},{9,1... | collective-permute-start | bytes 2359304 | tf_op jit(solution)/shard_map/ppermute | solution.py:50
  231.3 18.8 %collective-permute-start.54 = (bf16[128,1536]{1,0:T(8,128)(2,1)S(1)}, bf16[128,1536]{1,0:T(8,128)(2,1)S(1)}, u32[]{:S(2)}, u32[]{:S(2)}) collective-permute-start(bf16[128,1536]{1,0:T(8,128)(2,1)S(1)} %slice.403), channel_id=1, source_target_pairs={{0,4},{4,0},{1,5},{5,1},{2,6},{6,2},{3,7},{7,3},{8,12},{12,8},{9,1... | collective-permute-start | bytes 1179656 | tf_op jit(solution)/shard_map/ppermute | solution.py:50
  241.9 10.0 %collective-permute-start.52 = (bf16[128,1536]{1,0:T(8,128)(2,1)S(1)}, bf16[128,1536]{1,0:T(8,128)(2,1)S(1)}, u32[]{:S(2)}, u32[]{:S(2)}) collective-permute-start(bf16[128,1536]{1,0:T(8,128)(2,1)S(1)} %slice.404), channel_id=1, source_target_pairs={{0,2},{2,0},{1,3},{3,1},{4,6},{6,4},{5,7},{7,5},{8,10},{10,8},{9,1... | collective-permute-start | bytes 1179656 | tf_op jit(solution)/shard_map/ppermute | solution.py:50
  250.1 22.3 %collective-permute-start.57 = (bf16[128,1536]{1,0:T(8,128)(2,1)S(1)}, bf16[128,1536]{1,0:T(8,128)(2,1)}, u32[]{:S(2)}, u32[]{:S(2)}) collective-permute-start(bf16[128,1536]{1,0:T(8,128)(2,1)S(1)} %slice_add_fusion.4), channel_id=1, source_target_pairs={{0,16},{16,0},{1,17},{17,1},{2,18},{18,2},{3,19},{19,3},{4,20},{20... | collective-permute-start | bytes 1179656 | tf_op jit(solution)/shard_map/ppermute | solution.py:50
  270.0 36.3 %collective-permute-start.55 = (bf16[256,1536]{1,0:T(8,128)(2,1)}, bf16[256,1536]{1,0:T(8,128)(2,1)}, u32[]{:S(2)}, u32[]{:S(2)}) collective-permute-start(bf16[256,1536]{1,0:T(8,128)(2,1)} %slice.254), channel_id=1, source_target_pairs={{0,4},{4,0},{1,5},{5,1},{2,6},{6,2},{3,7},{7,3},{8,12},{12,8},{9,1... | collective-permute-start | bytes 2359304 | tf_op jit(solution)/shard_map/ppermute | solution.py:50
  271.9 35.8 %collective-permute-start.64 = (bf16[256,1536]{1,0:T(8,128)(2,1)}, bf16[256,1536]{1,0:T(8,128)(2,1)}, u32[]{:S(2)}, u32[]{:S(2)}) collective-permute-start(bf16[256,1536]{1,0:T(8,128)(2,1)} %slice.264), channel_id=1, source_target_pairs={{0,2},{2,0},{1,3},{3,1},{4,6},{6,4},{5,7},{7,5},{8,10},{10,8},{9,1... | collective-permute-start | bytes 2359304 | tf_op jit(solution)/shard_map/ppermute | solution.py:50
  279.3 13.8 %collective-permute-start.58 = (bf16[128,1536]{1,0:T(8,128)(2,1)}, bf16[128,1536]{1,0:T(8,128)(2,1)}, u32[]{:S(2)}, u32[]{:S(2)}) collective-permute-start(bf16[128,1536]{1,0:T(8,128)(2,1)} %get-tuple-element.95.refs_4_), channel_id=1, source_target_pairs={{0,2},{2,0},{4,6},{6,4},{1,3},{3,1},{5,7},{7,5},{8,10},{10,8},{12,... | collective-permute-start | bytes 1179656 | tf_op jit(solution)/shard_map/ppermute | solution.py:68
  280.3 12.8 %collective-permute-start.59 = (bf16[128,1536]{1,0:T(8,128)(2,1)}, bf16[128,1536]{1,0:T(8,128)(2,1)}, u32[]{:S(2)}, u32[]{:S(2)}) collective-permute-start(bf16[128,1536]{1,0:T(8,128)(2,1)} %get-tuple-element.95.refs_4_), channel_id=1, source_target_pairs={{0,4},{2,6},{4,0},{6,2},{1,5},{3,7},{5,1},{7,3},{8,12},{10,14},{12... | collective-permute-start | bytes 1179656 | tf_op jit(solution)/shard_map/ppermute | solution.py:68
  280.8 52.8 %collective-permute-start.74 = (bf16[128,1536]{1,0:T(8,128)(2,1)}, bf16[128,1536]{1,0:T(8,128)(2,1)}, u32[]{:S(2)}, u32[]{:S(2)}) collective-permute-start(bf16[128,1536]{1,0:T(8,128)(2,1)} %get-tuple-element.95.refs_4_), channel_id=1, source_target_pairs={{0,6},{2,4},{4,2},{6,0},{1,7},{3,5},{5,3},{7,1},{8,14},{10,12},{12... | collective-permute-start | bytes 1179656 | tf_op jit(solution)/shard_map/ppermute | solution.py:68
  294.5 15.4 %collective-permute-start.60 = (bf16[512,512]{1,0:T(8,128)(2,1)S(1)}, bf16[512,512]{1,0:T(8,128)(2,1)S(1)}, u32[]{:S(2)}, u32[]{:S(2)}) collective-permute-start(bf16[512,512]{1,0:T(8,128)(2,1)S(1)} %slice.400), channel_id=1, source_target_pairs={{0,1},{1,0},{2,3},{3,2},{4,5},{5,4},{6,7},{7,6},{8,9},{9,8},{10,11... | collective-permute-start | bytes 1572872 | tf_op jit(solution)/shard_map/ppermute | solution.py:50
  309.3 21.6 %collective-permute-start.65 = (bf16[128,1536]{1,0:T(8,128)(2,1)S(1)}, bf16[128,1536]{1,0:T(8,128)(2,1)S(1)}, u32[]{:S(2)}, u32[]{:S(2)}) collective-permute-start(bf16[128,1536]{1,0:T(8,128)(2,1)S(1)} %slice.401), channel_id=1, source_target_pairs={{0,4},{4,0},{1,5},{5,1},{2,6},{6,2},{3,7},{7,3},{8,12},{12,8},{9,1... | collective-permute-start | bytes 1179656 | tf_op jit(solution)/shard_map/ppermute | solution.py:50
  310.1 11.0 %collective-permute-start.61 = (bf16[128,512]{1,0:T(8,128)(2,1)S(1)}, bf16[128,512]{1,0:T(8,128)(2,1)S(1)}, u32[]{:S(2)}, u32[]{:S(2)}) collective-permute-start(bf16[128,512]{1,0:T(8,128)(2,1)S(1)} %get-tuple-element.200), channel_id=1, source_target_pairs={{0,2},{2,0},{4,6},{6,4},{1,3},{3,1},{5,7},{7,5},{8,10},{10,8},{12,... | collective-permute-start | bytes 393224 | tf_op jit(solution)/shard_map/ppermute | solution.py:68
  311.5 14.3 %collective-permute-start.62 = (bf16[128,512]{1,0:T(8,128)(2,1)S(1)}, bf16[128,512]{1,0:T(8,128)(2,1)S(1)}, u32[]{:S(2)}, u32[]{:S(2)}) collective-permute-start(bf16[128,512]{1,0:T(8,128)(2,1)S(1)} %get-tuple-element.199), channel_id=1, source_target_pairs={{0,4},{2,6},{4,0},{6,2},{1,5},{3,7},{5,1},{7,3},{8,12},{10,14},{12... | collective-permute-start | bytes 393224 | tf_op jit(solution)/shard_map/ppermute | solution.py:68
  311.7 14.1 %collective-permute-start.63 = (bf16[128,512]{1,0:T(8,128)(2,1)S(1)}, bf16[128,512]{1,0:T(8,128)(2,1)S(1)}, u32[]{:S(2)}, u32[]{:S(2)}) collective-permute-start(bf16[128,512]{1,0:T(8,128)(2,1)S(1)} %get-tuple-element.198), channel_id=1, source_target_pairs={{0,6},{2,4},{4,2},{6,0},{1,7},{3,5},{5,3},{7,1},{8,14},{10,12},{12... | collective-permute-start | bytes 393224 | tf_op jit(solution)/shard_map/ppermute | solution.py:68
  321.2 18.1 %collective-permute-start.56 = (bf16[128,1536]{1,0:T(8,128)(2,1)S(1)}, bf16[128,1536]{1,0:T(8,128)(2,1)}, u32[]{:S(2)}, u32[]{:S(2)}) collective-permute-start(bf16[128,1536]{1,0:T(8,128)(2,1)S(1)} %slice.402), channel_id=1, source_target_pairs={{0,2},{2,0},{1,3},{3,1},{4,6},{6,4},{5,7},{7,5},{8,10},{10,8},{9,1... | collective-permute-start | bytes 1179656 | tf_op jit(solution)/shard_map/ppermute | solution.py:50
  331.0 19.3 %collective-permute-start.66 = (bf16[128,1536]{1,0:T(8,128)(2,1)S(1)}, bf16[128,1536]{1,0:T(8,128)(2,1)S(1)}, u32[]{:S(2)}, u32[]{:S(2)}) collective-permute-start(bf16[128,1536]{1,0:T(8,128)(2,1)S(1)} %fusion.24), channel_id=1, source_target_pairs={{0,16},{16,0},{1,17},{17,1},{2,18},{18,2},{3,19},{19,3},{4,20},{20... | collective-permute-start | bytes 1179656 | tf_op jit(solution)/shard_map/ppermute | solution.py:50
  333.1 19.1 %collective-permute-start.67 = (bf16[144,2048]{1,0:T(8,128)(2,1)}, bf16[144,2048]{1,0:T(8,128)(2,1)S(1)}, u32[]{:S(2)}, u32[]{:S(2)}) collective-permute-start(bf16[144,2048]{1,0:T(8,128)(2,1)} %get-tuple-element.103.refs_4_), channel_id=1, source_target_pairs={{0,2},{2,0},{4,6},{6,4},{1,3},{3,1},{5,7},{7,5},{8,10},{10,8},{12,... | collective-permute-start | bytes 1769480 | tf_op jit(solution)/shard_map/ppermute | solution.py:68
  333.3 19.0 %collective-permute-start.68 = (bf16[144,2048]{1,0:T(8,128)(2,1)}, bf16[144,2048]{1,0:T(8,128)(2,1)S(1)}, u32[]{:S(2)}, u32[]{:S(2)}) collective-permute-start(bf16[144,2048]{1,0:T(8,128)(2,1)} %get-tuple-element.103.refs_4_), channel_id=1, source_target_pairs={{0,4},{2,6},{4,0},{6,2},{1,5},{3,7},{5,1},{7,3},{8,12},{10,14},{12... | collective-permute-start | bytes 1769480 | tf_op jit(solution)/shard_map/ppermute | solution.py:68
  333.6 26.4 %collective-permute-start.69 = (bf16[144,2048]{1,0:T(8,128)(2,1)}, bf16[144,2048]{1,0:T(8,128)(2,1)S(1)}, u32[]{:S(2)}, u32[]{:S(2)}) collective-permute-start(bf16[144,2048]{1,0:T(8,128)(2,1)} %get-tuple-element.103.refs_4_), channel_id=1, source_target_pairs={{0,6},{2,4},{4,2},{6,0},{1,7},{3,5},{5,3},{7,1},{8,14},{10,12},{12... | collective-permute-start | bytes 1769480 | tf_op jit(solution)/shard_map/ppermute | solution.py:68
  339.3 28.5 %collective-permute-start.75 = (bf16[192,1536]{1,0:T(8,128)(2,1)}, bf16[192,1536]{1,0:T(8,128)(2,1)S(1)}, u32[]{:S(2)}, u32[]{:S(2)}) collective-permute-start(bf16[192,1536]{1,0:T(8,128)(2,1)} %get-tuple-element.117), channel_id=1, source_target_pairs={{0,1},{1,0},{2,3},{3,2},{4,5},{5,4},{6,7},{7,6},{8,9},{9,8},{10,11... | collective-permute-start | bytes 1769480 | tf_op jit(solution)/shard_map/ppermute | solution.py:50
  368.7 34.2 %collective-permute-start.76 = (bf16[48,1536]{1,0:T(8,128)(2,1)}, bf16[48,1536]{1,0:T(8,128)(2,1)}, u32[]{:S(2)}, u32[]{:S(2)}) collective-permute-start(bf16[48,1536]{1,0:T(8,128)(2,1)} %get-tuple-element.195), channel_id=1, source_target_pairs={{0,24},{8,0},{16,8},{24,16},{1,25},{9,1},{17,9},{25,17},{2,26},{10... | collective-permute-start | bytes 442376 | tf_op jit(solution)/shard_map/ppermute | solution.py:50
  368.7 34.2 %collective-permute-start.77 = (bf16[48,1536]{1,0:T(8,128)(2,1)}, bf16[48,1536]{1,0:T(8,128)(2,1)}, u32[]{:S(2)}, u32[]{:S(2)}) collective-permute-start(bf16[48,1536]{1,0:T(8,128)(2,1)} %get-tuple-element.197), channel_id=1, source_target_pairs={{0,16},{8,24},{16,0},{24,8},{1,17},{9,25},{17,1},{25,9},{2,18},{10... | collective-permute-start | bytes 442376 | tf_op jit(solution)/shard_map/ppermute | solution.py:50
  371.3 29.0 %collective-permute-start.71 = (bf16[56,2048]{1,0:T(8,128)(2,1)}, bf16[56,2048]{1,0:T(8,128)(2,1)}, u32[]{:S(2)}, u32[]{:S(2)}) collective-permute-start(bf16[56,2048]{1,0:T(8,128)(2,1)} %get-tuple-element.192), channel_id=1, source_target_pairs={{0,24},{8,0},{16,8},{24,16},{1,25},{9,1},{17,9},{25,17},{2,26},{10... | collective-permute-start | bytes 688136 | tf_op jit(solution)/shard_map/ppermute | solution.py:50
  373.5 26.9 %collective-permute-start.72 = (bf16[56,2048]{1,0:T(8,128)(2,1)}, bf16[56,2048]{1,0:T(8,128)(2,1)}, u32[]{:S(2)}, u32[]{:S(2)}) collective-permute-start(bf16[56,2048]{1,0:T(8,128)(2,1)} %get-tuple-element.194), channel_id=1, source_target_pairs={{0,16},{8,24},{16,0},{24,8},{1,17},{9,25},{17,1},{25,9},{2,18},{10... | collective-permute-start | bytes 688136 | tf_op jit(solution)/shard_map/ppermute | solution.py:50
  373.5 26.9 %collective-permute-start.73 = (bf16[56,2048]{1,0:T(8,128)(2,1)}, bf16[56,2048]{1,0:T(8,128)(2,1)}, u32[]{:S(2)}, u32[]{:S(2)}) collective-permute-start(bf16[56,2048]{1,0:T(8,128)(2,1)} %get-tuple-element.193), channel_id=1, source_target_pairs={{0,8},{8,16},{16,24},{24,0},{1,9},{9,17},{17,25},{25,1},{2,10},{10... | collective-permute-start | bytes 688136 | tf_op jit(solution)/shard_map/ppermute | solution.py:50
  400.3 14.2 %collective-permute-start.78 = (bf16[48,1536]{1,0:T(8,128)(2,1)S(1)}, bf16[48,1536]{1,0:T(8,128)(2,1)}, u32[]{:S(2)}, u32[]{:S(2)}) collective-permute-start(bf16[48,1536]{1,0:T(8,128)(2,1)S(1)} %get-tuple-element.196), channel_id=1, source_target_pairs={{0,8},{8,16},{16,24},{24,0},{1,9},{9,17},{17,25},{25,1},{2,10},{10... | collective-permute-start | bytes 442376 | tf_op jit(solution)/shard_map/ppermute | solution.py:50
  (87 other events, 880.4 us)
Sparse Core Ops, SparseCore 0:
  11.6 122.2 all-gather.1
  269.2 113.5 reduce-scatter.1
